TPU v7x, 256 devices: a whole 4x4x8 slice. The times are simulated.
256 devices in a mesh: tile: 64 (over x, z, core), mem: 4 (over y).
Axes of the slice: x: 4, y: 4, z: 8, core: 2. Of those that a mesh axis runs over, the one named last changes fastest.
Arguments:
- ensemble: bfloat16 [909312, 512], P('tile', 'mem'), may hold values from -6 to 6
- obs_anom: bfloat16 [1024, 64, 512], P('tile', None, 'mem'), may hold values from -6 to 6
- inverses: bfloat16 [1024, 512, 512], P('tile', None, 'mem'), may hold values from -0.02 to 0.1
- innovations: bfloat16 [1024, 64, 512], P('tile', None, 'mem'), may hold values from -6 to 6
- precision: float32 [1024, 64], P('tile'), may hold values from 0.2 to 2
- obs_count: int32 [1024], P('tile'), may hold values from 16 to 64
- loc_tiles: int32 [1024, 4], P('tile'), may hold values from 0 to 63, all different within a row; in each aligned block of 16 rows (0 to 15, 16 to 31, ...) at most 2 rows name the same one
- taper_weight: float32 [1024, 4], P('tile'), may hold values from 0.25 to 1
Outputs:
- analysis: bfloat16 [909312, 512], P('tile', 'mem')
Inputs may be any that keep to these rules, and one draw needn't show every extreme that they name: `loc_tiles`: each block names 4 different tiles; among the 16 blocks of one tile's set, no tile is named more than 2 times, a bound that some block reaches.
All inputs are finite; a program needn't handle non-finite values.
Results may differ from a plain program's by a relative error of at most 0.024.
Values may be sent and summed in bfloat16 or wider, within the bound.
No kernel may reach another device: no remote copies, remote signals or barrier semaphores. Data moves between devices by JAX's collectives and lax.ppermute only.
A program may use at most 128 MiB of HBM per device.

v0:
```python
import math

import jax
import jax.numpy as jnp
from jax import lax
from jax.sharding import PartitionSpec as P


def per_device(
    ensemble, obs_anom, inverses, innovations, precision, obs_count, loc_tiles, taper_weight
):
    tile_count = lax.axis_size("tile")
    group_count = lax.axis_size("mem")
    nblock, obs_rows, part_width = obs_anom.shape
    members = part_width * group_count
    loc_count = loc_tiles.shape[1]
    capacity = min(
        nblock, max(2, (3 * nblock * loc_count + 2 * tile_count - 1) // (2 * tile_count))
    )
    slot_count = tile_count * capacity
    pairs = nblock * loc_count
    gain_terms = jnp.einsum("boj,bij->boi", obs_anom, inverses, preferred_element_type=jnp.float32)
    gain_rows = lax.psum_scatter(
        gain_terms.astype(jnp.bfloat16), "mem", scatter_dimension=2, tiled=True
    ).astype(jnp.float32)
    scaled = (
        (taper_weight[:, :, None, None] * gain_rows[:, None, :, :])
        .astype(jnp.bfloat16)
        .reshape(pairs, obs_rows, part_width)
    )
    position = lax.broadcasted_iota(jnp.int32, (nblock, obs_rows), 1)
    live_rows = (position < obs_count[:, None]).astype(jnp.float32)
    weighted = ((precision * live_rows)[:, :, None] * innovations.astype(jnp.float32)).astype(
        jnp.bfloat16
    )
    outgoing = lax.all_gather(weighted, "mem", axis=2, tiled=True)
    flat_loc = loc_tiles.reshape(pairs)
    tile_ids = lax.broadcasted_iota(jnp.int32, (pairs, tile_count), 1)
    tile_hits = (flat_loc[:, None] == tile_ids).astype(jnp.int32)
    before_count = jnp.cumsum(tile_hits, axis=0) - tile_hits
    slot_rank = jnp.sum(before_count * tile_hits, axis=1)
    slot_of = flat_loc * capacity + slot_rank
    slot_ids = lax.broadcasted_iota(jnp.int32, (slot_count, pairs), 0)
    chosen = (slot_of[None, :] == slot_ids).astype(jnp.int32)
    source = jnp.sum(chosen * lax.broadcasted_iota(jnp.int32, (slot_count, pairs), 1), axis=1)
    filled = jnp.sum(chosen, axis=1) > 0
    empty_value = jnp.zeros((), jnp.bfloat16)
    send_gain = jnp.where(filled[:, None, None], jnp.take(scaled, source, axis=0), empty_value)
    send_innov = jnp.where(
        filled[:, None, None], jnp.take(outgoing, source // loc_count, axis=0), empty_value
    )
    recv_gain, recv_innov = (
        lax.all_to_all(send_gain, "tile", split_axis=0, concat_axis=0, tiled=True),
        lax.all_to_all(send_innov, "tile", split_axis=0, concat_axis=0, tiled=True),
    )
    gain_flat = recv_gain.reshape(slot_count * obs_rows, part_width)
    contract = (((0,), (0,)), ((), ()))
    transform = lax.dot_general(
        gain_flat,
        recv_innov.reshape(slot_count * obs_rows, members),
        contract,
        preferred_element_type=jnp.float32,
    )
    transform = transform.astype(jnp.bfloat16)
    anomaly_scale = 1.0 / math.sqrt(members - 1)
    states = ensemble.astype(jnp.float32)
    row_sum = lax.psum(jnp.sum(states, axis=1).astype(jnp.bfloat16), "mem").astype(jnp.float32)
    row_mean = row_sum / members
    anomalies = ((states - row_mean[:, None]) * anomaly_scale).astype(jnp.bfloat16)
    partial_value = jnp.dot(anomalies, transform, preferred_element_type=jnp.float32)
    increment = lax.psum_scatter(
        partial_value.astype(jnp.bfloat16), "mem", scatter_dimension=1, tiled=True
    ).astype(jnp.float32)
    return (states + increment).astype(jnp.bfloat16)


def solution(mesh):
    return jax.shard_map(
        per_device,
        mesh=mesh,
        in_specs=(
            P("tile", "mem"),
            P("tile", None, "mem"),
            P("tile", None, "mem"),
            P("tile", None, "mem"),
            P("tile", None),
            P("tile"),
            P("tile", None),
            P("tile", None),
        ),
        out_specs=P("tile", "mem"),
        check_vma=False,
    )
```

profile of v0, /device:TPU:6, one launch (start us, length us, event | category | flops | bytes accessed | tf_op | source)
XLA Modules:
  0.0 484.7 jit_solution(210884598323344412)
XLA Ops:
  6.5 0.0 copy-start
  6.5 0.0 reduce-scatter.7.cloned.1.call-start
  6.5 1.6 copy-done
  8.1 1.8 convolution_convert_fusion.1
  9.9 0.0 copy-start.5
  9.9 2.0 copy.17
  12.0 2.3 reshape.122
  14.3 0.0 reduce-scatter.7.cloned.1.call-update
  14.3 0.0 copy-done.4
  14.3 0.1 copy.15
  14.4 0.1 reshape.104
  14.5 0.0 copy-done.5
  14.5 0.1 copy.16
  14.6 0.1 mul.57
  14.6 0.1 fusion.8
  14.7 0.1 reduce_window_sum.11
  14.8 0.2 select_reduce_fusion.1
  15.0 0.1 convert_reduce_fusion
  15.2 28.2 %reduce-scatter.7.cloned.1.call-done = bf16[128,1024]{1,0:T(8,128)(2,1)} async-done(((bf16[512,1024]{1,0:T(8,128)(2,1)}), bf16[128,1024]{1,0:T(8,128)(2,1)}) %reduce-scatter.7.cloned.1.call-update) | async-done | bytes 262160
  43.4 1.3 reshape.123
  44.7 0.5 copy.18
  45.2 0.2 fusion.6
  45.5 2.1 gather_fusion
  47.6 3.0 select_select_fusion.1
  50.6 10.8 %all-to-all-start = ((bf16[128,64,128]{2,1,0:T(8,128)(2,1)}), bf16[128,64,128]{2,1,0:T(8,128)(2,1)S(1)}, u32[]{:S(2)}, u32[]{:S(2)}) async-start(bf16[128,64,128]{2,1,0:T(8,128)(2,1)} %select_select_fusion.1), calls=%async_computation | async-start | bytes 4194304 | tf_op jit(solution)/shard_map/all_to_all | solution.py:53
  61.4 0.0 all-gather.2.cloned.1.call-start
  61.5 0.0 copy-done.3
  61.5 0.0 copy-done.6
  61.5 0.1 fusion.9
  61.6 0.0 copy-done.2
  61.6 0.9 multiply_convert_fusion
  62.5 0.0 all-gather.2.cloned.1.call-update
  62.5 29.5 %all-gather.2.cloned.1.call-done = bf16[16,64,512]{2,1,0:T(8,128)(2,1)} async-done(((bf16[16,64,128]{2,1,0:T(8,128)(2,1)}), bf16[16,64,512]{2,1,0:T(8,128)(2,1)}) %all-gather.2.cloned.1.call-update) | async-done | bytes 1048592 | tf_op jit(solution)/shard_map/all_gather | solution.py:36
  92.0 7.7 %gather_fusion.1 = bf16[128,64,512]{2,1,0:T(8,128)(2,1)} fusion(bf16[16,64,512]{2,1,0:T(8,128)(2,1)} %all-gather.2.cloned.1.call-done, s32[1024]{0:T(1024)S(1)} %pad_clamp_fusion), kind=kCustom, calls=%fused_computation.1 | custom fusion | bytes 16777728 | tf_op jit(solution)/shard_map/jit(_take)/gather | solution.py:50
  99.7 7.6 %select_select_fusion = bf16[128,64,512]{2,1,0:T(8,128)(2,1)} fusion(bf16[128,64,512]{2,1,0:T(8,128)(2,1)} %gather_fusion.1, pred[128]{0:T(512)(128)(4,1)S(1)} %get-tuple-element.7, pred[128]{0:T(512)(128)(4,1)S(1)} %get-tuple-element.11), kind=kLoop, calls=%fused_computation.5 | loop fusion | flops 8388608 | bytes 16777472 | tf_op jit(solution)/shard_map/jit(_where)/select_n | solution.py:49
  107.3 3.1 all-to-all-done
  110.4 8.3 %all-to-all-start.1 = ((bf16[128,64,512]{2,1,0:T(8,128)(2,1)}), bf16[128,64,512]{2,1,0:T(8,128)(2,1)}, u32[]{:S(2)}, u32[]{:S(2)}) async-start(bf16[128,64,512]{2,1,0:T(8,128)(2,1)} %select_select_fusion), calls=%async_computation.1 | async-start | bytes 16777216 | tf_op jit(solution)/shard_map/all_to_all | solution.py:54
  118.7 0.0 reduce-scatter.9.cloned.1.call-start
  118.7 3.4 reduce_sum.41
  122.1 15.8 %psum.7 = bf16[14208]{0:T(1024)(128)(2,1)S(1)} all-reduce(bf16[14208]{0:T(1024)(128)(2,1)S(1)} %reduce_sum.41), channel_id=1, replica_groups=mesh['tile'=64,'mem'=4] {'mem'}, use_global_device_ids=true, to_apply=%region_1.0 | all-reduce | flops 14208 | bytes 56832 | tf_op jit(solution)/shard_map/psum | solution.py:67
  138.0 164.0 %all-to-all-done.1 = bf16[128,64,512]{2,1,0:T(8,128)(2,1)} async-done(((bf16[128,64,512]{2,1,0:T(8,128)(2,1)}), bf16[128,64,512]{2,1,0:T(8,128)(2,1)}, u32[]{:S(2)}, u32[]{:S(2)}) %all-to-all-start.1) | async-done | bytes 8388640 | tf_op jit(solution)/shard_map/all_to_all | solution.py:54
  302.0 15.4 %convolution_convert_fusion = bf16[14208,512]{1,0:T(8,128)(2,1)} fusion(bf16[14208,128]{1,0:T(8,128)(2,1)} %param.8, f32[14208]{0:T(1024)S(1)} %convert_multiply_fusion, bf16[128,64,128]{2,1,0:T(8,128)(2,1)S(1)} %all-to-all-done, bf16[128,64,512]{2,1,0:T(8,128)(2,1)} %all-to-all-done.1), kind=kOutput, calls=%fused_computation.2 | convolution fusion | flops 2950627328 | bytes 28728832 | tf_op jit(solution)/shard_map/dot_general | solution.py:70
  317.4 18.5 %copy.19 = bf16[14208,512]{0,1:T(8,128)(2,1)} copy(bf16[14208,512]{1,0:T(8,128)(2,1)} %convolution_convert_fusion) | data formatting | bytes 29097984
  335.9 0.0 reduce-scatter.9.cloned.1.call-update
  335.9 131.2 %reduce-scatter.9.cloned.1.call-done = bf16[128,14208]{1,0:T(8,128)(2,1)} async-done(((bf16[512,14208]{1,0:T(8,128)(2,1)}), bf16[128,14208]{1,0:T(8,128)(2,1)}) %reduce-scatter.9.cloned.1.call-update) | async-done | bytes 3637264
  467.2 6.1 %copy.20 = bf16[14208,128]{1,0:T(8,128)(2,1)} copy(bf16[14208,128]{0,1:T(8,128)(2,1)} %bitcast.35) | data formatting | bytes 7274496
  473.3 4.8 fusion.2
  478.1 0.0 copy-done.1
  (12 shorter events, 0.1 us)
Async XLA Ops:
  6.5 1.6 copy-start
  6.5 36.8 %reduce-scatter.7.cloned.1.call-start = ((), (), s32[]{:S(2)}) async-start(), calls=%async_computation.5 | async-start | bytes 1310720
  9.9 4.4 copy-start.4
  9.9 4.5 copy-start.5
  47.6 13.9 %copy-start.3 = (f32[16,64]{1,0:T(8,128)S(1)}, f32[16,64]{1,0:T(8,128)}, u32[]{:S(2)}) copy-start(f32[16,64]{1,0:T(8,128)} %param.12) | copy-start | bytes 12292
  47.6 13.9 %copy-start.6 = (s32[16]{0:T(128)S(1)}, s32[16]{0:T(128)}, u32[]{:S(2)}) copy-start(s32[16]{0:T(128)} %param.13) | copy-start | bytes 196
  47.6 14.0 %copy-start.2 = (bf16[16,64,128]{2,1,0:T(8,128)(2,1)S(1)}, bf16[16,64,128]{2,1,0:T(8,128)(2,1)}, u32[]{:S(2)}) copy-start(bf16[16,64,128]{2,1,0:T(8,128)(2,1)} %param.11) | copy-start | bytes 786436
  50.6 59.7 %all-to-all-start = ((bf16[128,64,128]{2,1,0:T(8,128)(2,1)}), bf16[128,64,128]{2,1,0:T(8,128)(2,1)S(1)}, u32[]{:S(2)}, u32[]{:S(2)}) async-start(bf16[128,64,128]{2,1,0:T(8,128)(2,1)} %select_select_fusion.1), calls=%async_computation | async-start | bytes 4194304 | tf_op jit(solution)/shard_map/all_to_all | solution.py:53
  61.4 30.6 %all-gather.2.cloned.1.call-start = ((), (), s32[]{:S(2)}) async-start(), calls=%async_computation.4 | async-start | bytes 1310720 | tf_op jit(solution)/shard_map/all_gather | solution.py:36
  110.4 191.6 %all-to-all-start.1 = ((bf16[128,64,512]{2,1,0:T(8,128)(2,1)}), bf16[128,64,512]{2,1,0:T(8,128)(2,1)}, u32[]{:S(2)}, u32[]{:S(2)}) async-start(bf16[128,64,512]{2,1,0:T(8,128)(2,1)} %select_select_fusion), calls=%async_computation.1 | async-start | bytes 16777216 | tf_op jit(solution)/shard_map/all_to_all | solution.py:54
  118.7 348.5 %reduce-scatter.9.cloned.1.call-start = ((), (), s32[]{:S(2)}) async-start(), calls=%async_computation.6 | async-start | bytes 18186240
  467.2 11.0 %copy-start.1 = (bf16[16,512,128]{2,1,0:T(8,128)(2,1)S(1)}, bf16[16,512,128]{2,1,0:T(8,128)(2,1)}, u32[]{:S(2)}) copy-start(bf16[16,512,128]{2,1,0:T(8,128)(2,1)} %param.10) | copy-start | bytes 6291460
Sparse Core Ops, SparseCore 0:
  14.4 28.9 reduce-scatter.6
  64.2 27.7 all-gather.1
  336.1 131.0 reduce-scatter.8
where the time goes:
time: 487 us; the launch traced here: 485 us
  waiting for transfers between devices  356 us (73%)
  local copies, waits for them, and re-layouts  42.4 us (9%)
  other arithmetic  20.6 us (4%)
  starting transfers between devices  19.2 us (4%)
  matrix products  17.2 us (4%)
  blocking collectives  15.8 us (3%)
  between operations  13.3 us (3%)
    all_to_all x1, waiting for transfers between devices, per_device(): lax.all_to_all(send_innov, 'tile', split_axis=0, concat_axis=0, tiled=True)  164 us
    unnamed x5, waiting for transfers between devices  159 us
    unnamed x22, local copies, waits for them, and re-layouts  32.5 us
    all_gather x1, waiting for transfers between devices, per_device(): outgoing = lax.all_gather(weighted, 'mem', axis=2, tiled=True)  29.5 us
    psum x1, blocking collectives, per_device(): lax.psum(jnp.sum(states, axis=1).astype(jnp.bfloat16), 'mem')  15.8 us
    dot_general x1, matrix products, per_device(): jnp.dot(anomalies, transform, preferred_element_type=jnp.float32)  15.4 us
    all_to_all x1, starting transfers between devices, per_device(): lax.all_to_all(send_gain, 'tile', split_axis=0, concat_axis=0, tiled=True)  10.8 us
  transfers between devices with their start and end apart: 5, of which 5 were waited for; matrix products, arithmetic and copies ran while one was open for 4% of the time, Pallas kernels for 0%

commit v1 on v0

v1 whole, which is shorter than its diff:
```python
import functools
import math

import jax
import jax.numpy as jnp
from jax import lax
from jax.experimental import pallas as pl
from jax.experimental.pallas import tpu as pltpu
from jax.sharding import PartitionSpec as P

VMEM_LIMIT = 48 * 1024 * 1024
GROUPS = 4


def gain_kernel(q_ref, obs_ref, inv_ref, own_ref, s1_ref, s2_ref, s3_ref, rows_ref):
    quarter = own_ref.shape[1]
    q = q_ref[0]
    for k in range(obs_ref.shape[0]):
        rows_ref[...] = lax.dot_general(
            obs_ref[k], inv_ref[k], (((1,), (1,)), ((), ())), preferred_element_type=jnp.float32
        )
        for d, out_ref in enumerate((own_ref, s1_ref, s2_ref, s3_ref)):
            start = pl.multiple_of(lax.rem(q + d, GROUPS) * quarter, quarter)
            out_ref[k] = rows_ref[pl.ds(start, quarter), :].astype(out_ref.dtype)


def gain_parts(q, obs_anom, inverses):
    nblock, obs_rows, part = obs_anom.shape
    members = inverses.shape[1]
    quarter = obs_rows // GROUPS
    step = 4
    out = pl.BlockSpec((step, quarter, members), lambda i, q: (i, 0, 0))
    shape = (nblock, quarter, members)
    return pl.pallas_call(
        gain_kernel,
        grid_spec=pltpu.PrefetchScalarGridSpec(
            num_scalar_prefetch=1,
            grid=(nblock // step,),
            in_specs=[
                pl.BlockSpec((step, obs_rows, part), lambda i, q: (i, 0, 0)),
                pl.BlockSpec((step, members, part), lambda i, q: (i, 0, 0)),
            ],
            out_specs=[out] * GROUPS,
            scratch_shapes=[pltpu.VMEM((obs_rows, members), jnp.float32)],
        ),
        out_shape=[jax.ShapeDtypeStruct(shape, jnp.float32)]
        + [jax.ShapeDtypeStruct(shape, jnp.bfloat16)] * 3,
        compiler_params=pltpu.CompilerParams(vmem_limit_bytes=VMEM_LIMIT),
    )(q, obs_anom, inverses)


def scatter_slots(loc_ref, count_ref, out_ref, value_of):
    pairs = loc_ref.shape[0]
    tiles = count_ref.shape[0]
    capacity = out_ref.shape[0] // tiles
    out_ref[...] = jnp.zeros(out_ref.shape, out_ref.dtype)

    def clear(t, _):
        count_ref[t] = 0
        return 0

    def put(p, _):
        tile = loc_ref[p]
        rank = count_ref[tile]
        count_ref[tile] = rank + 1
        out_ref[tile * capacity + rank] = value_of(p)
        return 0

    lax.fori_loop(0, tiles, clear, 0)
    lax.fori_loop(0, pairs, put, 0)


def pack_innov_kernel(loc_count, q_ref, loc_ref, own_ref, r1_ref, r2_ref, r3_ref, out_ref, full_ref, count_ref):
    part = own_ref.shape[2]
    q = q_ref[0]
    for d, ref in enumerate((own_ref, r1_ref, r2_ref, r3_ref)):
        start = pl.multiple_of(lax.rem(q - d + GROUPS, GROUPS) * part, part)
        full_ref[:, :, pl.ds(start, part)] = ref[...]
    scatter_slots(loc_ref, count_ref, out_ref, lambda p: full_ref[p // loc_count])


def pack_gain_kernel(loc_count, loc_ref, taper_ref, own_ref, r1_ref, r2_ref, r3_ref, out_ref, full_ref, count_ref):
    full_ref[...] = (
        own_ref[...]
        + r1_ref[...].astype(jnp.float32)
        + r2_ref[...].astype(jnp.float32)
        + r3_ref[...].astype(jnp.float32)
    )
    scatter_slots(
        loc_ref,
        count_ref,
        out_ref,
        lambda p: (taper_ref[p] * full_ref[p // loc_count]).astype(out_ref.dtype),
    )


def pack(kernel, scalars, parts, full_dtype, members, tiles, slots):
    nblock, quarter, _ = parts[0].shape
    return pl.pallas_call(
        kernel,
        in_specs=[pl.BlockSpec(memory_space=pltpu.SMEM)] * len(scalars)
        + [pl.BlockSpec(memory_space=pltpu.VMEM)] * len(parts),
        out_specs=pl.BlockSpec(memory_space=pltpu.VMEM),
        out_shape=jax.ShapeDtypeStruct((slots, quarter, members), jnp.bfloat16),
        scratch_shapes=[
            pltpu.VMEM((nblock, quarter, members), full_dtype),
            pltpu.SMEM((tiles,), jnp.int32),
        ],
        compiler_params=pltpu.CompilerParams(vmem_limit_bytes=VMEM_LIMIT),
    )(*scalars, *parts)


def transform_kernel(q_ref, gain_ref, innov_ref, own_ref, s1_ref, s2_ref, s3_ref, total_ref):
    step = pl.program_id(0)
    part = own_ref.shape[1]

    @pl.when(step == 0)
    def _():
        total_ref[...] = jnp.zeros_like(total_ref)

    total_ref[...] += lax.dot_general(
        gain_ref[...], innov_ref[...], (((0,), (0,)), ((), ())), preferred_element_type=jnp.float32
    )

    @pl.when(step == pl.num_programs(0) - 1)
    def _():
        q = q_ref[0]
        for d, out_ref in enumerate((own_ref, s1_ref, s2_ref, s3_ref)):
            start = pl.multiple_of(lax.rem(q + d, GROUPS) * part, part)
            out_ref[...] = total_ref[:, pl.ds(start, part)].astype(out_ref.dtype)


def transform_parts(q, gain, innov):
    depth, members = gain.shape
    part = members // GROUPS
    step = 512
    out = pl.BlockSpec((members, part), lambda i, q: (0, 0))
    block = pl.BlockSpec((step, members), lambda i, q: (i, 0))
    return pl.pallas_call(
        transform_kernel,
        grid_spec=pltpu.PrefetchScalarGridSpec(
            num_scalar_prefetch=1,
            grid=(depth // step,),
            in_specs=[block, block],
            out_specs=[out] * GROUPS,
            scratch_shapes=[pltpu.VMEM((members, members), jnp.float32)],
        ),
        out_shape=[jax.ShapeDtypeStruct((members, part), jnp.float32)]
        + [jax.ShapeDtypeStruct((members, part), jnp.bfloat16)] * 3,
        compiler_params=pltpu.CompilerParams(vmem_limit_bytes=VMEM_LIMIT),
    )(q, gain, innov)


def update_kernel(
    half, order_ref, t0_ref, t1_ref, t2_ref, t3_ref, own_ref, a_ref, b_ref, oa_ref, ob_ref,
    out_ref, raw_ref, weights_ref, mean_ref, opp_ref,
):
    step = pl.program_id(0)
    part = own_ref.shape[1]
    members = t0_ref.shape[0]

    @pl.when(step == 0)
    def _():
        total = (
            t0_ref[...]
            + t1_ref[...].astype(jnp.float32)
            + t2_ref[...].astype(jnp.float32)
            + t3_ref[...].astype(jnp.float32)
        ).astype(jnp.bfloat16)
        raw_ref[...] = total.reshape(raw_ref.shape)
        mean_ref[...] = jnp.broadcast_to(
            jnp.sum(total.astype(jnp.float32), axis=0, keepdims=True) / members, mean_ref.shape
        )
        for k in range(GROUPS):
            weights_ref[pl.ds(k * part, part), :part] = raw_ref[order_ref[k]]
        weights_ref[:, part:] = jnp.ones((members, part), jnp.bfloat16)

    @pl.when(step < half)
    def _():
        opp_ref[...] = oa_ref[...]

    @pl.when(step >= half)
    def _():
        opp_ref[...] = ob_ref[...]

    own = own_ref[...]
    states = jnp.concatenate([own, a_ref[...], b_ref[...], opp_ref[...]], axis=1)
    both = jnp.dot(states, weights_ref[...], preferred_element_type=jnp.float32)
    increment = (both[:, :part] - both[:, part:] * mean_ref[0:1, :]) * (1.0 / math.sqrt(members - 1))
    out_ref[...] = (own.astype(jnp.float32) + increment).astype(out_ref.dtype)


def update(order, pieces, own, from_a, from_b, opp_a, opp_b):
    rows, part = own.shape
    members = pieces[0].shape[0]
    step = rows // 12
    half = 6
    whole = pl.BlockSpec((members, part), lambda i, o: (0, 0))
    block = pl.BlockSpec((step, part), lambda i, o: (i, 0))
    return pl.pallas_call(
        functools.partial(update_kernel, half),
        grid_spec=pltpu.PrefetchScalarGridSpec(
            num_scalar_prefetch=1,
            grid=(rows // step,),
            in_specs=[whole] * 4
            + [block] * 3
            + [
                pl.BlockSpec((step, part), lambda i, o: (jnp.minimum(i, half - 1), 0)),
                pl.BlockSpec((step, part), lambda i, o: (jnp.maximum(i - half, 0), 0)),
            ],
            out_specs=block,
            scratch_shapes=[
                pltpu.VMEM((GROUPS, part, part), jnp.bfloat16),
                pltpu.VMEM((members, 2 * part), jnp.bfloat16),
                pltpu.VMEM((8, part), jnp.float32),
                pltpu.VMEM((step, part), jnp.bfloat16),
            ],
        ),
        out_shape=jax.ShapeDtypeStruct((rows, part), jnp.bfloat16),
        compiler_params=pltpu.CompilerParams(vmem_limit_bytes=VMEM_LIMIT),
    )(order, *pieces, own, from_a, from_b, opp_a, opp_b)


def shift(x, d):
    return lax.ppermute(x, "mem", [(i, (i + d) % GROUPS) for i in range(GROUPS)])


def swap_a(x):
    return lax.ppermute(x, "mem", [(0, 1), (1, 0), (2, 3), (3, 2)])


def swap_b(x):
    return lax.ppermute(x, "mem", [(0, 3), (3, 0), (1, 2), (2, 1)])


def per_device(
    ensemble, obs_anom, inverses, innovations, precision, obs_count, loc_tiles, taper_weight
):
    tiles = lax.axis_size("tile")
    nblock, obs_rows, part = obs_anom.shape
    members = part * GROUPS
    rows = ensemble.shape[0]
    loc_count = loc_tiles.shape[1]
    quarter = obs_rows // GROUPS
    slots = tiles * 2
    q = lax.axis_index("mem").astype(jnp.int32)
    q1 = q.reshape(1)
    order = jnp.stack([q, q ^ 1, 3 - q, q ^ 2])
    loc = loc_tiles.reshape(nblock * loc_count)
    taper = taper_weight.reshape(nblock * loc_count)

    position = lax.broadcasted_iota(jnp.int32, (nblock, obs_rows), 1)
    live_rows = (position < obs_count[:, None]).astype(jnp.float32)
    weighted = ((precision * live_rows)[:, :, None] * innovations.astype(jnp.float32)).astype(
        jnp.bfloat16
    )

    def quarter_of(d):
        return lax.dynamic_slice_in_dim(weighted, ((q + d) & (GROUPS - 1)) * quarter, quarter, axis=1)

    innov_parts = [quarter_of(0)] + [shift(quarter_of(d), d) for d in (1, 2, 3)]
    g0, g1, g2, g3 = gain_parts(q1, obs_anom, inverses)
    g1, g2, g3 = shift(g1, 1), shift(g2, 2), shift(g3, 3)
    g1, g2, g3, states = lax.optimization_barrier((g1, g2, g3, ensemble))

    from_a, from_b = swap_a(states), swap_b(states)
    opp_a, opp_b = swap_b(from_a[: rows // 2]), swap_a(from_b[rows // 2 :])

    send_innov = pack(
        functools.partial(pack_innov_kernel, loc_count), (q1, loc), innov_parts, jnp.bfloat16,
        members, tiles, slots,
    )
    recv_innov = lax.all_to_all(send_innov, "tile", split_axis=0, concat_axis=0, tiled=True)
    send_gain = pack(
        functools.partial(pack_gain_kernel, loc_count), (loc, taper), [g0, g1, g2, g3],
        jnp.float32, members, tiles, slots,
    )
    recv_gain = lax.all_to_all(send_gain, "tile", split_axis=0, concat_axis=0, tiled=True)
    t0, t1, t2, t3 = transform_parts(
        q1,
        recv_gain.reshape(slots * quarter, members),
        recv_innov.reshape(slots * quarter, members),
    )
    pieces = [t0, shift(t1, 1), shift(t2, 2), shift(t3, 3)]
    return update(order, pieces, ensemble, from_a, from_b, opp_a, opp_b)


def solution(mesh):
    return jax.shard_map(
        per_device,
        mesh=mesh,
        in_specs=(
            P("tile", "mem"),
            P("tile", None, "mem"),
            P("tile", None, "mem"),
            P("tile", None, "mem"),
            P("tile", None),
            P("tile"),
            P("tile", None),
            P("tile", None),
        ),
        out_specs=P("tile", "mem"),
        check_vma=False,
    )
```

time: 487 us -> 196 us (0.40)
  waiting for transfers between devices: 356 us -> 120 us
  local copies, waits for them, and re-layouts: 42.4 us -> 9.7 us
  Pallas kernels: 0 us -> 23.9 us
  starting transfers between devices: 19.2 us -> 39.2 us
  other arithmetic: 20.6 us -> 2 us
  matrix products: 17.2 us -> 0 us
  blocking collectives: 15.8 us -> 0 us
  between operations: 13.3 us -> 0.13 us
    unnamed x5 -> x0, waiting for transfers between devices: 159 us -> none
    all_to_all x1, waiting for transfers between devices: 164 us -> 24 us  [per_device(): lax.all_to_all(send_innov, 'tile', split_axis=0, concat_axis=0, tiled=True)]
    ppermute x0 -> x13, waiting for transfers between devices: none -> 95.8 us  [the longest x9 52.6 us: shift(): lax.ppermute(x, 'mem', [(i, (i + d) % GROUPS) for i in range(GROUPS)])]
    all_gather x1 -> x0, waiting for transfers between devices: 29.5 us -> none  [per_device(): outgoing = lax.all_gather(weighted, 'mem', axis=2, tiled=True)]
    unnamed x22 -> x10, local copies, waits for them, and re-layouts: 32.5 us -> 3.82 us
    pallas_call x0 -> x5, Pallas kernels: none -> 23.9 us  [the longest x1 13.6 us: update(): pl.pallas_call(functools.partial(update_kernel, half), grid_spec=pltpu.Pr...]
    ppermute x0 -> x13, starting transfers between devices: none -> 18.6 us  [the longest x9 13 us: shift(): lax.ppermute(x, 'mem', [(i, (i + d) % GROUPS) for i in range(GROUPS)])]
    dot_general x2 -> x0, matrix products: 17.2 us -> none  [the longest x1 15.4 us: per_device(): jnp.dot(anomalies, transform, preferred_element_type=jnp.float32)]
  transfers between devices with their start and end apart: 5 -> 15, of which waited for: 5 -> 7; matrix products, arithmetic and copies ran while one was open for 4% -> 3% of each run, Pallas kernels for 0% -> 4%
where the time goes in v1:
time: 196 us; the launch traced here: 195 us
  waiting for transfers between devices  120 us (61%)
  starting transfers between devices  39.2 us (20%)
  Pallas kernels  23.9 us (12%)
  local copies, waits for them, and re-layouts  9.7 us (5%)
  other arithmetic  2 us (1%)
    ppermute x9, waiting for transfers between devices, shift(): lax.ppermute(x, 'mem', [(i, (i + d) % GROUPS) for i in range(GROUPS)])  52.6 us
    ppermute x2, waiting for transfers between devices, swap_b(): return lax.ppermute(x, 'mem', [(0, 3), (3, 0), (1, 2), (2, 1)])  43.3 us
    all_to_all x1, waiting for transfers between devices, per_device(): lax.all_to_all(send_innov, 'tile', split_axis=0, concat_axis=0, tiled=True)  24 us
    pallas_call x1, Pallas kernels, update(): pl.pallas_call(functools.partial(update_kernel, half), grid_spec=pltpu.Pr...  13.6 us
    ppermute x9, starting transfers between devices, shift(): lax.ppermute(x, 'mem', [(i, (i + d) % GROUPS) for i in range(GROUPS)])  13 us
    all_to_all x1, starting transfers between devices, per_device(): lax.all_to_all(send_innov, 'tile', split_axis=0, concat_axis=0, tiled=True)  12.3 us
    all_to_all x1, starting transfers between devices, per_device(): lax.all_to_all(send_gain, 'tile', split_axis=0, concat_axis=0, tiled=True)  8.31 us
    slice x2, local copies, waits for them, and re-layouts, per_device(): opp_a, opp_b = (swap_b(from_a[:rows // 2]), swap_a(from_b[rows // 2:]))  5.66 us
  transfers between devices with their start and end apart: 15, of which 7 were waited for; matrix products, arithmetic and copies ran while one was open for 3% of the time, Pallas kernels for 4%

profile of v1, /device:TPU:6, one launch (start us, length us, event | category | flops | bytes accessed | tf_op | source)
XLA Modules:
  0.0 194.8 jit_solution(11962900490314479827)
XLA Ops:
  0.0 0.8 fusion
  0.8 1.1 multiply_convert_fusion
  2.0 3.1 %collective-permute-start.5 = (bf16[16,16,128]{2,1,0:T(8,128)(2,1)S(1)}, bf16[16,16,128]{2,1,0:T(8,128)(2,1)S(1)}, u32[]{:S(2)}, u32[]{:S(2)}) collective-permute-start(bf16[16,16,128]{2,1,0:T(8,128)(2,1)S(1)} %get-tuple-element.29), channel_id=1, source_target_pairs={{0,3},{1,0},{2,1},{3,2},{4,7},{5,4},{6,5},{7,6},{8,11},{9,8},{10,9... | collective-permute-start | bytes 196616 | tf_op jit(solution)/shard_map/ppermute | solution.py:225
  5.1 0.6 collective-permute-start.4
  5.7 1.0 collective-permute-start.3
  6.7 0.8 copy.11
  7.4 0.1 reshape.15.loc_ref
  7.5 0.0 collective-permute-done.5.r3_ref
  7.5 3.4 %collective-permute-done.4.r2_ref = bf16[16,16,128]{2,1,0:T(8,128)(2,1)S(1)} collective-permute-done((bf16[16,16,128]{2,1,0:T(8,128)(2,1)S(1)}, bf16[16,16,128]{2,1,0:T(8,128)(2,1)S(1)}, u32[]{:S(2)}, u32[]{:S(2)}) %collective-permute-start.4) | collective-permute-done | bytes 65568 | tf_op jit(solution)/shard_map/ppermute | solution.py:225
  10.9 0.7 collective-permute-done.3.r1_ref
  11.5 1.9 shard_map.84
  13.4 0.0 copy-start
  13.4 1.4 copy-done
  14.8 12.3 %all-to-all-start.1 = ((bf16[128,16,512]{2,1,0:T(8,128)(2,1)}), bf16[128,16,512]{2,1,0:T(8,128)(2,1)S(1)}, u32[]{:S(2)}, u32[]{:S(2)}) async-start(bf16[128,16,512]{2,1,0:T(8,128)(2,1)} %copy-done), calls=%async_computation.1 | async-start | bytes 4194304 | tf_op jit(solution)/shard_map/all_to_all | solution.py:273
  27.2 0.0 copy-start.1
  27.2 1.6 copy-done.1
  28.7 1.3 shard_map.82
  30.0 0.1 collective-permute-start
  30.1 2.0 %collective-permute-start.1 = (bf16[16,16,512]{2,1,0:T(8,128)(2,1)S(1)}, bf16[16,16,512]{2,1,0:T(8,128)(2,1)S(1)}, u32[]{:S(2)}, u32[]{:S(2)}) collective-permute-start(bf16[16,16,512]{2,1,0:T(8,128)(2,1)S(1)} %get-tuple-element.19), channel_id=1, source_target_pairs={{0,2},{1,3},{2,0},{3,1},{4,6},{5,7},{6,4},{7,5},{8,10},{9,11},{10,... | collective-permute-start | bytes 786440 | tf_op jit(solution)/shard_map/ppermute | solution.py:225
  32.1 1.9 collective-permute-start.2
  34.1 11.2 %collective-permute-done.r1_ref = bf16[16,16,512]{2,1,0:T(8,128)(2,1)S(1)} collective-permute-done((bf16[16,16,512]{2,1,0:T(8,128)(2,1)S(1)}, bf16[16,16,512]{2,1,0:T(8,128)(2,1)S(1)}, u32[]{:S(2)}, u32[]{:S(2)}) %collective-permute-start) | collective-permute-done | bytes 262176 | tf_op jit(solution)/shard_map/ppermute | solution.py:225
  45.3 0.0 collective-permute-done.1.r2_ref
  45.3 0.6 collective-permute-done.2.r3_ref
  45.9 2.6 %collective-permute-start.10 = (bf16[14208,128]{1,0:T(8,128)(2,1)}, bf16[14208,128]{1,0:T(8,128)(2,1)}, u32[]{:S(2)}, u32[]{:S(2)}) collective-permute-start(bf16[14208,128]{1,0:T(8,128)(2,1)} %own_ref.1), channel_id=1, source_target_pairs={{0,3},{3,0},{1,2},{2,1},{4,7},{7,4},{5,6},{6,5},{8,11},{11,8},{9,1... | collective-permute-start | bytes 10911752 | tf_op jit(solution)/shard_map/ppermute | solution.py:233
  48.5 0.0 collective-permute-start.9
  48.5 0.1 copy.12
  48.6 0.1 reshape.16.taper_ref
  48.7 3.3 %shard_map.83 = bf16[128,16,512]{2,1,0:T(8,128)(2,1)} custom-call(s32[64]{0:T(128)S(1)} %reshape.15.loc_ref, f32[64]{0:T(128)S(1)} %reshape.16.taper_ref, f32[16,16,512]{2,1,0:T(8,128)S(1)} %get-tuple-element.17.own_ref, bf16[16,16,512]{2,1,0:T(8,128)(2,1)S(1)} %collective-permute-done.r1_ref, bf16[16,16,512]{2,1,0:T(8,128)(2,1)S(1)} %collective-permute-done.1.r2_ref, ...), custom_call_target="tpu_custom_call" | custom-call | tf_op jit(solution)/shard_map/pallas_call | solution.py:99
  52.1 24.0 %all-to-all-done.1 = bf16[128,16,512]{2,1,0:T(8,128)(2,1)S(1)} async-done(((bf16[128,16,512]{2,1,0:T(8,128)(2,1)}), bf16[128,16,512]{2,1,0:T(8,128)(2,1)S(1)}, u32[]{:S(2)}, u32[]{:S(2)}) %all-to-all-start.1) | async-done | bytes 2097184 | tf_op jit(solution)/shard_map/all_to_all | solution.py:273
  76.1 8.3 %all-to-all-start = ((bf16[128,16,512]{2,1,0:T(8,128)(2,1)}), bf16[128,16,512]{2,1,0:T(8,128)(2,1)}, u32[]{:S(2)}, u32[]{:S(2)}) async-start(bf16[128,16,512]{2,1,0:T(8,128)(2,1)} %shard_map.83), calls=%async_computation | async-start | bytes 4194304 | tf_op jit(solution)/shard_map/all_to_all | solution.py:278
  84.4 43.3 %collective-permute-done.10.b_ref = bf16[14208,128]{1,0:T(8,128)(2,1)} collective-permute-done((bf16[14208,128]{1,0:T(8,128)(2,1)}, bf16[14208,128]{1,0:T(8,128)(2,1)}, u32[]{:S(2)}, u32[]{:S(2)}) %collective-permute-start.10) | collective-permute-done | bytes 3637280 | tf_op jit(solution)/shard_map/ppermute | solution.py:233
  127.7 2.8 %slice.9 = bf16[7104,128]{1,0:T(8,128)(2,1)} slice(bf16[14208,128]{1,0:T(8,128)(2,1)} %collective-permute-done.10.b_ref), slice={[7104:14208], [0:128]} | slice | bytes 3637248 | tf_op jit(solution)/shard_map/slice | solution.py:267
  130.5 0.0 collective-permute-start.12
  130.5 0.0 collective-permute-done.9.a_ref
  130.5 2.8 %slice.8 = bf16[7104,128]{1,0:T(8,128)(2,1)} slice(bf16[14208,128]{1,0:T(8,128)(2,1)} %collective-permute-done.9.a_ref), slice={[0:7104], [0:128]} | slice | bytes 3637248 | tf_op jit(solution)/shard_map/slice | solution.py:267
  133.3 3.0 %collective-permute-start.11 = (bf16[7104,128]{1,0:T(8,128)(2,1)}, bf16[7104,128]{1,0:T(8,128)(2,1)}, u32[]{:S(2)}, u32[]{:S(2)}) collective-permute-start(bf16[7104,128]{1,0:T(8,128)(2,1)} %slice.8), channel_id=1, source_target_pairs={{0,3},{3,0},{1,2},{2,1},{4,7},{7,4},{5,6},{6,5},{8,11},{11,8},{9,1... | collective-permute-start | bytes 5455880 | tf_op jit(solution)/shard_map/ppermute | solution.py:233
  136.3 0.0 all-to-all-done
  136.3 3.8 %shard_map.85 = (f32[512,128]{1,0:T(8,128)S(1)}, bf16[512,128]{1,0:T(8,128)(2,1)S(1)}, bf16[512,128]{1,0:T(8,128)(2,1)S(1)}, bf16[512,128]{1,0:T(8,128)(2,1)S(1)}) custom-call(s32[1]{0:T(128)} %bitcast.q_ref, bf16[2048,512]{1,0:T(8,128)(2,1)} %bitcast.4.gain_ref, bf16[2048,512]{1,0:T(8,128)(2,1)S(1)} %bitcast.6), custom_call_target="tpu_custom_call" | custom-call | tf_op jit(solution)/shard_map/pallas_call | solution.py:139
  140.1 1.5 collective-permute-start.6
  141.6 0.3 collective-permute-start.7
  141.9 2.4 %collective-permute-start.8 = (bf16[512,128]{1,0:T(8,128)(2,1)S(1)}, bf16[512,128]{1,0:T(8,128)(2,1)S(1)}, u32[]{:S(2)}, u32[]{:S(2)}) collective-permute-start(bf16[512,128]{1,0:T(8,128)(2,1)S(1)} %get-tuple-element.27), channel_id=1, source_target_pairs={{0,3},{1,0},{2,1},{3,2},{4,7},{5,4},{6,5},{7,6},{8,11},{9,8},{10,9... | collective-permute-start | bytes 393224 | tf_op jit(solution)/shard_map/ppermute | solution.py:225
  144.3 0.1 pad_add_fusion.order_ref
  144.4 36.7 %collective-permute-done.6.t1_ref = bf16[512,128]{1,0:T(8,128)(2,1)S(1)} collective-permute-done((bf16[512,128]{1,0:T(8,128)(2,1)S(1)}, bf16[512,128]{1,0:T(8,128)(2,1)S(1)}, u32[]{:S(2)}, u32[]{:S(2)}) %collective-permute-start.6) | collective-permute-done | bytes 131104 | tf_op jit(solution)/shard_map/ppermute | solution.py:225
  181.1 0.0 collective-permute-done.7.t2_ref
  181.1 0.0 collective-permute-done.8.t3_ref
  181.1 0.0 collective-permute-done.12.ob_ref
  181.1 0.0 collective-permute-done.11.oa_ref
  181.1 13.6 %shard_map.86 = bf16[14208,128]{1,0:T(8,128)(2,1)} custom-call(s32[4]{0:T(128)S(1)} %pad_add_fusion.order_ref, f32[512,128]{1,0:T(8,128)S(1)} %get-tuple-element.24.t0_ref, bf16[512,128]{1,0:T(8,128)(2,1)S(1)} %collective-permute-done.6.t1_ref, bf16[512,128]{1,0:T(8,128)(2,1)S(1)} %collective-permute-done.7.t2_ref, ...), custom_call_target="tpu_custom_call" | custom-call | tf_op jit(solution)/shard_map/pallas_call | solution.py:200
  (5 shorter events, 0.1 us)
Async XLA Ops:
  2.0 5.5 %collective-permute-start.5 = (bf16[16,16,128]{2,1,0:T(8,128)(2,1)S(1)}, bf16[16,16,128]{2,1,0:T(8,128)(2,1)S(1)}, u32[]{:S(2)}, u32[]{:S(2)}) collective-permute-start(bf16[16,16,128]{2,1,0:T(8,128)(2,1)S(1)} %get-tuple-element.29), channel_id=1, source_target_pairs={{0,3},{1,0},{2,1},{3,2},{4,7},{5,4},{6,5},{7,6},{8,11},{9,8},{10,9... | collective-permute-start | bytes 196616 | tf_op jit(solution)/shard_map/ppermute | solution.py:225
  5.1 5.8 %collective-permute-start.4 = (bf16[16,16,128]{2,1,0:T(8,128)(2,1)S(1)}, bf16[16,16,128]{2,1,0:T(8,128)(2,1)S(1)}, u32[]{:S(2)}, u32[]{:S(2)}) collective-permute-start(bf16[16,16,128]{2,1,0:T(8,128)(2,1)S(1)} %get-tuple-element.30), channel_id=1, source_target_pairs={{0,2},{1,3},{2,0},{3,1},{4,6},{5,7},{6,4},{7,5},{8,10},{9,11},{10,... | collective-permute-start | bytes 196616 | tf_op jit(solution)/shard_map/ppermute | solution.py:225
  5.7 5.8 %collective-permute-start.3 = (bf16[16,16,128]{2,1,0:T(8,128)(2,1)S(1)}, bf16[16,16,128]{2,1,0:T(8,128)(2,1)S(1)}, u32[]{:S(2)}, u32[]{:S(2)}) collective-permute-start(bf16[16,16,128]{2,1,0:T(8,128)(2,1)S(1)} %get-tuple-element.31), channel_id=1, source_target_pairs={{0,1},{1,2},{2,3},{3,0},{4,5},{5,6},{6,7},{7,4},{8,9},{9,10},{10,1... | collective-permute-start | bytes 196616 | tf_op jit(solution)/shard_map/ppermute | solution.py:225
  13.4 1.4 copy-start
  14.8 12.3 %copy-start.2 = (bf16[16,64,128]{2,1,0:T(8,128)(2,1)S(1)}, bf16[16,64,128]{2,1,0:T(8,128)(2,1)}, u32[]{:S(2)}) copy-start(bf16[16,64,128]{2,1,0:T(8,128)(2,1)} %obs_ref.1) | copy-start | bytes 786436
  14.8 61.3 %all-to-all-start.1 = ((bf16[128,16,512]{2,1,0:T(8,128)(2,1)}), bf16[128,16,512]{2,1,0:T(8,128)(2,1)S(1)}, u32[]{:S(2)}, u32[]{:S(2)}) async-start(bf16[128,16,512]{2,1,0:T(8,128)(2,1)} %copy-done), calls=%async_computation.1 | async-start | bytes 4194304 | tf_op jit(solution)/shard_map/all_to_all | solution.py:273
  27.2 1.6 copy-start.1
  28.7 19.8 %copy-start.3 = (f32[16,4]{0,1:T(4,128)S(1)}, f32[16,4]{0,1:T(4,128)}, u32[]{:S(2)}) copy-start(f32[16,4]{0,1:T(4,128)} %param.15) | copy-start | bytes 772
  30.0 15.2 %collective-permute-start = (bf16[16,16,512]{2,1,0:T(8,128)(2,1)S(1)}, bf16[16,16,512]{2,1,0:T(8,128)(2,1)S(1)}, u32[]{:S(2)}, u32[]{:S(2)}) collective-permute-start(bf16[16,16,512]{2,1,0:T(8,128)(2,1)S(1)} %get-tuple-element.18), channel_id=1, source_target_pairs={{0,1},{1,2},{2,3},{3,0},{4,5},{5,6},{6,7},{7,4},{8,9},{9,10},{10,1... | collective-permute-start | bytes 786440 | tf_op jit(solution)/shard_map/ppermute | solution.py:225
  30.1 15.2 %collective-permute-start.1 = (bf16[16,16,512]{2,1,0:T(8,128)(2,1)S(1)}, bf16[16,16,512]{2,1,0:T(8,128)(2,1)S(1)}, u32[]{:S(2)}, u32[]{:S(2)}) collective-permute-start(bf16[16,16,512]{2,1,0:T(8,128)(2,1)S(1)} %get-tuple-element.19), channel_id=1, source_target_pairs={{0,2},{1,3},{2,0},{3,1},{4,6},{5,7},{6,4},{7,5},{8,10},{9,11},{10,... | collective-permute-start | bytes 786440 | tf_op jit(solution)/shard_map/ppermute | solution.py:225
  32.1 13.8 %collective-permute-start.2 = (bf16[16,16,512]{2,1,0:T(8,128)(2,1)S(1)}, bf16[16,16,512]{2,1,0:T(8,128)(2,1)S(1)}, u32[]{:S(2)}, u32[]{:S(2)}) collective-permute-start(bf16[16,16,512]{2,1,0:T(8,128)(2,1)S(1)} %get-tuple-element.20), channel_id=1, source_target_pairs={{0,3},{1,0},{2,1},{3,2},{4,7},{5,4},{6,5},{7,6},{8,11},{9,8},{10,9... | collective-permute-start | bytes 786440 | tf_op jit(solution)/shard_map/ppermute | solution.py:225
  45.9 81.8 %collective-permute-start.10 = (bf16[14208,128]{1,0:T(8,128)(2,1)}, bf16[14208,128]{1,0:T(8,128)(2,1)}, u32[]{:S(2)}, u32[]{:S(2)}) collective-permute-start(bf16[14208,128]{1,0:T(8,128)(2,1)} %own_ref.1), channel_id=1, source_target_pairs={{0,3},{3,0},{1,2},{2,1},{4,7},{7,4},{5,6},{6,5},{8,11},{11,8},{9,1... | collective-permute-start | bytes 10911752 | tf_op jit(solution)/shard_map/ppermute | solution.py:233
  48.5 82.0 %collective-permute-start.9 = (bf16[14208,128]{1,0:T(8,128)(2,1)}, bf16[14208,128]{1,0:T(8,128)(2,1)}, u32[]{:S(2)}, u32[]{:S(2)}) collective-permute-start(bf16[14208,128]{1,0:T(8,128)(2,1)} %own_ref.1), channel_id=1, source_target_pairs={{0,1},{1,0},{2,3},{3,2},{4,5},{5,4},{6,7},{7,6},{8,9},{9,8},{10,11... | collective-permute-start | bytes 10911752 | tf_op jit(solution)/shard_map/ppermute | solution.py:229
  76.1 60.2 %all-to-all-start = ((bf16[128,16,512]{2,1,0:T(8,128)(2,1)}), bf16[128,16,512]{2,1,0:T(8,128)(2,1)}, u32[]{:S(2)}, u32[]{:S(2)}) async-start(bf16[128,16,512]{2,1,0:T(8,128)(2,1)} %shard_map.83), calls=%async_computation | async-start | bytes 4194304 | tf_op jit(solution)/shard_map/all_to_all | solution.py:278
  130.5 50.6 %collective-permute-start.12 = (bf16[7104,128]{1,0:T(8,128)(2,1)}, bf16[7104,128]{1,0:T(8,128)(2,1)}, u32[]{:S(2)}, u32[]{:S(2)}) collective-permute-start(bf16[7104,128]{1,0:T(8,128)(2,1)} %slice.9), channel_id=1, source_target_pairs={{0,1},{1,0},{2,3},{3,2},{4,5},{5,4},{6,7},{7,6},{8,9},{9,8},{10,11... | collective-permute-start | bytes 5455880 | tf_op jit(solution)/shard_map/ppermute | solution.py:229
  133.3 47.8 %collective-permute-start.11 = (bf16[7104,128]{1,0:T(8,128)(2,1)}, bf16[7104,128]{1,0:T(8,128)(2,1)}, u32[]{:S(2)}, u32[]{:S(2)}) collective-permute-start(bf16[7104,128]{1,0:T(8,128)(2,1)} %slice.8), channel_id=1, source_target_pairs={{0,3},{3,0},{1,2},{2,1},{4,7},{7,4},{5,6},{6,5},{8,11},{11,8},{9,1... | collective-permute-start | bytes 5455880 | tf_op jit(solution)/shard_map/ppermute | solution.py:233
  140.1 41.0 %collective-permute-start.6 = (bf16[512,128]{1,0:T(8,128)(2,1)S(1)}, bf16[512,128]{1,0:T(8,128)(2,1)S(1)}, u32[]{:S(2)}, u32[]{:S(2)}) collective-permute-start(bf16[512,128]{1,0:T(8,128)(2,1)S(1)} %get-tuple-element.25), channel_id=1, source_target_pairs={{0,1},{1,2},{2,3},{3,0},{4,5},{5,6},{6,7},{7,4},{8,9},{9,10},{10,1... | collective-permute-start | bytes 393224 | tf_op jit(solution)/shard_map/ppermute | solution.py:225
  141.6 39.6 %collective-permute-start.7 = (bf16[512,128]{1,0:T(8,128)(2,1)S(1)}, bf16[512,128]{1,0:T(8,128)(2,1)S(1)}, u32[]{:S(2)}, u32[]{:S(2)}) collective-permute-start(bf16[512,128]{1,0:T(8,128)(2,1)S(1)} %get-tuple-element.26), channel_id=1, source_target_pairs={{0,2},{1,3},{2,0},{3,1},{4,6},{5,7},{6,4},{7,5},{8,10},{9,11},{10,... | collective-permute-start | bytes 393224 | tf_op jit(solution)/shard_map/ppermute | solution.py:225
  141.9 39.2 %collective-permute-start.8 = (bf16[512,128]{1,0:T(8,128)(2,1)S(1)}, bf16[512,128]{1,0:T(8,128)(2,1)S(1)}, u32[]{:S(2)}, u32[]{:S(2)}) collective-permute-start(bf16[512,128]{1,0:T(8,128)(2,1)S(1)} %get-tuple-element.27), channel_id=1, source_target_pairs={{0,3},{1,0},{2,1},{3,2},{4,7},{5,4},{6,5},{7,6},{8,11},{9,8},{10,9... | collective-permute-start | bytes 393224 | tf_op jit(solution)/shard_map/ppermute | solution.py:225

commit v2 on v1

--- a/solution.py
+++ b/solution.py
@@ -12,41 +12,65 @@
 GROUPS = 4
 
 
-def gain_kernel(q_ref, obs_ref, inv_ref, own_ref, s1_ref, s2_ref, s3_ref, rows_ref):
-    quarter = own_ref.shape[1]
+def first_kernel(
+    q_ref, obs_ref, inv_ref, innov_ref, precision_ref, count_ref,
+    g0_ref, g1_ref, g2_ref, g3_ref, w0_ref, w1_ref, w2_ref, w3_ref, rows_ref, live_ref,
+):
+    quarter = g0_ref.shape[1]
+    obs_rows, part = innov_ref.shape[1:]
+    blocks = obs_ref.shape[0]
     q = q_ref[0]
-    for k in range(obs_ref.shape[0]):
+    step = pl.program_id(0)
+    starts = [pl.multiple_of(lax.rem(q + d, GROUPS) * quarter, quarter) for d in range(GROUPS)]
+    position = lax.broadcasted_iota(jnp.int32, (obs_rows, part), 0)
+    for k in range(blocks):
         rows_ref[...] = lax.dot_general(
             obs_ref[k], inv_ref[k], (((1,), (1,)), ((), ())), preferred_element_type=jnp.float32
         )
-        for d, out_ref in enumerate((own_ref, s1_ref, s2_ref, s3_ref)):
-            start = pl.multiple_of(lax.rem(q + d, GROUPS) * quarter, quarter)
-            out_ref[k] = rows_ref[pl.ds(start, quarter), :].astype(out_ref.dtype)
-
-
-def gain_parts(q, obs_anom, inverses):
+        block = step * blocks + k
+        scale = jnp.broadcast_to(precision_ref[pl.ds(block, 1), :], (part, obs_rows)).T
+        live_ref[...] = jnp.where(
+            position < count_ref[block], scale * innov_ref[k].astype(jnp.float32), 0.0
+        )
+        for start, g_ref, w_ref in zip(
+            starts, (g0_ref, g1_ref, g2_ref, g3_ref), (w0_ref, w1_ref, w2_ref, w3_ref)
+        ):
+            g_ref[k] = rows_ref[pl.ds(start, quarter), :].astype(g_ref.dtype)
+            w_ref[k] = live_ref[pl.ds(start, quarter), :].astype(w_ref.dtype)
+
+
+def first_parts(q, obs_anom, inverses, innovations, precision, obs_count):
     nblock, obs_rows, part = obs_anom.shape
     members = inverses.shape[1]
     quarter = obs_rows // GROUPS
     step = 4
-    out = pl.BlockSpec((step, quarter, members), lambda i, q: (i, 0, 0))
-    shape = (nblock, quarter, members)
+    g_out = pl.BlockSpec((step, quarter, members), lambda i, q: (i, 0, 0))
+    w_out = pl.BlockSpec((step, quarter, part), lambda i, q: (i, 0, 0))
+    g_shape = (nblock, quarter, members)
+    rows = pl.BlockSpec((step, obs_rows, part), lambda i, q: (i, 0, 0))
     return pl.pallas_call(
-        gain_kernel,
+        first_kernel,
         grid_spec=pltpu.PrefetchScalarGridSpec(
             num_scalar_prefetch=1,
             grid=(nblock // step,),
             in_specs=[
-                pl.BlockSpec((step, obs_rows, part), lambda i, q: (i, 0, 0)),
+                rows,
                 pl.BlockSpec((step, members, part), lambda i, q: (i, 0, 0)),
+                rows,
+                pl.BlockSpec((nblock, obs_rows), lambda i, q: (0, 0)),
+                pl.BlockSpec(memory_space=pltpu.SMEM),
             ],
-            out_specs=[out] * GROUPS,
-            scratch_shapes=[pltpu.VMEM((obs_rows, members), jnp.float32)],
+            out_specs=[g_out] * GROUPS + [w_out] * GROUPS,
+            scratch_shapes=[
+                pltpu.VMEM((obs_rows, members), jnp.float32),
+                pltpu.VMEM((obs_rows, part), jnp.float32),
+            ],
         ),
-        out_shape=[jax.ShapeDtypeStruct(shape, jnp.float32)]
-        + [jax.ShapeDtypeStruct(shape, jnp.bfloat16)] * 3,
+        out_shape=[jax.ShapeDtypeStruct(g_shape, jnp.float32)]
+        + [jax.ShapeDtypeStruct(g_shape, jnp.bfloat16)] * 3
+        + [jax.ShapeDtypeStruct((nblock, quarter, part), jnp.bfloat16)] * 4,
         compiler_params=pltpu.CompilerParams(vmem_limit_bytes=VMEM_LIMIT),
-    )(q, obs_anom, inverses)
+    )(q, obs_anom, inverses, innovations, precision, obs_count)
 
 
 def scatter_slots(loc_ref, count_ref, out_ref, value_of):
@@ -152,10 +176,11 @@
 
 
 def update_kernel(
-    half, order_ref, t0_ref, t1_ref, t2_ref, t3_ref, own_ref, a_ref, b_ref, oa_ref, ob_ref,
-    out_ref, raw_ref, weights_ref, mean_ref, opp_ref,
+    order_ref, t0_ref, t1_ref, t2_ref, t3_ref, own_ref, a1_ref, a2_ref, b1_ref, b2_ref, o1_ref, o2_ref,
+    out_ref, raw_ref, weights_ref, mean_ref, states_ref,
 ):
     step = pl.program_id(0)
+    half = pl.num_programs(0) // 2
     part = own_ref.shape[1]
     members = t0_ref.shape[0]
 
@@ -175,50 +200,49 @@
             weights_ref[pl.ds(k * part, part), :part] = raw_ref[order_ref[k]]
         weights_ref[:, part:] = jnp.ones((members, part), jnp.bfloat16)
 
+    states_ref[:, :part] = own_ref[...]
+
     @pl.when(step < half)
     def _():
-        opp_ref[...] = oa_ref[...]
+        for k, ref in enumerate((a1_ref, b1_ref, o1_ref)):
+            states_ref[:, pl.ds((k + 1) * part, part)] = ref[...]
 
     @pl.when(step >= half)
     def _():
-        opp_ref[...] = ob_ref[...]
-
-    own = own_ref[...]
-    states = jnp.concatenate([own, a_ref[...], b_ref[...], opp_ref[...]], axis=1)
-    both = jnp.dot(states, weights_ref[...], preferred_element_type=jnp.float32)
+        for k, ref in enumerate((a2_ref, b2_ref, o2_ref)):
+            states_ref[:, pl.ds((k + 1) * part, part)] = ref[...]
+
+    both = jnp.dot(states_ref[...], weights_ref[...], preferred_element_type=jnp.float32)
     increment = (both[:, :part] - both[:, part:] * mean_ref[0:1, :]) * (1.0 / math.sqrt(members - 1))
-    out_ref[...] = (own.astype(jnp.float32) + increment).astype(out_ref.dtype)
-
-
-def update(order, pieces, own, from_a, from_b, opp_a, opp_b):
+    out_ref[...] = (own_ref[...].astype(jnp.float32) + increment).astype(out_ref.dtype)
+
+
+def update(order, pieces, own, halves):
     rows, part = own.shape
     members = pieces[0].shape[0]
-    step = rows // 12
     half = 6
+    step = rows // (2 * half)
     whole = pl.BlockSpec((members, part), lambda i, o: (0, 0))
     block = pl.BlockSpec((step, part), lambda i, o: (i, 0))
+    low = pl.BlockSpec((step, part), lambda i, o: (jnp.minimum(i, half - 1), 0))
+    high = pl.BlockSpec((step, part), lambda i, o: (jnp.maximum(i - half, 0), 0))
     return pl.pallas_call(
-        functools.partial(update_kernel, half),
+        update_kernel,
         grid_spec=pltpu.PrefetchScalarGridSpec(
             num_scalar_prefetch=1,
-            grid=(rows // step,),
-            in_specs=[whole] * 4
-            + [block] * 3
-            + [
-                pl.BlockSpec((step, part), lambda i, o: (jnp.minimum(i, half - 1), 0)),
-                pl.BlockSpec((step, part), lambda i, o: (jnp.maximum(i - half, 0), 0)),
-            ],
+            grid=(2 * half,),
+            in_specs=[whole] * 4 + [block] + [low, high] * 3,
             out_specs=block,
             scratch_shapes=[
                 pltpu.VMEM((GROUPS, part, part), jnp.bfloat16),
                 pltpu.VMEM((members, 2 * part), jnp.bfloat16),
                 pltpu.VMEM((8, part), jnp.float32),
-                pltpu.VMEM((step, part), jnp.bfloat16),
+                pltpu.VMEM((step, members), jnp.bfloat16),
             ],
         ),
         out_shape=jax.ShapeDtypeStruct((rows, part), jnp.bfloat16),
         compiler_params=pltpu.CompilerParams(vmem_limit_bytes=VMEM_LIMIT),
-    )(order, *pieces, own, from_a, from_b, opp_a, opp_b)
+    )(order, *pieces, own, *halves)
 
 
 def shift(x, d):
@@ -249,22 +273,17 @@
     loc = loc_tiles.reshape(nblock * loc_count)
     taper = taper_weight.reshape(nblock * loc_count)
 
-    position = lax.broadcasted_iota(jnp.int32, (nblock, obs_rows), 1)
-    live_rows = (position < obs_count[:, None]).astype(jnp.float32)
-    weighted = ((precision * live_rows)[:, :, None] * innovations.astype(jnp.float32)).astype(
-        jnp.bfloat16
-    )
-
-    def quarter_of(d):
-        return lax.dynamic_slice_in_dim(weighted, ((q + d) & (GROUPS - 1)) * quarter, quarter, axis=1)
-
-    innov_parts = [quarter_of(0)] + [shift(quarter_of(d), d) for d in (1, 2, 3)]
-    g0, g1, g2, g3 = gain_parts(q1, obs_anom, inverses)
+    g0, g1, g2, g3, w0, w1, w2, w3 = first_parts(
+        q1, obs_anom, inverses, innovations, precision, obs_count
+    )
+    innov_parts = [w0, shift(w1, 1), shift(w2, 2), shift(w3, 3)]
     g1, g2, g3 = shift(g1, 1), shift(g2, 2), shift(g3, 3)
     g1, g2, g3, states = lax.optimization_barrier((g1, g2, g3, ensemble))
 
-    from_a, from_b = swap_a(states), swap_b(states)
-    opp_a, opp_b = swap_b(from_a[: rows // 2]), swap_a(from_b[rows // 2 :])
+    low, high = states[: rows // 2], states[rows // 2 :]
+    a1, b2 = swap_a(low), swap_b(high)
+    a2, b1 = swap_a(high), swap_b(low)
+    o1, o2 = swap_b(a1), swap_a(b2)
 
     send_innov = pack(
         functools.partial(pack_innov_kernel, loc_count), (q1, loc), innov_parts, jnp.bfloat16,
@@ -282,7 +301,7 @@
         recv_innov.reshape(slots * quarter, members),
     )
     pieces = [t0, shift(t1, 1), shift(t2, 2), shift(t3, 3)]
-    return update(order, pieces, ensemble, from_a, from_b, opp_a, opp_b)
+    return update(order, pieces, ensemble, (a1, a2, b1, b2, o1, o2))
 
 
 def solution(mesh):

time: 196 us -> 237 us (1.21)
  waiting for transfers between devices: 120 us -> 157 us
  Pallas kernels: 23.9 us -> 26.9 us
    ppermute x2 -> x3, waiting for transfers between devices: 0.01 us -> 70.1 us  [swap_a(): return lax.ppermute(x, 'mem', [(0, 1), (1, 0), (2, 3), (3, 2)])]
    ppermute x9, waiting for transfers between devices: 52.6 us -> 19.1 us  [shift(): lax.ppermute(x, 'mem', [(i, (i + d) % GROUPS) for i in range(GROUPS)])]
    all_to_all x1, waiting for transfers between devices: 24 us -> 29.3 us  [per_device(): lax.all_to_all(send_innov, 'tile', split_axis=0, concat_axis=0, tiled=True)]
    ppermute x2 -> x3, waiting for transfers between devices: 43.3 us -> 38.8 us  [swap_b(): return lax.ppermute(x, 'mem', [(0, 3), (3, 0), (1, 2), (2, 1)])]
    pallas_call x2, Pallas kernels: 14.9 us -> 17.9 us  [the longest x1 15 us: update(): pl.pallas_call(update_kernel, grid_spec=pltpu.PrefetchScalarGridSpec(num_...]
    unnamed x10 -> x20, local copies, waits for them, and re-layouts: 3.82 us -> 6.38 us
    slice x2 -> x1, local copies, waits for them, and re-layouts: 5.66 us -> 4.05 us  [per_device(): low, high = (states[:rows // 2], states[rows // 2:])]
    ppermute x2 -> x3, starting transfers between devices: 5.58 us -> 4.42 us  [swap_b(): return lax.ppermute(x, 'mem', [(0, 3), (3, 0), (1, 2), (2, 1)])]
  transfers between devices with their start and end apart: 15 -> 17, of which waited for: 7 -> 11; matrix products, arithmetic and copies ran while one was open for 3% -> 2% of each run, Pallas kernels for 4% -> 3%
where the time goes in v2:
time: 237 us; the launch traced here: 236 us
  waiting for transfers between devices  157 us (66%)
  starting transfers between devices  41.2 us (17%)
  Pallas kernels  26.9 us (11%)
  local copies, waits for them, and re-layouts  10.6 us (4%)
    ppermute x3, waiting for transfers between devices, swap_a(): return lax.ppermute(x, 'mem', [(0, 1), (1, 0), (2, 3), (3, 2)])  70.1 us
    ppermute x3, waiting for transfers between devices, swap_b(): return lax.ppermute(x, 'mem', [(0, 3), (3, 0), (1, 2), (2, 1)])  38.8 us
    all_to_all x1, waiting for transfers between devices, per_device(): lax.all_to_all(send_innov, 'tile', split_axis=0, concat_axis=0, tiled=True)  29.3 us
    ppermute x9, waiting for transfers between devices, shift(): lax.ppermute(x, 'mem', [(i, (i + d) % GROUPS) for i in range(GROUPS)])  19.1 us
    pallas_call x1, Pallas kernels, update(): pl.pallas_call(update_kernel, grid_spec=pltpu.PrefetchScalarGridSpec(num_...  15 us
    ppermute x9, starting transfers between devices, shift(): lax.ppermute(x, 'mem', [(i, (i + d) % GROUPS) for i in range(GROUPS)])  14.2 us
    all_to_all x1, starting transfers between devices, per_device(): lax.all_to_all(send_innov, 'tile', split_axis=0, concat_axis=0, tiled=True)  12.3 us
    all_to_all x1, starting transfers between devices, per_device(): lax.all_to_all(send_gain, 'tile', split_axis=0, concat_axis=0, tiled=True)  8.31 us
  transfers between devices with their start and end apart: 17, of which 11 were waited for; matrix products, arithmetic and copies ran while one was open for 2% of the time, Pallas kernels for 3%

profile of v2, /device:TPU:6, one launch (start us, length us, event | category | flops | bytes accessed | tf_op | source)
XLA Modules:
  0.0 236.2 jit_solution(7720820248189185411)
XLA Ops:
  0.0 1.6 copy-done.1
  1.6 0.9 copy-done.2
  2.6 0.9 copy-done.3
  3.5 0.7 copy-done.4
  4.2 0.7 copy-done.5
  4.9 2.8 %shard_map.82 = (f32[16,16,512]{2,1,0:T(8,128)S(1)}, bf16[16,16,512]{2,1,0:T(8,128)(2,1)}, bf16[16,16,512]{2,1,0:T(8,128)(2,1)}, bf16[16,16,512]{2,1,0:T(8,128)(...) custom-call(s32[1]{0:T(128)} %bitcast.q_ref, ...), custom_call_target="tpu_custom_call" | custom-call | tf_op jit(solution)/shard_map/pallas_call | solution.py:51
  7.7 1.6 collective-permute-start.3
  9.3 2.9 %collective-permute-start.4 = (bf16[16,16,128]{2,1,0:T(8,128)(2,1)S(1)}, bf16[16,16,128]{2,1,0:T(8,128)(2,1)S(1)}, u32[]{:S(2)}, u32[]{:S(2)}) collective-permute-start(bf16[16,16,128]{2,1,0:T(8,128)(2,1)S(1)} %get-tuple-element.30), channel_id=1, source_target_pairs={{0,2},{1,3},{2,0},{3,1},{4,6},{5,7},{6,4},{7,5},{8,10},{9,11},{10,... | collective-permute-start | bytes 196616 | tf_op jit(solution)/shard_map/ppermute | solution.py:249
  12.2 1.3 collective-permute-start.5
  13.5 0.1 copy.11
  13.6 0.1 reshape.13.loc_ref
  13.7 0.0 collective-permute-done.3.r1_ref
  13.7 1.7 collective-permute-done.4.r2_ref
  15.4 1.1 collective-permute-done.5.r3_ref
  16.4 1.9 shard_map.84
  18.3 1.3 copy-done
  19.7 12.3 %all-to-all-start.1 = ((bf16[128,16,512]{2,1,0:T(8,128)(2,1)}), bf16[128,16,512]{2,1,0:T(8,128)(2,1)S(1)}, u32[]{:S(2)}, u32[]{:S(2)}) async-start(bf16[128,16,512]{2,1,0:T(8,128)(2,1)} %copy-done), calls=%async_computation.1 | async-start | bytes 4194304 | tf_op jit(solution)/shard_map/all_to_all | solution.py:292
  32.0 0.4 collective-permute-start
  32.4 3.7 %collective-permute-start.1 = (bf16[16,16,512]{2,1,0:T(8,128)(2,1)}, bf16[16,16,512]{2,1,0:T(8,128)(2,1)S(1)}, u32[]{:S(2)}, u32[]{:S(2)}) collective-permute-start(bf16[16,16,512]{2,1,0:T(8,128)(2,1)} %get-tuple-element.23), channel_id=1, source_target_pairs={{0,2},{1,3},{2,0},{3,1},{4,6},{5,7},{6,4},{7,5},{8,10},{9,11},{10,... | collective-permute-start | bytes 786440 | tf_op jit(solution)/shard_map/ppermute | solution.py:249
  36.1 0.1 collective-permute-start.2
  36.2 0.1 copy.12
  36.3 0.1 reshape.14.taper_ref
  36.4 5.5 %collective-permute-done.r1_ref = bf16[16,16,512]{2,1,0:T(8,128)(2,1)S(1)} collective-permute-done((bf16[16,16,512]{2,1,0:T(8,128)(2,1)}, bf16[16,16,512]{2,1,0:T(8,128)(2,1)S(1)}, u32[]{:S(2)}, u32[]{:S(2)}) %collective-permute-start) | collective-permute-done | bytes 262176 | tf_op jit(solution)/shard_map/ppermute | solution.py:249
  41.9 6.4 %collective-permute-done.1.r2_ref = bf16[16,16,512]{2,1,0:T(8,128)(2,1)S(1)} collective-permute-done((bf16[16,16,512]{2,1,0:T(8,128)(2,1)}, bf16[16,16,512]{2,1,0:T(8,128)(2,1)S(1)}, u32[]{:S(2)}, u32[]{:S(2)}) %collective-permute-start.1) | collective-permute-done | bytes 262176 | tf_op jit(solution)/shard_map/ppermute | solution.py:249
  48.2 0.0 collective-permute-done.2.r3_ref
  48.2 3.4 %shard_map.83 = bf16[128,16,512]{2,1,0:T(8,128)(2,1)} custom-call(s32[64]{0:T(128)S(1)} %reshape.13.loc_ref, f32[64]{0:T(128)S(1)} %reshape.14.taper_ref, f32[16,16,512]{2,1,0:T(8,128)S(1)} %get-tuple-element.21.own_ref, bf16[16,16,512]{2,1,0:T(8,128)(2,1)S(1)} %collective-permute-done.r1_ref, bf16[16,16,512]{2,1,0:T(8,128)(2,1)S(1)} %collective-permute-done.1.r2_ref, ...), custom_call_target="tpu_custom_call" | custom-call | tf_op jit(solution)/shard_map/pallas_call | solution.py:123
  51.6 29.3 %all-to-all-done.1 = bf16[128,16,512]{2,1,0:T(8,128)(2,1)S(1)} async-done(((bf16[128,16,512]{2,1,0:T(8,128)(2,1)}), bf16[128,16,512]{2,1,0:T(8,128)(2,1)S(1)}, u32[]{:S(2)}, u32[]{:S(2)}) %all-to-all-start.1) | async-done | bytes 2097184 | tf_op jit(solution)/shard_map/all_to_all | solution.py:292
  80.9 8.3 %all-to-all-start = ((bf16[128,16,512]{2,1,0:T(8,128)(2,1)}), bf16[128,16,512]{2,1,0:T(8,128)(2,1)}, u32[]{:S(2)}, u32[]{:S(2)}) async-start(bf16[128,16,512]{2,1,0:T(8,128)(2,1)} %shard_map.83), calls=%async_computation | async-start | bytes 4194304 | tf_op jit(solution)/shard_map/all_to_all | solution.py:297
  89.2 4.0 %fusion = (bf16[7104,128]{1,0:T(8,128)(2,1)}, bf16[7104,128]{1,0:T(8,128)(2,1)}) fusion(bf16[14208,128]{1,0:T(8,128)(2,1)} %own_ref.1), kind=kLoop, calls=%fused_computation.1 | loop fusion | bytes 7274496 | tf_op jit(solution)/shard_map/slice | solution.py:283
  93.3 2.5 %collective-permute-start.12 = (bf16[7104,128]{1,0:T(8,128)(2,1)}, bf16[7104,128]{1,0:T(8,128)(2,1)}, u32[]{:S(2)}, u32[]{:S(2)}) collective-permute-start(bf16[7104,128]{1,0:T(8,128)(2,1)} %get-tuple-element.37), channel_id=1, source_target_pairs={{0,3},{3,0},{1,2},{2,1},{4,7},{7,4},{5,6},{6,5},{8,11},{11,8},{9,1... | collective-permute-start | bytes 5455880 | tf_op jit(solution)/shard_map/ppermute | solution.py:257
  95.8 0.0 collective-permute-start.9
  95.9 2.0 collective-permute-start.10
  97.9 0.7 collective-permute-start.11
  98.6 38.8 %collective-permute-done.12.b2_ref = bf16[7104,128]{1,0:T(8,128)(2,1)} collective-permute-done((bf16[7104,128]{1,0:T(8,128)(2,1)}, bf16[7104,128]{1,0:T(8,128)(2,1)}, u32[]{:S(2)}, u32[]{:S(2)}) %collective-permute-start.12) | collective-permute-done | bytes 1818656 | tf_op jit(solution)/shard_map/ppermute | solution.py:257
  137.3 1.4 collective-permute-done.9.a1_ref
  138.7 1.2 collective-permute-start.13
  139.9 0.0 all-to-all-done
  139.9 3.8 %shard_map.85 = (f32[512,128]{1,0:T(8,128)S(1)}, bf16[512,128]{1,0:T(8,128)(2,1)S(1)}, bf16[512,128]{1,0:T(8,128)(2,1)S(1)}, bf16[512,128]{1,0:T(8,128)(2,1)S(1)}) custom-call(s32[1]{0:T(128)} %bitcast.q_ref, bf16[2048,512]{1,0:T(8,128)(2,1)} %bitcast.4.gain_ref, bf16[2048,512]{1,0:T(8,128)(2,1)S(1)} %bitcast.6), custom_call_target="tpu_custom_call" | custom-call | tf_op jit(solution)/shard_map/pallas_call | solution.py:163
  143.7 1.5 collective-permute-start.6
  145.2 32.5 %collective-permute-done.10.a2_ref = bf16[7104,128]{1,0:T(8,128)(2,1)} collective-permute-done((bf16[7104,128]{1,0:T(8,128)(2,1)}, bf16[7104,128]{1,0:T(8,128)(2,1)}, u32[]{:S(2)}, u32[]{:S(2)}) %collective-permute-start.10) | collective-permute-done | bytes 1818656 | tf_op jit(solution)/shard_map/ppermute | solution.py:253
  177.7 0.1 collective-permute-start.7
  177.8 0.0 collective-permute-done.11.b1_ref
  177.8 2.5 %collective-permute-start.8 = (bf16[512,128]{1,0:T(8,128)(2,1)S(1)}, bf16[512,128]{1,0:T(8,128)(2,1)S(1)}, u32[]{:S(2)}, u32[]{:S(2)}) collective-permute-start(bf16[512,128]{1,0:T(8,128)(2,1)S(1)} %get-tuple-element.35), channel_id=1, source_target_pairs={{0,3},{1,0},{2,1},{3,2},{4,7},{5,4},{6,5},{7,6},{8,11},{9,8},{10,9... | collective-permute-start | bytes 393224 | tf_op jit(solution)/shard_map/ppermute | solution.py:249
  180.3 0.1 pad_add_fusion.order_ref
  180.4 36.3 %collective-permute-done.14.o2_ref = bf16[7104,128]{1,0:T(8,128)(2,1)} collective-permute-done((bf16[7104,128]{1,0:T(8,128)(2,1)}, bf16[7104,128]{1,0:T(8,128)(2,1)}, u32[]{:S(2)}, u32[]{:S(2)}) %collective-permute-start.14) | collective-permute-done | bytes 1818656 | tf_op jit(solution)/shard_map/ppermute | solution.py:253
  216.7 0.5 collective-permute-done.6.t1_ref
  217.2 4.0 %collective-permute-done.7.t2_ref = bf16[512,128]{1,0:T(8,128)(2,1)S(1)} collective-permute-done((bf16[512,128]{1,0:T(8,128)(2,1)S(1)}, bf16[512,128]{1,0:T(8,128)(2,1)S(1)}, u32[]{:S(2)}, u32[]{:S(2)}) %collective-permute-start.7) | collective-permute-done | bytes 131104 | tf_op jit(solution)/shard_map/ppermute | solution.py:249
  221.2 15.0 %shard_map.86 = bf16[14208,128]{1,0:T(8,128)(2,1)} custom-call(s32[4]{0:T(128)S(1)} %pad_add_fusion.order_ref, f32[512,128]{1,0:T(8,128)S(1)} %get-tuple-element.32.t0_ref, bf16[512,128]{1,0:T(8,128)(2,1)S(1)} %collective-permute-done.6.t1_ref, bf16[512,128]{1,0:T(8,128)(2,1)S(1)} %collective-permute-done.7.t2_ref, ...), custom_call_target="tpu_custom_call" | custom-call | tf_op jit(solution)/shard_map/pallas_call | solution.py:229
  (15 shorter events, 0.0 us)
Async XLA Ops:
  0.0 13.5 %copy-start.7 = (s32[16,4]{0,1:T(4,128)S(1)}, s32[16,4]{0,1:T(4,128)}, u32[]{:S(2)}) copy-start(s32[16,4]{0,1:T(4,128)} %param.14) | copy-start | bytes 772
  0.0 1.6 copy-start.1
  1.6 0.9 copy-start.2
  2.6 0.9 copy-start.3
  3.5 0.7 copy-start.4
  4.2 0.7 copy-start.5
  7.7 12.0 %copy-start.6 = (bf16[16,16,512]{2,1,0:T(8,128)(2,1)}, bf16[16,16,512]{2,1,0:T(8,128)(2,1)S(1)}, u32[]{:S(2)}) copy-start(bf16[16,16,512]{2,1,0:T(8,128)(2,1)S(1)} %get-tuple-element.24) | copy-start | bytes 786436
  7.7 6.0 %collective-permute-start.3 = (bf16[16,16,128]{2,1,0:T(8,128)(2,1)S(1)}, bf16[16,16,128]{2,1,0:T(8,128)(2,1)S(1)}, u32[]{:S(2)}, u32[]{:S(2)}) collective-permute-start(bf16[16,16,128]{2,1,0:T(8,128)(2,1)S(1)} %get-tuple-element.29), channel_id=1, source_target_pairs={{0,1},{1,2},{2,3},{3,0},{4,5},{5,6},{6,7},{7,4},{8,9},{9,10},{10,1... | collective-permute-start | bytes 196616 | tf_op jit(solution)/shard_map/ppermute | solution.py:249
  9.3 6.1 %collective-permute-start.4 = (bf16[16,16,128]{2,1,0:T(8,128)(2,1)S(1)}, bf16[16,16,128]{2,1,0:T(8,128)(2,1)S(1)}, u32[]{:S(2)}, u32[]{:S(2)}) collective-permute-start(bf16[16,16,128]{2,1,0:T(8,128)(2,1)S(1)} %get-tuple-element.30), channel_id=1, source_target_pairs={{0,2},{1,3},{2,0},{3,1},{4,6},{5,7},{6,4},{7,5},{8,10},{9,11},{10,... | collective-permute-start | bytes 196616 | tf_op jit(solution)/shard_map/ppermute | solution.py:249
  12.2 4.3 %collective-permute-start.5 = (bf16[16,16,128]{2,1,0:T(8,128)(2,1)S(1)}, bf16[16,16,128]{2,1,0:T(8,128)(2,1)S(1)}, u32[]{:S(2)}, u32[]{:S(2)}) collective-permute-start(bf16[16,16,128]{2,1,0:T(8,128)(2,1)S(1)} %get-tuple-element.31), channel_id=1, source_target_pairs={{0,3},{1,0},{2,1},{3,2},{4,7},{5,4},{6,5},{7,6},{8,11},{9,8},{10,9... | collective-permute-start | bytes 196616 | tf_op jit(solution)/shard_map/ppermute | solution.py:249
  18.3 1.4 copy-start
  19.7 16.5 %copy-start.8 = (f32[16,4]{0,1:T(4,128)S(1)}, f32[16,4]{0,1:T(4,128)}, u32[]{:S(2)}) copy-start(f32[16,4]{0,1:T(4,128)} %param.15) | copy-start | bytes 772
  19.7 61.3 %all-to-all-start.1 = ((bf16[128,16,512]{2,1,0:T(8,128)(2,1)}), bf16[128,16,512]{2,1,0:T(8,128)(2,1)S(1)}, u32[]{:S(2)}, u32[]{:S(2)}) async-start(bf16[128,16,512]{2,1,0:T(8,128)(2,1)} %copy-done), calls=%async_computation.1 | async-start | bytes 4194304 | tf_op jit(solution)/shard_map/all_to_all | solution.py:292
  32.0 9.9 %collective-permute-start = (bf16[16,16,512]{2,1,0:T(8,128)(2,1)}, bf16[16,16,512]{2,1,0:T(8,128)(2,1)S(1)}, u32[]{:S(2)}, u32[]{:S(2)}) collective-permute-start(bf16[16,16,512]{2,1,0:T(8,128)(2,1)} %get-tuple-element.22), channel_id=1, source_target_pairs={{0,1},{1,2},{2,3},{3,0},{4,5},{5,6},{6,7},{7,4},{8,9},{9,10},{10,1... | collective-permute-start | bytes 786440 | tf_op jit(solution)/shard_map/ppermute | solution.py:249
  32.4 15.9 %collective-permute-start.1 = (bf16[16,16,512]{2,1,0:T(8,128)(2,1)}, bf16[16,16,512]{2,1,0:T(8,128)(2,1)S(1)}, u32[]{:S(2)}, u32[]{:S(2)}) collective-permute-start(bf16[16,16,512]{2,1,0:T(8,128)(2,1)} %get-tuple-element.23), channel_id=1, source_target_pairs={{0,2},{1,3},{2,0},{3,1},{4,6},{5,7},{6,4},{7,5},{8,10},{9,11},{10,... | collective-permute-start | bytes 786440 | tf_op jit(solution)/shard_map/ppermute | solution.py:249
  36.1 12.2 %collective-permute-start.2 = (bf16[16,16,512]{2,1,0:T(8,128)(2,1)}, bf16[16,16,512]{2,1,0:T(8,128)(2,1)S(1)}, u32[]{:S(2)}, u32[]{:S(2)}) collective-permute-start(bf16[16,16,512]{2,1,0:T(8,128)(2,1)} %copy-done.6), channel_id=1, source_target_pairs={{0,3},{1,0},{2,1},{3,2},{4,7},{5,4},{6,5},{7,6},{8,11},{9,8},{10,9... | collective-permute-start | bytes 786440 | tf_op jit(solution)/shard_map/ppermute | solution.py:249
  80.9 59.0 %all-to-all-start = ((bf16[128,16,512]{2,1,0:T(8,128)(2,1)}), bf16[128,16,512]{2,1,0:T(8,128)(2,1)}, u32[]{:S(2)}, u32[]{:S(2)}) async-start(bf16[128,16,512]{2,1,0:T(8,128)(2,1)} %shard_map.83), calls=%async_computation | async-start | bytes 4194304 | tf_op jit(solution)/shard_map/all_to_all | solution.py:297
  93.3 44.0 %collective-permute-start.12 = (bf16[7104,128]{1,0:T(8,128)(2,1)}, bf16[7104,128]{1,0:T(8,128)(2,1)}, u32[]{:S(2)}, u32[]{:S(2)}) collective-permute-start(bf16[7104,128]{1,0:T(8,128)(2,1)} %get-tuple-element.37), channel_id=1, source_target_pairs={{0,3},{3,0},{1,2},{2,1},{4,7},{7,4},{5,6},{6,5},{8,11},{11,8},{9,1... | collective-permute-start | bytes 5455880 | tf_op jit(solution)/shard_map/ppermute | solution.py:257
  95.8 42.9 %collective-permute-start.9 = (bf16[7104,128]{1,0:T(8,128)(2,1)}, bf16[7104,128]{1,0:T(8,128)(2,1)}, u32[]{:S(2)}, u32[]{:S(2)}) collective-permute-start(bf16[7104,128]{1,0:T(8,128)(2,1)} %get-tuple-element.38), channel_id=1, source_target_pairs={{0,1},{1,0},{2,3},{3,2},{4,5},{5,4},{6,7},{7,6},{8,9},{9,8},{10,11... | collective-permute-start | bytes 5455880 | tf_op jit(solution)/shard_map/ppermute | solution.py:253
  95.9 81.8 %collective-permute-start.10 = (bf16[7104,128]{1,0:T(8,128)(2,1)}, bf16[7104,128]{1,0:T(8,128)(2,1)}, u32[]{:S(2)}, u32[]{:S(2)}) collective-permute-start(bf16[7104,128]{1,0:T(8,128)(2,1)} %get-tuple-element.37), channel_id=1, source_target_pairs={{0,1},{1,0},{2,3},{3,2},{4,5},{5,4},{6,7},{7,6},{8,9},{9,8},{10,11... | collective-permute-start | bytes 5455880 | tf_op jit(solution)/shard_map/ppermute | solution.py:253
  97.9 79.9 %collective-permute-start.11 = (bf16[7104,128]{1,0:T(8,128)(2,1)}, bf16[7104,128]{1,0:T(8,128)(2,1)}, u32[]{:S(2)}, u32[]{:S(2)}) collective-permute-start(bf16[7104,128]{1,0:T(8,128)(2,1)} %get-tuple-element.38), channel_id=1, source_target_pairs={{0,3},{3,0},{1,2},{2,1},{4,7},{7,4},{5,6},{6,5},{8,11},{11,8},{9,1... | collective-permute-start | bytes 5455880 | tf_op jit(solution)/shard_map/ppermute | solution.py:257
  137.3 79.3 %collective-permute-start.14 = (bf16[7104,128]{1,0:T(8,128)(2,1)}, bf16[7104,128]{1,0:T(8,128)(2,1)}, u32[]{:S(2)}, u32[]{:S(2)}) collective-permute-start(bf16[7104,128]{1,0:T(8,128)(2,1)} %collective-permute-done.12.b2_ref), channel_id=1, source_target_pairs={{0,1},{1,0},{2,3},{3,2},{4,5},{5,4},{6,7},{7,6},{8,9},{9,8},{10,11... | collective-permute-start | bytes 5455880 | tf_op jit(solution)/shard_map/ppermute | solution.py:253
  138.7 77.9 %collective-permute-start.13 = (bf16[7104,128]{1,0:T(8,128)(2,1)}, bf16[7104,128]{1,0:T(8,128)(2,1)}, u32[]{:S(2)}, u32[]{:S(2)}) collective-permute-start(bf16[7104,128]{1,0:T(8,128)(2,1)} %collective-permute-done.9.a1_ref), channel_id=1, source_target_pairs={{0,3},{3,0},{1,2},{2,1},{4,7},{7,4},{5,6},{6,5},{8,11},{11,8},{9,1... | collective-permute-start | bytes 5455880 | tf_op jit(solution)/shard_map/ppermute | solution.py:257
  143.7 73.5 %collective-permute-start.6 = (bf16[512,128]{1,0:T(8,128)(2,1)S(1)}, bf16[512,128]{1,0:T(8,128)(2,1)S(1)}, u32[]{:S(2)}, u32[]{:S(2)}) collective-permute-start(bf16[512,128]{1,0:T(8,128)(2,1)S(1)} %get-tuple-element.33), channel_id=1, source_target_pairs={{0,1},{1,2},{2,3},{3,0},{4,5},{5,6},{6,7},{7,4},{8,9},{9,10},{10,1... | collective-permute-start | bytes 393224 | tf_op jit(solution)/shard_map/ppermute | solution.py:249
  177.7 43.5 %collective-permute-start.7 = (bf16[512,128]{1,0:T(8,128)(2,1)S(1)}, bf16[512,128]{1,0:T(8,128)(2,1)S(1)}, u32[]{:S(2)}, u32[]{:S(2)}) collective-permute-start(bf16[512,128]{1,0:T(8,128)(2,1)S(1)} %get-tuple-element.34), channel_id=1, source_target_pairs={{0,2},{1,3},{2,0},{3,1},{4,6},{5,7},{6,4},{7,5},{8,10},{9,11},{10,... | collective-permute-start | bytes 393224 | tf_op jit(solution)/shard_map/ppermute | solution.py:249
  177.8 43.4 %collective-permute-start.8 = (bf16[512,128]{1,0:T(8,128)(2,1)S(1)}, bf16[512,128]{1,0:T(8,128)(2,1)S(1)}, u32[]{:S(2)}, u32[]{:S(2)}) collective-permute-start(bf16[512,128]{1,0:T(8,128)(2,1)S(1)} %get-tuple-element.35), channel_id=1, source_target_pairs={{0,3},{1,0},{2,1},{3,2},{4,7},{5,4},{6,5},{7,6},{8,11},{9,8},{10,9... | collective-permute-start | bytes 393224 | tf_op jit(solution)/shard_map/ppermute | solution.py:249

commit v3 on v2

v3 whole, which is shorter than its diff:
```python
import functools
import math

import jax
import jax.numpy as jnp
from jax import lax
from jax.experimental import pallas as pl
from jax.experimental.pallas import tpu as pltpu
from jax.sharding import PartitionSpec as P

VMEM_LIMIT = 56 * 1024 * 1024
GROUPS = 4


def first_kernel(
    q_ref, obs_ref, inv_ref, innov_ref, precision_ref, count_ref,
    gain_ref, innov_out_ref, m1_ref, m2_ref, m3_ref, rows_ref, live_ref,
):
    quarter, members = gain_ref.shape[1:]
    obs_rows, part = innov_ref.shape[1:]
    blocks = obs_ref.shape[0]
    q = q_ref[0]
    step = pl.program_id(0)
    position = lax.broadcasted_iota(jnp.int32, (obs_rows, part), 0)
    for k in range(blocks):
        rows_ref[...] = lax.dot_general(
            obs_ref[k], inv_ref[k], (((1,), (1,)), ((), ())), preferred_element_type=jnp.float32
        )
        block = step * blocks + k
        scale = jnp.broadcast_to(precision_ref[pl.ds(block, 1), :], (part, obs_rows)).T
        live_ref[...] = jnp.where(
            position < count_ref[block], scale * innov_ref[k].astype(jnp.float32), 0.0
        )
        own = pl.ds(pl.multiple_of(q * quarter, quarter), quarter)
        gain_ref[k] = rows_ref[own, :]
        innov_out_ref[k] = live_ref[own, :].astype(jnp.bfloat16)
        for d, ref in ((1, m1_ref), (2, m2_ref), (3, m3_ref)):
            rows = pl.ds(pl.multiple_of(lax.rem(q + d, GROUPS) * quarter, quarter), quarter)
            ref[k, :, :members] = rows_ref[rows, :].astype(jnp.bfloat16)
            ref[k, :, members:] = live_ref[rows, :].astype(jnp.bfloat16)


def first_parts(q, obs_anom, inverses, innovations, precision, obs_count):
    nblock, obs_rows, part = obs_anom.shape
    members = inverses.shape[1]
    quarter = obs_rows // GROUPS
    step = 4
    widths = [members, part] + [members + part] * 3
    types = [jnp.float32] + [jnp.bfloat16] * 4
    rows = pl.BlockSpec((step, obs_rows, part), lambda i, q: (i, 0, 0))
    return pl.pallas_call(
        first_kernel,
        grid_spec=pltpu.PrefetchScalarGridSpec(
            num_scalar_prefetch=1,
            grid=(nblock // step,),
            in_specs=[
                rows,
                pl.BlockSpec((step, members, part), lambda i, q: (i, 0, 0)),
                rows,
                pl.BlockSpec((nblock, obs_rows), lambda i, q: (0, 0)),
                pl.BlockSpec(memory_space=pltpu.SMEM),
            ],
            out_specs=[
                pl.BlockSpec((step, quarter, width), lambda i, q: (i, 0, 0)) for width in widths
            ],
            scratch_shapes=[
                pltpu.VMEM((obs_rows, members), jnp.float32),
                pltpu.VMEM((obs_rows, part), jnp.float32),
            ],
        ),
        out_shape=[
            jax.ShapeDtypeStruct((nblock, quarter, width), kind)
            for width, kind in zip(widths, types)
        ],
        compiler_params=pltpu.CompilerParams(vmem_limit_bytes=VMEM_LIMIT),
    )(q, obs_anom, inverses, innovations, precision, obs_count)


def pack_kernel(
    loc_count, q_ref, loc_ref, taper_ref, gain_ref, innov_ref, r1_ref, r2_ref, r3_ref,
    out_ref, gain_full_ref, innov_full_ref, count_ref,
):
    members = gain_ref.shape[2]
    part = innov_ref.shape[2]
    pairs = loc_ref.shape[0]
    tiles = count_ref.shape[0]
    capacity = out_ref.shape[0] // tiles
    q = q_ref[0]
    innov_full_ref[:, :, pl.ds(pl.multiple_of(q * part, part), part)] = innov_ref[...]
    for d, ref in ((1, r1_ref), (2, r2_ref), (3, r3_ref)):
        start = pl.multiple_of(lax.rem(q - d + GROUPS, GROUPS) * part, part)
        innov_full_ref[:, :, pl.ds(start, part)] = ref[:, :, members:]
    gain_full_ref[...] = (
        gain_ref[...]
        + r1_ref[:, :, :members].astype(jnp.float32)
        + r2_ref[:, :, :members].astype(jnp.float32)
        + r3_ref[:, :, :members].astype(jnp.float32)
    )
    out_ref[...] = jnp.zeros(out_ref.shape, out_ref.dtype)

    def clear(t, _):
        count_ref[t] = 0
        return 0

    def put(p, _):
        tile = loc_ref[p]
        block = p // loc_count
        rank = count_ref[tile]
        count_ref[tile] = rank + 1
        slot = tile * capacity + rank
        out_ref[slot, :, :members] = (taper_ref[p] * gain_full_ref[block]).astype(out_ref.dtype)
        out_ref[slot, :, members:] = innov_full_ref[block]
        return 0

    lax.fori_loop(0, tiles, clear, 0)
    lax.fori_loop(0, pairs, put, 0)


def pack(q, loc, taper, parts, tiles, slots, loc_count):
    nblock, quarter, members = parts[0].shape
    return pl.pallas_call(
        functools.partial(pack_kernel, loc_count),
        in_specs=[pl.BlockSpec(memory_space=pltpu.SMEM)] * 3
        + [pl.BlockSpec(memory_space=pltpu.VMEM)] * len(parts),
        out_specs=pl.BlockSpec(memory_space=pltpu.VMEM),
        out_shape=jax.ShapeDtypeStruct((slots, quarter, 2 * members), jnp.bfloat16),
        scratch_shapes=[
            pltpu.VMEM((nblock, quarter, members), jnp.float32),
            pltpu.VMEM((nblock, quarter, members), jnp.bfloat16),
            pltpu.SMEM((tiles,), jnp.int32),
        ],
        compiler_params=pltpu.CompilerParams(vmem_limit_bytes=VMEM_LIMIT),
    )(q, loc, taper, *parts)


def arrived_kernel(a1_ref, a2_ref, b1_ref, b2_ref, out_ref):
    out_ref[0] = 0


def arrived(*arrays):
    return pl.pallas_call(
        arrived_kernel,
        in_specs=[pl.BlockSpec(memory_space=pl.ANY)] * len(arrays),
        out_specs=pl.BlockSpec(memory_space=pltpu.SMEM),
        out_shape=jax.ShapeDtypeStruct((1,), jnp.int32),
        cost_estimate=pl.CostEstimate(flops=10**12, bytes_accessed=10**9, transcendentals=0),
    )(*arrays)


def transform_kernel(q_ref, token_ref, pairs_ref, own_ref, s1_ref, s2_ref, s3_ref, total_ref):
    step = pl.program_id(0)
    members, part = own_ref.shape

    @pl.when(step == 0)
    def _():
        total_ref[...] = jnp.zeros_like(total_ref)

    total_ref[...] += lax.dot_general(
        pairs_ref[:, :members],
        pairs_ref[:, members:],
        (((0,), (0,)), ((), ())),
        preferred_element_type=jnp.float32,
    )

    @pl.when(step == pl.num_programs(0) - 1)
    def _():
        q = q_ref[0]
        for d, out_ref in enumerate((own_ref, s1_ref, s2_ref, s3_ref)):
            start = pl.multiple_of(lax.rem(q + d, GROUPS) * part, part)
            columns = total_ref[:, pl.ds(start, part)]
            mean = jnp.sum(columns, axis=0, keepdims=True) / members
            scaled = (columns - mean) * (1.0 / math.sqrt(members - 1))
            out_ref[...] = scaled.astype(out_ref.dtype)


def transform_parts(q, token, pairs):
    depth, width = pairs.shape
    members = width // 2
    part = members // GROUPS
    step = 512
    out = pl.BlockSpec((members, part), lambda i, q, token: (0, 0))
    return pl.pallas_call(
        transform_kernel,
        grid_spec=pltpu.PrefetchScalarGridSpec(
            num_scalar_prefetch=2,
            grid=(depth // step,),
            in_specs=[pl.BlockSpec((step, width), lambda i, q, token: (i, 0))],
            out_specs=[out] * GROUPS,
            scratch_shapes=[pltpu.VMEM((members, members), jnp.float32)],
        ),
        out_shape=[jax.ShapeDtypeStruct((members, part), jnp.float32)]
        + [jax.ShapeDtypeStruct((members, part), jnp.bfloat16)] * 3,
        compiler_params=pltpu.CompilerParams(vmem_limit_bytes=VMEM_LIMIT),
    )(q, token, pairs)


def update_kernel(
    order_ref, t0_ref, t1_ref, t2_ref, t3_ref, own_ref, a1_ref, a2_ref, b1_ref, b2_ref, o1_ref, o2_ref,
    out_ref, raw_ref, weights_ref,
):
    step = pl.program_id(0)
    half = pl.num_programs(0) // 2
    part = own_ref.shape[1]

    @pl.when(step == 0)
    def _():
        total = (
            t0_ref[...]
            + t1_ref[...].astype(jnp.float32)
            + t2_ref[...].astype(jnp.float32)
            + t3_ref[...].astype(jnp.float32)
        ).astype(jnp.bfloat16)
        raw_ref[...] = total.reshape(raw_ref.shape)
        for k in range(GROUPS):
            weights_ref[pl.ds(k * part, part), :] = raw_ref[order_ref[k]]

    def rows(a_ref, b_ref, o_ref):
        own = own_ref[...]
        states = jnp.concatenate([own, a_ref[...], b_ref[...], o_ref[...]], axis=1)
        increment = jnp.dot(states, weights_ref[...], preferred_element_type=jnp.float32)
        out_ref[...] = (own.astype(jnp.float32) + increment).astype(out_ref.dtype)

    @pl.when(step < half)
    def _():
        rows(a1_ref, b1_ref, o1_ref)

    @pl.when(step >= half)
    def _():
        rows(a2_ref, b2_ref, o2_ref)


def update(order, pieces, own, halves):
    rows, part = own.shape
    members = pieces[0].shape[0]
    half = 3
    step = rows // (2 * half)
    whole = pl.BlockSpec((members, part), lambda i, o: (0, 0))
    block = pl.BlockSpec((step, part), lambda i, o: (i, 0))
    low = pl.BlockSpec((step, part), lambda i, o: (jnp.minimum(i, half - 1), 0))
    high = pl.BlockSpec((step, part), lambda i, o: (jnp.maximum(i - half, 0), 0))
    return pl.pallas_call(
        update_kernel,
        grid_spec=pltpu.PrefetchScalarGridSpec(
            num_scalar_prefetch=1,
            grid=(2 * half,),
            in_specs=[whole] * 4 + [block] + [low, high] * 3,
            out_specs=block,
            scratch_shapes=[
                pltpu.VMEM((GROUPS, part, part), jnp.bfloat16),
                pltpu.VMEM((members, part), jnp.bfloat16),
            ],
        ),
        out_shape=jax.ShapeDtypeStruct((rows, part), jnp.bfloat16),
        compiler_params=pltpu.CompilerParams(vmem_limit_bytes=VMEM_LIMIT),
    )(order, *pieces, own, *halves)


def shift(x, d):
    return lax.ppermute(x, "mem", [(i, (i + d) % GROUPS) for i in range(GROUPS)])


def swap_a(x):
    return lax.ppermute(x, "mem", [(0, 1), (1, 0), (2, 3), (3, 2)])


def swap_b(x):
    return lax.ppermute(x, "mem", [(0, 3), (3, 0), (1, 2), (2, 1)])


def per_device(
    ensemble, obs_anom, inverses, innovations, precision, obs_count, loc_tiles, taper_weight
):
    tiles = lax.axis_size("tile")
    nblock, obs_rows, part = obs_anom.shape
    members = part * GROUPS
    rows = ensemble.shape[0]
    loc_count = loc_tiles.shape[1]
    quarter = obs_rows // GROUPS
    slots = tiles * 2
    q = lax.axis_index("mem").astype(jnp.int32)
    q1 = q.reshape(1)
    order = jnp.stack([q, q ^ 1, 3 - q, q ^ 2])
    loc = loc_tiles.reshape(nblock * loc_count)
    taper = taper_weight.reshape(nblock * loc_count)

    gain, innov, m1, m2, m3 = first_parts(
        q1, obs_anom, inverses, innovations, precision, obs_count
    )
    m1, m2, m3 = shift(m1, 1), shift(m2, 2), shift(m3, 3)
    m1, m2, m3, low, high = lax.optimization_barrier(
        (m1, m2, m3, ensemble[: rows // 2], ensemble[rows // 2 :])
    )
    a1, b2 = swap_a(low), swap_b(high)
    a2, b1 = swap_a(high), swap_b(low)
    o1, o2 = swap_b(a1), swap_a(b2)

    send = pack(q1, loc, taper, (gain, innov, m1, m2, m3), tiles, slots, loc_count)
    received = lax.all_to_all(send, "tile", split_axis=0, concat_axis=0, tiled=True)
    token = arrived(a1, a2, b1, b2)
    t0, t1, t2, t3 = transform_parts(q1, token, received.reshape(slots * quarter, 2 * members))
    pieces = [t0, shift(t1, 1), shift(t2, 2), shift(t3, 3)]
    return update(order, pieces, ensemble, (a1, a2, b1, b2, o1, o2))


def solution(mesh):
    return jax.shard_map(
        per_device,
        mesh=mesh,
        in_specs=(
            P("tile", "mem"),
            P("tile", None, "mem"),
            P("tile", None, "mem"),
            P("tile", None, "mem"),
            P("tile", None),
            P("tile"),
            P("tile", None),
            P("tile", None),
        ),
        out_specs=P("tile", "mem"),
        check_vma=False,
    )
```

time: 237 us -> 172 us (0.73)
  waiting for transfers between devices: 157 us -> 106 us
  starting transfers between devices: 41.2 us -> 30.1 us
  local copies, waits for them, and re-layouts: 10.6 us -> 5.52 us
    ppermute x3, waiting for transfers between devices: 38.8 us -> 3.16 us  [swap_b(): return lax.ppermute(x, 'mem', [(0, 3), (3, 0), (1, 2), (2, 1)])]
    ppermute x3, waiting for transfers between devices: 70.1 us -> 55.7 us  [swap_a(): return lax.ppermute(x, 'mem', [(0, 1), (1, 0), (2, 3), (3, 2)])]
    all_to_all x2 -> x1, starting transfers between devices: 20.6 us -> 12.4 us  [per_device(): lax.all_to_all(send, 'tile', split_axis=0, concat_axis=0, tiled=True)]
    unnamed x20 -> x18, local copies, waits for them, and re-layouts: 6.38 us -> 0.84 us
    ppermute x9 -> x6, waiting for transfers between devices: 19.1 us -> 14.8 us  [shift(): lax.ppermute(x, 'mem', [(i, (i + d) % GROUPS) for i in range(GROUPS)])]
    pallas_call x1, Pallas kernels: 15 us -> 11.9 us  [update(): pl.pallas_call(update_kernel, grid_spec=pltpu.PrefetchScalarGridSpec(num_...]
    ppermute x9 -> x6, starting transfers between devices: 14.2 us -> 11 us  [shift(): lax.ppermute(x, 'mem', [(i, (i + d) % GROUPS) for i in range(GROUPS)])]
    all_to_all x2 -> x1, waiting for transfers between devices: 29.3 us -> 32.4 us  [per_device(): lax.all_to_all(send, 'tile', split_axis=0, concat_axis=0, tiled=True)]
  transfers between devices with their start and end apart: 17 -> 13, of which waited for: 11 -> 10; matrix products, arithmetic and copies ran while one was open for 2% -> 3% of each run, Pallas kernels for 3% -> 7%
where the time goes in v3:
time: 172 us; the launch traced here: 170 us
  waiting for transfers between devices  106 us (62%)
  starting transfers between devices  30.1 us (18%)
  Pallas kernels  27.3 us (16%)
  local copies, waits for them, and re-layouts  5.52 us (3%)
    ppermute x3, waiting for transfers between devices, swap_a(): return lax.ppermute(x, 'mem', [(0, 1), (1, 0), (2, 3), (3, 2)])  55.7 us
    all_to_all x1, waiting for transfers between devices, per_device(): lax.all_to_all(send, 'tile', split_axis=0, concat_axis=0, tiled=True)  32.4 us
    ppermute x6, waiting for transfers between devices, shift(): lax.ppermute(x, 'mem', [(i, (i + d) % GROUPS) for i in range(GROUPS)])  14.8 us
    all_to_all x1, starting transfers between devices, per_device(): lax.all_to_all(send, 'tile', split_axis=0, concat_axis=0, tiled=True)  12.4 us
    pallas_call x1, Pallas kernels, update(): pl.pallas_call(update_kernel, grid_spec=pltpu.PrefetchScalarGridSpec(num_...  11.9 us
    ppermute x6, starting transfers between devices, shift(): lax.ppermute(x, 'mem', [(i, (i + d) % GROUPS) for i in range(GROUPS)])  11 us
    pallas_call x1, Pallas kernels, transform_parts(): pl.pallas_call(transform_kernel, grid_spec=pltpu.PrefetchScalarGridSpec(n...  5.69 us
    ppermute x3, starting transfers between devices, swap_b(): return lax.ppermute(x, 'mem', [(0, 3), (3, 0), (1, 2), (2, 1)])  5.06 us
  transfers between devices with their start and end apart: 13, of which 10 were waited for; matrix products, arithmetic and copies ran while one was open for 3% of the time, Pallas kernels for 7%

profile of v3, /device:TPU:6, one launch (start us, length us, event | category | flops | bytes accessed | tf_op | source)
XLA Modules:
  0.0 169.6 jit_solution(1548449446232533045)
XLA Ops:
  0.0 4.2 %shard_map.82 = (f32[16,16,512]{2,1,0:T(8,128)}, bf16[16,16,128]{2,1,0:T(8,128)(2,1)}, bf16[16,16,640]{2,1,0:T(8,128)(2,1)}, bf16[16,16,640]{2,1,0:T(8,128)(2,1)}, bf16[16,16,640]{2,1,0:T(8,128)(2,1)}) custom-call(s32[1]{0:T(128)} %bitcast.q_ref, bf16[16,64,128]{2,1,0:T(8,128)(2,1)} %obs_ref.1, bf16[16,512,128]{2,1,0:T(8,128)(2,1)} %inv_ref.1, ...), custom_call_target="tpu_custom_call" | custom-call | tf_op jit(solution)/shard_map/pallas_call | solution.py:51
  4.2 1.6 collective-permute-start
  5.9 2.9 %collective-permute-start.1 = (bf16[16,16,640]{2,1,0:T(8,128)(2,1)}, bf16[16,16,640]{2,1,0:T(8,128)(2,1)S(1)}, u32[]{:S(2)}, u32[]{:S(2)}) collective-permute-start(bf16[16,16,640]{2,1,0:T(8,128)(2,1)} %get-tuple-element.20), channel_id=1, source_target_pairs={{0,2},{1,3},{2,0},{3,1},{4,6},{5,7},{6,4},{7,5},{8,10},{9,11},{10,... | collective-permute-start | bytes 983048 | tf_op jit(solution)/shard_map/ppermute | solution.py:259
  8.8 0.0 copy-start.6
  8.8 1.3 collective-permute-start.2
  10.1 3.5 %fusion = (bf16[7104,128]{1,0:T(8,128)(2,1)}, bf16[7104,128]{1,0:T(8,128)(2,1)S(1)}) fusion(bf16[14208,128]{1,0:T(8,128)(2,1)} %own_ref.1), kind=kLoop, calls=%fused_computation.1 | loop fusion | bytes 7274496 | tf_op jit(solution)/shard_map/slice | solution.py:291
  13.6 1.6 collective-permute-done.r1_ref
  15.2 0.0 copy-start
  15.2 8.2 %collective-permute-done.1.r2_ref = bf16[16,16,640]{2,1,0:T(8,128)(2,1)S(1)} collective-permute-done((bf16[16,16,640]{2,1,0:T(8,128)(2,1)}, bf16[16,16,640]{2,1,0:T(8,128)(2,1)S(1)}, u32[]{:S(2)}, u32[]{:S(2)}) %collective-permute-start.1) | collective-permute-done | bytes 327712 | tf_op jit(solution)/shard_map/ppermute | solution.py:259
  23.4 0.0 copy-start.1
  23.4 0.0 collective-permute-done.2.r3_ref
  23.4 1.2 collective-permute-start.3
  24.7 1.9 %collective-permute-start.6 = (bf16[7104,128]{1,0:T(8,128)(2,1)}, bf16[7104,128]{1,0:T(8,128)(2,1)}, u32[]{:S(2)}, u32[]{:S(2)}) collective-permute-start(bf16[7104,128]{1,0:T(8,128)(2,1)} %get-tuple-element.23), channel_id=1, source_target_pairs={{0,3},{3,0},{1,2},{2,1},{4,7},{7,4},{5,6},{6,5},{8,11},{11,8},{9,1... | collective-permute-start | bytes 5455880 | tf_op jit(solution)/shard_map/ppermute | solution.py:267
  26.6 0.4 collective-permute-start.4
  27.0 1.2 collective-permute-start.5
  28.2 0.0 copy-done.6
  28.2 0.1 copy.11
  28.3 0.6 reshape.10.loc_ref
  28.9 0.0 copy-done.7
  28.9 0.1 copy.12
  29.0 0.6 reshape.11.taper_ref
  29.5 0.0 copy-done
  29.5 0.0 copy-done.1
  29.5 0.0 copy-done.2
  29.5 5.0 %shard_map.84 = bf16[128,16,1024]{2,1,0:T(8,128)(2,1)} custom-call(s32[1]{0:T(128)} %bitcast.q_ref, s32[64]{0:T(128)} %reshape.10.loc_ref, f32[64]{0:T(128)} %reshape.11.taper_ref, f32[16,16,512]{2,1,0:T(8,128)} %get-tuple-element.24.gain_ref, bf16[16,16,128]{2,1,0:T(8,128)(2,1)} %get-tuple-element.25.innov_ref, bf16[16,16,640]{2,1,0:T(8,128)(2,1)} %copy-done, ...), custom_call_target="tpu_custom_call" | custom-call | tf_op jit(solution)/shard_map/pallas_call | solution.py:121
  34.5 12.4 %all-to-all-start = ((bf16[128,16,1024]{2,1,0:T(8,128)(2,1)}), bf16[128,16,1024]{2,1,0:T(8,128)(2,1)}, u32[]{:S(2)}, u32[]{:S(2)}) async-start(bf16[128,16,1024]{2,1,0:T(8,128)(2,1)} %shard_map.84), calls=%async_computation | async-start | bytes 8388608 | tf_op jit(solution)/shard_map/all_to_all | solution.py:298
  46.9 19.4 %collective-permute-done.3.a1_ref = bf16[7104,128]{1,0:T(8,128)(2,1)} collective-permute-done((bf16[7104,128]{1,0:T(8,128)(2,1)S(1)}, bf16[7104,128]{1,0:T(8,128)(2,1)}, u32[]{:S(2)}, u32[]{:S(2)}) %collective-permute-start.3) | collective-permute-done | bytes 1818656 | tf_op jit(solution)/shard_map/ppermute | solution.py:263
  66.2 2.0 %collective-permute-start.10 = (bf16[7104,128]{1,0:T(8,128)(2,1)}, bf16[7104,128]{1,0:T(8,128)(2,1)}, u32[]{:S(2)}, u32[]{:S(2)}) collective-permute-start(bf16[7104,128]{1,0:T(8,128)(2,1)} %collective-permute-done.3.a1_ref), channel_id=1, source_target_pairs={{0,3},{3,0},{1,2},{2,1},{4,7},{7,4},{5,6},{6,5},{8,11},{11,8},{9,1... | collective-permute-start | bytes 5455880 | tf_op jit(solution)/shard_map/ppermute | solution.py:267
  68.2 0.6 collective-permute-done.6.b2_ref
  68.8 0.0 collective-permute-start.11
  68.8 36.4 %collective-permute-done.4.a2_ref = bf16[7104,128]{1,0:T(8,128)(2,1)} collective-permute-done((bf16[7104,128]{1,0:T(8,128)(2,1)}, bf16[7104,128]{1,0:T(8,128)(2,1)}, u32[]{:S(2)}, u32[]{:S(2)}) %collective-permute-start.4) | collective-permute-done | bytes 1818656 | tf_op jit(solution)/shard_map/ppermute | solution.py:263
  105.2 2.6 %collective-permute-done.5.b1_ref = bf16[7104,128]{1,0:T(8,128)(2,1)} collective-permute-done((bf16[7104,128]{1,0:T(8,128)(2,1)S(1)}, bf16[7104,128]{1,0:T(8,128)(2,1)}, u32[]{:S(2)}, u32[]{:S(2)}) %collective-permute-start.5) | collective-permute-done | bytes 1818656 | tf_op jit(solution)/shard_map/ppermute | solution.py:267
  107.8 0.5 shard_map.83.token_ref
  108.3 32.4 %all-to-all-done = bf16[128,16,1024]{2,1,0:T(8,128)(2,1)} async-done(((bf16[128,16,1024]{2,1,0:T(8,128)(2,1)}), bf16[128,16,1024]{2,1,0:T(8,128)(2,1)}, u32[]{:S(2)}, u32[]{:S(2)}) %all-to-all-start) | async-done | bytes 4194336 | tf_op jit(solution)/shard_map/all_to_all | solution.py:298
  140.7 5.7 %shard_map.85 = (f32[512,128]{1,0:T(8,128)}, bf16[512,128]{1,0:T(8,128)(2,1)}, bf16[512,128]{1,0:T(8,128)(2,1)}, bf16[512,128]{1,0:T(8,128)(2,1)}) custom-call(s32[1]{0:T(128)} %bitcast.q_ref, s32[1]{0:T(128)} %shard_map.83.token_ref, bf16[2048,1024]{1,0:T(8,128)(2,1)} %bitcast.4.pairs_ref), custom_call_target="tpu_custom_call" | custom-call | tf_op jit(solution)/shard_map/pallas_call | solution.py:182
  146.4 1.2 collective-permute-start.7
  147.5 2.4 %collective-permute-start.8 = (bf16[512,128]{1,0:T(8,128)(2,1)}, bf16[512,128]{1,0:T(8,128)(2,1)S(1)}, u32[]{:S(2)}, u32[]{:S(2)}) collective-permute-start(bf16[512,128]{1,0:T(8,128)(2,1)} %get-tuple-element.31), channel_id=1, source_target_pairs={{0,2},{1,3},{2,0},{3,1},{4,6},{5,7},{6,4},{7,5},{8,10},{9,11},{10,... | collective-permute-start | bytes 393224 | tf_op jit(solution)/shard_map/ppermute | solution.py:259
  149.9 1.6 collective-permute-start.9
  151.5 0.6 pad_add_fusion.order_ref
  152.1 0.0 collective-permute-done.10.o1_ref
  152.1 0.0 collective-permute-done.11.o2_ref
  152.1 1.0 collective-permute-done.7.t1_ref
  153.1 3.1 %collective-permute-done.8.t2_ref = bf16[512,128]{1,0:T(8,128)(2,1)S(1)} collective-permute-done((bf16[512,128]{1,0:T(8,128)(2,1)}, bf16[512,128]{1,0:T(8,128)(2,1)S(1)}, u32[]{:S(2)}, u32[]{:S(2)}) %collective-permute-start.8) | collective-permute-done | bytes 131104 | tf_op jit(solution)/shard_map/ppermute | solution.py:259
  156.2 0.9 collective-permute-done.9.t3_ref
  157.1 0.0 copy-done.3
  157.1 0.0 copy-done.4
  157.1 0.6 copy-done.5
  157.7 11.9 %shard_map.86 = bf16[14208,128]{1,0:T(8,128)(2,1)} custom-call(s32[4]{0:T(128)} %pad_add_fusion.order_ref, f32[512,128]{1,0:T(8,128)} %get-tuple-element.29.t0_ref, bf16[512,128]{1,0:T(8,128)(2,1)} %copy-done.3, bf16[512,128]{1,0:T(8,128)(2,1)} %copy-done.4, bf16[512,128]{1,0:T(8,128)(2,1)} %copy-done.5, bf16[14208,128]{1,0:T(8,128)(2,1)} %own_ref.1, ...), custom_call_target="tpu_custom_call" | custom-call | tf_op jit(solution)/shard_map/pallas_call | solution.py:241
  (5 shorter events, 0.0 us)
Async XLA Ops:
  4.2 11.0 %collective-permute-start = (bf16[16,16,640]{2,1,0:T(8,128)(2,1)}, bf16[16,16,640]{2,1,0:T(8,128)(2,1)S(1)}, u32[]{:S(2)}, u32[]{:S(2)}) collective-permute-start(bf16[16,16,640]{2,1,0:T(8,128)(2,1)} %get-tuple-element.19), channel_id=1, source_target_pairs={{0,1},{1,2},{2,3},{3,0},{4,5},{5,6},{6,7},{7,4},{8,9},{9,10},{10,1... | collective-permute-start | bytes 983048 | tf_op jit(solution)/shard_map/ppermute | solution.py:259
  5.9 17.6 %collective-permute-start.1 = (bf16[16,16,640]{2,1,0:T(8,128)(2,1)}, bf16[16,16,640]{2,1,0:T(8,128)(2,1)S(1)}, u32[]{:S(2)}, u32[]{:S(2)}) collective-permute-start(bf16[16,16,640]{2,1,0:T(8,128)(2,1)} %get-tuple-element.20), channel_id=1, source_target_pairs={{0,2},{1,3},{2,0},{3,1},{4,6},{5,7},{6,4},{7,5},{8,10},{9,11},{10,... | collective-permute-start | bytes 983048 | tf_op jit(solution)/shard_map/ppermute | solution.py:259
  8.8 19.4 %copy-start.6 = (s32[16,4]{0,1:T(4,128)S(1)}, s32[16,4]{0,1:T(4,128)}, u32[]{:S(2)}) copy-start(s32[16,4]{0,1:T(4,128)} %param.14) | copy-start | bytes 772
  8.8 20.1 %copy-start.7 = (f32[16,4]{0,1:T(4,128)S(1)}, f32[16,4]{0,1:T(4,128)}, u32[]{:S(2)}) copy-start(f32[16,4]{0,1:T(4,128)} %param.15) | copy-start | bytes 772
  8.8 14.7 %collective-permute-start.2 = (bf16[16,16,640]{2,1,0:T(8,128)(2,1)}, bf16[16,16,640]{2,1,0:T(8,128)(2,1)S(1)}, u32[]{:S(2)}, u32[]{:S(2)}) collective-permute-start(bf16[16,16,640]{2,1,0:T(8,128)(2,1)} %get-tuple-element.21), channel_id=1, source_target_pairs={{0,3},{1,0},{2,1},{3,2},{4,7},{5,4},{6,5},{7,6},{8,11},{9,8},{10,9... | collective-permute-start | bytes 983048 | tf_op jit(solution)/shard_map/ppermute | solution.py:259
  15.2 14.3 %copy-start = (bf16[16,16,640]{2,1,0:T(8,128)(2,1)}, bf16[16,16,640]{2,1,0:T(8,128)(2,1)S(1)}, u32[]{:S(2)}) copy-start(bf16[16,16,640]{2,1,0:T(8,128)(2,1)S(1)} %collective-permute-done.r1_ref) | copy-start | bytes 983044
  23.4 6.1 %copy-start.1 = (bf16[16,16,640]{2,1,0:T(8,128)(2,1)}, bf16[16,16,640]{2,1,0:T(8,128)(2,1)S(1)}, u32[]{:S(2)}) copy-start(bf16[16,16,640]{2,1,0:T(8,128)(2,1)S(1)} %collective-permute-done.1.r2_ref) | copy-start | bytes 983044
  23.4 6.1 %copy-start.2 = (bf16[16,16,640]{2,1,0:T(8,128)(2,1)}, bf16[16,16,640]{2,1,0:T(8,128)(2,1)S(1)}, u32[]{:S(2)}) copy-start(bf16[16,16,640]{2,1,0:T(8,128)(2,1)S(1)} %collective-permute-done.2.r3_ref) | copy-start | bytes 983044
  23.4 42.8 %collective-permute-start.3 = (bf16[7104,128]{1,0:T(8,128)(2,1)S(1)}, bf16[7104,128]{1,0:T(8,128)(2,1)}, u32[]{:S(2)}, u32[]{:S(2)}) collective-permute-start(bf16[7104,128]{1,0:T(8,128)(2,1)S(1)} %get-tuple-element.22), channel_id=1, source_target_pairs={{0,1},{1,0},{2,3},{3,2},{4,5},{5,4},{6,7},{7,6},{8,9},{9,8},{10,11... | collective-permute-start | bytes 5455880 | tf_op jit(solution)/shard_map/ppermute | solution.py:263
  24.7 44.1 %collective-permute-start.6 = (bf16[7104,128]{1,0:T(8,128)(2,1)}, bf16[7104,128]{1,0:T(8,128)(2,1)}, u32[]{:S(2)}, u32[]{:S(2)}) collective-permute-start(bf16[7104,128]{1,0:T(8,128)(2,1)} %get-tuple-element.23), channel_id=1, source_target_pairs={{0,3},{3,0},{1,2},{2,1},{4,7},{7,4},{5,6},{6,5},{8,11},{11,8},{9,1... | collective-permute-start | bytes 5455880 | tf_op jit(solution)/shard_map/ppermute | solution.py:267
  26.6 78.6 %collective-permute-start.4 = (bf16[7104,128]{1,0:T(8,128)(2,1)}, bf16[7104,128]{1,0:T(8,128)(2,1)}, u32[]{:S(2)}, u32[]{:S(2)}) collective-permute-start(bf16[7104,128]{1,0:T(8,128)(2,1)} %get-tuple-element.23), channel_id=1, source_target_pairs={{0,1},{1,0},{2,3},{3,2},{4,5},{5,4},{6,7},{7,6},{8,9},{9,8},{10,11... | collective-permute-start | bytes 5455880 | tf_op jit(solution)/shard_map/ppermute | solution.py:263
  27.0 80.8 %collective-permute-start.5 = (bf16[7104,128]{1,0:T(8,128)(2,1)S(1)}, bf16[7104,128]{1,0:T(8,128)(2,1)}, u32[]{:S(2)}, u32[]{:S(2)}) collective-permute-start(bf16[7104,128]{1,0:T(8,128)(2,1)S(1)} %get-tuple-element.22), channel_id=1, source_target_pairs={{0,3},{3,0},{1,2},{2,1},{4,7},{7,4},{5,6},{6,5},{8,11},{11,8},{9,1... | collective-permute-start | bytes 5455880 | tf_op jit(solution)/shard_map/ppermute | solution.py:267
  34.5 106.2 %all-to-all-start = ((bf16[128,16,1024]{2,1,0:T(8,128)(2,1)}), bf16[128,16,1024]{2,1,0:T(8,128)(2,1)}, u32[]{:S(2)}, u32[]{:S(2)}) async-start(bf16[128,16,1024]{2,1,0:T(8,128)(2,1)} %shard_map.84), calls=%async_computation | async-start | bytes 8388608 | tf_op jit(solution)/shard_map/all_to_all | solution.py:298
  66.2 85.9 %collective-permute-start.10 = (bf16[7104,128]{1,0:T(8,128)(2,1)}, bf16[7104,128]{1,0:T(8,128)(2,1)}, u32[]{:S(2)}, u32[]{:S(2)}) collective-permute-start(bf16[7104,128]{1,0:T(8,128)(2,1)} %collective-permute-done.3.a1_ref), channel_id=1, source_target_pairs={{0,3},{3,0},{1,2},{2,1},{4,7},{7,4},{5,6},{6,5},{8,11},{11,8},{9,1... | collective-permute-start | bytes 5455880 | tf_op jit(solution)/shard_map/ppermute | solution.py:267
  68.8 83.3 %collective-permute-start.11 = (bf16[7104,128]{1,0:T(8,128)(2,1)}, bf16[7104,128]{1,0:T(8,128)(2,1)}, u32[]{:S(2)}, u32[]{:S(2)}) collective-permute-start(bf16[7104,128]{1,0:T(8,128)(2,1)} %collective-permute-done.6.b2_ref), channel_id=1, source_target_pairs={{0,1},{1,0},{2,3},{3,2},{4,5},{5,4},{6,7},{7,6},{8,9},{9,8},{10,11... | collective-permute-start | bytes 5455880 | tf_op jit(solution)/shard_map/ppermute | solution.py:263
  146.4 6.7 %collective-permute-start.7 = (bf16[512,128]{1,0:T(8,128)(2,1)}, bf16[512,128]{1,0:T(8,128)(2,1)S(1)}, u32[]{:S(2)}, u32[]{:S(2)}) collective-permute-start(bf16[512,128]{1,0:T(8,128)(2,1)} %get-tuple-element.30), channel_id=1, source_target_pairs={{0,1},{1,2},{2,3},{3,0},{4,5},{5,6},{6,7},{7,4},{8,9},{9,10},{10,1... | collective-permute-start | bytes 393224 | tf_op jit(solution)/shard_map/ppermute | solution.py:259
  147.5 8.7 %collective-permute-start.8 = (bf16[512,128]{1,0:T(8,128)(2,1)}, bf16[512,128]{1,0:T(8,128)(2,1)S(1)}, u32[]{:S(2)}, u32[]{:S(2)}) collective-permute-start(bf16[512,128]{1,0:T(8,128)(2,1)} %get-tuple-element.31), channel_id=1, source_target_pairs={{0,2},{1,3},{2,0},{3,1},{4,6},{5,7},{6,4},{7,5},{8,10},{9,11},{10,... | collective-permute-start | bytes 393224 | tf_op jit(solution)/shard_map/ppermute | solution.py:259
  149.9 7.1 %collective-permute-start.9 = (bf16[512,128]{1,0:T(8,128)(2,1)}, bf16[512,128]{1,0:T(8,128)(2,1)S(1)}, u32[]{:S(2)}, u32[]{:S(2)}) collective-permute-start(bf16[512,128]{1,0:T(8,128)(2,1)} %get-tuple-element.32), channel_id=1, source_target_pairs={{0,3},{1,0},{2,1},{3,2},{4,7},{5,4},{6,5},{7,6},{8,11},{9,8},{10,9... | collective-permute-start | bytes 393224 | tf_op jit(solution)/shard_map/ppermute | solution.py:259
  153.1 4.0 %copy-start.3 = (bf16[512,128]{1,0:T(8,128)(2,1)}, bf16[512,128]{1,0:T(8,128)(2,1)S(1)}, u32[]{:S(2)}) copy-start(bf16[512,128]{1,0:T(8,128)(2,1)S(1)} %collective-permute-done.7.t1_ref) | copy-start | bytes 393220
  156.2 0.9 copy-start.4
  157.1 0.7 copy-start.5

commit v4 on v3

v4 whole, which is shorter than its diff:
```python
import functools
import math

import jax
import jax.numpy as jnp
from jax import lax
from jax.experimental import pallas as pl
from jax.experimental.pallas import tpu as pltpu
from jax.sharding import PartitionSpec as P

VMEM_LIMIT = 24 * 1024 * 1024
FIRST_LIMIT = 60 * 1024 * 1024
GROUPS = 4
DEPTH = 8
CORES = 2
SLOTS = 2
STEPS = 6
SMALL = pl.CostEstimate(flops=10**6, bytes_accessed=10**6, transcendentals=0)


def first_kernel(
    q_ref, obs_ref, inv_ref, innov_ref, precision_ref, count_ref,
    gain_ref, innov_out_ref, m1_ref, m2_ref, m3_ref, rows_ref, live_ref,
):
    quarter, members = gain_ref.shape[1:]
    obs_rows, part = innov_ref.shape[1:]
    blocks = obs_ref.shape[0]
    q = q_ref[0]
    step = pl.program_id(0)
    position = lax.broadcasted_iota(jnp.int32, (obs_rows, part), 0)
    for k in range(blocks):
        rows_ref[...] = lax.dot_general(
            obs_ref[k], inv_ref[k], (((1,), (1,)), ((), ())), preferred_element_type=jnp.float32
        )
        block = step * blocks + k
        scale = jnp.broadcast_to(precision_ref[pl.ds(block, 1), :], (part, obs_rows)).T
        live_ref[...] = jnp.where(
            position < count_ref[block], scale * innov_ref[k].astype(jnp.float32), 0.0
        )
        own = pl.ds(pl.multiple_of(q * quarter, quarter), quarter)
        gain_ref[k] = rows_ref[own, :]
        innov_out_ref[k] = live_ref[own, :].astype(jnp.bfloat16)
        for d, ref in ((1, m1_ref), (2, m2_ref), (3, m3_ref)):
            rows = pl.ds(pl.multiple_of(lax.rem(q + d, GROUPS) * quarter, quarter), quarter)
            ref[k, :, :members] = rows_ref[rows, :].astype(jnp.bfloat16)
            ref[k, :, members:] = live_ref[rows, :].astype(jnp.bfloat16)


def first_parts(q, obs_anom, inverses, innovations, precision, obs_count):
    nblock, obs_rows, part = obs_anom.shape
    members = inverses.shape[1]
    quarter = obs_rows // GROUPS
    step = 4
    widths = [members, part] + [members + part] * 3
    types = [jnp.float32] + [jnp.bfloat16] * 4
    rows = pl.BlockSpec((step, obs_rows, part), lambda i, q: (i, 0, 0))
    return pl.pallas_call(
        first_kernel,
        grid_spec=pltpu.PrefetchScalarGridSpec(
            num_scalar_prefetch=1,
            grid=(nblock // step,),
            in_specs=[
                rows,
                pl.BlockSpec((step, members, part), lambda i, q: (i, 0, 0)),
                rows,
                pl.BlockSpec((nblock, obs_rows), lambda i, q: (0, 0)),
                pl.BlockSpec(memory_space=pltpu.SMEM),
            ],
            out_specs=[
                pl.BlockSpec((step, quarter, width), lambda i, q: (i, 0, 0)) for width in widths
            ],
            scratch_shapes=[
                pltpu.VMEM((obs_rows, members), jnp.float32),
                pltpu.VMEM((obs_rows, part), jnp.float32),
            ],
        ),
        out_shape=[
            jax.ShapeDtypeStruct((nblock, quarter, width), kind)
            for width, kind in zip(widths, types)
        ],
        compiler_params=pltpu.CompilerParams(vmem_limit_bytes=FIRST_LIMIT),
    )(q, obs_anom, inverses, innovations, precision, obs_count)


def merge_kernel(
    q_ref, chosen_ref, taper_ref, gain_ref, innov_ref, r1_ref, r2_ref, r3_ref, low_ref, high_ref
):
    members = gain_ref.shape[2]
    part = innov_ref.shape[2]
    half = high_ref.shape[0]
    q = q_ref[0]
    gain = (
        gain_ref[...]
        + r1_ref[:, :, :members].astype(jnp.float32)
        + r2_ref[:, :, :members].astype(jnp.float32)
        + r3_ref[:, :, :members].astype(jnp.float32)
    ).astype(jnp.bfloat16)
    for out_ref, blocks in ((low_ref, slice(0, half)), (high_ref, slice(half, 2 * half))):
        out_ref[:half, :, :members] = gain[blocks]
        start = pl.multiple_of(members + q * part, part)
        out_ref[:half, :, pl.ds(start, part)] = innov_ref[blocks]
        for d, ref in ((1, r1_ref), (2, r2_ref), (3, r3_ref)):
            start = pl.multiple_of(members + lax.rem(q - d + GROUPS, GROUPS) * part, part)
            out_ref[:half, :, pl.ds(start, part)] = ref[blocks, :, members:]
    lanes = chosen_ref.shape[1]
    low_ref[half] = jnp.zeros(low_ref.shape[1:], low_ref.dtype)
    quarter = low_ref.shape[1]
    rest = jnp.broadcast_to(taper_ref[...], (quarter, lanes))
    low_ref[half, :, :lanes] = jnp.broadcast_to(chosen_ref[...], (quarter, lanes)).astype(jnp.bfloat16)
    for k in range(1, 4):
        term = rest.astype(jnp.bfloat16)
        rest = rest - term.astype(jnp.float32)
        low_ref[half, :, k * lanes : (k + 1) * lanes] = term


def merge(q, chosen, taper, parts):
    nblock, quarter, members = parts[0].shape
    half = nblock // 2
    vmem = pl.BlockSpec(memory_space=pltpu.VMEM)
    return pl.pallas_call(
        merge_kernel,
        in_specs=[pl.BlockSpec(memory_space=pltpu.SMEM)] + [vmem] * (2 + len(parts)),
        out_specs=[vmem] * 2,
        out_shape=[
            jax.ShapeDtypeStruct((half + 1, quarter, 2 * members), jnp.bfloat16),
            jax.ShapeDtypeStruct((half, quarter, 2 * members), jnp.bfloat16),
        ],
        compiler_params=pltpu.CompilerParams(vmem_limit_bytes=VMEM_LIMIT),
        cost_estimate=SMALL,
    )(q, chosen, taper, *parts)


def sums_kernel(same, token_ref, place_ref, *refs):
    lows, highs, refs = refs[:DEPTH], refs[DEPTH : 2 * DEPTH], refs[2 * DEPTH :]
    others = ()
    if same:
        others, refs = refs[:GROUPS], refs[GROUPS:]
    outs, refs = refs[:GROUPS], refs[GROUPS:]
    all_ref, gain_ref, innov_ref, chosen_ref, taper_ref, chosen_smem, taper_smem, sems = refs
    half, quarter, width = highs[0].shape
    members = width // 2
    lanes = chosen_ref.shape[1]
    copies = []
    for k in range(DEPTH):
        copies.append(pltpu.make_async_copy(lows[k], all_ref.at[k, pl.ds(0, half + 1)], sems.at[2 * k]))
        copies.append(
            pltpu.make_async_copy(highs[k], all_ref.at[k, pl.ds(half + 1, half)], sems.at[2 * k + 1])
        )
    for copy in copies:
        copy.start()
    for k in range(DEPTH):
        copies[2 * k].wait()
        meta = all_ref[k, half, :, : 4 * lanes].astype(jnp.float32)[0:1]
        block = meta[:, :lanes].astype(jnp.int32)
        chosen_ref[pl.ds(k, 1), :] = block + jnp.where(block < half, 0, 1)
        taper_ref[pl.ds(k, 1), :] = (
            meta[:, lanes : 2 * lanes] + meta[:, 2 * lanes : 3 * lanes] + meta[:, 3 * lanes :]
        )
    tables = [
        pltpu.make_async_copy(chosen_ref, chosen_smem, sems.at[2 * DEPTH]),
        pltpu.make_async_copy(taper_ref, taper_smem, sems.at[2 * DEPTH + 1]),
    ]
    for copy in tables:
        copy.start()
    for k in range(DEPTH):
        copies[2 * k + 1].wait()
    for copy in tables:
        copy.wait()
    core = place_ref[2] if same else 1 - place_ref[2]
    for away in range(GROUPS):
        column = lax.rem(place_ref[0] + away, GROUPS)
        tile = (column * DEPTH + place_ref[1]) * CORES + core
        for k in range(DEPTH):
            for r in range(SLOTS):
                entry = r * (lanes // SLOTS) + tile
                block = chosen_smem[k, entry]
                rows = pl.ds((k * SLOTS + r) * quarter, quarter)
                gain = all_ref[k, block, :, :members].astype(jnp.float32)
                gain_ref[away, rows, :] = (taper_smem[k, entry] * gain).astype(jnp.bfloat16)
                innov_ref[away, rows, :] = all_ref[k, block, :, members:]
        total = lax.dot_general(
            gain_ref[away],
            innov_ref[away],
            (((0,), (0,)), ((), ())),
            preferred_element_type=jnp.float32,
        )
        if same:
            total = total + others[away][...].astype(jnp.float32)
        outs[away][...] = total.astype(outs[away].dtype)


def sums(same, token, place, lows, highs, others=()):
    half, quarter, width = highs[0].shape
    members = width // 2
    lanes = 128
    kinds = [jnp.float32 if same else jnp.bfloat16] + [jnp.bfloat16] * (GROUPS - 1)
    taken = (GROUPS, DEPTH * SLOTS * quarter, members)
    return pl.pallas_call(
        functools.partial(sums_kernel, same),
        in_specs=[pl.BlockSpec(memory_space=pltpu.SMEM)] * 2
        + [pl.BlockSpec(memory_space=pl.ANY)] * (2 * DEPTH)
        + [pl.BlockSpec(memory_space=pltpu.VMEM)] * len(others),
        out_specs=[pl.BlockSpec(memory_space=pltpu.VMEM)] * GROUPS,
        out_shape=[jax.ShapeDtypeStruct((members, members), kind) for kind in kinds],
        scratch_shapes=[
            pltpu.VMEM((DEPTH, 2 * half + 1, quarter, width), jnp.bfloat16),
            pltpu.VMEM(taken, jnp.bfloat16),
            pltpu.VMEM(taken, jnp.bfloat16),
            pltpu.VMEM((DEPTH, lanes), jnp.int32),
            pltpu.VMEM((DEPTH, lanes), jnp.float32),
            pltpu.SMEM((DEPTH, lanes), jnp.int32),
            pltpu.SMEM((DEPTH, lanes), jnp.float32),
            pltpu.SemaphoreType.DMA((2 * DEPTH + 2,)),
        ],
        compiler_params=pltpu.CompilerParams(vmem_limit_bytes=VMEM_LIMIT),
        cost_estimate=SMALL,
    )(token, place, *lows, *highs, *others)


def arrived_kernel(*refs):
    refs[-1][0] = 0


def arrived(*arrays):
    return pl.pallas_call(
        arrived_kernel,
        in_specs=[pl.BlockSpec(memory_space=pl.ANY)] * len(arrays),
        out_specs=pl.BlockSpec(memory_space=pltpu.SMEM),
        out_shape=jax.ShapeDtypeStruct((1,), jnp.int32),
        cost_estimate=pl.CostEstimate(flops=10**12, bytes_accessed=10**9, transcendentals=0),
    )(*arrays)


def transform_kernel(q_ref, token_ref, r0_ref, r1_ref, r2_ref, r3_ref, own_ref, s1_ref, s2_ref, s3_ref):
    q = q_ref[0]
    members, part = own_ref.shape
    for d, out_ref in enumerate((own_ref, s1_ref, s2_ref, s3_ref)):
        columns = pl.ds(pl.multiple_of(lax.rem(q + d, GROUPS) * part, part), part)
        total = (
            r0_ref[:, columns]
            + r1_ref[:, columns].astype(jnp.float32)
            + r2_ref[:, columns].astype(jnp.float32)
            + r3_ref[:, columns].astype(jnp.float32)
        )
        mean = jnp.sum(total, axis=0, keepdims=True) / members
        out_ref[...] = ((total - mean) * (1.0 / math.sqrt(members - 1))).astype(out_ref.dtype)


def transform_parts(q, token, sums_here):
    members = sums_here[0].shape[0]
    part = members // GROUPS
    return pl.pallas_call(
        transform_kernel,
        in_specs=[pl.BlockSpec(memory_space=pltpu.SMEM)] * 2
        + [pl.BlockSpec(memory_space=pltpu.VMEM)] * GROUPS,
        out_specs=[pl.BlockSpec(memory_space=pltpu.VMEM)] * GROUPS,
        out_shape=[jax.ShapeDtypeStruct((members, part), jnp.float32)]
        + [jax.ShapeDtypeStruct((members, part), jnp.bfloat16)] * 3,
        compiler_params=pltpu.CompilerParams(vmem_limit_bytes=VMEM_LIMIT),
        cost_estimate=SMALL,
    )(q, token, *sums_here)


def update_kernel(
    order_ref, t0_ref, t1_ref, t2_ref, t3_ref, own_ref, a1_ref, a2_ref, b1_ref, b2_ref, o1_ref, o2_ref,
    out_ref, raw_ref, weights_ref, states_ref, result_ref, in_sems, out_sems,
):
    part = own_ref.shape[1]
    step = result_ref.shape[1]
    half = STEPS // 2
    loads = []
    for i in range(STEPS):
        sources = (a1_ref, b1_ref, o1_ref) if i < half else (a2_ref, b2_ref, o2_ref)
        views = [own_ref.at[pl.ds(i * step, step)]]
        views += [ref.at[pl.ds((i % half) * step, step)] for ref in sources]
        loads.append(
            [
                pltpu.make_async_copy(view, states_ref.at[i, k], in_sems.at[i, k])
                for k, view in enumerate(views)
            ]
        )
        for load in loads[-1]:
            load.start()
    total = (
        t0_ref[...]
        + t1_ref[...].astype(jnp.float32)
        + t2_ref[...].astype(jnp.float32)
        + t3_ref[...].astype(jnp.float32)
    ).astype(jnp.bfloat16)
    raw_ref[...] = total.reshape(raw_ref.shape)
    for k in range(GROUPS):
        weights_ref[pl.ds(k * part, part), :] = raw_ref[order_ref[k]]
    stores = []
    for i in range(STEPS):
        for load in loads[i]:
            load.wait()
        states = jnp.concatenate([states_ref[i, k] for k in range(GROUPS)], axis=1)
        increment = jnp.dot(states, weights_ref[...], preferred_element_type=jnp.float32)
        result_ref[i] = (states_ref[i, 0].astype(jnp.float32) + increment).astype(result_ref.dtype)
        stores.append(
            pltpu.make_async_copy(
                result_ref.at[i], out_ref.at[pl.ds(i * step, step)], out_sems.at[i]
            )
        )
        stores[-1].start()
    for store in stores:
        store.wait()


def update(order, pieces, own, others):
    rows, part = own.shape
    members = pieces[0].shape[0]
    step = rows // STEPS
    return pl.pallas_call(
        update_kernel,
        in_specs=[pl.BlockSpec(memory_space=pltpu.SMEM)]
        + [pl.BlockSpec(memory_space=pltpu.VMEM)] * GROUPS
        + [pl.BlockSpec(memory_space=pl.ANY)] * (1 + len(others)),
        out_specs=pl.BlockSpec(memory_space=pl.ANY),
        out_shape=jax.ShapeDtypeStruct((rows, part), jnp.bfloat16),
        scratch_shapes=[
            pltpu.VMEM((GROUPS, part, part), jnp.bfloat16),
            pltpu.VMEM((members, part), jnp.bfloat16),
            pltpu.VMEM((STEPS, GROUPS, step, part), jnp.bfloat16),
            pltpu.VMEM((STEPS, step, part), jnp.bfloat16),
            pltpu.SemaphoreType.DMA((STEPS, GROUPS)),
            pltpu.SemaphoreType.DMA((STEPS,)),
        ],
        compiler_params=pltpu.CompilerParams(vmem_limit_bytes=FIRST_LIMIT),
    )(order, *pieces, own, *others)


def shift(x, d):
    return lax.ppermute(x, "mem", [(i, (i + d) % GROUPS) for i in range(GROUPS)])


def swap_a(x):
    return lax.ppermute(x, "mem", [(0, 1), (1, 0), (2, 3), (3, 2)])


def swap_b(x):
    return lax.ppermute(x, "mem", [(0, 3), (3, 0), (1, 2), (2, 1)])


def move(x, columns, away=(0, 0, 0)):
    pairs = []
    for c in range(columns):
        for z in range(DEPTH):
            for k in range(CORES):
                target = (c + away[0]) % columns, (z + away[1]) % DEPTH, (k + away[2]) % CORES
                pairs.append(
                    ((c * DEPTH + z) * CORES + k, (target[0] * DEPTH + target[1]) * CORES + target[2])
                )
    return lax.ppermute(x, "tile", pairs)


def per_device(
    ensemble, obs_anom, inverses, innovations, precision, obs_count, loc_tiles, taper_weight
):
    columns = lax.axis_size("tile") // (DEPTH * CORES)
    nblock = obs_anom.shape[0]
    rows = ensemble.shape[0]
    loc_count = loc_tiles.shape[1]
    pairs = nblock * loc_count
    q = lax.axis_index("mem").astype(jnp.int32)
    q1 = q.reshape(1)
    order = jnp.stack([q, q ^ 1, 3 - q, q ^ 2])
    tile = lax.axis_index("tile").astype(jnp.int32)
    place = jnp.stack([tile // (DEPTH * CORES), (tile // CORES) & (DEPTH - 1), tile & (CORES - 1)])

    gain, innov, m1, m2, m3 = first_parts(
        q1, obs_anom, inverses, innovations, precision, obs_count
    )
    m1, m2, m3 = shift(m1, 1), shift(m2, 2), shift(m3, 3)

    tiles = columns * DEPTH * CORES
    loc = loc_tiles.reshape(pairs, 1)
    hits = (loc == lax.broadcasted_iota(jnp.int32, (pairs, tiles), 1)).astype(jnp.float32)
    same_tile = (loc == loc_tiles.reshape(1, pairs)).astype(jnp.float32)
    pair_at = lax.broadcasted_iota(jnp.int32, (pairs, 1), 0)
    earlier = (lax.broadcasted_iota(jnp.int32, (pairs, pairs), 1) < pair_at).astype(jnp.float32)
    rank = jnp.sum(same_tile * earlier, axis=1, keepdims=True)
    ranked = jnp.concatenate([hits * (rank == r).astype(jnp.float32) for r in range(SLOTS)], axis=1)
    block_of = (pair_at // loc_count).astype(jnp.float32)
    chosen = jnp.sum(ranked * block_of, axis=0, keepdims=True)
    tapers = jnp.sum(ranked * taper_weight.reshape(pairs, 1), axis=0, keepdims=True)

    half = rows // 2
    chosen, tapers, m1, m2, m3, low, high = lax.optimization_barrier(
        (chosen, tapers, m1, m2, m3, ensemble[:half], ensemble[half:])
    )
    a1, b2 = swap_a(low), swap_b(high)
    a2, b1 = swap_a(high), swap_b(low)
    o1, o2 = swap_b(a1), swap_a(b2)

    up, down = (0, 1, 0), (0, -1, 0)
    own_blocks = tuple(merge(q1, chosen, tapers, (gain, innov, m1, m2, m3)))
    ups, downs = [own_blocks], [own_blocks]
    for _ in range(3):
        ups.append(tuple(move(x, columns, up) for x in ups[-1]))
        downs.append(tuple(move(x, columns, down) for x in downs[-1]))
    far = (move(ups[-1][0], columns, up), move(downs[-1][1], columns, down))
    held = ups + downs[1:] + [far]
    lows, highs = [h[0] for h in held], [h[1] for h in held]
    token = arrived(a1, b2, *far)
    others = sums(0, token, place, lows, highs)
    others = [move(x, columns, (0, 0, 1)) for x in others]
    here, e1, e2, e3 = sums(1, token, place, lows, highs, others)
    e1, e2, e3 = move(e1, columns, (1, 0, 0)), move(e2, columns, (2, 0, 0)), move(e3, columns, (3, 0, 0))
    token = arrived(a2, b1, e1, e2, e3)
    t0, t1, t2, t3 = transform_parts(q1, token, (here, e1, e2, e3))
    pieces = [t0, shift(t1, 1), shift(t2, 2), shift(t3, 3)]
    return update(order, pieces, ensemble, (a1, a2, b1, b2, o1, o2))


def solution(mesh):
    return jax.shard_map(
        per_device,
        mesh=mesh,
        in_specs=(
            P("tile", "mem"),
            P("tile", None, "mem"),
            P("tile", None, "mem"),
            P("tile", None, "mem"),
            P("tile", None),
            P("tile"),
            P("tile", None),
            P("tile", None),
        ),
        out_specs=P("tile", "mem"),
        check_vma=False,
    )
```

time: 172 us -> 171 us (level); the launches traced: 170 us -> 170 us
  waiting for transfers between devices: 106 us -> 81.3 us
  starting transfers between devices: 30.1 us -> 44.4 us
  local copies, waits for them, and re-layouts: 5.52 us -> 19 us
  Pallas kernels: 27.3 us -> 24.1 us
    ppermute x3, waiting for transfers between devices: 55.7 us -> 7.09 us  [swap_a(): return lax.ppermute(x, 'mem', [(0, 1), (1, 0), (2, 3), (3, 2)])]
    ppermute x0 -> x21, waiting for transfers between devices: none -> 35.7 us  [move(): return lax.ppermute(x, 'tile', pairs)]
    all_to_all x1 -> x0, waiting for transfers between devices: 32.4 us -> none  [per_device(): lax.all_to_all(send, 'tile', split_axis=0, concat_axis=0, tiled=True)]
    ppermute x0 -> x21, starting transfers between devices: none -> 24.5 us  [move(): return lax.ppermute(x, 'tile', pairs)]
    ppermute x6, waiting for transfers between devices: 14.8 us -> 28.7 us  [shift(): lax.ppermute(x, 'mem', [(i, (i + d) % GROUPS) for i in range(GROUPS)])]
    unnamed x18 -> x84, local copies, waits for them, and re-layouts: 0.84 us -> 14.6 us
    all_to_all x1 -> x0, starting transfers between devices: 12.4 us -> none  [per_device(): lax.all_to_all(send, 'tile', split_axis=0, concat_axis=0, tiled=True)]
    ppermute x3, waiting for transfers between devices: 3.16 us -> 9.87 us  [swap_b(): return lax.ppermute(x, 'mem', [(0, 3), (3, 0), (1, 2), (2, 1)])]
  transfers between devices with their start and end apart: 13 -> 33, of which waited for: 10 -> 18; matrix products, arithmetic and copies ran while one was open for 3% -> 3% of each run, Pallas kernels for 7% -> 6%
where the time goes in v4:
time: 171 us; the launch traced here: 170 us
  waiting for transfers between devices  81.3 us (48%)
  starting transfers between devices  44.4 us (26%)
  Pallas kernels  24.1 us (14%)
  local copies, waits for them, and re-layouts  19 us (11%)
    ppermute x21, waiting for transfers between devices, move(): return lax.ppermute(x, 'tile', pairs)  35.7 us
    ppermute x6, waiting for transfers between devices, shift(): lax.ppermute(x, 'mem', [(i, (i + d) % GROUPS) for i in range(GROUPS)])  28.7 us
    ppermute x21, starting transfers between devices, move(): return lax.ppermute(x, 'tile', pairs)  24.5 us
    unnamed x84, local copies, waits for them, and re-layouts  14.6 us
    ppermute x6, starting transfers between devices, shift(): lax.ppermute(x, 'mem', [(i, (i + d) % GROUPS) for i in range(GROUPS)])  11.8 us
    ppermute x3, waiting for transfers between devices, swap_b(): return lax.ppermute(x, 'mem', [(0, 3), (3, 0), (1, 2), (2, 1)])  9.87 us
    pallas_call x1, Pallas kernels, update(): pl.pallas_call(update_kernel, in_specs=[pl.BlockSpec(memory_space=pltpu.S...  8.94 us
    pallas_call x2, Pallas kernels, sums(): pl.pallas_call(functools.partial(sums_kernel, same), in_specs=[pl.BlockSp...  8.61 us
  transfers between devices with their start and end apart: 33, of which 18 were waited for; matrix products, arithmetic and copies ran while one was open for 3% of the time, Pallas kernels for 6%

profile of v4, /device:TPU:6, one launch (start us, length us, event | category | flops | bytes accessed | tf_op | source)
XLA Modules:
  0.0 170.4 jit_solution(8812837379855229944)
XLA Ops:
  0.0 4.3 %shard_map.82 = (f32[16,16,512]{2,1,0:T(8,128)}, bf16[16,16,128]{2,1,0:T(8,128)(2,1)}, bf16[16,16,640]{2,1,0:T(8,128)(2,1)}, bf16[16,16,640]{2,1,0:T(8,128)(2,1)}, bf16[16,16,640]{2,1,0:T(8,128)(2,1)}) custom-call(s32[1]{0:T(128)} %bitcast.q_ref, bf16[16,64,128]{2,1,0:T(8,128)(2,1)} %obs_ref.1, bf16[16,512,128]{2,1,0:T(8,128)(2,1)} %inv_ref.1, ...), custom_call_target="tpu_custom_call" | custom-call | tf_op jit(solution)/shard_map/pallas_call | solution.py:57
  4.3 1.6 collective-permute-start
  5.9 2.9 %collective-permute-start.1 = (bf16[16,16,640]{2,1,0:T(8,128)(2,1)}, bf16[16,16,640]{2,1,0:T(8,128)(2,1)S(1)}, u32[]{:S(2)}, u32[]{:S(2)}) collective-permute-start(bf16[16,16,640]{2,1,0:T(8,128)(2,1)} %get-tuple-element.32), channel_id=1, source_target_pairs={{0,2},{1,3},{2,0},{3,1},{4,6},{5,7},{6,4},{7,5},{8,10},{9,11},{10,... | collective-permute-start | bytes 983048 | tf_op jit(solution)/shard_map/ppermute | solution.py:334
  8.8 1.3 collective-permute-start.2
  10.8 4.2 %fusion.3 = (bf16[7104,128]{1,0:T(8,128)(2,1)}, bf16[7104,128]{1,0:T(8,128)(2,1)}) fusion(bf16[14208,128]{1,0:T(8,128)(2,1)} %own_ref.1), kind=kLoop, calls=%fused_computation.17 | loop fusion | bytes 7274496 | tf_op jit(solution)/shard_map/slice | solution.py:390
  15.3 8.2 %collective-permute-done.1.r2_ref = bf16[16,16,640]{2,1,0:T(8,128)(2,1)S(1)} collective-permute-done((bf16[16,16,640]{2,1,0:T(8,128)(2,1)}, bf16[16,16,640]{2,1,0:T(8,128)(2,1)S(1)}, u32[]{:S(2)}, u32[]{:S(2)}) %collective-permute-start.1) | collective-permute-done | bytes 327712 | tf_op jit(solution)/shard_map/ppermute | solution.py:334
  23.5 1.2 collective-permute-start.5
  24.7 1.9 %collective-permute-start.6 = (bf16[7104,128]{1,0:T(8,128)(2,1)}, bf16[7104,128]{1,0:T(8,128)(2,1)}, u32[]{:S(2)}, u32[]{:S(2)}) collective-permute-start(bf16[7104,128]{1,0:T(8,128)(2,1)} %get-tuple-element.34), channel_id=1, source_target_pairs={{0,3},{3,0},{1,2},{2,1},{4,7},{7,4},{5,6},{6,5},{8,11},{11,8},{9,1... | collective-permute-start | bytes 5455880 | tf_op jit(solution)/shard_map/ppermute | solution.py:342
  26.8 2.0 %collective-permute-start.7 = (bf16[9,16,1024]{2,1,0:T(8,128)(2,1)S(1)}, bf16[9,16,1024]{2,1,0:T(8,128)(2,1)S(1)}, u32[]{:S(2)}, u32[]{:S(2)}) collective-permute-start(bf16[9,16,1024]{2,1,0:T(8,128)(2,1)S(1)} %get-tuple-element.43.refs_0_), channel_id=1, source_target_pairs={{0,8},{4,12},{8,16},{12,20},{16,24},{20,28},{24,32},{28,36},{32,40... | collective-permute-start | bytes 884744 | tf_op jit(solution)/shard_map/ppermute | solution.py:354
  28.8 4.0 %collective-permute-start.11 = (bf16[8,16,1024]{2,1,0:T(8,128)(2,1)S(1)}, bf16[8,16,1024]{2,1,0:T(8,128)(2,1)S(1)}, u32[]{:S(2)}, u32[]{:S(2)}) collective-permute-start(bf16[8,16,1024]{2,1,0:T(8,128)(2,1)S(1)} %get-tuple-element.44.refs_8_), channel_id=1, source_target_pairs={{0,56},{4,60},{8,0},{12,4},{16,8},{20,12},{24,16},{28,20},{32,24},... | collective-permute-start | bytes 786440 | tf_op jit(solution)/shard_map/ppermute | solution.py:354
  32.8 0.7 copy-done.12
  33.6 7.1 %collective-permute-done.7.refs_1_ = bf16[9,16,1024]{2,1,0:T(8,128)(2,1)S(1)} collective-permute-done((bf16[9,16,1024]{2,1,0:T(8,128)(2,1)S(1)}, bf16[9,16,1024]{2,1,0:T(8,128)(2,1)S(1)}, u32[]{:S(2)}, u32[]{:S(2)}) %collective-permute-start.7) | collective-permute-done | bytes 294944 | tf_op jit(solution)/shard_map/ppermute | solution.py:354
  41.4 3.2 %collective-permute-start.15 = (bf16[9,16,1024]{2,1,0:T(8,128)(2,1)S(1)}, bf16[9,16,1024]{2,1,0:T(8,128)(2,1)S(1)}, u32[]{:S(2)}, u32[]{:S(2)}) collective-permute-start(bf16[9,16,1024]{2,1,0:T(8,128)(2,1)S(1)} %get-tuple-element.43.refs_0_), channel_id=1, source_target_pairs={{0,56},{4,60},{8,0},{12,4},{16,8},{20,12},{24,16},{28,20},{32,24},... | collective-permute-start | bytes 884744 | tf_op jit(solution)/shard_map/ppermute | solution.py:354
  45.3 0.9 collective-permute-done.18.refs_9_
  46.3 2.0 %collective-permute-start.12 = (bf16[8,16,1024]{2,1,0:T(8,128)(2,1)S(1)}, bf16[8,16,1024]{2,1,0:T(8,128)(2,1)S(1)}, u32[]{:S(2)}, u32[]{:S(2)}) collective-permute-start(bf16[8,16,1024]{2,1,0:T(8,128)(2,1)S(1)} %collective-permute-done.11.refs_12_), channel_id=1, source_target_pairs={{0,56},{4,60},{8,0},{12,4},{16,8},{20,12},{24,16},{28,20},{32,24},... | collective-permute-start | bytes 786440 | tf_op jit(solution)/shard_map/ppermute | solution.py:354
  49.0 1.6 collective-permute-done.8.refs_2_
  52.0 1.8 %collective-permute-done.12.refs_13_ = bf16[8,16,1024]{2,1,0:T(8,128)(2,1)S(1)} collective-permute-done((bf16[8,16,1024]{2,1,0:T(8,128)(2,1)S(1)}, bf16[8,16,1024]{2,1,0:T(8,128)(2,1)S(1)}, u32[]{:S(2)}, u32[]{:S(2)}) %collective-permute-start.12) | collective-permute-done | bytes 262176 | tf_op jit(solution)/shard_map/ppermute | solution.py:354
  53.9 2.7 %collective-permute-start.13 = (bf16[8,16,1024]{2,1,0:T(8,128)(2,1)S(1)}, bf16[8,16,1024]{2,1,0:T(8,128)(2,1)S(1)}, u32[]{:S(2)}, u32[]{:S(2)}) collective-permute-start(bf16[8,16,1024]{2,1,0:T(8,128)(2,1)S(1)} %collective-permute-done.12.refs_13_), channel_id=1, source_target_pairs={{0,56},{4,60},{8,0},{12,4},{16,8},{20,12},{24,16},{28,20},{32,24},... | collective-permute-start | bytes 786440 | tf_op jit(solution)/shard_map/ppermute | solution.py:354
  57.3 7.4 %collective-permute-done.19.refs_10_ = bf16[8,16,1024]{2,1,0:T(8,128)(2,1)} collective-permute-done((bf16[8,16,1024]{2,1,0:T(8,128)(2,1)S(1)}, bf16[8,16,1024]{2,1,0:T(8,128)(2,1)}, u32[]{:S(2)}, u32[]{:S(2)}) %collective-permute-start.19) | collective-permute-done | bytes 262176 | tf_op jit(solution)/shard_map/ppermute | solution.py:354
  65.6 1.8 %collective-permute-start.10 = (bf16[9,16,1024]{2,1,0:T(8,128)(2,1)S(1)}, bf16[9,16,1024]{2,1,0:T(8,128)(2,1)S(1)}, u32[]{:S(2)}, u32[]{:S(2)}) collective-permute-start(bf16[9,16,1024]{2,1,0:T(8,128)(2,1)S(1)} %collective-permute-done.9.refs_3_), channel_id=1, source_target_pairs={{0,8},{4,12},{8,16},{12,20},{16,24},{20,28},{24,32},{28,36},{32,40... | collective-permute-start | bytes 884744 | tf_op jit(solution)/shard_map/ppermute | solution.py:354
  68.1 1.5 collective-permute-start.14
  70.4 3.4 %collective-permute-done.16.refs_5_ = bf16[9,16,1024]{2,1,0:T(8,128)(2,1)} collective-permute-done((bf16[9,16,1024]{2,1,0:T(8,128)(2,1)S(1)}, bf16[9,16,1024]{2,1,0:T(8,128)(2,1)}, u32[]{:S(2)}, u32[]{:S(2)}) %collective-permute-start.16) | collective-permute-done | bytes 294944 | tf_op jit(solution)/shard_map/ppermute | solution.py:354
  73.8 2.4 %collective-permute-start.3 = (bf16[7104,128]{1,0:T(8,128)(2,1)}, bf16[7104,128]{1,0:T(8,128)(2,1)}, u32[]{:S(2)}, u32[]{:S(2)}) collective-permute-start(bf16[7104,128]{1,0:T(8,128)(2,1)} %get-tuple-element.34), channel_id=1, source_target_pairs={{0,1},{1,0},{2,3},{3,2},{4,5},{5,4},{6,7},{7,6},{8,9},{9,8},{10,11... | collective-permute-start | bytes 5455880 | tf_op jit(solution)/shard_map/ppermute | solution.py:338
  76.5 1.1 collective-permute-start.4
  77.7 3.2 %collective-permute-start.17 = (bf16[9,16,1024]{2,1,0:T(8,128)(2,1)}, bf16[9,16,1024]{2,1,0:T(8,128)(2,1)}, u32[]{:S(2)}, u32[]{:S(2)}) collective-permute-start(bf16[9,16,1024]{2,1,0:T(8,128)(2,1)} %collective-permute-done.16.refs_5_), channel_id=1, source_target_pairs={{0,56},{4,60},{8,0},{12,4},{16,8},{20,12},{24,16},{28,20},{32,24},... | collective-permute-start | bytes 884744 | tf_op jit(solution)/shard_map/ppermute | solution.py:354
  81.5 4.0 %collective-permute-done.20.refs_11_ = bf16[8,16,1024]{2,1,0:T(8,128)(2,1)} collective-permute-done((bf16[8,16,1024]{2,1,0:T(8,128)(2,1)}, bf16[8,16,1024]{2,1,0:T(8,128)(2,1)}, u32[]{:S(2)}, u32[]{:S(2)}) %collective-permute-start.20) | collective-permute-done | bytes 262176 | tf_op jit(solution)/shard_map/ppermute | solution.py:354
  85.7 1.0 copy-done.11
  86.6 0.9 copy-done.25
  87.6 4.3 %shard_map.85 = (bf16[512,512]{1,0:T(8,128)(2,1)S(1)}, bf16[512,512]{1,0:T(8,128)(2,1)S(1)}, bf16[512,512]{1,0:T(8,128)(2,1)S(1)}, bf16[512,512]{1,0:T(8,128)(2,1)S(1)}) custom-call(s32[1]{0:T(128)} %shard_map.84.token_ref, s32[3]{0:T(128)S(1)} %pad_add_fusion.1.place_ref, bf16[9,16,1024]{2,1,0:T(8,128)(2,1)S(1)} %copy-done.1, ...), custom_call_target="tpu_custom_call" | custom-call | flops 1000000 | bytes 1000000 | tf_op jit(solution)/shard_map/pallas_call | solution.py:198
  92.6 1.3 collective-permute-done.21.refs_16_
  94.7 0.7 collective-permute-done.23.refs_18_
  95.4 0.7 collective-permute-done.24.refs_19_
  96.2 4.3 %shard_map.86 = (f32[512,512]{1,0:T(8,128)S(1)}, bf16[512,512]{1,0:T(8,128)(2,1)S(1)}, bf16[512,512]{1,0:T(8,128)(2,1)S(1)}, bf16[512,512]{1,0:T(8,128)(2,1)S(1)}) custom-call(s32[1]{0:T(128)} %shard_map.84.token_ref, s32[3]{0:T(128)S(1)} %pad_add_fusion.1.place_ref, bf16[9,16,1024]{2,1,0:T(8,128)(2,1)S(1)} %copy-done.1, bf16[9,16,1024]{2,1,0:T(8,128)(2,1)S(1)} %copy-done.3, ...), custom_call_target="tpu_custom_call" | custom-call | flops 1000000 | bytes 1000000 | tf_op jit(solution)/shard_map/pallas_call | solution.py:198
  101.0 2.4 %collective-permute-start.26 = (bf16[512,512]{1,0:T(8,128)(2,1)S(1)}, bf16[512,512]{1,0:T(8,128)(2,1)S(1)}, u32[]{:S(2)}, u32[]{:S(2)}) collective-permute-start(bf16[512,512]{1,0:T(8,128)(2,1)S(1)} %get-tuple-element.50), channel_id=1, source_target_pairs={{0,128},{4,132},{8,136},{12,140},{16,144},{20,148},{24,152},{28,15... | collective-permute-start | bytes 1572872 | tf_op jit(solution)/shard_map/ppermute | solution.py:354
  103.4 7.1 %collective-permute-done.3.refs_0_.a2_ref = bf16[7104,128]{1,0:T(8,128)(2,1)} collective-permute-done((bf16[7104,128]{1,0:T(8,128)(2,1)}, bf16[7104,128]{1,0:T(8,128)(2,1)}, u32[]{:S(2)}, u32[]{:S(2)}) %collective-permute-start.3) | collective-permute-done | bytes 1818656 | tf_op jit(solution)/shard_map/ppermute | solution.py:338
  110.8 9.9 %collective-permute-done.4.refs_1_.b1_ref = bf16[7104,128]{1,0:T(8,128)(2,1)} collective-permute-done((bf16[7104,128]{1,0:T(8,128)(2,1)}, bf16[7104,128]{1,0:T(8,128)(2,1)}, u32[]{:S(2)}, u32[]{:S(2)}) %collective-permute-start.4) | collective-permute-done | bytes 1818656 | tf_op jit(solution)/shard_map/ppermute | solution.py:342
  120.6 1.2 collective-permute-start.32
  121.8 5.6 %collective-permute-done.27.refs_4_.r3_ref = bf16[512,512]{1,0:T(8,128)(2,1)S(1)} collective-permute-done((bf16[512,512]{1,0:T(8,128)(2,1)S(1)}, bf16[512,512]{1,0:T(8,128)(2,1)S(1)}, u32[]{:S(2)}, u32[]{:S(2)}) %collective-permute-start.27) | collective-permute-done | bytes 524320 | tf_op jit(solution)/shard_map/ppermute | solution.py:354
  127.4 0.8 copy-done.32
  128.8 1.0 copy-done.29
  129.8 1.0 copy-done.31
  130.9 1.0 copy-done.33
  131.9 1.1 shard_map.88
  133.7 1.3 collective-permute-start.28
  135.0 2.2 %collective-permute-start.29 = (bf16[512,128]{1,0:T(8,128)(2,1)S(1)}, bf16[512,128]{1,0:T(8,128)(2,1)S(1)}, u32[]{:S(2)}, u32[]{:S(2)}) collective-permute-start(bf16[512,128]{1,0:T(8,128)(2,1)S(1)} %get-tuple-element.55), channel_id=1, source_target_pairs={{0,2},{1,3},{2,0},{3,1},{4,6},{5,7},{6,4},{7,5},{8,10},{9,11},{10,... | collective-permute-start | bytes 393224 | tf_op jit(solution)/shard_map/ppermute | solution.py:334
  137.2 2.4 %collective-permute-start.30 = (bf16[512,128]{1,0:T(8,128)(2,1)S(1)}, bf16[512,128]{1,0:T(8,128)(2,1)S(1)}, u32[]{:S(2)}, u32[]{:S(2)}) collective-permute-start(bf16[512,128]{1,0:T(8,128)(2,1)S(1)} %get-tuple-element.56), channel_id=1, source_target_pairs={{0,3},{1,0},{2,1},{3,2},{4,7},{5,4},{6,5},{7,6},{8,11},{9,8},{10,9... | collective-permute-start | bytes 393224 | tf_op jit(solution)/shard_map/ppermute | solution.py:334
  140.2 20.3 %collective-permute-done.28.t1_ref = bf16[512,128]{1,0:T(8,128)(2,1)S(1)} collective-permute-done((bf16[512,128]{1,0:T(8,128)(2,1)S(1)}, bf16[512,128]{1,0:T(8,128)(2,1)S(1)}, u32[]{:S(2)}, u32[]{:S(2)}) %collective-permute-start.28) | collective-permute-done | bytes 131104 | tf_op jit(solution)/shard_map/ppermute | solution.py:334
  161.3 8.9 %shard_map.89 = bf16[14208,128]{1,0:T(8,128)(2,1)} custom-call(s32[4]{0:T(128)} %pad_add_fusion.order_ref, f32[512,128]{1,0:T(8,128)} %copy-done.34, bf16[512,128]{1,0:T(8,128)(2,1)} %copy-done.36, bf16[512,128]{1,0:T(8,128)(2,1)} %copy-done.37, bf16[512,128]{1,0:T(8,128)(2,1)} %copy-done.38, bf16[14208,128]{1,0:T(8,128)(2,1)} %own_ref.1, ...), custom_call_target="tpu_custom_call" | custom-call | tf_op jit(solution)/shard_map/pallas_call | solution.py:314
  (120 shorter events, 13.5 us)
Async XLA Ops:
  0.0 10.2 %copy-start.39 = (s32[16,4]{0,1:T(4,128)S(1)}, s32[16,4]{0,1:T(4,128)}, u32[]{:S(2)}) copy-start(s32[16,4]{0,1:T(4,128)} %param.14) | copy-start | bytes 772
  0.0 10.6 %copy-start.40 = (f32[16,4]{0,1:T(4,128)S(1)}, f32[16,4]{0,1:T(4,128)}, u32[]{:S(2)}) copy-start(f32[16,4]{0,1:T(4,128)} %param.15) | copy-start | bytes 772
  4.3 11.0 %collective-permute-start = (bf16[16,16,640]{2,1,0:T(8,128)(2,1)}, bf16[16,16,640]{2,1,0:T(8,128)(2,1)S(1)}, u32[]{:S(2)}, u32[]{:S(2)}) collective-permute-start(bf16[16,16,640]{2,1,0:T(8,128)(2,1)} %get-tuple-element.31), channel_id=1, source_target_pairs={{0,1},{1,2},{2,3},{3,0},{4,5},{5,6},{6,7},{7,4},{8,9},{9,10},{10,1... | collective-permute-start | bytes 983048 | tf_op jit(solution)/shard_map/ppermute | solution.py:334
  5.9 17.6 %collective-permute-start.1 = (bf16[16,16,640]{2,1,0:T(8,128)(2,1)}, bf16[16,16,640]{2,1,0:T(8,128)(2,1)S(1)}, u32[]{:S(2)}, u32[]{:S(2)}) collective-permute-start(bf16[16,16,640]{2,1,0:T(8,128)(2,1)} %get-tuple-element.32), channel_id=1, source_target_pairs={{0,2},{1,3},{2,0},{3,1},{4,6},{5,7},{6,4},{7,5},{8,10},{9,11},{10,... | collective-permute-start | bytes 983048 | tf_op jit(solution)/shard_map/ppermute | solution.py:334
  8.8 14.7 %collective-permute-start.2 = (bf16[16,16,640]{2,1,0:T(8,128)(2,1)}, bf16[16,16,640]{2,1,0:T(8,128)(2,1)S(1)}, u32[]{:S(2)}, u32[]{:S(2)}) collective-permute-start(bf16[16,16,640]{2,1,0:T(8,128)(2,1)} %get-tuple-element.33), channel_id=1, source_target_pairs={{0,3},{1,0},{2,1},{3,2},{4,7},{5,4},{6,5},{7,6},{8,11},{9,8},{10,9... | collective-permute-start | bytes 983048 | tf_op jit(solution)/shard_map/ppermute | solution.py:334
  10.7 15.9 %copy-start.27 = (f32[16,16,512]{2,1,0:T(8,128)S(1)}, f32[16,16,512]{2,1,0:T(8,128)}, u32[]{:S(2)}) copy-start(f32[16,16,512]{2,1,0:T(8,128)} %get-tuple-element.38.gain_ref) | copy-start | bytes 1572868
  10.7 15.9 %copy-start.35 = (bf16[16,16,128]{2,1,0:T(8,128)(2,1)S(1)}, bf16[16,16,128]{2,1,0:T(8,128)(2,1)}, u32[]{:S(2)}) copy-start(bf16[16,16,128]{2,1,0:T(8,128)(2,1)} %get-tuple-element.39.innov_ref) | copy-start | bytes 196612
  23.5 54.2 %collective-permute-start.5 = (bf16[7104,128]{1,0:T(8,128)(2,1)}, bf16[7104,128]{1,0:T(8,128)(2,1)}, u32[]{:S(2)}, u32[]{:S(2)}) collective-permute-start(bf16[7104,128]{1,0:T(8,128)(2,1)} %get-tuple-element.35), channel_id=1, source_target_pairs={{0,1},{1,0},{2,3},{3,2},{4,5},{5,4},{6,7},{7,6},{8,9},{9,8},{10,11... | collective-permute-start | bytes 5455880 | tf_op jit(solution)/shard_map/ppermute | solution.py:338
  24.7 56.2 %collective-permute-start.6 = (bf16[7104,128]{1,0:T(8,128)(2,1)}, bf16[7104,128]{1,0:T(8,128)(2,1)}, u32[]{:S(2)}, u32[]{:S(2)}) collective-permute-start(bf16[7104,128]{1,0:T(8,128)(2,1)} %get-tuple-element.34), channel_id=1, source_target_pairs={{0,3},{3,0},{1,2},{2,1},{4,7},{7,4},{5,6},{6,5},{8,11},{11,8},{9,1... | collective-permute-start | bytes 5455880 | tf_op jit(solution)/shard_map/ppermute | solution.py:342
  26.8 13.9 %collective-permute-start.7 = (bf16[9,16,1024]{2,1,0:T(8,128)(2,1)S(1)}, bf16[9,16,1024]{2,1,0:T(8,128)(2,1)S(1)}, u32[]{:S(2)}, u32[]{:S(2)}) collective-permute-start(bf16[9,16,1024]{2,1,0:T(8,128)(2,1)S(1)} %get-tuple-element.43.refs_0_), channel_id=1, source_target_pairs={{0,8},{4,12},{8,16},{12,20},{16,24},{20,28},{24,32},{28,36},{32,40... | collective-permute-start | bytes 884744 | tf_op jit(solution)/shard_map/ppermute | solution.py:354
  28.8 12.6 %collective-permute-start.11 = (bf16[8,16,1024]{2,1,0:T(8,128)(2,1)S(1)}, bf16[8,16,1024]{2,1,0:T(8,128)(2,1)S(1)}, u32[]{:S(2)}, u32[]{:S(2)}) collective-permute-start(bf16[8,16,1024]{2,1,0:T(8,128)(2,1)S(1)} %get-tuple-element.44.refs_8_), channel_id=1, source_target_pairs={{0,56},{4,60},{8,0},{12,4},{16,8},{20,12},{24,16},{28,20},{32,24},... | collective-permute-start | bytes 786440 | tf_op jit(solution)/shard_map/ppermute | solution.py:354
  32.8 13.5 %collective-permute-start.18 = (bf16[8,16,1024]{2,1,0:T(8,128)(2,1)S(1)}, bf16[8,16,1024]{2,1,0:T(8,128)(2,1)S(1)}, u32[]{:S(2)}, u32[]{:S(2)}) collective-permute-start(bf16[8,16,1024]{2,1,0:T(8,128)(2,1)S(1)} %get-tuple-element.44.refs_8_), channel_id=1, source_target_pairs={{0,8},{4,12},{8,16},{12,20},{16,24},{20,28},{24,32},{28,36},{32,40... | collective-permute-start | bytes 786440 | tf_op jit(solution)/shard_map/ppermute | solution.py:354
  40.7 9.9 %collective-permute-start.8 = (bf16[9,16,1024]{2,1,0:T(8,128)(2,1)S(1)}, bf16[9,16,1024]{2,1,0:T(8,128)(2,1)S(1)}, u32[]{:S(2)}, u32[]{:S(2)}) collective-permute-start(bf16[9,16,1024]{2,1,0:T(8,128)(2,1)S(1)} %collective-permute-done.7.refs_1_), channel_id=1, source_target_pairs={{0,8},{4,12},{8,16},{12,20},{16,24},{20,28},{24,32},{28,36},{32,40... | collective-permute-start | bytes 884744 | tf_op jit(solution)/shard_map/ppermute | solution.py:354
  41.4 9.9 %collective-permute-start.15 = (bf16[9,16,1024]{2,1,0:T(8,128)(2,1)S(1)}, bf16[9,16,1024]{2,1,0:T(8,128)(2,1)S(1)}, u32[]{:S(2)}, u32[]{:S(2)}) collective-permute-start(bf16[9,16,1024]{2,1,0:T(8,128)(2,1)S(1)} %get-tuple-element.43.refs_0_), channel_id=1, source_target_pairs={{0,56},{4,60},{8,0},{12,4},{16,8},{20,12},{24,16},{28,20},{32,24},... | collective-permute-start | bytes 884744 | tf_op jit(solution)/shard_map/ppermute | solution.py:354
  46.3 7.6 %collective-permute-start.12 = (bf16[8,16,1024]{2,1,0:T(8,128)(2,1)S(1)}, bf16[8,16,1024]{2,1,0:T(8,128)(2,1)S(1)}, u32[]{:S(2)}, u32[]{:S(2)}) collective-permute-start(bf16[8,16,1024]{2,1,0:T(8,128)(2,1)S(1)} %collective-permute-done.11.refs_12_), channel_id=1, source_target_pairs={{0,56},{4,60},{8,0},{12,4},{16,8},{20,12},{24,16},{28,20},{32,24},... | collective-permute-start | bytes 786440 | tf_op jit(solution)/shard_map/ppermute | solution.py:354
  50.6 15.0 %collective-permute-start.9 = (bf16[9,16,1024]{2,1,0:T(8,128)(2,1)S(1)}, bf16[9,16,1024]{2,1,0:T(8,128)(2,1)S(1)}, u32[]{:S(2)}, u32[]{:S(2)}) collective-permute-start(bf16[9,16,1024]{2,1,0:T(8,128)(2,1)S(1)} %collective-permute-done.8.refs_2_), channel_id=1, source_target_pairs={{0,8},{4,12},{8,16},{12,20},{16,24},{20,28},{24,32},{28,36},{32,40... | collective-permute-start | bytes 884744 | tf_op jit(solution)/shard_map/ppermute | solution.py:354
  51.3 13.3 %collective-permute-start.19 = (bf16[8,16,1024]{2,1,0:T(8,128)(2,1)S(1)}, bf16[8,16,1024]{2,1,0:T(8,128)(2,1)}, u32[]{:S(2)}, u32[]{:S(2)}) collective-permute-start(bf16[8,16,1024]{2,1,0:T(8,128)(2,1)S(1)} %collective-permute-done.18.refs_9_), channel_id=1, source_target_pairs={{0,8},{4,12},{8,16},{12,20},{16,24},{20,28},{24,32},{28,36},{32,40... | collective-permute-start | bytes 786440 | tf_op jit(solution)/shard_map/ppermute | solution.py:354
  53.9 14.3 %collective-permute-start.13 = (bf16[8,16,1024]{2,1,0:T(8,128)(2,1)S(1)}, bf16[8,16,1024]{2,1,0:T(8,128)(2,1)S(1)}, u32[]{:S(2)}, u32[]{:S(2)}) collective-permute-start(bf16[8,16,1024]{2,1,0:T(8,128)(2,1)S(1)} %collective-permute-done.12.refs_13_), channel_id=1, source_target_pairs={{0,56},{4,60},{8,0},{12,4},{16,8},{20,12},{24,16},{28,20},{32,24},... | collective-permute-start | bytes 786440 | tf_op jit(solution)/shard_map/ppermute | solution.py:354
  64.7 9.1 %collective-permute-start.16 = (bf16[9,16,1024]{2,1,0:T(8,128)(2,1)S(1)}, bf16[9,16,1024]{2,1,0:T(8,128)(2,1)}, u32[]{:S(2)}, u32[]{:S(2)}) collective-permute-start(bf16[9,16,1024]{2,1,0:T(8,128)(2,1)S(1)} %collective-permute-done.15.refs_4_), channel_id=1, source_target_pairs={{0,56},{4,60},{8,0},{12,4},{16,8},{20,12},{24,16},{28,20},{32,24},... | collective-permute-start | bytes 884744 | tf_op jit(solution)/shard_map/ppermute | solution.py:354
  65.6 12.0 %collective-permute-start.10 = (bf16[9,16,1024]{2,1,0:T(8,128)(2,1)S(1)}, bf16[9,16,1024]{2,1,0:T(8,128)(2,1)S(1)}, u32[]{:S(2)}, u32[]{:S(2)}) collective-permute-start(bf16[9,16,1024]{2,1,0:T(8,128)(2,1)S(1)} %collective-permute-done.9.refs_3_), channel_id=1, source_target_pairs={{0,8},{4,12},{8,16},{12,20},{16,24},{20,28},{24,32},{28,36},{32,40... | collective-permute-start | bytes 884744 | tf_op jit(solution)/shard_map/ppermute | solution.py:354
  68.1 8.4 %collective-permute-start.14 = (bf16[8,16,1024]{2,1,0:T(8,128)(2,1)S(1)}, bf16[8,16,1024]{2,1,0:T(8,128)(2,1)S(1)}, u32[]{:S(2)}, u32[]{:S(2)}) collective-permute-start(bf16[8,16,1024]{2,1,0:T(8,128)(2,1)S(1)} %collective-permute-done.13.refs_14_), channel_id=1, source_target_pairs={{0,56},{4,60},{8,0},{12,4},{16,8},{20,12},{24,16},{28,20},{32,24},... | collective-permute-start | bytes 786440 | tf_op jit(solution)/shard_map/ppermute | solution.py:354
  73.8 36.7 %collective-permute-start.3 = (bf16[7104,128]{1,0:T(8,128)(2,1)}, bf16[7104,128]{1,0:T(8,128)(2,1)}, u32[]{:S(2)}, u32[]{:S(2)}) collective-permute-start(bf16[7104,128]{1,0:T(8,128)(2,1)} %get-tuple-element.34), channel_id=1, source_target_pairs={{0,1},{1,0},{2,3},{3,2},{4,5},{5,4},{6,7},{7,6},{8,9},{9,8},{10,11... | collective-permute-start | bytes 5455880 | tf_op jit(solution)/shard_map/ppermute | solution.py:338
  76.5 44.1 %collective-permute-start.4 = (bf16[7104,128]{1,0:T(8,128)(2,1)}, bf16[7104,128]{1,0:T(8,128)(2,1)}, u32[]{:S(2)}, u32[]{:S(2)}) collective-permute-start(bf16[7104,128]{1,0:T(8,128)(2,1)} %get-tuple-element.35), channel_id=1, source_target_pairs={{0,3},{3,0},{1,2},{2,1},{4,7},{7,4},{5,6},{6,5},{8,11},{11,8},{9,1... | collective-permute-start | bytes 5455880 | tf_op jit(solution)/shard_map/ppermute | solution.py:342
  77.7 7.9 %collective-permute-start.20 = (bf16[8,16,1024]{2,1,0:T(8,128)(2,1)}, bf16[8,16,1024]{2,1,0:T(8,128)(2,1)}, u32[]{:S(2)}, u32[]{:S(2)}) collective-permute-start(bf16[8,16,1024]{2,1,0:T(8,128)(2,1)} %collective-permute-done.19.refs_10_), channel_id=1, source_target_pairs={{0,8},{4,12},{8,16},{12,20},{16,24},{20,28},{24,32},{28,36},{32,40... | collective-permute-start | bytes 786440 | tf_op jit(solution)/shard_map/ppermute | solution.py:354
  77.7 7.9 %collective-permute-start.17 = (bf16[9,16,1024]{2,1,0:T(8,128)(2,1)}, bf16[9,16,1024]{2,1,0:T(8,128)(2,1)}, u32[]{:S(2)}, u32[]{:S(2)}) collective-permute-start(bf16[9,16,1024]{2,1,0:T(8,128)(2,1)} %collective-permute-done.16.refs_5_), channel_id=1, source_target_pairs={{0,56},{4,60},{8,0},{12,4},{16,8},{20,12},{24,16},{28,20},{32,24},... | collective-permute-start | bytes 884744 | tf_op jit(solution)/shard_map/ppermute | solution.py:354
  80.9 4.7 %copy-start.1 = (bf16[9,16,1024]{2,1,0:T(8,128)(2,1)S(1)}, bf16[9,16,1024]{2,1,0:T(8,128)(2,1)}, u32[]{:S(2)}) copy-start(bf16[9,16,1024]{2,1,0:T(8,128)(2,1)} %copy-done) | copy-start | bytes 884740
  80.9 4.6 %copy-start.3 = (bf16[9,16,1024]{2,1,0:T(8,128)(2,1)S(1)}, bf16[9,16,1024]{2,1,0:T(8,128)(2,1)}, u32[]{:S(2)}) copy-start(bf16[9,16,1024]{2,1,0:T(8,128)(2,1)} %copy-done.2) | copy-start | bytes 884740
  80.9 4.6 %copy-start.5 = (bf16[9,16,1024]{2,1,0:T(8,128)(2,1)S(1)}, bf16[9,16,1024]{2,1,0:T(8,128)(2,1)}, u32[]{:S(2)}) copy-start(bf16[9,16,1024]{2,1,0:T(8,128)(2,1)} %copy-done.4) | copy-start | bytes 884740
  80.9 4.6 %copy-start.7 = (bf16[9,16,1024]{2,1,0:T(8,128)(2,1)S(1)}, bf16[9,16,1024]{2,1,0:T(8,128)(2,1)}, u32[]{:S(2)}) copy-start(bf16[9,16,1024]{2,1,0:T(8,128)(2,1)} %copy-done.6) | copy-start | bytes 884740
  81.0 4.6 %copy-start.9 = (bf16[9,16,1024]{2,1,0:T(8,128)(2,1)S(1)}, bf16[9,16,1024]{2,1,0:T(8,128)(2,1)}, u32[]{:S(2)}) copy-start(bf16[9,16,1024]{2,1,0:T(8,128)(2,1)} %copy-done.8) | copy-start | bytes 884740
  81.0 4.6 %copy-start.13 = (bf16[8,16,1024]{2,1,0:T(8,128)(2,1)S(1)}, bf16[8,16,1024]{2,1,0:T(8,128)(2,1)}, u32[]{:S(2)}) copy-start(bf16[8,16,1024]{2,1,0:T(8,128)(2,1)} %copy-done.12) | copy-start | bytes 786436
  87.6 8.6 %copy-start.20 = (bf16[8,16,1024]{2,1,0:T(8,128)(2,1)S(1)}, bf16[8,16,1024]{2,1,0:T(8,128)(2,1)}, u32[]{:S(2)}) copy-start(bf16[8,16,1024]{2,1,0:T(8,128)(2,1)} %copy-done.18) | copy-start | bytes 786436
  87.6 8.6 %copy-start.23 = (bf16[8,16,1024]{2,1,0:T(8,128)(2,1)S(1)}, bf16[8,16,1024]{2,1,0:T(8,128)(2,1)}, u32[]{:S(2)}) copy-start(bf16[8,16,1024]{2,1,0:T(8,128)(2,1)} %copy-done.21) | copy-start | bytes 786436
  87.6 8.6 %copy-start.26 = (bf16[8,16,1024]{2,1,0:T(8,128)(2,1)S(1)}, bf16[8,16,1024]{2,1,0:T(8,128)(2,1)}, u32[]{:S(2)}) copy-start(bf16[8,16,1024]{2,1,0:T(8,128)(2,1)} %copy-done.24) | copy-start | bytes 786436
  91.9 2.0 %collective-permute-start.21 = (bf16[512,512]{1,0:T(8,128)(2,1)S(1)}, bf16[512,512]{1,0:T(8,128)(2,1)S(1)}, u32[]{:S(2)}, u32[]{:S(2)}) collective-permute-start(bf16[512,512]{1,0:T(8,128)(2,1)S(1)} %get-tuple-element.45), channel_id=1, source_target_pairs={{0,4},{4,0},{8,12},{12,8},{16,20},{20,16},{24,28},{28,24},{32,36},... | collective-permute-start | bytes 1572872 | tf_op jit(solution)/shard_map/ppermute | solution.py:354
  92.0 2.6 %collective-permute-start.22 = (bf16[512,512]{1,0:T(8,128)(2,1)S(1)}, bf16[512,512]{1,0:T(8,128)(2,1)S(1)}, u32[]{:S(2)}, u32[]{:S(2)}) collective-permute-start(bf16[512,512]{1,0:T(8,128)(2,1)S(1)} %get-tuple-element.46), channel_id=1, source_target_pairs={{0,4},{4,0},{8,12},{12,8},{16,20},{20,16},{24,28},{28,24},{32,36},... | collective-permute-start | bytes 1572872 | tf_op jit(solution)/shard_map/ppermute | solution.py:354
  92.5 2.9 %collective-permute-start.23 = (bf16[512,512]{1,0:T(8,128)(2,1)S(1)}, bf16[512,512]{1,0:T(8,128)(2,1)S(1)}, u32[]{:S(2)}, u32[]{:S(2)}) collective-permute-start(bf16[512,512]{1,0:T(8,128)(2,1)S(1)} %get-tuple-element.47), channel_id=1, source_target_pairs={{0,4},{4,0},{8,12},{12,8},{16,20},{20,16},{24,28},{28,24},{32,36},... | collective-permute-start | bytes 1572872 | tf_op jit(solution)/shard_map/ppermute | solution.py:354
  93.9 2.2 %collective-permute-start.24 = (bf16[512,512]{1,0:T(8,128)(2,1)S(1)}, bf16[512,512]{1,0:T(8,128)(2,1)S(1)}, u32[]{:S(2)}, u32[]{:S(2)}) collective-permute-start(bf16[512,512]{1,0:T(8,128)(2,1)S(1)} %get-tuple-element.48), channel_id=1, source_target_pairs={{0,4},{4,0},{8,12},{12,8},{16,20},{20,16},{24,28},{28,24},{32,36},... | collective-permute-start | bytes 1572872 | tf_op jit(solution)/shard_map/ppermute | solution.py:354
  100.5 21.4 %collective-permute-start.25 = (bf16[512,512]{1,0:T(8,128)(2,1)S(1)}, bf16[512,512]{1,0:T(8,128)(2,1)S(1)}, u32[]{:S(2)}, u32[]{:S(2)}) collective-permute-start(bf16[512,512]{1,0:T(8,128)(2,1)S(1)} %get-tuple-element.49), channel_id=1, source_target_pairs={{0,64},{4,68},{8,72},{12,76},{16,80},{20,84},{24,88},{28,92},{32,9... | collective-permute-start | bytes 1572872 | tf_op jit(solution)/shard_map/ppermute | solution.py:354
  101.0 20.8 %collective-permute-start.26 = (bf16[512,512]{1,0:T(8,128)(2,1)S(1)}, bf16[512,512]{1,0:T(8,128)(2,1)S(1)}, u32[]{:S(2)}, u32[]{:S(2)}) collective-permute-start(bf16[512,512]{1,0:T(8,128)(2,1)S(1)} %get-tuple-element.50), channel_id=1, source_target_pairs={{0,128},{4,132},{8,136},{12,140},{16,144},{20,148},{24,152},{28,15... | collective-permute-start | bytes 1572872 | tf_op jit(solution)/shard_map/ppermute | solution.py:354
  103.4 24.0 %collective-permute-start.27 = (bf16[512,512]{1,0:T(8,128)(2,1)S(1)}, bf16[512,512]{1,0:T(8,128)(2,1)S(1)}, u32[]{:S(2)}, u32[]{:S(2)}) collective-permute-start(bf16[512,512]{1,0:T(8,128)(2,1)S(1)} %get-tuple-element.51), channel_id=1, source_target_pairs={{0,192},{4,196},{8,200},{12,204},{16,208},{20,212},{24,216},{28,22... | collective-permute-start | bytes 1572872 | tf_op jit(solution)/shard_map/ppermute | solution.py:354
  110.5 50.1 %collective-permute-start.31 = (bf16[7104,128]{1,0:T(8,128)(2,1)}, bf16[7104,128]{1,0:T(8,128)(2,1)}, u32[]{:S(2)}, u32[]{:S(2)}) collective-permute-start(bf16[7104,128]{1,0:T(8,128)(2,1)} %collective-permute-done.5.refs_0_.a1_ref), channel_id=1, source_target_pairs={{0,3},{3,0},{1,2},{2,1},{4,7},{7,4},{5,6},{6,5},{8,11},{11,8},{9,1... | collective-permute-start | bytes 5455880 | tf_op jit(solution)/shard_map/ppermute | solution.py:342
  120.6 40.0 %collective-permute-start.32 = (bf16[7104,128]{1,0:T(8,128)(2,1)}, bf16[7104,128]{1,0:T(8,128)(2,1)}, u32[]{:S(2)}, u32[]{:S(2)}) collective-permute-start(bf16[7104,128]{1,0:T(8,128)(2,1)} %collective-permute-done.6.refs_1_.b2_ref), channel_id=1, source_target_pairs={{0,1},{1,0},{2,3},{3,2},{4,5},{5,4},{6,7},{7,6},{8,9},{9,8},{10,11... | collective-permute-start | bytes 5455880 | tf_op jit(solution)/shard_map/ppermute | solution.py:338
  121.8 5.6 %copy-start.28 = (bf16[512,512]{1,0:T(8,128)(2,1)}, bf16[512,512]{1,0:T(8,128)(2,1)S(1)}, u32[]{:S(2)}) copy-start(bf16[512,512]{1,0:T(8,128)(2,1)S(1)} %collective-permute-done.25.refs_2_.r1_ref) | copy-start | bytes 1572868
  121.8 5.6 %copy-start.30 = (bf16[512,512]{1,0:T(8,128)(2,1)}, bf16[512,512]{1,0:T(8,128)(2,1)S(1)}, u32[]{:S(2)}) copy-start(bf16[512,512]{1,0:T(8,128)(2,1)S(1)} %collective-permute-done.26.refs_3_.r2_ref) | copy-start | bytes 1572868
  133.7 26.9 %collective-permute-start.28 = (bf16[512,128]{1,0:T(8,128)(2,1)S(1)}, bf16[512,128]{1,0:T(8,128)(2,1)S(1)}, u32[]{:S(2)}, u32[]{:S(2)}) collective-permute-start(bf16[512,128]{1,0:T(8,128)(2,1)S(1)} %get-tuple-element.54), channel_id=1, source_target_pairs={{0,1},{1,2},{2,3},{3,0},{4,5},{5,6},{6,7},{7,4},{8,9},{9,10},{10,1... | collective-permute-start | bytes 393224 | tf_op jit(solution)/shard_map/ppermute | solution.py:334
  135.0 25.6 %collective-permute-start.29 = (bf16[512,128]{1,0:T(8,128)(2,1)S(1)}, bf16[512,128]{1,0:T(8,128)(2,1)S(1)}, u32[]{:S(2)}, u32[]{:S(2)}) collective-permute-start(bf16[512,128]{1,0:T(8,128)(2,1)S(1)} %get-tuple-element.55), channel_id=1, source_target_pairs={{0,2},{1,3},{2,0},{3,1},{4,6},{5,7},{6,4},{7,5},{8,10},{9,11},{10,... | collective-permute-start | bytes 393224 | tf_op jit(solution)/shard_map/ppermute | solution.py:334
  137.2 23.3 %collective-permute-start.30 = (bf16[512,128]{1,0:T(8,128)(2,1)S(1)}, bf16[512,128]{1,0:T(8,128)(2,1)S(1)}, u32[]{:S(2)}, u32[]{:S(2)}) collective-permute-start(bf16[512,128]{1,0:T(8,128)(2,1)S(1)} %get-tuple-element.56), channel_id=1, source_target_pairs={{0,3},{1,0},{2,1},{3,2},{4,7},{5,4},{6,5},{7,6},{8,11},{9,8},{10,9... | collective-permute-start | bytes 393224 | tf_op jit(solution)/shard_map/ppermute | solution.py:334
  (26 other events, 42.0 us)

commit v5 on v4

--- a/solution.py
+++ b/solution.py
@@ -14,7 +14,7 @@
 DEPTH = 8
 CORES = 2
 SLOTS = 2
-STEPS = 6
+STEPS = 4
 SMALL = pl.CostEstimate(flops=10**6, bytes_accessed=10**6, transcendentals=0)
 
 
@@ -132,10 +132,12 @@
 
 def sums_kernel(same, token_ref, place_ref, *refs):
     lows, highs, refs = refs[:DEPTH], refs[DEPTH : 2 * DEPTH], refs[2 * DEPTH :]
-    others = ()
+    others, outs = (), ()
     if same:
-        others, refs = refs[:GROUPS], refs[GROUPS:]
-    outs, refs = refs[:GROUPS], refs[GROUPS:]
+        others, outs, refs = refs[:CORES], refs[CORES : CORES + GROUPS], refs[CORES + GROUPS :]
+    else:
+        outs, refs = refs[:CORES], refs[CORES:]
+    pack = GROUPS // CORES
     all_ref, gain_ref, innov_ref, chosen_ref, taper_ref, chosen_smem, taper_smem, sems = refs
     half, quarter, width = highs[0].shape
     members = width // 2
@@ -185,23 +187,31 @@
             preferred_element_type=jnp.float32,
         )
         if same:
-            total = total + others[away][...].astype(jnp.float32)
-        outs[away][...] = total.astype(outs[away].dtype)
+            total = total + others[away // pack][away % pack].astype(jnp.float32)
+            outs[away][...] = total.astype(outs[away].dtype)
+        else:
+            outs[away // pack][away % pack] = total.astype(jnp.bfloat16)
 
 
 def sums(same, token, place, lows, highs, others=()):
     half, quarter, width = highs[0].shape
     members = width // 2
     lanes = 128
-    kinds = [jnp.float32 if same else jnp.bfloat16] + [jnp.bfloat16] * (GROUPS - 1)
+    square = (members, members)
+    if same:
+        kinds = [jnp.float32] + [jnp.bfloat16] * (GROUPS - 1)
+        out_shape = [jax.ShapeDtypeStruct(square, kind) for kind in kinds]
+    else:
+        shape = (GROUPS // CORES,) + square
+        out_shape = [jax.ShapeDtypeStruct(shape, jnp.bfloat16)] * CORES
     taken = (GROUPS, DEPTH * SLOTS * quarter, members)
     return pl.pallas_call(
         functools.partial(sums_kernel, same),
         in_specs=[pl.BlockSpec(memory_space=pltpu.SMEM)] * 2
         + [pl.BlockSpec(memory_space=pl.ANY)] * (2 * DEPTH)
         + [pl.BlockSpec(memory_space=pltpu.VMEM)] * len(others),
-        out_specs=[pl.BlockSpec(memory_space=pltpu.VMEM)] * GROUPS,
-        out_shape=[jax.ShapeDtypeStruct((members, members), kind) for kind in kinds],
+        out_specs=[pl.BlockSpec(memory_space=pltpu.VMEM)] * len(out_shape),
+        out_shape=out_shape,
         scratch_shapes=[
             pltpu.VMEM((DEPTH, 2 * half + 1, quarter, width), jnp.bfloat16),
             pltpu.VMEM(taken, jnp.bfloat16),
@@ -257,30 +267,53 @@
         out_shape=[jax.ShapeDtypeStruct((members, part), jnp.float32)]
         + [jax.ShapeDtypeStruct((members, part), jnp.bfloat16)] * 3,
         compiler_params=pltpu.CompilerParams(vmem_limit_bytes=VMEM_LIMIT),
+        cost_estimate=pl.CostEstimate(flops=5*10**9, bytes_accessed=10**6, transcendentals=0),
+    )(q, token, *sums_here)
+
+
+def hold_kernel(own_ref, a1_ref, a2_ref, b1_ref, b2_ref, out_ref, sems):
+    half = a1_ref.shape[0]
+    copies = [pltpu.make_async_copy(own_ref, out_ref.at[0], sems.at[0])]
+    for k, (low, high) in enumerate(((a1_ref, a2_ref), (b1_ref, b2_ref))):
+        copies.append(
+            pltpu.make_async_copy(low, out_ref.at[k + 1, pl.ds(0, half)], sems.at[2 * k + 1])
+        )
+        copies.append(
+            pltpu.make_async_copy(high, out_ref.at[k + 1, pl.ds(half, half)], sems.at[2 * k + 2])
+        )
+    for copy in copies:
+        copy.start()
+    for copy in copies:
+        copy.wait()
+
+
+def hold(own, others):
+    rows, part = own.shape
+    return pl.pallas_call(
+        hold_kernel,
+        in_specs=[pl.BlockSpec(memory_space=pl.ANY)] * (1 + len(others)),
+        out_specs=pl.BlockSpec(memory_space=pltpu.VMEM),
+        out_shape=jax.ShapeDtypeStruct((GROUPS - 1, rows, part), jnp.bfloat16),
+        scratch_shapes=[pltpu.SemaphoreType.DMA((5,))],
+        compiler_params=pltpu.CompilerParams(vmem_limit_bytes=16 * 1024 * 1024),
         cost_estimate=SMALL,
-    )(q, token, *sums_here)
+    )(own, *others)
 
 
 def update_kernel(
-    order_ref, t0_ref, t1_ref, t2_ref, t3_ref, own_ref, a1_ref, a2_ref, b1_ref, b2_ref, o1_ref, o2_ref,
-    out_ref, raw_ref, weights_ref, states_ref, result_ref, in_sems, out_sems,
+    order_ref, t0_ref, t1_ref, t2_ref, t3_ref, held_ref, o1_ref, o2_ref,
+    out_ref, raw_ref, weights_ref, far_ref, result_ref, in_sems, out_sems,
 ):
-    part = own_ref.shape[1]
+    part = held_ref.shape[2]
     step = result_ref.shape[1]
     half = STEPS // 2
     loads = []
     for i in range(STEPS):
-        sources = (a1_ref, b1_ref, o1_ref) if i < half else (a2_ref, b2_ref, o2_ref)
-        views = [own_ref.at[pl.ds(i * step, step)]]
-        views += [ref.at[pl.ds((i % half) * step, step)] for ref in sources]
+        ref = o1_ref if i < half else o2_ref
         loads.append(
-            [
-                pltpu.make_async_copy(view, states_ref.at[i, k], in_sems.at[i, k])
-                for k, view in enumerate(views)
-            ]
-        )
-        for load in loads[-1]:
-            load.start()
+            pltpu.make_async_copy(ref.at[pl.ds((i % half) * step, step)], far_ref.at[i], in_sems.at[i])
+        )
+        loads[-1].start()
     total = (
         t0_ref[...]
         + t1_ref[...].astype(jnp.float32)
@@ -292,42 +325,39 @@
         weights_ref[pl.ds(k * part, part), :] = raw_ref[order_ref[k]]
     stores = []
     for i in range(STEPS):
-        for load in loads[i]:
-            load.wait()
-        states = jnp.concatenate([states_ref[i, k] for k in range(GROUPS)], axis=1)
+        loads[i].wait()
+        rows = pl.ds(i * step, step)
+        near = [held_ref[k, rows, :] for k in range(GROUPS - 1)]
+        states = jnp.concatenate(near + [far_ref[i]], axis=1)
         increment = jnp.dot(states, weights_ref[...], preferred_element_type=jnp.float32)
-        result_ref[i] = (states_ref[i, 0].astype(jnp.float32) + increment).astype(result_ref.dtype)
-        stores.append(
-            pltpu.make_async_copy(
-                result_ref.at[i], out_ref.at[pl.ds(i * step, step)], out_sems.at[i]
-            )
-        )
+        result_ref[i] = (near[0].astype(jnp.float32) + increment).astype(result_ref.dtype)
+        stores.append(pltpu.make_async_copy(result_ref.at[i], out_ref.at[rows], out_sems.at[i]))
         stores[-1].start()
     for store in stores:
         store.wait()
 
 
-def update(order, pieces, own, others):
-    rows, part = own.shape
+def update(order, pieces, held, others):
+    rows, part = held.shape[1:]
     members = pieces[0].shape[0]
     step = rows // STEPS
     return pl.pallas_call(
         update_kernel,
         in_specs=[pl.BlockSpec(memory_space=pltpu.SMEM)]
-        + [pl.BlockSpec(memory_space=pltpu.VMEM)] * GROUPS
-        + [pl.BlockSpec(memory_space=pl.ANY)] * (1 + len(others)),
+        + [pl.BlockSpec(memory_space=pltpu.VMEM)] * (GROUPS + 1)
+        + [pl.BlockSpec(memory_space=pl.ANY)] * len(others),
         out_specs=pl.BlockSpec(memory_space=pl.ANY),
         out_shape=jax.ShapeDtypeStruct((rows, part), jnp.bfloat16),
         scratch_shapes=[
             pltpu.VMEM((GROUPS, part, part), jnp.bfloat16),
             pltpu.VMEM((members, part), jnp.bfloat16),
-            pltpu.VMEM((STEPS, GROUPS, step, part), jnp.bfloat16),
             pltpu.VMEM((STEPS, step, part), jnp.bfloat16),
-            pltpu.SemaphoreType.DMA((STEPS, GROUPS)),
+            pltpu.VMEM((STEPS, step, part), jnp.bfloat16),
+            pltpu.SemaphoreType.DMA((STEPS,)),
             pltpu.SemaphoreType.DMA((STEPS,)),
         ],
-        compiler_params=pltpu.CompilerParams(vmem_limit_bytes=FIRST_LIMIT),
-    )(order, *pieces, own, *others)
+        compiler_params=pltpu.CompilerParams(vmem_limit_bytes=VMEM_LIMIT),
+    )(order, *pieces, held, *others)
 
 
 def shift(x, d):
@@ -389,9 +419,8 @@
     chosen, tapers, m1, m2, m3, low, high = lax.optimization_barrier(
         (chosen, tapers, m1, m2, m3, ensemble[:half], ensemble[half:])
     )
+    a2, b1 = swap_a(high), swap_b(low)
     a1, b2 = swap_a(low), swap_b(high)
-    a2, b1 = swap_a(high), swap_b(low)
-    o1, o2 = swap_b(a1), swap_a(b2)
 
     up, down = (0, 1, 0), (0, -1, 0)
     own_blocks = tuple(merge(q1, chosen, tapers, (gain, innov, m1, m2, m3)))
@@ -399,18 +428,21 @@
     for _ in range(3):
         ups.append(tuple(move(x, columns, up) for x in ups[-1]))
         downs.append(tuple(move(x, columns, down) for x in downs[-1]))
-    far = (move(ups[-1][0], columns, up), move(downs[-1][1], columns, down))
+    token = arrived(a2, b1)
+    token, far = lax.optimization_barrier((token, (ups[-1][0], downs[-1][1])))
+    far = (move(far[0], columns, up), move(far[1], columns, down))
     held = ups + downs[1:] + [far]
     lows, highs = [h[0] for h in held], [h[1] for h in held]
-    token = arrived(a1, b2, *far)
     others = sums(0, token, place, lows, highs)
     others = [move(x, columns, (0, 0, 1)) for x in others]
     here, e1, e2, e3 = sums(1, token, place, lows, highs, others)
+    here, a1, b2 = lax.optimization_barrier((here, a1, b2))
+    o1, o2 = swap_b(a1), swap_a(b2)
     e1, e2, e3 = move(e1, columns, (1, 0, 0)), move(e2, columns, (2, 0, 0)), move(e3, columns, (3, 0, 0))
-    token = arrived(a2, b1, e1, e2, e3)
     t0, t1, t2, t3 = transform_parts(q1, token, (here, e1, e2, e3))
     pieces = [t0, shift(t1, 1), shift(t2, 2), shift(t3, 3)]
-    return update(order, pieces, ensemble, (a1, a2, b1, b2, o1, o2))
+    held = hold(ensemble, (a1, a2, b1, b2))
+    return update(order, pieces, held, (o1, o2))
 
 
 def solution(mesh):

time: 171 us -> 162 us (0.947)
  local copies, waits for them, and re-layouts: 19 us -> 12.2 us
  waiting for transfers between devices: 81.3 us -> 76.3 us
  starting transfers between devices: 44.4 us -> 47.9 us
    ppermute x21 -> x19, waiting for transfers between devices: 35.7 us -> 55.1 us  [move(): return lax.ppermute(x, 'tile', pairs)]
    ppermute x6, waiting for transfers between devices: 28.7 us -> 17.9 us  [shift(): lax.ppermute(x, 'mem', [(i, (i + d) % GROUPS) for i in range(GROUPS)])]
    ppermute x3, waiting for transfers between devices: 7.09 us -> 0.24 us  [swap_a(): return lax.ppermute(x, 'mem', [(0, 1), (1, 0), (2, 3), (3, 2)])]
    ppermute x3, waiting for transfers between devices: 9.87 us -> 3.07 us  [swap_b(): return lax.ppermute(x, 'mem', [(0, 3), (3, 0), (1, 2), (2, 1)])]
    unnamed x84 -> x44, local copies, waits for them, and re-layouts: 14.6 us -> 7.85 us
    ppermute x21 -> x19, starting transfers between devices: 24.5 us -> 29.9 us  [move(): return lax.ppermute(x, 'tile', pairs)]
    pallas_call x0 -> x1, Pallas kernels: none -> 3.26 us  [hold(): pl.pallas_call(hold_kernel, in_specs=[pl.BlockSpec(memory_space=pl.ANY)]...]
    ppermute x3, starting transfers between devices: 4.8 us -> 2.97 us  [swap_a(): return lax.ppermute(x, 'mem', [(0, 1), (1, 0), (2, 3), (3, 2)])]
  transfers between devices with their start and end apart: 33 -> 31, of which waited for: 18 -> 22; matrix products, arithmetic and copies ran while one was open for 3% -> 3% of each run, Pallas kernels for 6% -> 8%
where the time goes in v5:
time: 162 us
  waiting for transfers between devices  76.3 us (47%)
  starting transfers between devices  47.9 us (30%)
  Pallas kernels  24.8 us (15%)
  local copies, waits for them, and re-layouts  12.2 us (8%)
    ppermute x19, waiting for transfers between devices, move(): return lax.ppermute(x, 'tile', pairs)  55.1 us
    ppermute x19, starting transfers between devices, move(): return lax.ppermute(x, 'tile', pairs)  29.9 us
    ppermute x6, waiting for transfers between devices, shift(): lax.ppermute(x, 'mem', [(i, (i + d) % GROUPS) for i in range(GROUPS)])  17.9 us
    ppermute x6, starting transfers between devices, shift(): lax.ppermute(x, 'mem', [(i, (i + d) % GROUPS) for i in range(GROUPS)])  10.5 us
    pallas_call x2, Pallas kernels, sums(): pl.pallas_call(functools.partial(sums_kernel, same), in_specs=[pl.BlockSp...  8.23 us
    unnamed x44, local copies, waits for them, and re-layouts  7.85 us
    pallas_call x1, Pallas kernels, update(): pl.pallas_call(update_kernel, in_specs=[pl.BlockSpec(memory_space=pltpu.S...  7.3 us
    ppermute x3, starting transfers between devices, swap_b(): return lax.ppermute(x, 'mem', [(0, 3), (3, 0), (1, 2), (2, 1)])  4.58 us
  transfers between devices with their start and end apart: 31, of which 22 were waited for; matrix products, arithmetic and copies ran while one was open for 3% of the time, Pallas kernels for 8%

profile of v5, /device:TPU:6, one launch (start us, length us, event | category | flops | bytes accessed | tf_op | source)
XLA Modules:
  0.0 162.1 jit_solution(15017109460040327971)
XLA Ops:
  0.0 4.3 %shard_map.82 = (f32[16,16,512]{2,1,0:T(8,128)}, bf16[16,16,128]{2,1,0:T(8,128)(2,1)}, bf16[16,16,640]{2,1,0:T(8,128)(2,1)}, bf16[16,16,640]{2,1,0:T(8,128)(2,1)}, bf16[16,16,640]{2,1,0:T(8,128)(2,1)}) custom-call(s32[1]{0:T(128)} %bitcast.q_ref, bf16[16,64,128]{2,1,0:T(8,128)(2,1)} %obs_ref.1, bf16[16,512,128]{2,1,0:T(8,128)(2,1)} %inv_ref.1, ...), custom_call_target="tpu_custom_call" | custom-call | tf_op jit(solution)/shard_map/pallas_call | solution.py:57
  4.3 1.6 collective-permute-start
  5.9 2.9 %collective-permute-start.1 = (bf16[16,16,640]{2,1,0:T(8,128)(2,1)}, bf16[16,16,640]{2,1,0:T(8,128)(2,1)S(1)}, u32[]{:S(2)}, u32[]{:S(2)}) collective-permute-start(bf16[16,16,640]{2,1,0:T(8,128)(2,1)} %get-tuple-element.36), channel_id=1, source_target_pairs={{0,2},{1,3},{2,0},{3,1},{4,6},{5,7},{6,4},{7,5},{8,10},{9,11},{10,... | collective-permute-start | bytes 983048 | tf_op jit(solution)/shard_map/ppermute | solution.py:364
  8.8 1.3 collective-permute-start.2
  10.8 4.2 %fusion.3 = (bf16[7104,128]{1,0:T(8,128)(2,1)}, bf16[7104,128]{1,0:T(8,128)(2,1)}) fusion(bf16[14208,128]{1,0:T(8,128)(2,1)} %own_ref.1), kind=kLoop, calls=%fused_computation.17 | loop fusion | bytes 7274496 | tf_op jit(solution)/shard_map/slice | solution.py:420
  15.3 8.2 %collective-permute-done.1.r2_ref = bf16[16,16,640]{2,1,0:T(8,128)(2,1)S(1)} collective-permute-done((bf16[16,16,640]{2,1,0:T(8,128)(2,1)}, bf16[16,16,640]{2,1,0:T(8,128)(2,1)S(1)}, u32[]{:S(2)}, u32[]{:S(2)}) %collective-permute-start.1) | collective-permute-done | bytes 327712 | tf_op jit(solution)/shard_map/ppermute | solution.py:364
  23.5 1.2 collective-permute-start.3
  24.7 1.9 %collective-permute-start.4 = (bf16[7104,128]{1,0:T(8,128)(2,1)}, bf16[7104,128]{1,0:T(8,128)(2,1)}, u32[]{:S(2)}, u32[]{:S(2)}) collective-permute-start(bf16[7104,128]{1,0:T(8,128)(2,1)} %get-tuple-element.39), channel_id=1, source_target_pairs={{0,3},{3,0},{1,2},{2,1},{4,7},{7,4},{5,6},{6,5},{8,11},{11,8},{9,1... | collective-permute-start | bytes 5455880 | tf_op jit(solution)/shard_map/ppermute | solution.py:372
  26.8 5.9 %collective-permute-start.8 = (bf16[8,16,1024]{2,1,0:T(8,128)(2,1)S(1)}, bf16[8,16,1024]{2,1,0:T(8,128)(2,1)S(1)}, u32[]{:S(2)}, u32[]{:S(2)}) collective-permute-start(bf16[8,16,1024]{2,1,0:T(8,128)(2,1)S(1)} %get-tuple-element.48.refs_8_), channel_id=1, source_target_pairs={{0,56},{4,60},{8,0},{12,4},{16,8},{20,12},{24,16},{28,20},{32,24},... | collective-permute-start | bytes 786440 | tf_op jit(solution)/shard_map/ppermute | solution.py:384
  33.4 3.8 %collective-permute-done.8.refs_12_ = bf16[8,16,1024]{2,1,0:T(8,128)(2,1)S(1)} collective-permute-done((bf16[8,16,1024]{2,1,0:T(8,128)(2,1)S(1)}, bf16[8,16,1024]{2,1,0:T(8,128)(2,1)S(1)}, u32[]{:S(2)}, u32[]{:S(2)}) %collective-permute-start.8) | collective-permute-done | bytes 262176 | tf_op jit(solution)/shard_map/ppermute | solution.py:384
  37.2 3.7 %collective-permute-start.11 = (bf16[9,16,1024]{2,1,0:T(8,128)(2,1)S(1)}, bf16[9,16,1024]{2,1,0:T(8,128)(2,1)S(1)}, u32[]{:S(2)}, u32[]{:S(2)}) collective-permute-start(bf16[9,16,1024]{2,1,0:T(8,128)(2,1)S(1)} %get-tuple-element.47.refs_0_), channel_id=1, source_target_pairs={{0,56},{4,60},{8,0},{12,4},{16,8},{20,12},{24,16},{28,20},{32,24},... | collective-permute-start | bytes 884744 | tf_op jit(solution)/shard_map/ppermute | solution.py:384
  40.9 0.7 copy-done.3
  41.6 1.6 collective-permute-done.15.refs_9_
  43.9 3.1 %collective-permute-done.5.refs_1_ = bf16[9,16,1024]{2,1,0:T(8,128)(2,1)S(1)} collective-permute-done((bf16[9,16,1024]{2,1,0:T(8,128)(2,1)S(1)}, bf16[9,16,1024]{2,1,0:T(8,128)(2,1)S(1)}, u32[]{:S(2)}, u32[]{:S(2)}) %collective-permute-start.5) | collective-permute-done | bytes 294944 | tf_op jit(solution)/shard_map/ppermute | solution.py:384
  47.0 0.7 copy-done.5
  48.1 3.7 %collective-permute-start.12 = (bf16[9,16,1024]{2,1,0:T(8,128)(2,1)S(1)}, bf16[9,16,1024]{2,1,0:T(8,128)(2,1)S(1)}, u32[]{:S(2)}, u32[]{:S(2)}) collective-permute-start(bf16[9,16,1024]{2,1,0:T(8,128)(2,1)S(1)} %collective-permute-done.11.refs_4_), channel_id=1, source_target_pairs={{0,56},{4,60},{8,0},{12,4},{16,8},{20,12},{24,16},{28,20},{32,24},... | collective-permute-start | bytes 884744 | tf_op jit(solution)/shard_map/ppermute | solution.py:384
  51.8 0.7 copy-done.7
  52.5 0.8 collective-permute-done.9.refs_13_
  53.3 0.7 copy-done.15
  54.0 7.5 %collective-permute-done.16.refs_10_ = bf16[8,16,1024]{2,1,0:T(8,128)(2,1)} collective-permute-done((bf16[8,16,1024]{2,1,0:T(8,128)(2,1)S(1)}, bf16[8,16,1024]{2,1,0:T(8,128)(2,1)}, u32[]{:S(2)}, u32[]{:S(2)}) %collective-permute-start.16) | collective-permute-done | bytes 262176 | tf_op jit(solution)/shard_map/ppermute | solution.py:384
  61.6 1.7 %collective-permute-start.21 = (bf16[7104,128]{1,0:T(8,128)(2,1)}, bf16[7104,128]{1,0:T(8,128)(2,1)}, u32[]{:S(2)}, u32[]{:S(2)}) collective-permute-start(bf16[7104,128]{1,0:T(8,128)(2,1)} %get-tuple-element.39), channel_id=1, source_target_pairs={{0,1},{1,0},{2,3},{3,2},{4,5},{5,4},{6,7},{7,6},{8,9},{9,8},{10,11... | collective-permute-start | bytes 5455880 | tf_op jit(solution)/shard_map/ppermute | solution.py:368
  63.3 0.7 collective-permute-start.22
  64.0 2.0 %collective-permute-start.10 = (bf16[8,16,1024]{2,1,0:T(8,128)(2,1)}, bf16[8,16,1024]{2,1,0:T(8,128)(2,1)}, u32[]{:S(2)}, u32[]{:S(2)}) collective-permute-start(bf16[8,16,1024]{2,1,0:T(8,128)(2,1)} %collective-permute-done.9.refs_13_), channel_id=1, source_target_pairs={{0,56},{4,60},{8,0},{12,4},{16,8},{20,12},{24,16},{28,20},{32,24},... | collective-permute-start | bytes 786440 | tf_op jit(solution)/shard_map/ppermute | solution.py:384
  66.3 1.9 %collective-permute-start.17 = (bf16[8,16,1024]{2,1,0:T(8,128)(2,1)}, bf16[8,16,1024]{2,1,0:T(8,128)(2,1)}, u32[]{:S(2)}, u32[]{:S(2)}) collective-permute-start(bf16[8,16,1024]{2,1,0:T(8,128)(2,1)} %collective-permute-done.16.refs_10_), channel_id=1, source_target_pairs={{0,8},{4,12},{8,16},{12,20},{16,24},{20,28},{24,32},{28,36},{32,40... | collective-permute-start | bytes 786440 | tf_op jit(solution)/shard_map/ppermute | solution.py:384
  68.9 1.9 %collective-permute-start.7 = (bf16[9,16,1024]{2,1,0:T(8,128)(2,1)}, bf16[9,16,1024]{2,1,0:T(8,128)(2,1)}, u32[]{:S(2)}, u32[]{:S(2)}) collective-permute-start(bf16[9,16,1024]{2,1,0:T(8,128)(2,1)} %collective-permute-done.6.refs_2_), channel_id=1, source_target_pairs={{0,8},{4,12},{8,16},{12,20},{16,24},{20,28},{24,32},{28,36},{32,40... | collective-permute-start | bytes 884744 | tf_op jit(solution)/shard_map/ppermute | solution.py:384
  71.7 3.9 %collective-permute-start.13 = (bf16[9,16,1024]{2,1,0:T(8,128)(2,1)S(1)}, bf16[9,16,1024]{2,1,0:T(8,128)(2,1)S(1)}, u32[]{:S(2)}, u32[]{:S(2)}) collective-permute-start(bf16[9,16,1024]{2,1,0:T(8,128)(2,1)S(1)} %copy-done.10), channel_id=1, source_target_pairs={{0,56},{4,60},{8,0},{12,4},{16,8},{20,12},{24,16},{28,20},{32,24},... | collective-permute-start | bytes 884744 | tf_op jit(solution)/shard_map/ppermute | solution.py:384
  75.7 6.0 %collective-permute-done.7.refs_3_ = bf16[9,16,1024]{2,1,0:T(8,128)(2,1)} collective-permute-done((bf16[9,16,1024]{2,1,0:T(8,128)(2,1)}, bf16[9,16,1024]{2,1,0:T(8,128)(2,1)}, u32[]{:S(2)}, u32[]{:S(2)}) %collective-permute-start.7) | collective-permute-done | bytes 294944 | tf_op jit(solution)/shard_map/ppermute | solution.py:384
  81.7 3.2 %collective-permute-start.18 = (bf16[8,16,1024]{2,1,0:T(8,128)(2,1)}, bf16[8,16,1024]{2,1,0:T(8,128)(2,1)S(1)}, u32[]{:S(2)}, u32[]{:S(2)}) collective-permute-start(bf16[8,16,1024]{2,1,0:T(8,128)(2,1)} %collective-permute-done.10.refs_14_), channel_id=1, source_target_pairs={{0,56},{4,60},{8,0},{12,4},{16,8},{20,12},{24,16},{28,20},{32,24},... | collective-permute-start | bytes 786440 | tf_op jit(solution)/shard_map/ppermute | solution.py:384
  85.0 4.1 %collective-permute-done.18.refs_15_ = bf16[8,16,1024]{2,1,0:T(8,128)(2,1)S(1)} collective-permute-done((bf16[8,16,1024]{2,1,0:T(8,128)(2,1)}, bf16[8,16,1024]{2,1,0:T(8,128)(2,1)S(1)}, u32[]{:S(2)}, u32[]{:S(2)}) %collective-permute-start.18) | collective-permute-done | bytes 262176 | tf_op jit(solution)/shard_map/ppermute | solution.py:384
  89.9 0.9 copy-done.16
  90.8 4.1 %shard_map.85 = (bf16[2,512,512]{2,1,0:T(8,128)(2,1)S(1)}, bf16[2,512,512]{2,1,0:T(8,128)(2,1)S(1)}) custom-call(s32[1]{0:T(128)} %shard_map.83.token_ref, s32[3]{0:T(128)S(1)} %pad_add_fusion.1.place_ref, bf16[9,16,1024]{2,1,0:T(8,128)(2,1)S(1)} %copy-done.4, bf16[9,16,1024]{2,1,0:T(8,128)(2,1)S(1)} %copy-done.6, ...), custom_call_target="tpu_custom_call" | custom-call | flops 1000000 | bytes 1000000 | tf_op jit(solution)/shard_map/pallas_call | solution.py:208
  95.5 2.1 %collective-permute-done.19.refs_16_ = bf16[2,512,512]{2,1,0:T(8,128)(2,1)S(1)} collective-permute-done((bf16[2,512,512]{2,1,0:T(8,128)(2,1)S(1)}, bf16[2,512,512]{2,1,0:T(8,128)(2,1)S(1)}, u32[]{:S(2)}, u32[]{:S(2)}) %collective-permute-start.19) | collective-permute-done | bytes 1048608 | tf_op jit(solution)/shard_map/ppermute | solution.py:384
  97.7 1.5 collective-permute-done.20.refs_17_
  99.2 4.1 %shard_map.86 = (f32[512,512]{1,0:T(8,128)S(1)}, bf16[512,512]{1,0:T(8,128)(2,1)S(1)}, bf16[512,512]{1,0:T(8,128)(2,1)S(1)}, bf16[512,512]{1,0:T(8,128)(2,1)S(1)}) custom-call(s32[1]{0:T(128)} %shard_map.83.token_ref, s32[3]{0:T(128)S(1)} %pad_add_fusion.1.place_ref, bf16[9,16,1024]{2,1,0:T(8,128)(2,1)S(1)} %copy-done.4, bf16[9,16,1024]{2,1,0:T(8,128)(2,1)S(1)} %copy-done.6, ...), custom_call_target="tpu_custom_call" | custom-call | flops 1000000 | bytes 1000000 | tf_op jit(solution)/shard_map/pallas_call | solution.py:208
  103.3 2.4 %collective-permute-done.22.b2_ref = bf16[7104,128]{1,0:T(8,128)(2,1)} collective-permute-done((bf16[7104,128]{1,0:T(8,128)(2,1)}, bf16[7104,128]{1,0:T(8,128)(2,1)}, u32[]{:S(2)}, u32[]{:S(2)}) %collective-permute-start.22) | collective-permute-done | bytes 1818656 | tf_op jit(solution)/shard_map/ppermute | solution.py:372
  105.8 2.0 %collective-permute-start.29 = (bf16[7104,128]{1,0:T(8,128)(2,1)}, bf16[7104,128]{1,0:T(8,128)(2,1)}, u32[]{:S(2)}, u32[]{:S(2)}) collective-permute-start(bf16[7104,128]{1,0:T(8,128)(2,1)} %collective-permute-done.21.a1_ref), channel_id=1, source_target_pairs={{0,3},{3,0},{1,2},{2,1},{4,7},{7,4},{5,6},{6,5},{8,11},{11,8},{9,1... | collective-permute-start | bytes 5455880 | tf_op jit(solution)/shard_map/ppermute | solution.py:372
  108.2 2.4 %collective-permute-start.24 = (bf16[512,512]{1,0:T(8,128)(2,1)S(1)}, bf16[512,512]{1,0:T(8,128)(2,1)S(1)}, u32[]{:S(2)}, u32[]{:S(2)}) collective-permute-start(bf16[512,512]{1,0:T(8,128)(2,1)S(1)} %get-tuple-element.57), channel_id=1, source_target_pairs={{0,128},{4,132},{8,136},{12,140},{16,144},{20,148},{24,152},{28,15... | collective-permute-start | bytes 1572872 | tf_op jit(solution)/shard_map/ppermute | solution.py:384
  110.6 12.0 %collective-permute-done.23.r1_ref = bf16[512,512]{1,0:T(8,128)(2,1)S(1)} collective-permute-done((bf16[512,512]{1,0:T(8,128)(2,1)S(1)}, bf16[512,512]{1,0:T(8,128)(2,1)S(1)}, u32[]{:S(2)}, u32[]{:S(2)}) %collective-permute-start.23) | collective-permute-done | bytes 524320 | tf_op jit(solution)/shard_map/ppermute | solution.py:384
  122.6 2.0 %collective-permute-done.24.r2_ref = bf16[512,512]{1,0:T(8,128)(2,1)S(1)} collective-permute-done((bf16[512,512]{1,0:T(8,128)(2,1)S(1)}, bf16[512,512]{1,0:T(8,128)(2,1)S(1)}, u32[]{:S(2)}, u32[]{:S(2)}) %collective-permute-start.24) | collective-permute-done | bytes 524320 | tf_op jit(solution)/shard_map/ppermute | solution.py:384
  124.6 9.4 %collective-permute-done.25.r3_ref = bf16[512,512]{1,0:T(8,128)(2,1)S(1)} collective-permute-done((bf16[512,512]{1,0:T(8,128)(2,1)S(1)}, bf16[512,512]{1,0:T(8,128)(2,1)S(1)}, u32[]{:S(2)}, u32[]{:S(2)}) %collective-permute-start.25) | collective-permute-done | bytes 524320 | tf_op jit(solution)/shard_map/ppermute | solution.py:384
  134.0 1.1 shard_map.87
  135.1 1.8 %collective-permute-start.26 = (bf16[512,128]{1,0:T(8,128)(2,1)S(1)}, bf16[512,128]{1,0:T(8,128)(2,1)S(1)}, u32[]{:S(2)}, u32[]{:S(2)}) collective-permute-start(bf16[512,128]{1,0:T(8,128)(2,1)S(1)} %get-tuple-element.60), channel_id=1, source_target_pairs={{0,1},{1,2},{2,3},{3,0},{4,5},{5,6},{6,7},{7,4},{8,9},{9,10},{10,1... | collective-permute-start | bytes 393224 | tf_op jit(solution)/shard_map/ppermute | solution.py:364
  137.1 2.6 %collective-permute-start.28 = (bf16[512,128]{1,0:T(8,128)(2,1)S(1)}, bf16[512,128]{1,0:T(8,128)(2,1)S(1)}, u32[]{:S(2)}, u32[]{:S(2)}) collective-permute-start(bf16[512,128]{1,0:T(8,128)(2,1)S(1)} %get-tuple-element.62), channel_id=1, source_target_pairs={{0,3},{1,0},{2,1},{3,2},{4,7},{5,4},{6,5},{7,6},{8,11},{9,8},{10,9... | collective-permute-start | bytes 393224 | tf_op jit(solution)/shard_map/ppermute | solution.py:364
  139.8 2.0 %copy-done = bf16[14208,128]{1,0:T(8,128)(2,1)S(1)} copy-done((bf16[14208,128]{1,0:T(8,128)(2,1)S(1)}, bf16[14208,128]{1,0:T(8,128)(2,1)}, u32[]{:S(2)}) %copy-start) | copy-done | bytes 3637272
  141.8 3.3 %shard_map.88.held_ref = bf16[3,14208,128]{2,1,0:T(8,128)(2,1)S(1)} custom-call(bf16[14208,128]{1,0:T(8,128)(2,1)S(1)} %copy-done, bf16[7104,128]{1,0:T(8,128)(2,1)} %collective-permute-done.21.a1_ref, bf16[7104,128]{1,0:T(8,128)(2,1)S(1)} %copy-done.2, bf16[7104,128]{1,0:T(8,128)(2,1)} %collective-permute-done.4.refs_1_.b1_ref, ...), custom_call_target="tpu_custom_call" | custom-call | flops 1000000 | bytes 1000000 | tf_op jit(solution)/shard_map/pallas_call | solution.py:292
  145.1 6.4 %collective-permute-done.26.t1_ref = bf16[512,128]{1,0:T(8,128)(2,1)S(1)} collective-permute-done((bf16[512,128]{1,0:T(8,128)(2,1)S(1)}, bf16[512,128]{1,0:T(8,128)(2,1)S(1)}, u32[]{:S(2)}, u32[]{:S(2)}) %collective-permute-start.26) | collective-permute-done | bytes 131104 | tf_op jit(solution)/shard_map/ppermute | solution.py:364
  151.5 3.0 %collective-permute-done.27.t2_ref = bf16[512,128]{1,0:T(8,128)(2,1)S(1)} collective-permute-done((bf16[512,128]{1,0:T(8,128)(2,1)S(1)}, bf16[512,128]{1,0:T(8,128)(2,1)S(1)}, u32[]{:S(2)}, u32[]{:S(2)}) %collective-permute-start.27) | collective-permute-done | bytes 131104 | tf_op jit(solution)/shard_map/ppermute | solution.py:364
  154.7 7.3 %shard_map.89 = bf16[14208,128]{1,0:T(8,128)(2,1)} custom-call(s32[4]{0:T(128)S(1)} %pad_add_fusion.order_ref, f32[512,128]{1,0:T(8,128)S(1)} %get-tuple-element.59.t0_ref, bf16[512,128]{1,0:T(8,128)(2,1)S(1)} %collective-permute-done.26.t1_ref, bf16[512,128]{1,0:T(8,128)(2,1)S(1)} %collective-permute-done.27.t2_ref, ...), custom_call_target="tpu_custom_call" | custom-call | tf_op jit(solution)/shard_map/pallas_call | solution.py:344
  (76 shorter events, 7.0 us)
Async XLA Ops:
  0.0 10.2 %copy-start.19 = (f32[16,4]{0,1:T(4,128)S(1)}, f32[16,4]{0,1:T(4,128)}, u32[]{:S(2)}) copy-start(f32[16,4]{0,1:T(4,128)} %param.15) | copy-start | bytes 772
  0.0 10.4 %copy-start.20 = (s32[16,4]{0,1:T(4,128)S(1)}, s32[16,4]{0,1:T(4,128)}, u32[]{:S(2)}) copy-start(s32[16,4]{0,1:T(4,128)} %param.14) | copy-start | bytes 772
  4.3 11.0 %collective-permute-start = (bf16[16,16,640]{2,1,0:T(8,128)(2,1)}, bf16[16,16,640]{2,1,0:T(8,128)(2,1)S(1)}, u32[]{:S(2)}, u32[]{:S(2)}) collective-permute-start(bf16[16,16,640]{2,1,0:T(8,128)(2,1)} %get-tuple-element.35), channel_id=1, source_target_pairs={{0,1},{1,2},{2,3},{3,0},{4,5},{5,6},{6,7},{7,4},{8,9},{9,10},{10,1... | collective-permute-start | bytes 983048 | tf_op jit(solution)/shard_map/ppermute | solution.py:364
  5.9 17.6 %collective-permute-start.1 = (bf16[16,16,640]{2,1,0:T(8,128)(2,1)}, bf16[16,16,640]{2,1,0:T(8,128)(2,1)S(1)}, u32[]{:S(2)}, u32[]{:S(2)}) collective-permute-start(bf16[16,16,640]{2,1,0:T(8,128)(2,1)} %get-tuple-element.36), channel_id=1, source_target_pairs={{0,2},{1,3},{2,0},{3,1},{4,6},{5,7},{6,4},{7,5},{8,10},{9,11},{10,... | collective-permute-start | bytes 983048 | tf_op jit(solution)/shard_map/ppermute | solution.py:364
  8.8 14.7 %collective-permute-start.2 = (bf16[16,16,640]{2,1,0:T(8,128)(2,1)}, bf16[16,16,640]{2,1,0:T(8,128)(2,1)S(1)}, u32[]{:S(2)}, u32[]{:S(2)}) collective-permute-start(bf16[16,16,640]{2,1,0:T(8,128)(2,1)} %get-tuple-element.37), channel_id=1, source_target_pairs={{0,3},{1,0},{2,1},{3,2},{4,7},{5,4},{6,5},{7,6},{8,11},{9,8},{10,9... | collective-permute-start | bytes 983048 | tf_op jit(solution)/shard_map/ppermute | solution.py:364
  10.7 15.9 %copy-start.17 = (f32[16,16,512]{2,1,0:T(8,128)S(1)}, f32[16,16,512]{2,1,0:T(8,128)}, u32[]{:S(2)}) copy-start(f32[16,16,512]{2,1,0:T(8,128)} %get-tuple-element.42.gain_ref) | copy-start | bytes 1572868
  10.7 15.9 %copy-start.18 = (bf16[16,16,128]{2,1,0:T(8,128)(2,1)S(1)}, bf16[16,16,128]{2,1,0:T(8,128)(2,1)}, u32[]{:S(2)}) copy-start(bf16[16,16,128]{2,1,0:T(8,128)(2,1)} %get-tuple-element.43.innov_ref) | copy-start | bytes 196612
  23.5 42.8 %collective-permute-start.3 = (bf16[7104,128]{1,0:T(8,128)(2,1)}, bf16[7104,128]{1,0:T(8,128)(2,1)S(1)}, u32[]{:S(2)}, u32[]{:S(2)}) collective-permute-start(bf16[7104,128]{1,0:T(8,128)(2,1)} %get-tuple-element.38), channel_id=1, source_target_pairs={{0,1},{1,0},{2,3},{3,2},{4,5},{5,4},{6,7},{7,6},{8,9},{9,8},{10,11... | collective-permute-start | bytes 5455880 | tf_op jit(solution)/shard_map/ppermute | solution.py:368
  24.7 44.1 %collective-permute-start.4 = (bf16[7104,128]{1,0:T(8,128)(2,1)}, bf16[7104,128]{1,0:T(8,128)(2,1)}, u32[]{:S(2)}, u32[]{:S(2)}) collective-permute-start(bf16[7104,128]{1,0:T(8,128)(2,1)} %get-tuple-element.39), channel_id=1, source_target_pairs={{0,3},{3,0},{1,2},{2,1},{4,7},{7,4},{5,6},{6,5},{8,11},{11,8},{9,1... | collective-permute-start | bytes 5455880 | tf_op jit(solution)/shard_map/ppermute | solution.py:372
  26.8 10.4 %collective-permute-start.8 = (bf16[8,16,1024]{2,1,0:T(8,128)(2,1)S(1)}, bf16[8,16,1024]{2,1,0:T(8,128)(2,1)S(1)}, u32[]{:S(2)}, u32[]{:S(2)}) collective-permute-start(bf16[8,16,1024]{2,1,0:T(8,128)(2,1)S(1)} %get-tuple-element.48.refs_8_), channel_id=1, source_target_pairs={{0,56},{4,60},{8,0},{12,4},{16,8},{20,12},{24,16},{28,20},{32,24},... | collective-permute-start | bytes 786440 | tf_op jit(solution)/shard_map/ppermute | solution.py:384
  32.7 10.5 %collective-permute-start.15 = (bf16[8,16,1024]{2,1,0:T(8,128)(2,1)S(1)}, bf16[8,16,1024]{2,1,0:T(8,128)(2,1)S(1)}, u32[]{:S(2)}, u32[]{:S(2)}) collective-permute-start(bf16[8,16,1024]{2,1,0:T(8,128)(2,1)S(1)} %get-tuple-element.48.refs_8_), channel_id=1, source_target_pairs={{0,8},{4,12},{8,16},{12,20},{16,24},{20,28},{24,32},{28,36},{32,40... | collective-permute-start | bytes 786440 | tf_op jit(solution)/shard_map/ppermute | solution.py:384
  33.4 13.5 %collective-permute-start.5 = (bf16[9,16,1024]{2,1,0:T(8,128)(2,1)S(1)}, bf16[9,16,1024]{2,1,0:T(8,128)(2,1)S(1)}, u32[]{:S(2)}, u32[]{:S(2)}) collective-permute-start(bf16[9,16,1024]{2,1,0:T(8,128)(2,1)S(1)} %get-tuple-element.47.refs_0_), channel_id=1, source_target_pairs={{0,8},{4,12},{8,16},{12,20},{16,24},{20,28},{24,32},{28,36},{32,40... | collective-permute-start | bytes 884744 | tf_op jit(solution)/shard_map/ppermute | solution.py:384
  37.2 10.9 %collective-permute-start.11 = (bf16[9,16,1024]{2,1,0:T(8,128)(2,1)S(1)}, bf16[9,16,1024]{2,1,0:T(8,128)(2,1)S(1)}, u32[]{:S(2)}, u32[]{:S(2)}) collective-permute-start(bf16[9,16,1024]{2,1,0:T(8,128)(2,1)S(1)} %get-tuple-element.47.refs_0_), channel_id=1, source_target_pairs={{0,56},{4,60},{8,0},{12,4},{16,8},{20,12},{24,16},{28,20},{32,24},... | collective-permute-start | bytes 884744 | tf_op jit(solution)/shard_map/ppermute | solution.py:384
  43.2 10.1 %collective-permute-start.9 = (bf16[8,16,1024]{2,1,0:T(8,128)(2,1)S(1)}, bf16[8,16,1024]{2,1,0:T(8,128)(2,1)}, u32[]{:S(2)}, u32[]{:S(2)}) collective-permute-start(bf16[8,16,1024]{2,1,0:T(8,128)(2,1)S(1)} %collective-permute-done.8.refs_12_), channel_id=1, source_target_pairs={{0,56},{4,60},{8,0},{12,4},{16,8},{20,12},{24,16},{28,20},{32,24},... | collective-permute-start | bytes 786440 | tf_op jit(solution)/shard_map/ppermute | solution.py:384
  47.0 16.4 %collective-permute-start.6 = (bf16[9,16,1024]{2,1,0:T(8,128)(2,1)S(1)}, bf16[9,16,1024]{2,1,0:T(8,128)(2,1)}, u32[]{:S(2)}, u32[]{:S(2)}) collective-permute-start(bf16[9,16,1024]{2,1,0:T(8,128)(2,1)S(1)} %collective-permute-done.5.refs_1_), channel_id=1, source_target_pairs={{0,8},{4,12},{8,16},{12,20},{16,24},{20,28},{24,32},{28,36},{32,40... | collective-permute-start | bytes 884744 | tf_op jit(solution)/shard_map/ppermute | solution.py:384
  47.0 0.7 copy-start.5
  48.1 15.9 %collective-permute-start.12 = (bf16[9,16,1024]{2,1,0:T(8,128)(2,1)S(1)}, bf16[9,16,1024]{2,1,0:T(8,128)(2,1)S(1)}, u32[]{:S(2)}, u32[]{:S(2)}) collective-permute-start(bf16[9,16,1024]{2,1,0:T(8,128)(2,1)S(1)} %collective-permute-done.11.refs_4_), channel_id=1, source_target_pairs={{0,56},{4,60},{8,0},{12,4},{16,8},{20,12},{24,16},{28,20},{32,24},... | collective-permute-start | bytes 884744 | tf_op jit(solution)/shard_map/ppermute | solution.py:384
  51.8 0.7 copy-start.7
  53.3 8.3 %collective-permute-start.16 = (bf16[8,16,1024]{2,1,0:T(8,128)(2,1)S(1)}, bf16[8,16,1024]{2,1,0:T(8,128)(2,1)}, u32[]{:S(2)}, u32[]{:S(2)}) collective-permute-start(bf16[8,16,1024]{2,1,0:T(8,128)(2,1)S(1)} %collective-permute-done.15.refs_9_), channel_id=1, source_target_pairs={{0,8},{4,12},{8,16},{12,20},{16,24},{20,28},{24,32},{28,36},{32,40... | collective-permute-start | bytes 786440 | tf_op jit(solution)/shard_map/ppermute | solution.py:384
  61.6 41.8 %collective-permute-start.21 = (bf16[7104,128]{1,0:T(8,128)(2,1)}, bf16[7104,128]{1,0:T(8,128)(2,1)}, u32[]{:S(2)}, u32[]{:S(2)}) collective-permute-start(bf16[7104,128]{1,0:T(8,128)(2,1)} %get-tuple-element.39), channel_id=1, source_target_pairs={{0,1},{1,0},{2,3},{3,2},{4,5},{5,4},{6,7},{7,6},{8,9},{9,8},{10,11... | collective-permute-start | bytes 5455880 | tf_op jit(solution)/shard_map/ppermute | solution.py:368
  63.3 42.5 %collective-permute-start.22 = (bf16[7104,128]{1,0:T(8,128)(2,1)}, bf16[7104,128]{1,0:T(8,128)(2,1)}, u32[]{:S(2)}, u32[]{:S(2)}) collective-permute-start(bf16[7104,128]{1,0:T(8,128)(2,1)} %get-tuple-element.38), channel_id=1, source_target_pairs={{0,3},{3,0},{1,2},{2,1},{4,7},{7,4},{5,6},{6,5},{8,11},{11,8},{9,1... | collective-permute-start | bytes 5455880 | tf_op jit(solution)/shard_map/ppermute | solution.py:372
  64.0 4.8 %copy-start.9 = (bf16[9,16,1024]{2,1,0:T(8,128)(2,1)}, bf16[9,16,1024]{2,1,0:T(8,128)(2,1)S(1)}, u32[]{:S(2)}) copy-start(bf16[9,16,1024]{2,1,0:T(8,128)(2,1)S(1)} %collective-permute-done.12.refs_5_) | copy-start | bytes 884740
  64.0 7.3 %collective-permute-start.10 = (bf16[8,16,1024]{2,1,0:T(8,128)(2,1)}, bf16[8,16,1024]{2,1,0:T(8,128)(2,1)}, u32[]{:S(2)}, u32[]{:S(2)}) collective-permute-start(bf16[8,16,1024]{2,1,0:T(8,128)(2,1)} %collective-permute-done.9.refs_13_), channel_id=1, source_target_pairs={{0,56},{4,60},{8,0},{12,4},{16,8},{20,12},{24,16},{28,20},{32,24},... | collective-permute-start | bytes 786440 | tf_op jit(solution)/shard_map/ppermute | solution.py:384
  66.3 4.5 %copy-start.1 = (bf16[7104,128]{1,0:T(8,128)(2,1)}, bf16[7104,128]{1,0:T(8,128)(2,1)S(1)}, u32[]{:S(2)}) copy-start(bf16[7104,128]{1,0:T(8,128)(2,1)S(1)} %collective-permute-done.3.refs_0_.a2_ref) | copy-start | bytes 5455876
  66.3 15.4 %collective-permute-start.17 = (bf16[8,16,1024]{2,1,0:T(8,128)(2,1)}, bf16[8,16,1024]{2,1,0:T(8,128)(2,1)}, u32[]{:S(2)}, u32[]{:S(2)}) collective-permute-start(bf16[8,16,1024]{2,1,0:T(8,128)(2,1)} %collective-permute-done.16.refs_10_), channel_id=1, source_target_pairs={{0,8},{4,12},{8,16},{12,20},{16,24},{20,28},{24,32},{28,36},{32,40... | collective-permute-start | bytes 786440 | tf_op jit(solution)/shard_map/ppermute | solution.py:384
  68.9 12.9 %collective-permute-start.7 = (bf16[9,16,1024]{2,1,0:T(8,128)(2,1)}, bf16[9,16,1024]{2,1,0:T(8,128)(2,1)}, u32[]{:S(2)}, u32[]{:S(2)}) collective-permute-start(bf16[9,16,1024]{2,1,0:T(8,128)(2,1)} %collective-permute-done.6.refs_2_), channel_id=1, source_target_pairs={{0,8},{4,12},{8,16},{12,20},{16,24},{20,28},{24,32},{28,36},{32,40... | collective-permute-start | bytes 884744 | tf_op jit(solution)/shard_map/ppermute | solution.py:384
  70.8 1.0 copy-start.10
  70.8 19.1 %copy-start.4 = (bf16[9,16,1024]{2,1,0:T(8,128)(2,1)S(1)}, bf16[9,16,1024]{2,1,0:T(8,128)(2,1)}, u32[]{:S(2)}) copy-start(bf16[9,16,1024]{2,1,0:T(8,128)(2,1)} %copy-done.3) | copy-start | bytes 884740
  70.8 19.1 %copy-start.6 = (bf16[9,16,1024]{2,1,0:T(8,128)(2,1)S(1)}, bf16[9,16,1024]{2,1,0:T(8,128)(2,1)}, u32[]{:S(2)}) copy-start(bf16[9,16,1024]{2,1,0:T(8,128)(2,1)} %copy-done.5) | copy-start | bytes 884740
  70.8 19.1 %copy-start.8 = (bf16[9,16,1024]{2,1,0:T(8,128)(2,1)S(1)}, bf16[9,16,1024]{2,1,0:T(8,128)(2,1)}, u32[]{:S(2)}) copy-start(bf16[9,16,1024]{2,1,0:T(8,128)(2,1)} %copy-done.7) | copy-start | bytes 884740
  70.8 19.1 %copy-start.12 = (bf16[8,16,1024]{2,1,0:T(8,128)(2,1)S(1)}, bf16[8,16,1024]{2,1,0:T(8,128)(2,1)}, u32[]{:S(2)}) copy-start(bf16[8,16,1024]{2,1,0:T(8,128)(2,1)} %copy-done.11) | copy-start | bytes 786436
  70.8 19.1 %copy-start.14 = (bf16[8,16,1024]{2,1,0:T(8,128)(2,1)S(1)}, bf16[8,16,1024]{2,1,0:T(8,128)(2,1)}, u32[]{:S(2)}) copy-start(bf16[8,16,1024]{2,1,0:T(8,128)(2,1)} %copy-done.13) | copy-start | bytes 786436
  71.7 13.3 %collective-permute-start.13 = (bf16[9,16,1024]{2,1,0:T(8,128)(2,1)S(1)}, bf16[9,16,1024]{2,1,0:T(8,128)(2,1)S(1)}, u32[]{:S(2)}, u32[]{:S(2)}) collective-permute-start(bf16[9,16,1024]{2,1,0:T(8,128)(2,1)S(1)} %copy-done.10), channel_id=1, source_target_pairs={{0,56},{4,60},{8,0},{12,4},{16,8},{20,12},{24,16},{28,20},{32,24},... | collective-permute-start | bytes 884744 | tf_op jit(solution)/shard_map/ppermute | solution.py:384
  81.7 8.1 %collective-permute-start.14 = (bf16[9,16,1024]{2,1,0:T(8,128)(2,1)}, bf16[9,16,1024]{2,1,0:T(8,128)(2,1)S(1)}, u32[]{:S(2)}, u32[]{:S(2)}) collective-permute-start(bf16[9,16,1024]{2,1,0:T(8,128)(2,1)} %collective-permute-done.7.refs_3_), channel_id=1, source_target_pairs={{0,8},{4,12},{8,16},{12,20},{16,24},{20,28},{24,32},{28,36},{32,40... | collective-permute-start | bytes 884744 | tf_op jit(solution)/shard_map/ppermute | solution.py:384
  81.7 7.4 %collective-permute-start.18 = (bf16[8,16,1024]{2,1,0:T(8,128)(2,1)}, bf16[8,16,1024]{2,1,0:T(8,128)(2,1)S(1)}, u32[]{:S(2)}, u32[]{:S(2)}) collective-permute-start(bf16[8,16,1024]{2,1,0:T(8,128)(2,1)} %collective-permute-done.10.refs_14_), channel_id=1, source_target_pairs={{0,56},{4,60},{8,0},{12,4},{16,8},{20,12},{24,16},{28,20},{32,24},... | collective-permute-start | bytes 786440 | tf_op jit(solution)/shard_map/ppermute | solution.py:384
  89.9 1.0 copy-start.16
  94.9 2.7 %collective-permute-start.19 = (bf16[2,512,512]{2,1,0:T(8,128)(2,1)S(1)}, bf16[2,512,512]{2,1,0:T(8,128)(2,1)S(1)}, u32[]{:S(2)}, u32[]{:S(2)}) collective-permute-start(bf16[2,512,512]{2,1,0:T(8,128)(2,1)S(1)} %get-tuple-element.52), channel_id=1, source_target_pairs={{0,4},{4,0},{8,12},{12,8},{16,20},{20,16},{24,28},{28,24},{32,36},... | collective-permute-start | bytes 3145736 | tf_op jit(solution)/shard_map/ppermute | solution.py:384
  95.0 4.1 %collective-permute-start.20 = (bf16[2,512,512]{2,1,0:T(8,128)(2,1)S(1)}, bf16[2,512,512]{2,1,0:T(8,128)(2,1)S(1)}, u32[]{:S(2)}, u32[]{:S(2)}) collective-permute-start(bf16[2,512,512]{2,1,0:T(8,128)(2,1)S(1)} %get-tuple-element.53), channel_id=1, source_target_pairs={{0,4},{4,0},{8,12},{12,8},{16,20},{20,16},{24,28},{28,24},{32,36},... | collective-permute-start | bytes 3145736 | tf_op jit(solution)/shard_map/ppermute | solution.py:384
  105.8 48.9 %collective-permute-start.29 = (bf16[7104,128]{1,0:T(8,128)(2,1)}, bf16[7104,128]{1,0:T(8,128)(2,1)}, u32[]{:S(2)}, u32[]{:S(2)}) collective-permute-start(bf16[7104,128]{1,0:T(8,128)(2,1)} %collective-permute-done.21.a1_ref), channel_id=1, source_target_pairs={{0,3},{3,0},{1,2},{2,1},{4,7},{7,4},{5,6},{6,5},{8,11},{11,8},{9,1... | collective-permute-start | bytes 5455880 | tf_op jit(solution)/shard_map/ppermute | solution.py:372
  107.7 46.9 %collective-permute-start.30 = (bf16[7104,128]{1,0:T(8,128)(2,1)}, bf16[7104,128]{1,0:T(8,128)(2,1)}, u32[]{:S(2)}, u32[]{:S(2)}) collective-permute-start(bf16[7104,128]{1,0:T(8,128)(2,1)} %collective-permute-done.22.b2_ref), channel_id=1, source_target_pairs={{0,1},{1,0},{2,3},{3,2},{4,5},{5,4},{6,7},{7,6},{8,9},{9,8},{10,11... | collective-permute-start | bytes 5455880 | tf_op jit(solution)/shard_map/ppermute | solution.py:368
  107.7 14.9 %collective-permute-start.23 = (bf16[512,512]{1,0:T(8,128)(2,1)S(1)}, bf16[512,512]{1,0:T(8,128)(2,1)S(1)}, u32[]{:S(2)}, u32[]{:S(2)}) collective-permute-start(bf16[512,512]{1,0:T(8,128)(2,1)S(1)} %get-tuple-element.56), channel_id=1, source_target_pairs={{0,64},{4,68},{8,72},{12,76},{16,80},{20,84},{24,88},{28,92},{32,9... | collective-permute-start | bytes 1572872 | tf_op jit(solution)/shard_map/ppermute | solution.py:384
  108.2 16.4 %collective-permute-start.24 = (bf16[512,512]{1,0:T(8,128)(2,1)S(1)}, bf16[512,512]{1,0:T(8,128)(2,1)S(1)}, u32[]{:S(2)}, u32[]{:S(2)}) collective-permute-start(bf16[512,512]{1,0:T(8,128)(2,1)S(1)} %get-tuple-element.57), channel_id=1, source_target_pairs={{0,128},{4,132},{8,136},{12,140},{16,144},{20,148},{24,152},{28,15... | collective-permute-start | bytes 1572872 | tf_op jit(solution)/shard_map/ppermute | solution.py:384
  110.6 29.2 %copy-start.2 = (bf16[7104,128]{1,0:T(8,128)(2,1)S(1)}, bf16[7104,128]{1,0:T(8,128)(2,1)}, u32[]{:S(2)}) copy-start(bf16[7104,128]{1,0:T(8,128)(2,1)} %copy-done.1) | copy-start | bytes 5455876
  110.6 23.4 %collective-permute-start.25 = (bf16[512,512]{1,0:T(8,128)(2,1)S(1)}, bf16[512,512]{1,0:T(8,128)(2,1)S(1)}, u32[]{:S(2)}, u32[]{:S(2)}) collective-permute-start(bf16[512,512]{1,0:T(8,128)(2,1)S(1)} %get-tuple-element.58), channel_id=1, source_target_pairs={{0,192},{4,196},{8,200},{12,204},{16,208},{20,212},{24,216},{28,22... | collective-permute-start | bytes 1572872 | tf_op jit(solution)/shard_map/ppermute | solution.py:384
  135.1 16.4 %collective-permute-start.26 = (bf16[512,128]{1,0:T(8,128)(2,1)S(1)}, bf16[512,128]{1,0:T(8,128)(2,1)S(1)}, u32[]{:S(2)}, u32[]{:S(2)}) collective-permute-start(bf16[512,128]{1,0:T(8,128)(2,1)S(1)} %get-tuple-element.60), channel_id=1, source_target_pairs={{0,1},{1,2},{2,3},{3,0},{4,5},{5,6},{6,7},{7,4},{8,9},{9,10},{10,1... | collective-permute-start | bytes 393224 | tf_op jit(solution)/shard_map/ppermute | solution.py:364
  136.9 17.5 %collective-permute-start.27 = (bf16[512,128]{1,0:T(8,128)(2,1)S(1)}, bf16[512,128]{1,0:T(8,128)(2,1)S(1)}, u32[]{:S(2)}, u32[]{:S(2)}) collective-permute-start(bf16[512,128]{1,0:T(8,128)(2,1)S(1)} %get-tuple-element.61), channel_id=1, source_target_pairs={{0,2},{1,3},{2,0},{3,1},{4,6},{5,7},{6,4},{7,5},{8,10},{9,11},{10,... | collective-permute-start | bytes 393224 | tf_op jit(solution)/shard_map/ppermute | solution.py:364
  137.1 17.5 %collective-permute-start.28 = (bf16[512,128]{1,0:T(8,128)(2,1)S(1)}, bf16[512,128]{1,0:T(8,128)(2,1)S(1)}, u32[]{:S(2)}, u32[]{:S(2)}) collective-permute-start(bf16[512,128]{1,0:T(8,128)(2,1)S(1)} %get-tuple-element.62), channel_id=1, source_target_pairs={{0,3},{1,0},{2,1},{3,2},{4,7},{5,4},{6,5},{7,6},{8,11},{9,8},{10,9... | collective-permute-start | bytes 393224 | tf_op jit(solution)/shard_map/ppermute | solution.py:364
  139.8 2.0 %copy-start = (bf16[14208,128]{1,0:T(8,128)(2,1)S(1)}, bf16[14208,128]{1,0:T(8,128)(2,1)}, u32[]{:S(2)}) copy-start(bf16[14208,128]{1,0:T(8,128)(2,1)} %own_ref.1) | copy-start | bytes 10911748
  (4 other events, 2.8 us)

commit v6 on v5

--- a/solution.py
+++ b/solution.py
@@ -50,7 +50,7 @@
     nblock, obs_rows, part = obs_anom.shape
     members = inverses.shape[1]
     quarter = obs_rows // GROUPS
-    step = 4
+    step = 8
     widths = [members, part] + [members + part] * 3
     types = [jnp.float32] + [jnp.bfloat16] * 4
     rows = pl.BlockSpec((step, obs_rows, part), lambda i, q: (i, 0, 0))
@@ -83,7 +83,7 @@
 
 
 def merge_kernel(
-    q_ref, chosen_ref, taper_ref, gain_ref, innov_ref, r1_ref, r2_ref, r3_ref, low_ref, high_ref
+    q_ref, early_ref, chosen_ref, taper_ref, gain_ref, innov_ref, r1_ref, r2_ref, r3_ref, low_ref, high_ref
 ):
     members = gain_ref.shape[2]
     part = innov_ref.shape[2]
@@ -113,13 +113,13 @@
         low_ref[half, :, k * lanes : (k + 1) * lanes] = term
 
 
-def merge(q, chosen, taper, parts):
+def merge(q, early, chosen, taper, parts):
     nblock, quarter, members = parts[0].shape
     half = nblock // 2
     vmem = pl.BlockSpec(memory_space=pltpu.VMEM)
     return pl.pallas_call(
         merge_kernel,
-        in_specs=[pl.BlockSpec(memory_space=pltpu.SMEM)] + [vmem] * (2 + len(parts)),
+        in_specs=[pl.BlockSpec(memory_space=pltpu.SMEM)] * 2 + [vmem] * (2 + len(parts)),
         out_specs=[vmem] * 2,
         out_shape=[
             jax.ShapeDtypeStruct((half + 1, quarter, 2 * members), jnp.bfloat16),
@@ -127,7 +127,7 @@
         ],
         compiler_params=pltpu.CompilerParams(vmem_limit_bytes=VMEM_LIMIT),
         cost_estimate=SMALL,
-    )(q, chosen, taper, *parts)
+    )(q, early, chosen, taper, *parts)
 
 
 def sums_kernel(same, token_ref, place_ref, *refs):
@@ -416,14 +416,13 @@
     tapers = jnp.sum(ranked * taper_weight.reshape(pairs, 1), axis=0, keepdims=True)
 
     half = rows // 2
-    chosen, tapers, m1, m2, m3, low, high = lax.optimization_barrier(
-        (chosen, tapers, m1, m2, m3, ensemble[:half], ensemble[half:])
-    )
+    early = arrived(m1, m3)
+    m1, m3, low, high = lax.optimization_barrier((m1, m3, ensemble[:half], ensemble[half:]))
     a2, b1 = swap_a(high), swap_b(low)
     a1, b2 = swap_a(low), swap_b(high)
 
     up, down = (0, 1, 0), (0, -1, 0)
-    own_blocks = tuple(merge(q1, chosen, tapers, (gain, innov, m1, m2, m3)))
+    own_blocks = tuple(merge(q1, early, chosen, tapers, (gain, innov, m1, m2, m3)))
     ups, downs = [own_blocks], [own_blocks]
     for _ in range(3):
         ups.append(tuple(move(x, columns, up) for x in ups[-1]))

time: 162 us -> 159 us (0.981)
  waiting for transfers between devices: 76.3 us -> 72.4 us
  starting transfers between devices: 47.9 us -> 46 us
    ppermute x3, starting transfers between devices: 4.58 us -> 8.35 us  [swap_b(): return lax.ppermute(x, 'mem', [(0, 3), (3, 0), (1, 2), (2, 1)])]
    ppermute x19, starting transfers between devices: 29.9 us -> 26.4 us  [move(): return lax.ppermute(x, 'tile', pairs)]
    ppermute x6, waiting for transfers between devices: 17.9 us -> 15.2 us  [shift(): lax.ppermute(x, 'mem', [(i, (i + d) % GROUPS) for i in range(GROUPS)])]
    ppermute x3, waiting for transfers between devices: 3.07 us -> 1.12 us  [swap_b(): return lax.ppermute(x, 'mem', [(0, 3), (3, 0), (1, 2), (2, 1)])]
    unnamed x44 -> x48, local copies, waits for them, and re-layouts: 7.85 us -> 8.95 us
  transfers between devices with their start and end apart: 31 -> 31, of which waited for: 22 -> 23; matrix products, arithmetic and copies ran while one was open for 3% -> 3% of each run, Pallas kernels for 8% -> 10%
where the time goes in v6:
time: 159 us; the launch traced here: 158 us
  waiting for transfers between devices  72.4 us (46%)
  starting transfers between devices  46 us (29%)
  Pallas kernels  25.5 us (16%)
  local copies, waits for them, and re-layouts  13.3 us (8%)
    ppermute x19, waiting for transfers between devices, move(): return lax.ppermute(x, 'tile', pairs)  55.5 us
    ppermute x19, starting transfers between devices, move(): return lax.ppermute(x, 'tile', pairs)  26.4 us
    ppermute x6, waiting for transfers between devices, shift(): lax.ppermute(x, 'mem', [(i, (i + d) % GROUPS) for i in range(GROUPS)])  15.2 us
    ppermute x6, starting transfers between devices, shift(): lax.ppermute(x, 'mem', [(i, (i + d) % GROUPS) for i in range(GROUPS)])  9.87 us
    unnamed x48, local copies, waits for them, and re-layouts  8.95 us
    ppermute x3, starting transfers between devices, swap_b(): return lax.ppermute(x, 'mem', [(0, 3), (3, 0), (1, 2), (2, 1)])  8.35 us
    pallas_call x2, Pallas kernels, sums(): pl.pallas_call(functools.partial(sums_kernel, same), in_specs=[pl.BlockSp...  8.09 us
    pallas_call x1, Pallas kernels, update(): pl.pallas_call(update_kernel, in_specs=[pl.BlockSpec(memory_space=pltpu.S...  6.63 us
  transfers between devices with their start and end apart: 31, of which 23 were waited for; matrix products, arithmetic and copies ran while one was open for 3% of the time, Pallas kernels for 10%

profile of v6, /device:TPU:6, one launch (start us, length us, event | category | flops | bytes accessed | tf_op | source)
XLA Modules:
  0.0 158.0 jit_solution(5139730885660273939)
XLA Ops:
  0.0 3.3 %shard_map.82 = (f32[16,16,512]{2,1,0:T(8,128)}, bf16[16,16,128]{2,1,0:T(8,128)(2,1)}, bf16[16,16,640]{2,1,0:T(8,128)(2,1)}, bf16[16,16,640]{2,1,0:T(8,128)(2,1)}, bf16[16,16,640]{2,1,0:T(8,128)(2,1)}) custom-call(s32[1]{0:T(128)} %bitcast.q_ref, bf16[16,64,128]{2,1,0:T(8,128)(2,1)} %obs_ref.1, bf16[16,512,128]{2,1,0:T(8,128)(2,1)} %inv_ref.1, ...), custom_call_target="tpu_custom_call" | custom-call | tf_op jit(solution)/shard_map/pallas_call | solution.py:57
  3.3 1.6 %collective-permute-start = (bf16[16,16,640]{2,1,0:T(8,128)(2,1)}, bf16[16,16,640]{2,1,0:T(8,128)(2,1)S(1)}, u32[]{:S(2)}, u32[]{:S(2)}) collective-permute-start(bf16[16,16,640]{2,1,0:T(8,128)(2,1)} %get-tuple-element.32), channel_id=1, source_target_pairs={{0,1},{1,2},{2,3},{3,0},{4,5},{5,6},{6,7},{7,4},{8,9},{9,10},{10,1... | collective-permute-start | bytes 983048 | tf_op jit(solution)/shard_map/ppermute | solution.py:364
  4.9 1.7 %collective-permute-start.1 = (bf16[16,16,640]{2,1,0:T(8,128)(2,1)}, bf16[16,16,640]{2,1,0:T(8,128)(2,1)S(1)}, u32[]{:S(2)}, u32[]{:S(2)}) collective-permute-start(bf16[16,16,640]{2,1,0:T(8,128)(2,1)} %get-tuple-element.33), channel_id=1, source_target_pairs={{0,3},{1,0},{2,1},{3,2},{4,7},{5,4},{6,5},{7,6},{8,11},{9,8},{10,9... | collective-permute-start | bytes 983048 | tf_op jit(solution)/shard_map/ppermute | solution.py:364
  6.6 2.0 %collective-permute-start.4 = (bf16[16,16,640]{2,1,0:T(8,128)(2,1)}, bf16[16,16,640]{2,1,0:T(8,128)(2,1)}, u32[]{:S(2)}, u32[]{:S(2)}) collective-permute-start(bf16[16,16,640]{2,1,0:T(8,128)(2,1)} %get-tuple-element.39), channel_id=1, source_target_pairs={{0,2},{1,3},{2,0},{3,1},{4,6},{5,7},{6,4},{7,5},{8,10},{9,11},{10,... | collective-permute-start | bytes 983048 | tf_op jit(solution)/shard_map/ppermute | solution.py:364
  8.6 4.1 %fusion.3 = (bf16[7104,128]{1,0:T(8,128)(2,1)}, bf16[7104,128]{1,0:T(8,128)(2,1)}) fusion(bf16[14208,128]{1,0:T(8,128)(2,1)} %own_ref.1), kind=kLoop, calls=%fused_computation.17 | loop fusion | bytes 7274496 | tf_op jit(solution)/shard_map/slice | solution.py:420
  13.5 0.8 collective-permute-done.refs_0_.r1_ref
  14.3 5.2 %collective-permute-done.1.refs_1_.r3_ref = bf16[16,16,640]{2,1,0:T(8,128)(2,1)S(1)} collective-permute-done((bf16[16,16,640]{2,1,0:T(8,128)(2,1)}, bf16[16,16,640]{2,1,0:T(8,128)(2,1)S(1)}, u32[]{:S(2)}, u32[]{:S(2)}) %collective-permute-start.1) | collective-permute-done | bytes 327712 | tf_op jit(solution)/shard_map/ppermute | solution.py:364
  19.5 4.1 %collective-permute-start.3 = (bf16[7104,128]{1,0:T(8,128)(2,1)}, bf16[7104,128]{1,0:T(8,128)(2,1)}, u32[]{:S(2)}, u32[]{:S(2)}) collective-permute-start(bf16[7104,128]{1,0:T(8,128)(2,1)} %get-tuple-element.35), channel_id=1, source_target_pairs={{0,3},{3,0},{1,2},{2,1},{4,7},{7,4},{5,6},{6,5},{8,11},{11,8},{9,1... | collective-permute-start | bytes 5455880 | tf_op jit(solution)/shard_map/ppermute | solution.py:372
  24.6 1.0 copy-done.17
  25.6 1.0 copy-done.19
  26.6 1.7 %shard_map.85 = (bf16[9,16,1024]{2,1,0:T(8,128)(2,1)S(1)}, bf16[8,16,1024]{2,1,0:T(8,128)(2,1)S(1)}) custom-call(s32[1]{0:T(128)} %bitcast.q_ref, s32[1]{0:T(128)} %shard_map.84.early_ref, f32[1,128]{1,0:T(1,128)S(1)} %bitcast.10, f32[1,128]{1,0:T(1,128)S(1)} %bitcast.9, f32[16,16,512]{2,1,0:T(8,128)S(1)} %copy-done.15, bf16[16,16,128]{2,1,0:T(8,128)(2,1)S(1)} %copy-done.20, ...), custom_call_target="tpu_custom_call" | custom-call | flops 1000000 | bytes 1000000 | tf_op jit(solution)/shard_map/pallas_call | solution.py:120
  28.3 5.9 %collective-permute-start.8 = (bf16[8,16,1024]{2,1,0:T(8,128)(2,1)S(1)}, bf16[8,16,1024]{2,1,0:T(8,128)(2,1)S(1)}, u32[]{:S(2)}, u32[]{:S(2)}) collective-permute-start(bf16[8,16,1024]{2,1,0:T(8,128)(2,1)S(1)} %get-tuple-element.42.refs_8_), channel_id=1, source_target_pairs={{0,56},{4,60},{8,0},{12,4},{16,8},{20,12},{24,16},{28,20},{32,24},... | collective-permute-start | bytes 786440 | tf_op jit(solution)/shard_map/ppermute | solution.py:384
  34.9 3.2 %collective-permute-done.8.refs_12_ = bf16[8,16,1024]{2,1,0:T(8,128)(2,1)S(1)} collective-permute-done((bf16[8,16,1024]{2,1,0:T(8,128)(2,1)S(1)}, bf16[8,16,1024]{2,1,0:T(8,128)(2,1)S(1)}, u32[]{:S(2)}, u32[]{:S(2)}) %collective-permute-start.8) | collective-permute-done | bytes 262176 | tf_op jit(solution)/shard_map/ppermute | solution.py:384
  38.1 3.7 %collective-permute-start.11 = (bf16[9,16,1024]{2,1,0:T(8,128)(2,1)S(1)}, bf16[9,16,1024]{2,1,0:T(8,128)(2,1)S(1)}, u32[]{:S(2)}, u32[]{:S(2)}) collective-permute-start(bf16[9,16,1024]{2,1,0:T(8,128)(2,1)S(1)} %get-tuple-element.41.refs_0_), channel_id=1, source_target_pairs={{0,56},{4,60},{8,0},{12,4},{16,8},{20,12},{24,16},{28,20},{32,24},... | collective-permute-start | bytes 884744 | tf_op jit(solution)/shard_map/ppermute | solution.py:384
  42.5 1.0 collective-permute-done.15.refs_9_
  44.2 2.7 %collective-permute-done.5.refs_1_ = bf16[9,16,1024]{2,1,0:T(8,128)(2,1)S(1)} collective-permute-done((bf16[9,16,1024]{2,1,0:T(8,128)(2,1)S(1)}, bf16[9,16,1024]{2,1,0:T(8,128)(2,1)S(1)}, u32[]{:S(2)}, u32[]{:S(2)}) %collective-permute-start.5) | collective-permute-done | bytes 294944 | tf_op jit(solution)/shard_map/ppermute | solution.py:384
  46.9 0.7 copy-done.3
  48.1 3.7 %collective-permute-start.12 = (bf16[9,16,1024]{2,1,0:T(8,128)(2,1)S(1)}, bf16[9,16,1024]{2,1,0:T(8,128)(2,1)S(1)}, u32[]{:S(2)}, u32[]{:S(2)}) collective-permute-start(bf16[9,16,1024]{2,1,0:T(8,128)(2,1)S(1)} %collective-permute-done.11.refs_4_), channel_id=1, source_target_pairs={{0,56},{4,60},{8,0},{12,4},{16,8},{20,12},{24,16},{28,20},{32,24},... | collective-permute-start | bytes 884744 | tf_op jit(solution)/shard_map/ppermute | solution.py:384
  51.8 0.7 copy-done.5
  52.6 0.7 collective-permute-done.9.refs_13_
  53.3 0.7 copy-done.13
  54.0 7.5 %collective-permute-done.16.refs_10_ = bf16[8,16,1024]{2,1,0:T(8,128)(2,1)} collective-permute-done((bf16[8,16,1024]{2,1,0:T(8,128)(2,1)S(1)}, bf16[8,16,1024]{2,1,0:T(8,128)(2,1)}, u32[]{:S(2)}, u32[]{:S(2)}) %collective-permute-start.16) | collective-permute-done | bytes 262176 | tf_op jit(solution)/shard_map/ppermute | solution.py:384
  61.5 1.4 collective-permute-start.21
  62.9 0.9 collective-permute-start.22
  63.7 1.8 %collective-permute-start.10 = (bf16[8,16,1024]{2,1,0:T(8,128)(2,1)}, bf16[8,16,1024]{2,1,0:T(8,128)(2,1)}, u32[]{:S(2)}, u32[]{:S(2)}) collective-permute-start(bf16[8,16,1024]{2,1,0:T(8,128)(2,1)} %collective-permute-done.9.refs_13_), channel_id=1, source_target_pairs={{0,56},{4,60},{8,0},{12,4},{16,8},{20,12},{24,16},{28,20},{32,24},... | collective-permute-start | bytes 786440 | tf_op jit(solution)/shard_map/ppermute | solution.py:384
  67.0 4.9 %collective-permute-done.10.refs_14_ = bf16[8,16,1024]{2,1,0:T(8,128)(2,1)} collective-permute-done((bf16[8,16,1024]{2,1,0:T(8,128)(2,1)}, bf16[8,16,1024]{2,1,0:T(8,128)(2,1)}, u32[]{:S(2)}, u32[]{:S(2)}) %collective-permute-start.10) | collective-permute-done | bytes 262176 | tf_op jit(solution)/shard_map/ppermute | solution.py:384
  71.8 3.7 %collective-permute-start.13 = (bf16[9,16,1024]{2,1,0:T(8,128)(2,1)S(1)}, bf16[9,16,1024]{2,1,0:T(8,128)(2,1)S(1)}, u32[]{:S(2)}, u32[]{:S(2)}) collective-permute-start(bf16[9,16,1024]{2,1,0:T(8,128)(2,1)S(1)} %copy-done.8), channel_id=1, source_target_pairs={{0,56},{4,60},{8,0},{12,4},{16,8},{20,12},{24,16},{28,20},{32,24},... | collective-permute-start | bytes 884744 | tf_op jit(solution)/shard_map/ppermute | solution.py:384
  75.5 2.8 %collective-permute-done.7.refs_3_ = bf16[9,16,1024]{2,1,0:T(8,128)(2,1)} collective-permute-done((bf16[9,16,1024]{2,1,0:T(8,128)(2,1)}, bf16[9,16,1024]{2,1,0:T(8,128)(2,1)}, u32[]{:S(2)}, u32[]{:S(2)}) %collective-permute-start.7) | collective-permute-done | bytes 294944 | tf_op jit(solution)/shard_map/ppermute | solution.py:384
  78.3 3.2 %collective-permute-start.18 = (bf16[8,16,1024]{2,1,0:T(8,128)(2,1)}, bf16[8,16,1024]{2,1,0:T(8,128)(2,1)S(1)}, u32[]{:S(2)}, u32[]{:S(2)}) collective-permute-start(bf16[8,16,1024]{2,1,0:T(8,128)(2,1)} %collective-permute-done.10.refs_14_), channel_id=1, source_target_pairs={{0,56},{4,60},{8,0},{12,4},{16,8},{20,12},{24,16},{28,20},{32,24},... | collective-permute-start | bytes 786440 | tf_op jit(solution)/shard_map/ppermute | solution.py:384
  82.0 3.8 %collective-permute-done.18.refs_15_ = bf16[8,16,1024]{2,1,0:T(8,128)(2,1)S(1)} collective-permute-done((bf16[8,16,1024]{2,1,0:T(8,128)(2,1)}, bf16[8,16,1024]{2,1,0:T(8,128)(2,1)S(1)}, u32[]{:S(2)}, u32[]{:S(2)}) %collective-permute-start.18) | collective-permute-done | bytes 262176 | tf_op jit(solution)/shard_map/ppermute | solution.py:384
  86.5 4.0 %shard_map.86 = (bf16[2,512,512]{2,1,0:T(8,128)(2,1)S(1)}, bf16[2,512,512]{2,1,0:T(8,128)(2,1)S(1)}) custom-call(s32[1]{0:T(128)} %shard_map.83.token_ref, s32[3]{0:T(128)S(1)} %pad_add_fusion.1.place_ref, bf16[9,16,1024]{2,1,0:T(8,128)(2,1)S(1)} %copy-done.2, bf16[9,16,1024]{2,1,0:T(8,128)(2,1)S(1)} %copy-done.4, ...), custom_call_target="tpu_custom_call" | custom-call | flops 1000000 | bytes 1000000 | tf_op jit(solution)/shard_map/pallas_call | solution.py:208
  91.1 2.1 %collective-permute-done.19.refs_16_ = bf16[2,512,512]{2,1,0:T(8,128)(2,1)S(1)} collective-permute-done((bf16[2,512,512]{2,1,0:T(8,128)(2,1)S(1)}, bf16[2,512,512]{2,1,0:T(8,128)(2,1)S(1)}, u32[]{:S(2)}, u32[]{:S(2)}) %collective-permute-start.19) | collective-permute-done | bytes 1048608 | tf_op jit(solution)/shard_map/ppermute | solution.py:384
  93.3 1.5 collective-permute-done.20.refs_17_
  94.8 4.1 %shard_map.87 = (f32[512,512]{1,0:T(8,128)S(1)}, bf16[512,512]{1,0:T(8,128)(2,1)S(1)}, bf16[512,512]{1,0:T(8,128)(2,1)S(1)}, bf16[512,512]{1,0:T(8,128)(2,1)S(1)}) custom-call(s32[1]{0:T(128)} %shard_map.83.token_ref, s32[3]{0:T(128)S(1)} %pad_add_fusion.1.place_ref, bf16[9,16,1024]{2,1,0:T(8,128)(2,1)S(1)} %copy-done.2, bf16[9,16,1024]{2,1,0:T(8,128)(2,1)S(1)} %copy-done.4, ...), custom_call_target="tpu_custom_call" | custom-call | flops 1000000 | bytes 1000000 | tf_op jit(solution)/shard_map/pallas_call | solution.py:208
  99.5 1.1 collective-permute-done.22.b2_ref
  100.6 3.4 %collective-permute-start.29 = (bf16[7104,128]{1,0:T(8,128)(2,1)}, bf16[7104,128]{1,0:T(8,128)(2,1)S(1)}, u32[]{:S(2)}, u32[]{:S(2)}) collective-permute-start(bf16[7104,128]{1,0:T(8,128)(2,1)} %collective-permute-done.21.a1_ref), channel_id=1, source_target_pairs={{0,3},{3,0},{1,2},{2,1},{4,7},{7,4},{5,6},{6,5},{8,11},{11,8},{9,1... | collective-permute-start | bytes 5455880 | tf_op jit(solution)/shard_map/ppermute | solution.py:372
  104.4 2.4 %collective-permute-start.24 = (bf16[512,512]{1,0:T(8,128)(2,1)S(1)}, bf16[512,512]{1,0:T(8,128)(2,1)S(1)}, u32[]{:S(2)}, u32[]{:S(2)}) collective-permute-start(bf16[512,512]{1,0:T(8,128)(2,1)S(1)} %get-tuple-element.51), channel_id=1, source_target_pairs={{0,128},{4,132},{8,136},{12,140},{16,144},{20,148},{24,152},{28,15... | collective-permute-start | bytes 1572872 | tf_op jit(solution)/shard_map/ppermute | solution.py:384
  106.9 11.9 %collective-permute-done.23.r1_ref = bf16[512,512]{1,0:T(8,128)(2,1)S(1)} collective-permute-done((bf16[512,512]{1,0:T(8,128)(2,1)S(1)}, bf16[512,512]{1,0:T(8,128)(2,1)S(1)}, u32[]{:S(2)}, u32[]{:S(2)}) %collective-permute-start.23) | collective-permute-done | bytes 524320 | tf_op jit(solution)/shard_map/ppermute | solution.py:384
  118.8 2.1 %collective-permute-done.24.r2_ref = bf16[512,512]{1,0:T(8,128)(2,1)S(1)} collective-permute-done((bf16[512,512]{1,0:T(8,128)(2,1)S(1)}, bf16[512,512]{1,0:T(8,128)(2,1)S(1)}, u32[]{:S(2)}, u32[]{:S(2)}) %collective-permute-start.24) | collective-permute-done | bytes 524320 | tf_op jit(solution)/shard_map/ppermute | solution.py:384
  120.8 9.7 %collective-permute-done.25.r3_ref = bf16[512,512]{1,0:T(8,128)(2,1)S(1)} collective-permute-done((bf16[512,512]{1,0:T(8,128)(2,1)S(1)}, bf16[512,512]{1,0:T(8,128)(2,1)S(1)}, u32[]{:S(2)}, u32[]{:S(2)}) %collective-permute-start.25) | collective-permute-done | bytes 524320 | tf_op jit(solution)/shard_map/ppermute | solution.py:384
  130.6 1.0 shard_map.88
  131.6 1.8 %collective-permute-start.26 = (bf16[512,128]{1,0:T(8,128)(2,1)S(1)}, bf16[512,128]{1,0:T(8,128)(2,1)S(1)}, u32[]{:S(2)}, u32[]{:S(2)}) collective-permute-start(bf16[512,128]{1,0:T(8,128)(2,1)S(1)} %get-tuple-element.54), channel_id=1, source_target_pairs={{0,1},{1,2},{2,3},{3,0},{4,5},{5,6},{6,7},{7,4},{8,9},{9,10},{10,1... | collective-permute-start | bytes 393224 | tf_op jit(solution)/shard_map/ppermute | solution.py:364
  133.6 2.6 %collective-permute-start.28 = (bf16[512,128]{1,0:T(8,128)(2,1)S(1)}, bf16[512,128]{1,0:T(8,128)(2,1)S(1)}, u32[]{:S(2)}, u32[]{:S(2)}) collective-permute-start(bf16[512,128]{1,0:T(8,128)(2,1)S(1)} %get-tuple-element.56), channel_id=1, source_target_pairs={{0,3},{1,0},{2,1},{3,2},{4,7},{5,4},{6,5},{7,6},{8,11},{9,8},{10,9... | collective-permute-start | bytes 393224 | tf_op jit(solution)/shard_map/ppermute | solution.py:364
  136.3 2.0 %copy-done = bf16[14208,128]{1,0:T(8,128)(2,1)S(1)} copy-done((bf16[14208,128]{1,0:T(8,128)(2,1)S(1)}, bf16[14208,128]{1,0:T(8,128)(2,1)}, u32[]{:S(2)}) %copy-start) | copy-done | bytes 3637272
  138.3 3.7 %shard_map.89.held_ref = bf16[3,14208,128]{2,1,0:T(8,128)(2,1)S(1)} custom-call(bf16[14208,128]{1,0:T(8,128)(2,1)S(1)} %copy-done, bf16[7104,128]{1,0:T(8,128)(2,1)} %collective-permute-done.21.a1_ref, bf16[7104,128]{1,0:T(8,128)(2,1)} %collective-permute-done.2.refs_0_.a2_ref, bf16[7104,128]{1,0:T(8,128)(2,1)} %collective-permute-done.3.refs_1_.b1_ref, ...), custom_call_target="tpu_custom_call" | custom-call | flops 1000000 | bytes 1000000 | tf_op jit(solution)/shard_map/pallas_call | solution.py:292
  142.0 5.0 %collective-permute-done.26.t1_ref = bf16[512,128]{1,0:T(8,128)(2,1)S(1)} collective-permute-done((bf16[512,128]{1,0:T(8,128)(2,1)S(1)}, bf16[512,128]{1,0:T(8,128)(2,1)S(1)}, u32[]{:S(2)}, u32[]{:S(2)}) %collective-permute-start.26) | collective-permute-done | bytes 131104 | tf_op jit(solution)/shard_map/ppermute | solution.py:364
  147.0 4.0 %collective-permute-done.27.t2_ref = bf16[512,128]{1,0:T(8,128)(2,1)S(1)} collective-permute-done((bf16[512,128]{1,0:T(8,128)(2,1)S(1)}, bf16[512,128]{1,0:T(8,128)(2,1)S(1)}, u32[]{:S(2)}, u32[]{:S(2)}) %collective-permute-start.27) | collective-permute-done | bytes 131104 | tf_op jit(solution)/shard_map/ppermute | solution.py:364
  151.2 6.6 %shard_map.90 = bf16[14208,128]{1,0:T(8,128)(2,1)} custom-call(s32[4]{0:T(128)S(1)} %pad_add_fusion.order_ref, f32[512,128]{1,0:T(8,128)S(1)} %get-tuple-element.53.t0_ref, bf16[512,128]{1,0:T(8,128)(2,1)S(1)} %collective-permute-done.26.t1_ref, bf16[512,128]{1,0:T(8,128)(2,1)S(1)} %collective-permute-done.27.t2_ref, ...), custom_call_target="tpu_custom_call" | custom-call | tf_op jit(solution)/shard_map/pallas_call | solution.py:344
  (81 shorter events, 9.1 us)
Async XLA Ops:
  3.3 11.0 %collective-permute-start = (bf16[16,16,640]{2,1,0:T(8,128)(2,1)}, bf16[16,16,640]{2,1,0:T(8,128)(2,1)S(1)}, u32[]{:S(2)}, u32[]{:S(2)}) collective-permute-start(bf16[16,16,640]{2,1,0:T(8,128)(2,1)} %get-tuple-element.32), channel_id=1, source_target_pairs={{0,1},{1,2},{2,3},{3,0},{4,5},{5,6},{6,7},{7,4},{8,9},{9,10},{10,1... | collective-permute-start | bytes 983048 | tf_op jit(solution)/shard_map/ppermute | solution.py:364
  4.9 14.5 %collective-permute-start.1 = (bf16[16,16,640]{2,1,0:T(8,128)(2,1)}, bf16[16,16,640]{2,1,0:T(8,128)(2,1)S(1)}, u32[]{:S(2)}, u32[]{:S(2)}) collective-permute-start(bf16[16,16,640]{2,1,0:T(8,128)(2,1)} %get-tuple-element.33), channel_id=1, source_target_pairs={{0,3},{1,0},{2,1},{3,2},{4,7},{5,4},{6,5},{7,6},{8,11},{9,8},{10,9... | collective-permute-start | bytes 983048 | tf_op jit(solution)/shard_map/ppermute | solution.py:364
  6.6 17.5 %collective-permute-start.4 = (bf16[16,16,640]{2,1,0:T(8,128)(2,1)}, bf16[16,16,640]{2,1,0:T(8,128)(2,1)}, u32[]{:S(2)}, u32[]{:S(2)}) collective-permute-start(bf16[16,16,640]{2,1,0:T(8,128)(2,1)} %get-tuple-element.39), channel_id=1, source_target_pairs={{0,2},{1,3},{2,0},{3,1},{4,6},{5,7},{6,4},{7,5},{8,10},{9,11},{10,... | collective-permute-start | bytes 983048 | tf_op jit(solution)/shard_map/ppermute | solution.py:364
  8.6 4.1 %copy-start.21 = (f32[16,4]{0,1:T(4,128)S(1)}, f32[16,4]{0,1:T(4,128)}, u32[]{:S(2)}) copy-start(f32[16,4]{0,1:T(4,128)} %param.15) | copy-start | bytes 772
  8.6 4.3 %copy-start.22 = (s32[16,4]{0,1:T(4,128)S(1)}, s32[16,4]{0,1:T(4,128)}, u32[]{:S(2)}) copy-start(s32[16,4]{0,1:T(4,128)} %param.14) | copy-start | bytes 772
  14.3 9.3 %copy-start.16 = (bf16[16,16,640]{2,1,0:T(8,128)(2,1)}, bf16[16,16,640]{2,1,0:T(8,128)(2,1)S(1)}, u32[]{:S(2)}) copy-start(bf16[16,16,640]{2,1,0:T(8,128)(2,1)S(1)} %collective-permute-done.refs_0_.r1_ref) | copy-start | bytes 983044
  19.5 4.1 %copy-start.18 = (bf16[16,16,640]{2,1,0:T(8,128)(2,1)}, bf16[16,16,640]{2,1,0:T(8,128)(2,1)S(1)}, u32[]{:S(2)}) copy-start(bf16[16,16,640]{2,1,0:T(8,128)(2,1)S(1)} %collective-permute-done.1.refs_1_.r3_ref) | copy-start | bytes 983044
  19.5 46.0 %collective-permute-start.2 = (bf16[7104,128]{1,0:T(8,128)(2,1)}, bf16[7104,128]{1,0:T(8,128)(2,1)}, u32[]{:S(2)}, u32[]{:S(2)}) collective-permute-start(bf16[7104,128]{1,0:T(8,128)(2,1)} %get-tuple-element.34), channel_id=1, source_target_pairs={{0,1},{1,0},{2,3},{3,2},{4,5},{5,4},{6,7},{7,6},{8,9},{9,8},{10,11... | collective-permute-start | bytes 5455880 | tf_op jit(solution)/shard_map/ppermute | solution.py:368
  19.5 46.3 %collective-permute-start.3 = (bf16[7104,128]{1,0:T(8,128)(2,1)}, bf16[7104,128]{1,0:T(8,128)(2,1)}, u32[]{:S(2)}, u32[]{:S(2)}) collective-permute-start(bf16[7104,128]{1,0:T(8,128)(2,1)} %get-tuple-element.35), channel_id=1, source_target_pairs={{0,3},{3,0},{1,2},{2,1},{4,7},{7,4},{5,6},{6,5},{8,11},{11,8},{9,1... | collective-permute-start | bytes 5455880 | tf_op jit(solution)/shard_map/ppermute | solution.py:372
  23.6 1.0 copy-start.15
  23.6 1.0 copy-start.20
  24.6 1.0 copy-start.17
  25.6 1.0 copy-start.19
  28.3 9.8 %collective-permute-start.8 = (bf16[8,16,1024]{2,1,0:T(8,128)(2,1)S(1)}, bf16[8,16,1024]{2,1,0:T(8,128)(2,1)S(1)}, u32[]{:S(2)}, u32[]{:S(2)}) collective-permute-start(bf16[8,16,1024]{2,1,0:T(8,128)(2,1)S(1)} %get-tuple-element.42.refs_8_), channel_id=1, source_target_pairs={{0,56},{4,60},{8,0},{12,4},{16,8},{20,12},{24,16},{28,20},{32,24},... | collective-permute-start | bytes 786440 | tf_op jit(solution)/shard_map/ppermute | solution.py:384
  34.2 9.3 %collective-permute-start.15 = (bf16[8,16,1024]{2,1,0:T(8,128)(2,1)S(1)}, bf16[8,16,1024]{2,1,0:T(8,128)(2,1)S(1)}, u32[]{:S(2)}, u32[]{:S(2)}) collective-permute-start(bf16[8,16,1024]{2,1,0:T(8,128)(2,1)S(1)} %get-tuple-element.42.refs_8_), channel_id=1, source_target_pairs={{0,8},{4,12},{8,16},{12,20},{16,24},{20,28},{24,32},{28,36},{32,40... | collective-permute-start | bytes 786440 | tf_op jit(solution)/shard_map/ppermute | solution.py:384
  34.9 12.0 %collective-permute-start.5 = (bf16[9,16,1024]{2,1,0:T(8,128)(2,1)S(1)}, bf16[9,16,1024]{2,1,0:T(8,128)(2,1)S(1)}, u32[]{:S(2)}, u32[]{:S(2)}) collective-permute-start(bf16[9,16,1024]{2,1,0:T(8,128)(2,1)S(1)} %get-tuple-element.41.refs_0_), channel_id=1, source_target_pairs={{0,8},{4,12},{8,16},{12,20},{16,24},{20,28},{24,32},{28,36},{32,40... | collective-permute-start | bytes 884744 | tf_op jit(solution)/shard_map/ppermute | solution.py:384
  38.1 10.0 %collective-permute-start.11 = (bf16[9,16,1024]{2,1,0:T(8,128)(2,1)S(1)}, bf16[9,16,1024]{2,1,0:T(8,128)(2,1)S(1)}, u32[]{:S(2)}, u32[]{:S(2)}) collective-permute-start(bf16[9,16,1024]{2,1,0:T(8,128)(2,1)S(1)} %get-tuple-element.41.refs_0_), channel_id=1, source_target_pairs={{0,56},{4,60},{8,0},{12,4},{16,8},{20,12},{24,16},{28,20},{32,24},... | collective-permute-start | bytes 884744 | tf_op jit(solution)/shard_map/ppermute | solution.py:384
  43.5 9.7 %collective-permute-start.9 = (bf16[8,16,1024]{2,1,0:T(8,128)(2,1)S(1)}, bf16[8,16,1024]{2,1,0:T(8,128)(2,1)}, u32[]{:S(2)}, u32[]{:S(2)}) collective-permute-start(bf16[8,16,1024]{2,1,0:T(8,128)(2,1)S(1)} %collective-permute-done.8.refs_12_), channel_id=1, source_target_pairs={{0,56},{4,60},{8,0},{12,4},{16,8},{20,12},{24,16},{28,20},{32,24},... | collective-permute-start | bytes 786440 | tf_op jit(solution)/shard_map/ppermute | solution.py:384
  46.9 16.0 %collective-permute-start.6 = (bf16[9,16,1024]{2,1,0:T(8,128)(2,1)S(1)}, bf16[9,16,1024]{2,1,0:T(8,128)(2,1)}, u32[]{:S(2)}, u32[]{:S(2)}) collective-permute-start(bf16[9,16,1024]{2,1,0:T(8,128)(2,1)S(1)} %collective-permute-done.5.refs_1_), channel_id=1, source_target_pairs={{0,8},{4,12},{8,16},{12,20},{16,24},{20,28},{24,32},{28,36},{32,40... | collective-permute-start | bytes 884744 | tf_op jit(solution)/shard_map/ppermute | solution.py:384
  48.1 15.6 %collective-permute-start.12 = (bf16[9,16,1024]{2,1,0:T(8,128)(2,1)S(1)}, bf16[9,16,1024]{2,1,0:T(8,128)(2,1)S(1)}, u32[]{:S(2)}, u32[]{:S(2)}) collective-permute-start(bf16[9,16,1024]{2,1,0:T(8,128)(2,1)S(1)} %collective-permute-done.11.refs_4_), channel_id=1, source_target_pairs={{0,56},{4,60},{8,0},{12,4},{16,8},{20,12},{24,16},{28,20},{32,24},... | collective-permute-start | bytes 884744 | tf_op jit(solution)/shard_map/ppermute | solution.py:384
  53.3 8.3 %collective-permute-start.16 = (bf16[8,16,1024]{2,1,0:T(8,128)(2,1)S(1)}, bf16[8,16,1024]{2,1,0:T(8,128)(2,1)}, u32[]{:S(2)}, u32[]{:S(2)}) collective-permute-start(bf16[8,16,1024]{2,1,0:T(8,128)(2,1)S(1)} %collective-permute-done.15.refs_9_), channel_id=1, source_target_pairs={{0,8},{4,12},{8,16},{12,20},{16,24},{20,28},{24,32},{28,36},{32,40... | collective-permute-start | bytes 786440 | tf_op jit(solution)/shard_map/ppermute | solution.py:384
  61.5 37.9 %collective-permute-start.21 = (bf16[7104,128]{1,0:T(8,128)(2,1)}, bf16[7104,128]{1,0:T(8,128)(2,1)}, u32[]{:S(2)}, u32[]{:S(2)}) collective-permute-start(bf16[7104,128]{1,0:T(8,128)(2,1)} %get-tuple-element.35), channel_id=1, source_target_pairs={{0,1},{1,0},{2,3},{3,2},{4,5},{5,4},{6,7},{7,6},{8,9},{9,8},{10,11... | collective-permute-start | bytes 5455880 | tf_op jit(solution)/shard_map/ppermute | solution.py:368
  62.9 37.7 %collective-permute-start.22 = (bf16[7104,128]{1,0:T(8,128)(2,1)}, bf16[7104,128]{1,0:T(8,128)(2,1)}, u32[]{:S(2)}, u32[]{:S(2)}) collective-permute-start(bf16[7104,128]{1,0:T(8,128)(2,1)} %get-tuple-element.34), channel_id=1, source_target_pairs={{0,3},{3,0},{1,2},{2,1},{4,7},{7,4},{5,6},{6,5},{8,11},{11,8},{9,1... | collective-permute-start | bytes 5455880 | tf_op jit(solution)/shard_map/ppermute | solution.py:372
  63.7 2.0 %copy-start.7 = (bf16[9,16,1024]{2,1,0:T(8,128)(2,1)}, bf16[9,16,1024]{2,1,0:T(8,128)(2,1)S(1)}, u32[]{:S(2)}) copy-start(bf16[9,16,1024]{2,1,0:T(8,128)(2,1)S(1)} %collective-permute-done.12.refs_5_) | copy-start | bytes 884740
  63.7 8.1 %collective-permute-start.10 = (bf16[8,16,1024]{2,1,0:T(8,128)(2,1)}, bf16[8,16,1024]{2,1,0:T(8,128)(2,1)}, u32[]{:S(2)}, u32[]{:S(2)}) collective-permute-start(bf16[8,16,1024]{2,1,0:T(8,128)(2,1)} %collective-permute-done.9.refs_13_), channel_id=1, source_target_pairs={{0,56},{4,60},{8,0},{12,4},{16,8},{20,12},{24,16},{28,20},{32,24},... | collective-permute-start | bytes 786440 | tf_op jit(solution)/shard_map/ppermute | solution.py:384
  65.5 12.8 %collective-permute-start.17 = (bf16[8,16,1024]{2,1,0:T(8,128)(2,1)}, bf16[8,16,1024]{2,1,0:T(8,128)(2,1)}, u32[]{:S(2)}, u32[]{:S(2)}) collective-permute-start(bf16[8,16,1024]{2,1,0:T(8,128)(2,1)} %collective-permute-done.16.refs_10_), channel_id=1, source_target_pairs={{0,8},{4,12},{8,16},{12,20},{16,24},{20,28},{24,32},{28,36},{32,40... | collective-permute-start | bytes 786440 | tf_op jit(solution)/shard_map/ppermute | solution.py:384
  65.8 12.5 %collective-permute-start.7 = (bf16[9,16,1024]{2,1,0:T(8,128)(2,1)}, bf16[9,16,1024]{2,1,0:T(8,128)(2,1)}, u32[]{:S(2)}, u32[]{:S(2)}) collective-permute-start(bf16[9,16,1024]{2,1,0:T(8,128)(2,1)} %collective-permute-done.6.refs_2_), channel_id=1, source_target_pairs={{0,8},{4,12},{8,16},{12,20},{16,24},{20,28},{24,32},{28,36},{32,40... | collective-permute-start | bytes 884744 | tf_op jit(solution)/shard_map/ppermute | solution.py:384
  66.4 5.5 %copy-start.8 = (bf16[9,16,1024]{2,1,0:T(8,128)(2,1)S(1)}, bf16[9,16,1024]{2,1,0:T(8,128)(2,1)}, u32[]{:S(2)}) copy-start(bf16[9,16,1024]{2,1,0:T(8,128)(2,1)} %copy-done.7) | copy-start | bytes 884740
  66.4 20.1 %copy-start.2 = (bf16[9,16,1024]{2,1,0:T(8,128)(2,1)S(1)}, bf16[9,16,1024]{2,1,0:T(8,128)(2,1)}, u32[]{:S(2)}) copy-start(bf16[9,16,1024]{2,1,0:T(8,128)(2,1)} %copy-done.1) | copy-start | bytes 884740
  66.4 20.1 %copy-start.4 = (bf16[9,16,1024]{2,1,0:T(8,128)(2,1)S(1)}, bf16[9,16,1024]{2,1,0:T(8,128)(2,1)}, u32[]{:S(2)}) copy-start(bf16[9,16,1024]{2,1,0:T(8,128)(2,1)} %copy-done.3) | copy-start | bytes 884740
  66.4 20.1 %copy-start.6 = (bf16[9,16,1024]{2,1,0:T(8,128)(2,1)S(1)}, bf16[9,16,1024]{2,1,0:T(8,128)(2,1)}, u32[]{:S(2)}) copy-start(bf16[9,16,1024]{2,1,0:T(8,128)(2,1)} %copy-done.5) | copy-start | bytes 884740
  66.4 20.1 %copy-start.10 = (bf16[8,16,1024]{2,1,0:T(8,128)(2,1)S(1)}, bf16[8,16,1024]{2,1,0:T(8,128)(2,1)}, u32[]{:S(2)}) copy-start(bf16[8,16,1024]{2,1,0:T(8,128)(2,1)} %copy-done.9) | copy-start | bytes 786436
  66.4 20.1 %copy-start.12 = (bf16[8,16,1024]{2,1,0:T(8,128)(2,1)S(1)}, bf16[8,16,1024]{2,1,0:T(8,128)(2,1)}, u32[]{:S(2)}) copy-start(bf16[8,16,1024]{2,1,0:T(8,128)(2,1)} %copy-done.11) | copy-start | bytes 786436
  66.4 20.1 %copy-start.14 = (bf16[8,16,1024]{2,1,0:T(8,128)(2,1)S(1)}, bf16[8,16,1024]{2,1,0:T(8,128)(2,1)}, u32[]{:S(2)}) copy-start(bf16[8,16,1024]{2,1,0:T(8,128)(2,1)} %copy-done.13) | copy-start | bytes 786436
  71.8 10.1 %collective-permute-start.13 = (bf16[9,16,1024]{2,1,0:T(8,128)(2,1)S(1)}, bf16[9,16,1024]{2,1,0:T(8,128)(2,1)S(1)}, u32[]{:S(2)}, u32[]{:S(2)}) collective-permute-start(bf16[9,16,1024]{2,1,0:T(8,128)(2,1)S(1)} %copy-done.8), channel_id=1, source_target_pairs={{0,56},{4,60},{8,0},{12,4},{16,8},{20,12},{24,16},{28,20},{32,24},... | collective-permute-start | bytes 884744 | tf_op jit(solution)/shard_map/ppermute | solution.py:384
  78.3 8.1 %collective-permute-start.14 = (bf16[9,16,1024]{2,1,0:T(8,128)(2,1)}, bf16[9,16,1024]{2,1,0:T(8,128)(2,1)S(1)}, u32[]{:S(2)}, u32[]{:S(2)}) collective-permute-start(bf16[9,16,1024]{2,1,0:T(8,128)(2,1)} %collective-permute-done.7.refs_3_), channel_id=1, source_target_pairs={{0,8},{4,12},{8,16},{12,20},{16,24},{20,28},{24,32},{28,36},{32,40... | collective-permute-start | bytes 884744 | tf_op jit(solution)/shard_map/ppermute | solution.py:384
  78.3 7.4 %collective-permute-start.18 = (bf16[8,16,1024]{2,1,0:T(8,128)(2,1)}, bf16[8,16,1024]{2,1,0:T(8,128)(2,1)S(1)}, u32[]{:S(2)}, u32[]{:S(2)}) collective-permute-start(bf16[8,16,1024]{2,1,0:T(8,128)(2,1)} %collective-permute-done.10.refs_14_), channel_id=1, source_target_pairs={{0,56},{4,60},{8,0},{12,4},{16,8},{20,12},{24,16},{28,20},{32,24},... | collective-permute-start | bytes 786440 | tf_op jit(solution)/shard_map/ppermute | solution.py:384
  90.5 2.7 %collective-permute-start.19 = (bf16[2,512,512]{2,1,0:T(8,128)(2,1)S(1)}, bf16[2,512,512]{2,1,0:T(8,128)(2,1)S(1)}, u32[]{:S(2)}, u32[]{:S(2)}) collective-permute-start(bf16[2,512,512]{2,1,0:T(8,128)(2,1)S(1)} %get-tuple-element.46), channel_id=1, source_target_pairs={{0,4},{4,0},{8,12},{12,8},{16,20},{20,16},{24,28},{28,24},{32,36},... | collective-permute-start | bytes 3145736 | tf_op jit(solution)/shard_map/ppermute | solution.py:384
  90.6 4.1 %collective-permute-start.20 = (bf16[2,512,512]{2,1,0:T(8,128)(2,1)S(1)}, bf16[2,512,512]{2,1,0:T(8,128)(2,1)S(1)}, u32[]{:S(2)}, u32[]{:S(2)}) collective-permute-start(bf16[2,512,512]{2,1,0:T(8,128)(2,1)S(1)} %get-tuple-element.47), channel_id=1, source_target_pairs={{0,4},{4,0},{8,12},{12,8},{16,20},{20,16},{24,28},{28,24},{32,36},... | collective-permute-start | bytes 3145736 | tf_op jit(solution)/shard_map/ppermute | solution.py:384
  100.6 50.7 %collective-permute-start.29 = (bf16[7104,128]{1,0:T(8,128)(2,1)}, bf16[7104,128]{1,0:T(8,128)(2,1)S(1)}, u32[]{:S(2)}, u32[]{:S(2)}) collective-permute-start(bf16[7104,128]{1,0:T(8,128)(2,1)} %collective-permute-done.21.a1_ref), channel_id=1, source_target_pairs={{0,3},{3,0},{1,2},{2,1},{4,7},{7,4},{5,6},{6,5},{8,11},{11,8},{9,1... | collective-permute-start | bytes 5455880 | tf_op jit(solution)/shard_map/ppermute | solution.py:372
  104.0 47.3 %collective-permute-start.30 = (bf16[7104,128]{1,0:T(8,128)(2,1)}, bf16[7104,128]{1,0:T(8,128)(2,1)}, u32[]{:S(2)}, u32[]{:S(2)}) collective-permute-start(bf16[7104,128]{1,0:T(8,128)(2,1)} %collective-permute-done.22.b2_ref), channel_id=1, source_target_pairs={{0,1},{1,0},{2,3},{3,2},{4,5},{5,4},{6,7},{7,6},{8,9},{9,8},{10,11... | collective-permute-start | bytes 5455880 | tf_op jit(solution)/shard_map/ppermute | solution.py:368
  104.0 14.8 %collective-permute-start.23 = (bf16[512,512]{1,0:T(8,128)(2,1)S(1)}, bf16[512,512]{1,0:T(8,128)(2,1)S(1)}, u32[]{:S(2)}, u32[]{:S(2)}) collective-permute-start(bf16[512,512]{1,0:T(8,128)(2,1)S(1)} %get-tuple-element.50), channel_id=1, source_target_pairs={{0,64},{4,68},{8,72},{12,76},{16,80},{20,84},{24,88},{28,92},{32,9... | collective-permute-start | bytes 1572872 | tf_op jit(solution)/shard_map/ppermute | solution.py:384
  104.4 16.4 %collective-permute-start.24 = (bf16[512,512]{1,0:T(8,128)(2,1)S(1)}, bf16[512,512]{1,0:T(8,128)(2,1)S(1)}, u32[]{:S(2)}, u32[]{:S(2)}) collective-permute-start(bf16[512,512]{1,0:T(8,128)(2,1)S(1)} %get-tuple-element.51), channel_id=1, source_target_pairs={{0,128},{4,132},{8,136},{12,140},{16,144},{20,148},{24,152},{28,15... | collective-permute-start | bytes 1572872 | tf_op jit(solution)/shard_map/ppermute | solution.py:384
  106.9 23.7 %collective-permute-start.25 = (bf16[512,512]{1,0:T(8,128)(2,1)S(1)}, bf16[512,512]{1,0:T(8,128)(2,1)S(1)}, u32[]{:S(2)}, u32[]{:S(2)}) collective-permute-start(bf16[512,512]{1,0:T(8,128)(2,1)S(1)} %get-tuple-element.52), channel_id=1, source_target_pairs={{0,192},{4,196},{8,200},{12,204},{16,208},{20,212},{24,216},{28,22... | collective-permute-start | bytes 1572872 | tf_op jit(solution)/shard_map/ppermute | solution.py:384
  131.6 15.4 %collective-permute-start.26 = (bf16[512,128]{1,0:T(8,128)(2,1)S(1)}, bf16[512,128]{1,0:T(8,128)(2,1)S(1)}, u32[]{:S(2)}, u32[]{:S(2)}) collective-permute-start(bf16[512,128]{1,0:T(8,128)(2,1)S(1)} %get-tuple-element.54), channel_id=1, source_target_pairs={{0,1},{1,2},{2,3},{3,0},{4,5},{5,6},{6,7},{7,4},{8,9},{9,10},{10,1... | collective-permute-start | bytes 393224 | tf_op jit(solution)/shard_map/ppermute | solution.py:364
  133.4 17.6 %collective-permute-start.27 = (bf16[512,128]{1,0:T(8,128)(2,1)S(1)}, bf16[512,128]{1,0:T(8,128)(2,1)S(1)}, u32[]{:S(2)}, u32[]{:S(2)}) collective-permute-start(bf16[512,128]{1,0:T(8,128)(2,1)S(1)} %get-tuple-element.55), channel_id=1, source_target_pairs={{0,2},{1,3},{2,0},{3,1},{4,6},{5,7},{6,4},{7,5},{8,10},{9,11},{10,... | collective-permute-start | bytes 393224 | tf_op jit(solution)/shard_map/ppermute | solution.py:364
  133.6 17.6 %collective-permute-start.28 = (bf16[512,128]{1,0:T(8,128)(2,1)S(1)}, bf16[512,128]{1,0:T(8,128)(2,1)S(1)}, u32[]{:S(2)}, u32[]{:S(2)}) collective-permute-start(bf16[512,128]{1,0:T(8,128)(2,1)S(1)} %get-tuple-element.56), channel_id=1, source_target_pairs={{0,3},{1,0},{2,1},{3,2},{4,7},{5,4},{6,5},{7,6},{8,11},{9,8},{10,9... | collective-permute-start | bytes 393224 | tf_op jit(solution)/shard_map/ppermute | solution.py:364
  136.3 2.0 %copy-start = (bf16[14208,128]{1,0:T(8,128)(2,1)S(1)}, bf16[14208,128]{1,0:T(8,128)(2,1)}, u32[]{:S(2)}) copy-start(bf16[14208,128]{1,0:T(8,128)(2,1)} %own_ref.1) | copy-start | bytes 10911748
  (6 other events, 4.3 us)

commit v7 on v6

--- a/solution.py
+++ b/solution.py
@@ -417,7 +417,7 @@
 
     half = rows // 2
     early = arrived(m1, m3)
-    m1, m3, low, high = lax.optimization_barrier((m1, m3, ensemble[:half], ensemble[half:]))
+    m1, low, high = lax.optimization_barrier((m1, ensemble[:half], ensemble[half:]))
     a2, b1 = swap_a(high), swap_b(low)
     a1, b2 = swap_a(low), swap_b(high)
 

time: 159 us -> 156 us (0.981)
  waiting for transfers between devices: 72.4 us -> 67.6 us
    ppermute x6, waiting for transfers between devices: 15.2 us -> 10.2 us  [shift(): lax.ppermute(x, 'mem', [(i, (i + d) % GROUPS) for i in range(GROUPS)])]
  transfers between devices with their start and end apart: 31 -> 31, of which waited for: 23 -> 20; matrix products, arithmetic and copies ran while one was open for 3% -> 3% of each run, Pallas kernels for 10% -> 10%
where the time goes in v7:
time: 156 us; the launch traced here: 155 us
  waiting for transfers between devices  67.6 us (43%)
  starting transfers between devices  47.5 us (30%)
  Pallas kernels  25.5 us (16%)
  local copies, waits for them, and re-layouts  14 us (9%)
    ppermute x19, waiting for transfers between devices, move(): return lax.ppermute(x, 'tile', pairs)  55.4 us
    ppermute x19, starting transfers between devices, move(): return lax.ppermute(x, 'tile', pairs)  25.9 us
    ppermute x6, waiting for transfers between devices, shift(): lax.ppermute(x, 'mem', [(i, (i + d) % GROUPS) for i in range(GROUPS)])  10.2 us
    ppermute x6, starting transfers between devices, shift(): lax.ppermute(x, 'mem', [(i, (i + d) % GROUPS) for i in range(GROUPS)])  10.1 us
    unnamed x48, local copies, waits for them, and re-layouts  9.67 us
    ppermute x3, starting transfers between devices, swap_b(): return lax.ppermute(x, 'mem', [(0, 3), (3, 0), (1, 2), (2, 1)])  9.47 us
    pallas_call x2, Pallas kernels, sums(): pl.pallas_call(functools.partial(sums_kernel, same), in_specs=[pl.BlockSp...  8.09 us
    pallas_call x1, Pallas kernels, update(): pl.pallas_call(update_kernel, in_specs=[pl.BlockSpec(memory_space=pltpu.S...  6.63 us
  transfers between devices with their start and end apart: 31, of which 20 were waited for; matrix products, arithmetic and copies ran while one was open for 3% of the time, Pallas kernels for 10%

profile of v7, /device:TPU:6, one launch (start us, length us, event | category | flops | bytes accessed | tf_op | source)
XLA Modules:
  0.0 155.5 jit_solution(15725686338197097918)
XLA Ops:
  0.0 3.3 %shard_map.82 = (f32[16,16,512]{2,1,0:T(8,128)}, bf16[16,16,128]{2,1,0:T(8,128)(2,1)}, bf16[16,16,640]{2,1,0:T(8,128)(2,1)}, bf16[16,16,640]{2,1,0:T(8,128)(2,1)}, bf16[16,16,640]{2,1,0:T(8,128)(2,1)}) custom-call(s32[1]{0:T(128)} %bitcast.q_ref, bf16[16,64,128]{2,1,0:T(8,128)(2,1)} %obs_ref.1, bf16[16,512,128]{2,1,0:T(8,128)(2,1)} %inv_ref.1, ...), custom_call_target="tpu_custom_call" | custom-call | tf_op jit(solution)/shard_map/pallas_call | solution.py:57
  3.3 1.6 %collective-permute-start = (bf16[16,16,640]{2,1,0:T(8,128)(2,1)}, bf16[16,16,640]{2,1,0:T(8,128)(2,1)S(1)}, u32[]{:S(2)}, u32[]{:S(2)}) collective-permute-start(bf16[16,16,640]{2,1,0:T(8,128)(2,1)} %get-tuple-element.31), channel_id=1, source_target_pairs={{0,1},{1,2},{2,3},{3,0},{4,5},{5,6},{6,7},{7,4},{8,9},{9,10},{10,1... | collective-permute-start | bytes 983048 | tf_op jit(solution)/shard_map/ppermute | solution.py:364
  4.9 1.7 %collective-permute-start.3 = (bf16[16,16,640]{2,1,0:T(8,128)(2,1)}, bf16[16,16,640]{2,1,0:T(8,128)(2,1)S(1)}, u32[]{:S(2)}, u32[]{:S(2)}) collective-permute-start(bf16[16,16,640]{2,1,0:T(8,128)(2,1)} %get-tuple-element.34), channel_id=1, source_target_pairs={{0,3},{1,0},{2,1},{3,2},{4,7},{5,4},{6,5},{7,6},{8,11},{9,8},{10,9... | collective-permute-start | bytes 983048 | tf_op jit(solution)/shard_map/ppermute | solution.py:364
  6.6 2.0 %collective-permute-start.4 = (bf16[16,16,640]{2,1,0:T(8,128)(2,1)}, bf16[16,16,640]{2,1,0:T(8,128)(2,1)}, u32[]{:S(2)}, u32[]{:S(2)}) collective-permute-start(bf16[16,16,640]{2,1,0:T(8,128)(2,1)} %get-tuple-element.38), channel_id=1, source_target_pairs={{0,2},{1,3},{2,0},{3,1},{4,6},{5,7},{6,4},{7,5},{8,10},{9,11},{10,... | collective-permute-start | bytes 983048 | tf_op jit(solution)/shard_map/ppermute | solution.py:364
  8.6 4.1 %fusion.3 = (bf16[7104,128]{1,0:T(8,128)(2,1)}, bf16[7104,128]{1,0:T(8,128)(2,1)}) fusion(bf16[14208,128]{1,0:T(8,128)(2,1)} %own_ref.1), kind=kLoop, calls=%fused_computation.17 | loop fusion | bytes 7274496 | tf_op jit(solution)/shard_map/slice | solution.py:420
  13.5 0.8 collective-permute-done.refs_0_.r1_ref
  14.3 1.4 collective-permute-start.1
  15.7 7.0 %collective-permute-start.2 = (bf16[7104,128]{1,0:T(8,128)(2,1)}, bf16[7104,128]{1,0:T(8,128)(2,1)}, u32[]{:S(2)}, u32[]{:S(2)}) collective-permute-start(bf16[7104,128]{1,0:T(8,128)(2,1)} %get-tuple-element.33), channel_id=1, source_target_pairs={{0,3},{3,0},{1,2},{2,1},{4,7},{7,4},{5,6},{6,5},{8,11},{11,8},{9,1... | collective-permute-start | bytes 5455880 | tf_op jit(solution)/shard_map/ppermute | solution.py:372
  22.7 0.7 copy-done.18
  24.5 1.0 copy-done.17
  25.5 1.0 copy-done.19
  26.4 1.7 %shard_map.85 = (bf16[9,16,1024]{2,1,0:T(8,128)(2,1)S(1)}, bf16[8,16,1024]{2,1,0:T(8,128)(2,1)S(1)}) custom-call(s32[1]{0:T(128)} %bitcast.q_ref, s32[1]{0:T(128)} %shard_map.84.early_ref, f32[1,128]{1,0:T(1,128)S(1)} %bitcast.10, f32[1,128]{1,0:T(1,128)S(1)} %bitcast.9, f32[16,16,512]{2,1,0:T(8,128)S(1)} %copy-done.15, bf16[16,16,128]{2,1,0:T(8,128)(2,1)S(1)} %copy-done.20, ...), custom_call_target="tpu_custom_call" | custom-call | flops 1000000 | bytes 1000000 | tf_op jit(solution)/shard_map/pallas_call | solution.py:120
  28.2 5.9 %collective-permute-start.8 = (bf16[8,16,1024]{2,1,0:T(8,128)(2,1)S(1)}, bf16[8,16,1024]{2,1,0:T(8,128)(2,1)S(1)}, u32[]{:S(2)}, u32[]{:S(2)}) collective-permute-start(bf16[8,16,1024]{2,1,0:T(8,128)(2,1)S(1)} %get-tuple-element.40.refs_8_), channel_id=1, source_target_pairs={{0,56},{4,60},{8,0},{12,4},{16,8},{20,12},{24,16},{28,20},{32,24},... | collective-permute-start | bytes 786440 | tf_op jit(solution)/shard_map/ppermute | solution.py:384
  34.8 3.2 %collective-permute-done.8.refs_12_ = bf16[8,16,1024]{2,1,0:T(8,128)(2,1)S(1)} collective-permute-done((bf16[8,16,1024]{2,1,0:T(8,128)(2,1)S(1)}, bf16[8,16,1024]{2,1,0:T(8,128)(2,1)S(1)}, u32[]{:S(2)}, u32[]{:S(2)}) %collective-permute-start.8) | collective-permute-done | bytes 262176 | tf_op jit(solution)/shard_map/ppermute | solution.py:384
  38.0 3.7 %collective-permute-start.11 = (bf16[9,16,1024]{2,1,0:T(8,128)(2,1)S(1)}, bf16[9,16,1024]{2,1,0:T(8,128)(2,1)S(1)}, u32[]{:S(2)}, u32[]{:S(2)}) collective-permute-start(bf16[9,16,1024]{2,1,0:T(8,128)(2,1)S(1)} %get-tuple-element.39.refs_0_), channel_id=1, source_target_pairs={{0,56},{4,60},{8,0},{12,4},{16,8},{20,12},{24,16},{28,20},{32,24},... | collective-permute-start | bytes 884744 | tf_op jit(solution)/shard_map/ppermute | solution.py:384
  42.4 1.1 collective-permute-done.15.refs_9_
  44.2 2.6 %collective-permute-done.5.refs_1_ = bf16[9,16,1024]{2,1,0:T(8,128)(2,1)S(1)} collective-permute-done((bf16[9,16,1024]{2,1,0:T(8,128)(2,1)S(1)}, bf16[9,16,1024]{2,1,0:T(8,128)(2,1)S(1)}, u32[]{:S(2)}, u32[]{:S(2)}) %collective-permute-start.5) | collective-permute-done | bytes 294944 | tf_op jit(solution)/shard_map/ppermute | solution.py:384
  48.0 3.7 %collective-permute-start.12 = (bf16[9,16,1024]{2,1,0:T(8,128)(2,1)S(1)}, bf16[9,16,1024]{2,1,0:T(8,128)(2,1)S(1)}, u32[]{:S(2)}, u32[]{:S(2)}) collective-permute-start(bf16[9,16,1024]{2,1,0:T(8,128)(2,1)S(1)} %collective-permute-done.11.refs_4_), channel_id=1, source_target_pairs={{0,56},{4,60},{8,0},{12,4},{16,8},{20,12},{24,16},{28,20},{32,24},... | collective-permute-start | bytes 884744 | tf_op jit(solution)/shard_map/ppermute | solution.py:384
  51.7 0.7 copy-done.5
  52.4 0.8 collective-permute-done.9.refs_13_
  54.0 7.5 %collective-permute-done.16.refs_10_ = bf16[8,16,1024]{2,1,0:T(8,128)(2,1)} collective-permute-done((bf16[8,16,1024]{2,1,0:T(8,128)(2,1)S(1)}, bf16[8,16,1024]{2,1,0:T(8,128)(2,1)}, u32[]{:S(2)}, u32[]{:S(2)}) %collective-permute-start.16) | collective-permute-done | bytes 262176 | tf_op jit(solution)/shard_map/ppermute | solution.py:384
  62.7 2.0 %collective-permute-start.10 = (bf16[8,16,1024]{2,1,0:T(8,128)(2,1)}, bf16[8,16,1024]{2,1,0:T(8,128)(2,1)}, u32[]{:S(2)}, u32[]{:S(2)}) collective-permute-start(bf16[8,16,1024]{2,1,0:T(8,128)(2,1)} %collective-permute-done.9.refs_13_), channel_id=1, source_target_pairs={{0,56},{4,60},{8,0},{12,4},{16,8},{20,12},{24,16},{28,20},{32,24},... | collective-permute-start | bytes 786440 | tf_op jit(solution)/shard_map/ppermute | solution.py:384
  64.8 1.0 collective-permute-start.7
  66.3 5.8 %collective-permute-done.10.refs_14_ = bf16[8,16,1024]{2,1,0:T(8,128)(2,1)} collective-permute-done((bf16[8,16,1024]{2,1,0:T(8,128)(2,1)}, bf16[8,16,1024]{2,1,0:T(8,128)(2,1)}, u32[]{:S(2)}, u32[]{:S(2)}) %collective-permute-start.10) | collective-permute-done | bytes 262176 | tf_op jit(solution)/shard_map/ppermute | solution.py:384
  72.1 2.9 %collective-permute-start.13 = (bf16[9,16,1024]{2,1,0:T(8,128)(2,1)S(1)}, bf16[9,16,1024]{2,1,0:T(8,128)(2,1)S(1)}, u32[]{:S(2)}, u32[]{:S(2)}) collective-permute-start(bf16[9,16,1024]{2,1,0:T(8,128)(2,1)S(1)} %copy-done.8), channel_id=1, source_target_pairs={{0,56},{4,60},{8,0},{12,4},{16,8},{20,12},{24,16},{28,20},{32,24},... | collective-permute-start | bytes 884744 | tf_op jit(solution)/shard_map/ppermute | solution.py:384
  75.0 3.1 %collective-permute-done.7.refs_3_ = bf16[9,16,1024]{2,1,0:T(8,128)(2,1)} collective-permute-done((bf16[9,16,1024]{2,1,0:T(8,128)(2,1)}, bf16[9,16,1024]{2,1,0:T(8,128)(2,1)}, u32[]{:S(2)}, u32[]{:S(2)}) %collective-permute-start.7) | collective-permute-done | bytes 294944 | tf_op jit(solution)/shard_map/ppermute | solution.py:384
  78.1 3.2 %collective-permute-start.18 = (bf16[8,16,1024]{2,1,0:T(8,128)(2,1)}, bf16[8,16,1024]{2,1,0:T(8,128)(2,1)S(1)}, u32[]{:S(2)}, u32[]{:S(2)}) collective-permute-start(bf16[8,16,1024]{2,1,0:T(8,128)(2,1)} %collective-permute-done.10.refs_14_), channel_id=1, source_target_pairs={{0,56},{4,60},{8,0},{12,4},{16,8},{20,12},{24,16},{28,20},{32,24},... | collective-permute-start | bytes 786440 | tf_op jit(solution)/shard_map/ppermute | solution.py:384
  81.4 4.1 %collective-permute-done.18.refs_15_ = bf16[8,16,1024]{2,1,0:T(8,128)(2,1)S(1)} collective-permute-done((bf16[8,16,1024]{2,1,0:T(8,128)(2,1)}, bf16[8,16,1024]{2,1,0:T(8,128)(2,1)S(1)}, u32[]{:S(2)}, u32[]{:S(2)}) %collective-permute-start.18) | collective-permute-done | bytes 262176 | tf_op jit(solution)/shard_map/ppermute | solution.py:384
  86.2 4.0 %shard_map.86 = (bf16[2,512,512]{2,1,0:T(8,128)(2,1)S(1)}, bf16[2,512,512]{2,1,0:T(8,128)(2,1)S(1)}) custom-call(s32[1]{0:T(128)} %shard_map.83.token_ref, s32[3]{0:T(128)S(1)} %pad_add_fusion.1.place_ref, bf16[9,16,1024]{2,1,0:T(8,128)(2,1)S(1)} %copy-done.2, bf16[9,16,1024]{2,1,0:T(8,128)(2,1)S(1)} %copy-done.4, ...), custom_call_target="tpu_custom_call" | custom-call | flops 1000000 | bytes 1000000 | tf_op jit(solution)/shard_map/pallas_call | solution.py:208
  90.9 2.1 %collective-permute-done.19.refs_16_ = bf16[2,512,512]{2,1,0:T(8,128)(2,1)S(1)} collective-permute-done((bf16[2,512,512]{2,1,0:T(8,128)(2,1)S(1)}, bf16[2,512,512]{2,1,0:T(8,128)(2,1)S(1)}, u32[]{:S(2)}, u32[]{:S(2)}) %collective-permute-start.19) | collective-permute-done | bytes 1048608 | tf_op jit(solution)/shard_map/ppermute | solution.py:384
  93.0 1.5 collective-permute-done.20.refs_17_
  94.5 4.1 %shard_map.87 = (f32[512,512]{1,0:T(8,128)S(1)}, bf16[512,512]{1,0:T(8,128)(2,1)S(1)}, bf16[512,512]{1,0:T(8,128)(2,1)S(1)}, bf16[512,512]{1,0:T(8,128)(2,1)S(1)}) custom-call(s32[1]{0:T(128)} %shard_map.83.token_ref, s32[3]{0:T(128)S(1)} %pad_add_fusion.1.place_ref, bf16[9,16,1024]{2,1,0:T(8,128)(2,1)S(1)} %copy-done.2, bf16[9,16,1024]{2,1,0:T(8,128)(2,1)S(1)} %copy-done.4, ...), custom_call_target="tpu_custom_call" | custom-call | flops 1000000 | bytes 1000000 | tf_op jit(solution)/shard_map/pallas_call | solution.py:208
  98.6 0.8 collective-permute-done.21.a1_ref
  99.4 1.1 collective-permute-done.22.b2_ref
  100.5 1.9 %collective-permute-start.29 = (bf16[7104,128]{1,0:T(8,128)(2,1)}, bf16[7104,128]{1,0:T(8,128)(2,1)S(1)}, u32[]{:S(2)}, u32[]{:S(2)}) collective-permute-start(bf16[7104,128]{1,0:T(8,128)(2,1)} %collective-permute-done.21.a1_ref), channel_id=1, source_target_pairs={{0,3},{3,0},{1,2},{2,1},{4,7},{7,4},{5,6},{6,5},{8,11},{11,8},{9,1... | collective-permute-start | bytes 5455880 | tf_op jit(solution)/shard_map/ppermute | solution.py:372
  102.9 2.4 %collective-permute-start.24 = (bf16[512,512]{1,0:T(8,128)(2,1)S(1)}, bf16[512,512]{1,0:T(8,128)(2,1)S(1)}, u32[]{:S(2)}, u32[]{:S(2)}) collective-permute-start(bf16[512,512]{1,0:T(8,128)(2,1)S(1)} %get-tuple-element.49), channel_id=1, source_target_pairs={{0,128},{4,132},{8,136},{12,140},{16,144},{20,148},{24,152},{28,15... | collective-permute-start | bytes 1572872 | tf_op jit(solution)/shard_map/ppermute | solution.py:384
  105.3 12.0 %collective-permute-done.23.r1_ref = bf16[512,512]{1,0:T(8,128)(2,1)S(1)} collective-permute-done((bf16[512,512]{1,0:T(8,128)(2,1)S(1)}, bf16[512,512]{1,0:T(8,128)(2,1)S(1)}, u32[]{:S(2)}, u32[]{:S(2)}) %collective-permute-start.23) | collective-permute-done | bytes 524320 | tf_op jit(solution)/shard_map/ppermute | solution.py:384
  117.3 2.0 %collective-permute-done.24.r2_ref = bf16[512,512]{1,0:T(8,128)(2,1)S(1)} collective-permute-done((bf16[512,512]{1,0:T(8,128)(2,1)S(1)}, bf16[512,512]{1,0:T(8,128)(2,1)S(1)}, u32[]{:S(2)}, u32[]{:S(2)}) %collective-permute-start.24) | collective-permute-done | bytes 524320 | tf_op jit(solution)/shard_map/ppermute | solution.py:384
  119.3 8.4 %collective-permute-done.25.r3_ref = bf16[512,512]{1,0:T(8,128)(2,1)S(1)} collective-permute-done((bf16[512,512]{1,0:T(8,128)(2,1)S(1)}, bf16[512,512]{1,0:T(8,128)(2,1)S(1)}, u32[]{:S(2)}, u32[]{:S(2)}) %collective-permute-start.25) | collective-permute-done | bytes 524320 | tf_op jit(solution)/shard_map/ppermute | solution.py:384
  127.7 1.0 shard_map.88
  128.7 1.6 %collective-permute-start.26 = (bf16[512,128]{1,0:T(8,128)(2,1)S(1)}, bf16[512,128]{1,0:T(8,128)(2,1)S(1)}, u32[]{:S(2)}, u32[]{:S(2)}) collective-permute-start(bf16[512,128]{1,0:T(8,128)(2,1)S(1)} %get-tuple-element.52), channel_id=1, source_target_pairs={{0,1},{1,2},{2,3},{3,0},{4,5},{5,6},{6,7},{7,4},{8,9},{9,10},{10,1... | collective-permute-start | bytes 393224 | tf_op jit(solution)/shard_map/ppermute | solution.py:364
  130.3 0.9 collective-permute-start.27
  131.2 2.3 %collective-permute-start.28 = (bf16[512,128]{1,0:T(8,128)(2,1)S(1)}, bf16[512,128]{1,0:T(8,128)(2,1)S(1)}, u32[]{:S(2)}, u32[]{:S(2)}) collective-permute-start(bf16[512,128]{1,0:T(8,128)(2,1)S(1)} %get-tuple-element.54), channel_id=1, source_target_pairs={{0,3},{1,0},{2,1},{3,2},{4,7},{5,4},{6,5},{7,6},{8,11},{9,8},{10,9... | collective-permute-start | bytes 393224 | tf_op jit(solution)/shard_map/ppermute | solution.py:364
  133.5 2.0 %copy-done = bf16[14208,128]{1,0:T(8,128)(2,1)S(1)} copy-done((bf16[14208,128]{1,0:T(8,128)(2,1)S(1)}, bf16[14208,128]{1,0:T(8,128)(2,1)}, u32[]{:S(2)}) %copy-start) | copy-done | bytes 3637272
  135.6 3.7 %shard_map.89.held_ref = bf16[3,14208,128]{2,1,0:T(8,128)(2,1)S(1)} custom-call(bf16[14208,128]{1,0:T(8,128)(2,1)S(1)} %copy-done, bf16[7104,128]{1,0:T(8,128)(2,1)} %collective-permute-done.21.a1_ref, bf16[7104,128]{1,0:T(8,128)(2,1)} %collective-permute-done.1.refs_0_.a2_ref, bf16[7104,128]{1,0:T(8,128)(2,1)} %collective-permute-done.2.refs_1_.b1_ref, ...), custom_call_target="tpu_custom_call" | custom-call | flops 1000000 | bytes 1000000 | tf_op jit(solution)/shard_map/pallas_call | solution.py:292
  139.3 6.8 %collective-permute-done.26.t1_ref = bf16[512,128]{1,0:T(8,128)(2,1)S(1)} collective-permute-done((bf16[512,128]{1,0:T(8,128)(2,1)S(1)}, bf16[512,128]{1,0:T(8,128)(2,1)S(1)}, u32[]{:S(2)}, u32[]{:S(2)}) %collective-permute-start.26) | collective-permute-done | bytes 131104 | tf_op jit(solution)/shard_map/ppermute | solution.py:364
  146.0 2.6 %collective-permute-done.27.t2_ref = bf16[512,128]{1,0:T(8,128)(2,1)S(1)} collective-permute-done((bf16[512,128]{1,0:T(8,128)(2,1)S(1)}, bf16[512,128]{1,0:T(8,128)(2,1)S(1)}, u32[]{:S(2)}, u32[]{:S(2)}) %collective-permute-start.27) | collective-permute-done | bytes 131104 | tf_op jit(solution)/shard_map/ppermute | solution.py:364
  148.6 6.6 %shard_map.90 = bf16[14208,128]{1,0:T(8,128)(2,1)} custom-call(s32[4]{0:T(128)S(1)} %pad_add_fusion.order_ref, f32[512,128]{1,0:T(8,128)S(1)} %get-tuple-element.51.t0_ref, bf16[512,128]{1,0:T(8,128)(2,1)S(1)} %collective-permute-done.26.t1_ref, bf16[512,128]{1,0:T(8,128)(2,1)S(1)} %collective-permute-done.27.t2_ref, ...), custom_call_target="tpu_custom_call" | custom-call | tf_op jit(solution)/shard_map/pallas_call | solution.py:344
  (81 shorter events, 9.5 us)
Async XLA Ops:
  3.3 11.0 %collective-permute-start = (bf16[16,16,640]{2,1,0:T(8,128)(2,1)}, bf16[16,16,640]{2,1,0:T(8,128)(2,1)S(1)}, u32[]{:S(2)}, u32[]{:S(2)}) collective-permute-start(bf16[16,16,640]{2,1,0:T(8,128)(2,1)} %get-tuple-element.31), channel_id=1, source_target_pairs={{0,1},{1,2},{2,3},{3,0},{4,5},{5,6},{6,7},{7,4},{8,9},{9,10},{10,1... | collective-permute-start | bytes 983048 | tf_op jit(solution)/shard_map/ppermute | solution.py:364
  4.9 17.8 %collective-permute-start.3 = (bf16[16,16,640]{2,1,0:T(8,128)(2,1)}, bf16[16,16,640]{2,1,0:T(8,128)(2,1)S(1)}, u32[]{:S(2)}, u32[]{:S(2)}) collective-permute-start(bf16[16,16,640]{2,1,0:T(8,128)(2,1)} %get-tuple-element.34), channel_id=1, source_target_pairs={{0,3},{1,0},{2,1},{3,2},{4,7},{5,4},{6,5},{7,6},{8,11},{9,8},{10,9... | collective-permute-start | bytes 983048 | tf_op jit(solution)/shard_map/ppermute | solution.py:364
  6.6 17.4 %collective-permute-start.4 = (bf16[16,16,640]{2,1,0:T(8,128)(2,1)}, bf16[16,16,640]{2,1,0:T(8,128)(2,1)}, u32[]{:S(2)}, u32[]{:S(2)}) collective-permute-start(bf16[16,16,640]{2,1,0:T(8,128)(2,1)} %get-tuple-element.38), channel_id=1, source_target_pairs={{0,2},{1,3},{2,0},{3,1},{4,6},{5,7},{6,4},{7,5},{8,10},{9,11},{10,... | collective-permute-start | bytes 983048 | tf_op jit(solution)/shard_map/ppermute | solution.py:364
  8.6 4.1 %copy-start.21 = (f32[16,4]{0,1:T(4,128)S(1)}, f32[16,4]{0,1:T(4,128)}, u32[]{:S(2)}) copy-start(f32[16,4]{0,1:T(4,128)} %param.15) | copy-start | bytes 772
  8.6 4.3 %copy-start.22 = (s32[16,4]{0,1:T(4,128)S(1)}, s32[16,4]{0,1:T(4,128)}, u32[]{:S(2)}) copy-start(s32[16,4]{0,1:T(4,128)} %param.14) | copy-start | bytes 772
  14.3 8.4 %copy-start.16 = (bf16[16,16,640]{2,1,0:T(8,128)(2,1)}, bf16[16,16,640]{2,1,0:T(8,128)(2,1)S(1)}, u32[]{:S(2)}) copy-start(bf16[16,16,640]{2,1,0:T(8,128)(2,1)S(1)} %collective-permute-done.refs_0_.r1_ref) | copy-start | bytes 983044
  14.3 50.4 %collective-permute-start.1 = (bf16[7104,128]{1,0:T(8,128)(2,1)}, bf16[7104,128]{1,0:T(8,128)(2,1)}, u32[]{:S(2)}, u32[]{:S(2)}) collective-permute-start(bf16[7104,128]{1,0:T(8,128)(2,1)} %get-tuple-element.32), channel_id=1, source_target_pairs={{0,1},{1,0},{2,3},{3,2},{4,5},{5,4},{6,7},{7,6},{8,9},{9,8},{10,11... | collective-permute-start | bytes 5455880 | tf_op jit(solution)/shard_map/ppermute | solution.py:368
  15.7 49.0 %collective-permute-start.2 = (bf16[7104,128]{1,0:T(8,128)(2,1)}, bf16[7104,128]{1,0:T(8,128)(2,1)}, u32[]{:S(2)}, u32[]{:S(2)}) collective-permute-start(bf16[7104,128]{1,0:T(8,128)(2,1)} %get-tuple-element.33), channel_id=1, source_target_pairs={{0,3},{3,0},{1,2},{2,1},{4,7},{7,4},{5,6},{6,5},{8,11},{11,8},{9,1... | collective-permute-start | bytes 5455880 | tf_op jit(solution)/shard_map/ppermute | solution.py:372
  23.4 1.0 copy-start.15
  23.4 1.0 copy-start.20
  24.5 1.0 copy-start.17
  25.5 1.0 copy-start.19
  28.2 9.8 %collective-permute-start.8 = (bf16[8,16,1024]{2,1,0:T(8,128)(2,1)S(1)}, bf16[8,16,1024]{2,1,0:T(8,128)(2,1)S(1)}, u32[]{:S(2)}, u32[]{:S(2)}) collective-permute-start(bf16[8,16,1024]{2,1,0:T(8,128)(2,1)S(1)} %get-tuple-element.40.refs_8_), channel_id=1, source_target_pairs={{0,56},{4,60},{8,0},{12,4},{16,8},{20,12},{24,16},{28,20},{32,24},... | collective-permute-start | bytes 786440 | tf_op jit(solution)/shard_map/ppermute | solution.py:384
  34.1 9.4 %collective-permute-start.15 = (bf16[8,16,1024]{2,1,0:T(8,128)(2,1)S(1)}, bf16[8,16,1024]{2,1,0:T(8,128)(2,1)S(1)}, u32[]{:S(2)}, u32[]{:S(2)}) collective-permute-start(bf16[8,16,1024]{2,1,0:T(8,128)(2,1)S(1)} %get-tuple-element.40.refs_8_), channel_id=1, source_target_pairs={{0,8},{4,12},{8,16},{12,20},{16,24},{20,28},{24,32},{28,36},{32,40... | collective-permute-start | bytes 786440 | tf_op jit(solution)/shard_map/ppermute | solution.py:384
  34.8 12.0 %collective-permute-start.5 = (bf16[9,16,1024]{2,1,0:T(8,128)(2,1)S(1)}, bf16[9,16,1024]{2,1,0:T(8,128)(2,1)S(1)}, u32[]{:S(2)}, u32[]{:S(2)}) collective-permute-start(bf16[9,16,1024]{2,1,0:T(8,128)(2,1)S(1)} %get-tuple-element.39.refs_0_), channel_id=1, source_target_pairs={{0,8},{4,12},{8,16},{12,20},{16,24},{20,28},{24,32},{28,36},{32,40... | collective-permute-start | bytes 884744 | tf_op jit(solution)/shard_map/ppermute | solution.py:384
  38.0 10.0 %collective-permute-start.11 = (bf16[9,16,1024]{2,1,0:T(8,128)(2,1)S(1)}, bf16[9,16,1024]{2,1,0:T(8,128)(2,1)S(1)}, u32[]{:S(2)}, u32[]{:S(2)}) collective-permute-start(bf16[9,16,1024]{2,1,0:T(8,128)(2,1)S(1)} %get-tuple-element.39.refs_0_), channel_id=1, source_target_pairs={{0,56},{4,60},{8,0},{12,4},{16,8},{20,12},{24,16},{28,20},{32,24},... | collective-permute-start | bytes 884744 | tf_op jit(solution)/shard_map/ppermute | solution.py:384
  43.5 9.7 %collective-permute-start.9 = (bf16[8,16,1024]{2,1,0:T(8,128)(2,1)S(1)}, bf16[8,16,1024]{2,1,0:T(8,128)(2,1)}, u32[]{:S(2)}, u32[]{:S(2)}) collective-permute-start(bf16[8,16,1024]{2,1,0:T(8,128)(2,1)S(1)} %collective-permute-done.8.refs_12_), channel_id=1, source_target_pairs={{0,56},{4,60},{8,0},{12,4},{16,8},{20,12},{24,16},{28,20},{32,24},... | collective-permute-start | bytes 786440 | tf_op jit(solution)/shard_map/ppermute | solution.py:384
  46.8 15.3 %collective-permute-start.6 = (bf16[9,16,1024]{2,1,0:T(8,128)(2,1)S(1)}, bf16[9,16,1024]{2,1,0:T(8,128)(2,1)}, u32[]{:S(2)}, u32[]{:S(2)}) collective-permute-start(bf16[9,16,1024]{2,1,0:T(8,128)(2,1)S(1)} %collective-permute-done.5.refs_1_), channel_id=1, source_target_pairs={{0,8},{4,12},{8,16},{12,20},{16,24},{20,28},{24,32},{28,36},{32,40... | collective-permute-start | bytes 884744 | tf_op jit(solution)/shard_map/ppermute | solution.py:384
  48.0 14.7 %collective-permute-start.12 = (bf16[9,16,1024]{2,1,0:T(8,128)(2,1)S(1)}, bf16[9,16,1024]{2,1,0:T(8,128)(2,1)S(1)}, u32[]{:S(2)}, u32[]{:S(2)}) collective-permute-start(bf16[9,16,1024]{2,1,0:T(8,128)(2,1)S(1)} %collective-permute-done.11.refs_4_), channel_id=1, source_target_pairs={{0,56},{4,60},{8,0},{12,4},{16,8},{20,12},{24,16},{28,20},{32,24},... | collective-permute-start | bytes 884744 | tf_op jit(solution)/shard_map/ppermute | solution.py:384
  51.7 0.7 copy-start.5
  53.2 8.3 %collective-permute-start.16 = (bf16[8,16,1024]{2,1,0:T(8,128)(2,1)S(1)}, bf16[8,16,1024]{2,1,0:T(8,128)(2,1)}, u32[]{:S(2)}, u32[]{:S(2)}) collective-permute-start(bf16[8,16,1024]{2,1,0:T(8,128)(2,1)S(1)} %collective-permute-done.15.refs_9_), channel_id=1, source_target_pairs={{0,8},{4,12},{8,16},{12,20},{16,24},{20,28},{24,32},{28,36},{32,40... | collective-permute-start | bytes 786440 | tf_op jit(solution)/shard_map/ppermute | solution.py:384
  61.5 37.9 %collective-permute-start.21 = (bf16[7104,128]{1,0:T(8,128)(2,1)}, bf16[7104,128]{1,0:T(8,128)(2,1)}, u32[]{:S(2)}, u32[]{:S(2)}) collective-permute-start(bf16[7104,128]{1,0:T(8,128)(2,1)} %get-tuple-element.33), channel_id=1, source_target_pairs={{0,1},{1,0},{2,3},{3,2},{4,5},{5,4},{6,7},{7,6},{8,9},{9,8},{10,11... | collective-permute-start | bytes 5455880 | tf_op jit(solution)/shard_map/ppermute | solution.py:368
  62.1 38.5 %collective-permute-start.22 = (bf16[7104,128]{1,0:T(8,128)(2,1)}, bf16[7104,128]{1,0:T(8,128)(2,1)}, u32[]{:S(2)}, u32[]{:S(2)}) collective-permute-start(bf16[7104,128]{1,0:T(8,128)(2,1)} %get-tuple-element.32), channel_id=1, source_target_pairs={{0,3},{3,0},{1,2},{2,1},{4,7},{7,4},{5,6},{6,5},{8,11},{11,8},{9,1... | collective-permute-start | bytes 5455880 | tf_op jit(solution)/shard_map/ppermute | solution.py:372
  62.7 2.0 %copy-start.7 = (bf16[9,16,1024]{2,1,0:T(8,128)(2,1)}, bf16[9,16,1024]{2,1,0:T(8,128)(2,1)S(1)}, u32[]{:S(2)}) copy-start(bf16[9,16,1024]{2,1,0:T(8,128)(2,1)S(1)} %collective-permute-done.12.refs_5_) | copy-start | bytes 884740
  62.7 9.4 %collective-permute-start.10 = (bf16[8,16,1024]{2,1,0:T(8,128)(2,1)}, bf16[8,16,1024]{2,1,0:T(8,128)(2,1)}, u32[]{:S(2)}, u32[]{:S(2)}) collective-permute-start(bf16[8,16,1024]{2,1,0:T(8,128)(2,1)} %collective-permute-done.9.refs_13_), channel_id=1, source_target_pairs={{0,56},{4,60},{8,0},{12,4},{16,8},{20,12},{24,16},{28,20},{32,24},... | collective-permute-start | bytes 786440 | tf_op jit(solution)/shard_map/ppermute | solution.py:384
  64.7 13.3 %collective-permute-start.17 = (bf16[8,16,1024]{2,1,0:T(8,128)(2,1)}, bf16[8,16,1024]{2,1,0:T(8,128)(2,1)}, u32[]{:S(2)}, u32[]{:S(2)}) collective-permute-start(bf16[8,16,1024]{2,1,0:T(8,128)(2,1)} %collective-permute-done.16.refs_10_), channel_id=1, source_target_pairs={{0,8},{4,12},{8,16},{12,20},{16,24},{20,28},{24,32},{28,36},{32,40... | collective-permute-start | bytes 786440 | tf_op jit(solution)/shard_map/ppermute | solution.py:384
  64.8 13.3 %collective-permute-start.7 = (bf16[9,16,1024]{2,1,0:T(8,128)(2,1)}, bf16[9,16,1024]{2,1,0:T(8,128)(2,1)}, u32[]{:S(2)}, u32[]{:S(2)}) collective-permute-start(bf16[9,16,1024]{2,1,0:T(8,128)(2,1)} %collective-permute-done.6.refs_2_), channel_id=1, source_target_pairs={{0,8},{4,12},{8,16},{12,20},{16,24},{20,28},{24,32},{28,36},{32,40... | collective-permute-start | bytes 884744 | tf_op jit(solution)/shard_map/ppermute | solution.py:384
  65.8 6.4 %copy-start.8 = (bf16[9,16,1024]{2,1,0:T(8,128)(2,1)S(1)}, bf16[9,16,1024]{2,1,0:T(8,128)(2,1)}, u32[]{:S(2)}) copy-start(bf16[9,16,1024]{2,1,0:T(8,128)(2,1)} %copy-done.7) | copy-start | bytes 884740
  65.8 20.4 %copy-start.2 = (bf16[9,16,1024]{2,1,0:T(8,128)(2,1)S(1)}, bf16[9,16,1024]{2,1,0:T(8,128)(2,1)}, u32[]{:S(2)}) copy-start(bf16[9,16,1024]{2,1,0:T(8,128)(2,1)} %copy-done.1) | copy-start | bytes 884740
  65.8 20.4 %copy-start.4 = (bf16[9,16,1024]{2,1,0:T(8,128)(2,1)S(1)}, bf16[9,16,1024]{2,1,0:T(8,128)(2,1)}, u32[]{:S(2)}) copy-start(bf16[9,16,1024]{2,1,0:T(8,128)(2,1)} %copy-done.3) | copy-start | bytes 884740
  65.8 20.4 %copy-start.6 = (bf16[9,16,1024]{2,1,0:T(8,128)(2,1)S(1)}, bf16[9,16,1024]{2,1,0:T(8,128)(2,1)}, u32[]{:S(2)}) copy-start(bf16[9,16,1024]{2,1,0:T(8,128)(2,1)} %copy-done.5) | copy-start | bytes 884740
  65.8 20.4 %copy-start.10 = (bf16[8,16,1024]{2,1,0:T(8,128)(2,1)S(1)}, bf16[8,16,1024]{2,1,0:T(8,128)(2,1)}, u32[]{:S(2)}) copy-start(bf16[8,16,1024]{2,1,0:T(8,128)(2,1)} %copy-done.9) | copy-start | bytes 786436
  65.8 20.4 %copy-start.12 = (bf16[8,16,1024]{2,1,0:T(8,128)(2,1)S(1)}, bf16[8,16,1024]{2,1,0:T(8,128)(2,1)}, u32[]{:S(2)}) copy-start(bf16[8,16,1024]{2,1,0:T(8,128)(2,1)} %copy-done.11) | copy-start | bytes 786436
  65.8 20.4 %copy-start.14 = (bf16[8,16,1024]{2,1,0:T(8,128)(2,1)S(1)}, bf16[8,16,1024]{2,1,0:T(8,128)(2,1)}, u32[]{:S(2)}) copy-start(bf16[8,16,1024]{2,1,0:T(8,128)(2,1)} %copy-done.13) | copy-start | bytes 786436
  72.1 9.3 %collective-permute-start.13 = (bf16[9,16,1024]{2,1,0:T(8,128)(2,1)S(1)}, bf16[9,16,1024]{2,1,0:T(8,128)(2,1)S(1)}, u32[]{:S(2)}, u32[]{:S(2)}) collective-permute-start(bf16[9,16,1024]{2,1,0:T(8,128)(2,1)S(1)} %copy-done.8), channel_id=1, source_target_pairs={{0,56},{4,60},{8,0},{12,4},{16,8},{20,12},{24,16},{28,20},{32,24},... | collective-permute-start | bytes 884744 | tf_op jit(solution)/shard_map/ppermute | solution.py:384
  78.1 8.1 %collective-permute-start.14 = (bf16[9,16,1024]{2,1,0:T(8,128)(2,1)}, bf16[9,16,1024]{2,1,0:T(8,128)(2,1)S(1)}, u32[]{:S(2)}, u32[]{:S(2)}) collective-permute-start(bf16[9,16,1024]{2,1,0:T(8,128)(2,1)} %collective-permute-done.7.refs_3_), channel_id=1, source_target_pairs={{0,8},{4,12},{8,16},{12,20},{16,24},{20,28},{24,32},{28,36},{32,40... | collective-permute-start | bytes 884744 | tf_op jit(solution)/shard_map/ppermute | solution.py:384
  78.1 7.4 %collective-permute-start.18 = (bf16[8,16,1024]{2,1,0:T(8,128)(2,1)}, bf16[8,16,1024]{2,1,0:T(8,128)(2,1)S(1)}, u32[]{:S(2)}, u32[]{:S(2)}) collective-permute-start(bf16[8,16,1024]{2,1,0:T(8,128)(2,1)} %collective-permute-done.10.refs_14_), channel_id=1, source_target_pairs={{0,56},{4,60},{8,0},{12,4},{16,8},{20,12},{24,16},{28,20},{32,24},... | collective-permute-start | bytes 786440 | tf_op jit(solution)/shard_map/ppermute | solution.py:384
  90.3 2.7 %collective-permute-start.19 = (bf16[2,512,512]{2,1,0:T(8,128)(2,1)S(1)}, bf16[2,512,512]{2,1,0:T(8,128)(2,1)S(1)}, u32[]{:S(2)}, u32[]{:S(2)}) collective-permute-start(bf16[2,512,512]{2,1,0:T(8,128)(2,1)S(1)} %get-tuple-element.44), channel_id=1, source_target_pairs={{0,4},{4,0},{8,12},{12,8},{16,20},{20,16},{24,28},{28,24},{32,36},... | collective-permute-start | bytes 3145736 | tf_op jit(solution)/shard_map/ppermute | solution.py:384
  90.4 4.1 %collective-permute-start.20 = (bf16[2,512,512]{2,1,0:T(8,128)(2,1)S(1)}, bf16[2,512,512]{2,1,0:T(8,128)(2,1)S(1)}, u32[]{:S(2)}, u32[]{:S(2)}) collective-permute-start(bf16[2,512,512]{2,1,0:T(8,128)(2,1)S(1)} %get-tuple-element.45), channel_id=1, source_target_pairs={{0,4},{4,0},{8,12},{12,8},{16,20},{20,16},{24,28},{28,24},{32,36},... | collective-permute-start | bytes 3145736 | tf_op jit(solution)/shard_map/ppermute | solution.py:384
  100.5 48.1 %collective-permute-start.29 = (bf16[7104,128]{1,0:T(8,128)(2,1)}, bf16[7104,128]{1,0:T(8,128)(2,1)S(1)}, u32[]{:S(2)}, u32[]{:S(2)}) collective-permute-start(bf16[7104,128]{1,0:T(8,128)(2,1)} %collective-permute-done.21.a1_ref), channel_id=1, source_target_pairs={{0,3},{3,0},{1,2},{2,1},{4,7},{7,4},{5,6},{6,5},{8,11},{11,8},{9,1... | collective-permute-start | bytes 5455880 | tf_op jit(solution)/shard_map/ppermute | solution.py:372
  102.4 46.2 %collective-permute-start.30 = (bf16[7104,128]{1,0:T(8,128)(2,1)}, bf16[7104,128]{1,0:T(8,128)(2,1)}, u32[]{:S(2)}, u32[]{:S(2)}) collective-permute-start(bf16[7104,128]{1,0:T(8,128)(2,1)} %collective-permute-done.22.b2_ref), channel_id=1, source_target_pairs={{0,1},{1,0},{2,3},{3,2},{4,5},{5,4},{6,7},{7,6},{8,9},{9,8},{10,11... | collective-permute-start | bytes 5455880 | tf_op jit(solution)/shard_map/ppermute | solution.py:368
  102.4 14.9 %collective-permute-start.23 = (bf16[512,512]{1,0:T(8,128)(2,1)S(1)}, bf16[512,512]{1,0:T(8,128)(2,1)S(1)}, u32[]{:S(2)}, u32[]{:S(2)}) collective-permute-start(bf16[512,512]{1,0:T(8,128)(2,1)S(1)} %get-tuple-element.48), channel_id=1, source_target_pairs={{0,64},{4,68},{8,72},{12,76},{16,80},{20,84},{24,88},{28,92},{32,9... | collective-permute-start | bytes 1572872 | tf_op jit(solution)/shard_map/ppermute | solution.py:384
  102.9 16.4 %collective-permute-start.24 = (bf16[512,512]{1,0:T(8,128)(2,1)S(1)}, bf16[512,512]{1,0:T(8,128)(2,1)S(1)}, u32[]{:S(2)}, u32[]{:S(2)}) collective-permute-start(bf16[512,512]{1,0:T(8,128)(2,1)S(1)} %get-tuple-element.49), channel_id=1, source_target_pairs={{0,128},{4,132},{8,136},{12,140},{16,144},{20,148},{24,152},{28,15... | collective-permute-start | bytes 1572872 | tf_op jit(solution)/shard_map/ppermute | solution.py:384
  105.3 22.4 %collective-permute-start.25 = (bf16[512,512]{1,0:T(8,128)(2,1)S(1)}, bf16[512,512]{1,0:T(8,128)(2,1)S(1)}, u32[]{:S(2)}, u32[]{:S(2)}) collective-permute-start(bf16[512,512]{1,0:T(8,128)(2,1)S(1)} %get-tuple-element.50), channel_id=1, source_target_pairs={{0,192},{4,196},{8,200},{12,204},{16,208},{20,212},{24,216},{28,22... | collective-permute-start | bytes 1572872 | tf_op jit(solution)/shard_map/ppermute | solution.py:384
  128.7 17.4 %collective-permute-start.26 = (bf16[512,128]{1,0:T(8,128)(2,1)S(1)}, bf16[512,128]{1,0:T(8,128)(2,1)S(1)}, u32[]{:S(2)}, u32[]{:S(2)}) collective-permute-start(bf16[512,128]{1,0:T(8,128)(2,1)S(1)} %get-tuple-element.52), channel_id=1, source_target_pairs={{0,1},{1,2},{2,3},{3,0},{4,5},{5,6},{6,7},{7,4},{8,9},{9,10},{10,1... | collective-permute-start | bytes 393224 | tf_op jit(solution)/shard_map/ppermute | solution.py:364
  130.3 18.4 %collective-permute-start.27 = (bf16[512,128]{1,0:T(8,128)(2,1)S(1)}, bf16[512,128]{1,0:T(8,128)(2,1)S(1)}, u32[]{:S(2)}, u32[]{:S(2)}) collective-permute-start(bf16[512,128]{1,0:T(8,128)(2,1)S(1)} %get-tuple-element.53), channel_id=1, source_target_pairs={{0,2},{1,3},{2,0},{3,1},{4,6},{5,7},{6,4},{7,5},{8,10},{9,11},{10,... | collective-permute-start | bytes 393224 | tf_op jit(solution)/shard_map/ppermute | solution.py:364
  131.2 17.4 %collective-permute-start.28 = (bf16[512,128]{1,0:T(8,128)(2,1)S(1)}, bf16[512,128]{1,0:T(8,128)(2,1)S(1)}, u32[]{:S(2)}, u32[]{:S(2)}) collective-permute-start(bf16[512,128]{1,0:T(8,128)(2,1)S(1)} %get-tuple-element.54), channel_id=1, source_target_pairs={{0,3},{1,0},{2,1},{3,2},{4,7},{5,4},{6,5},{7,6},{8,11},{9,8},{10,9... | collective-permute-start | bytes 393224 | tf_op jit(solution)/shard_map/ppermute | solution.py:364
  133.5 2.0 %copy-start = (bf16[14208,128]{1,0:T(8,128)(2,1)S(1)}, bf16[14208,128]{1,0:T(8,128)(2,1)}, u32[]{:S(2)}) copy-start(bf16[14208,128]{1,0:T(8,128)(2,1)} %own_ref.1) | copy-start | bytes 10911748
  (6 other events, 4.3 us)

commit v8 on v7

--- a/solution.py
+++ b/solution.py
@@ -435,7 +435,8 @@
     others = sums(0, token, place, lows, highs)
     others = [move(x, columns, (0, 0, 1)) for x in others]
     here, e1, e2, e3 = sums(1, token, place, lows, highs, others)
-    here, a1, b2 = lax.optimization_barrier((here, a1, b2))
+    here, a1 = lax.optimization_barrier((here, a1))
+    e2, b2 = lax.optimization_barrier((e2, b2))
     o1, o2 = swap_b(a1), swap_a(b2)
     e1, e2, e3 = move(e1, columns, (1, 0, 0)), move(e2, columns, (2, 0, 0)), move(e3, columns, (3, 0, 0))
     t0, t1, t2, t3 = transform_parts(q1, token, (here, e1, e2, e3))

time: 156 us -> 156 us (level)
  no operation moved by 1% of the time
where the time goes in v8:
time: 156 us; the launch traced here: 155 us
  waiting for transfers between devices  67.6 us (43%)
  starting transfers between devices  47.5 us (30%)
  Pallas kernels  25.5 us (16%)
  local copies, waits for them, and re-layouts  14 us (9%)
    ppermute x19, waiting for transfers between devices, move(): return lax.ppermute(x, 'tile', pairs)  55.4 us
    ppermute x19, starting transfers between devices, move(): return lax.ppermute(x, 'tile', pairs)  25.9 us
    ppermute x6, waiting for transfers between devices, shift(): lax.ppermute(x, 'mem', [(i, (i + d) % GROUPS) for i in range(GROUPS)])  10.2 us
    ppermute x6, starting transfers between devices, shift(): lax.ppermute(x, 'mem', [(i, (i + d) % GROUPS) for i in range(GROUPS)])  10.1 us
    unnamed x48, local copies, waits for them, and re-layouts  9.67 us
    ppermute x3, starting transfers between devices, swap_b(): return lax.ppermute(x, 'mem', [(0, 3), (3, 0), (1, 2), (2, 1)])  9.47 us
    pallas_call x2, Pallas kernels, sums(): pl.pallas_call(functools.partial(sums_kernel, same), in_specs=[pl.BlockSp...  8.09 us
    pallas_call x1, Pallas kernels, update(): pl.pallas_call(update_kernel, in_specs=[pl.BlockSpec(memory_space=pltpu.S...  6.63 us
  transfers between devices with their start and end apart: 31, of which 20 were waited for; matrix products, arithmetic and copies ran while one was open for 3% of the time, Pallas kernels for 10%

profile of v8, /device:TPU:6, one launch (start us, length us, event | category | flops | bytes accessed | tf_op | source)
XLA Modules:
  0.0 155.5 jit_solution(5394536120964714471)
XLA Ops:
  0.0 3.3 %shard_map.82 = (f32[16,16,512]{2,1,0:T(8,128)}, bf16[16,16,128]{2,1,0:T(8,128)(2,1)}, bf16[16,16,640]{2,1,0:T(8,128)(2,1)}, bf16[16,16,640]{2,1,0:T(8,128)(2,1)}, bf16[16,16,640]{2,1,0:T(8,128)(2,1)}) custom-call(s32[1]{0:T(128)} %bitcast.q_ref, bf16[16,64,128]{2,1,0:T(8,128)(2,1)} %obs_ref.1, bf16[16,512,128]{2,1,0:T(8,128)(2,1)} %inv_ref.1, ...), custom_call_target="tpu_custom_call" | custom-call | tf_op jit(solution)/shard_map/pallas_call | solution.py:57
  3.3 1.6 %collective-permute-start = (bf16[16,16,640]{2,1,0:T(8,128)(2,1)}, bf16[16,16,640]{2,1,0:T(8,128)(2,1)S(1)}, u32[]{:S(2)}, u32[]{:S(2)}) collective-permute-start(bf16[16,16,640]{2,1,0:T(8,128)(2,1)} %get-tuple-element.32), channel_id=1, source_target_pairs={{0,1},{1,2},{2,3},{3,0},{4,5},{5,6},{6,7},{7,4},{8,9},{9,10},{10,1... | collective-permute-start | bytes 983048 | tf_op jit(solution)/shard_map/ppermute | solution.py:364
  4.9 1.7 %collective-permute-start.3 = (bf16[16,16,640]{2,1,0:T(8,128)(2,1)}, bf16[16,16,640]{2,1,0:T(8,128)(2,1)S(1)}, u32[]{:S(2)}, u32[]{:S(2)}) collective-permute-start(bf16[16,16,640]{2,1,0:T(8,128)(2,1)} %get-tuple-element.35), channel_id=1, source_target_pairs={{0,3},{1,0},{2,1},{3,2},{4,7},{5,4},{6,5},{7,6},{8,11},{9,8},{10,9... | collective-permute-start | bytes 983048 | tf_op jit(solution)/shard_map/ppermute | solution.py:364
  6.6 2.0 %collective-permute-start.4 = (bf16[16,16,640]{2,1,0:T(8,128)(2,1)}, bf16[16,16,640]{2,1,0:T(8,128)(2,1)}, u32[]{:S(2)}, u32[]{:S(2)}) collective-permute-start(bf16[16,16,640]{2,1,0:T(8,128)(2,1)} %get-tuple-element.39), channel_id=1, source_target_pairs={{0,2},{1,3},{2,0},{3,1},{4,6},{5,7},{6,4},{7,5},{8,10},{9,11},{10,... | collective-permute-start | bytes 983048 | tf_op jit(solution)/shard_map/ppermute | solution.py:364
  8.6 4.1 %fusion.3 = (bf16[7104,128]{1,0:T(8,128)(2,1)}, bf16[7104,128]{1,0:T(8,128)(2,1)}) fusion(bf16[14208,128]{1,0:T(8,128)(2,1)} %own_ref.1), kind=kLoop, calls=%fused_computation.17 | loop fusion | bytes 7274496 | tf_op jit(solution)/shard_map/slice | solution.py:420
  13.5 0.8 collective-permute-done.refs_0_.r1_ref
  14.3 1.4 collective-permute-start.1
  15.7 7.0 %collective-permute-start.2 = (bf16[7104,128]{1,0:T(8,128)(2,1)}, bf16[7104,128]{1,0:T(8,128)(2,1)}, u32[]{:S(2)}, u32[]{:S(2)}) collective-permute-start(bf16[7104,128]{1,0:T(8,128)(2,1)} %get-tuple-element.34), channel_id=1, source_target_pairs={{0,3},{3,0},{1,2},{2,1},{4,7},{7,4},{5,6},{6,5},{8,11},{11,8},{9,1... | collective-permute-start | bytes 5455880 | tf_op jit(solution)/shard_map/ppermute | solution.py:372
  22.7 0.7 copy-done.18
  24.5 1.0 copy-done.17
  25.5 1.0 copy-done.19
  26.4 1.7 %shard_map.85 = (bf16[9,16,1024]{2,1,0:T(8,128)(2,1)S(1)}, bf16[8,16,1024]{2,1,0:T(8,128)(2,1)S(1)}) custom-call(s32[1]{0:T(128)} %bitcast.q_ref, s32[1]{0:T(128)} %shard_map.84.early_ref, f32[1,128]{1,0:T(1,128)S(1)} %bitcast.10, f32[1,128]{1,0:T(1,128)S(1)} %bitcast.9, f32[16,16,512]{2,1,0:T(8,128)S(1)} %copy-done.15, bf16[16,16,128]{2,1,0:T(8,128)(2,1)S(1)} %copy-done.20, ...), custom_call_target="tpu_custom_call" | custom-call | flops 1000000 | bytes 1000000 | tf_op jit(solution)/shard_map/pallas_call | solution.py:120
  28.2 5.9 %collective-permute-start.8 = (bf16[8,16,1024]{2,1,0:T(8,128)(2,1)S(1)}, bf16[8,16,1024]{2,1,0:T(8,128)(2,1)S(1)}, u32[]{:S(2)}, u32[]{:S(2)}) collective-permute-start(bf16[8,16,1024]{2,1,0:T(8,128)(2,1)S(1)} %get-tuple-element.41.refs_8_), channel_id=1, source_target_pairs={{0,56},{4,60},{8,0},{12,4},{16,8},{20,12},{24,16},{28,20},{32,24},... | collective-permute-start | bytes 786440 | tf_op jit(solution)/shard_map/ppermute | solution.py:384
  34.8 3.2 %collective-permute-done.8.refs_12_ = bf16[8,16,1024]{2,1,0:T(8,128)(2,1)S(1)} collective-permute-done((bf16[8,16,1024]{2,1,0:T(8,128)(2,1)S(1)}, bf16[8,16,1024]{2,1,0:T(8,128)(2,1)S(1)}, u32[]{:S(2)}, u32[]{:S(2)}) %collective-permute-start.8) | collective-permute-done | bytes 262176 | tf_op jit(solution)/shard_map/ppermute | solution.py:384
  38.0 3.7 %collective-permute-start.11 = (bf16[9,16,1024]{2,1,0:T(8,128)(2,1)S(1)}, bf16[9,16,1024]{2,1,0:T(8,128)(2,1)S(1)}, u32[]{:S(2)}, u32[]{:S(2)}) collective-permute-start(bf16[9,16,1024]{2,1,0:T(8,128)(2,1)S(1)} %get-tuple-element.40.refs_0_), channel_id=1, source_target_pairs={{0,56},{4,60},{8,0},{12,4},{16,8},{20,12},{24,16},{28,20},{32,24},... | collective-permute-start | bytes 884744 | tf_op jit(solution)/shard_map/ppermute | solution.py:384
  42.4 1.1 collective-permute-done.15.refs_9_
  44.2 2.6 %collective-permute-done.5.refs_1_ = bf16[9,16,1024]{2,1,0:T(8,128)(2,1)S(1)} collective-permute-done((bf16[9,16,1024]{2,1,0:T(8,128)(2,1)S(1)}, bf16[9,16,1024]{2,1,0:T(8,128)(2,1)S(1)}, u32[]{:S(2)}, u32[]{:S(2)}) %collective-permute-start.5) | collective-permute-done | bytes 294944 | tf_op jit(solution)/shard_map/ppermute | solution.py:384
  48.0 3.7 %collective-permute-start.12 = (bf16[9,16,1024]{2,1,0:T(8,128)(2,1)S(1)}, bf16[9,16,1024]{2,1,0:T(8,128)(2,1)S(1)}, u32[]{:S(2)}, u32[]{:S(2)}) collective-permute-start(bf16[9,16,1024]{2,1,0:T(8,128)(2,1)S(1)} %collective-permute-done.11.refs_4_), channel_id=1, source_target_pairs={{0,56},{4,60},{8,0},{12,4},{16,8},{20,12},{24,16},{28,20},{32,24},... | collective-permute-start | bytes 884744 | tf_op jit(solution)/shard_map/ppermute | solution.py:384
  51.7 0.7 copy-done.5
  52.4 0.8 collective-permute-done.9.refs_13_
  54.0 7.5 %collective-permute-done.16.refs_10_ = bf16[8,16,1024]{2,1,0:T(8,128)(2,1)} collective-permute-done((bf16[8,16,1024]{2,1,0:T(8,128)(2,1)S(1)}, bf16[8,16,1024]{2,1,0:T(8,128)(2,1)}, u32[]{:S(2)}, u32[]{:S(2)}) %collective-permute-start.16) | collective-permute-done | bytes 262176 | tf_op jit(solution)/shard_map/ppermute | solution.py:384
  62.7 2.0 %collective-permute-start.10 = (bf16[8,16,1024]{2,1,0:T(8,128)(2,1)}, bf16[8,16,1024]{2,1,0:T(8,128)(2,1)}, u32[]{:S(2)}, u32[]{:S(2)}) collective-permute-start(bf16[8,16,1024]{2,1,0:T(8,128)(2,1)} %collective-permute-done.9.refs_13_), channel_id=1, source_target_pairs={{0,56},{4,60},{8,0},{12,4},{16,8},{20,12},{24,16},{28,20},{32,24},... | collective-permute-start | bytes 786440 | tf_op jit(solution)/shard_map/ppermute | solution.py:384
  64.8 1.0 collective-permute-start.7
  66.3 5.8 %collective-permute-done.10.refs_14_ = bf16[8,16,1024]{2,1,0:T(8,128)(2,1)} collective-permute-done((bf16[8,16,1024]{2,1,0:T(8,128)(2,1)}, bf16[8,16,1024]{2,1,0:T(8,128)(2,1)}, u32[]{:S(2)}, u32[]{:S(2)}) %collective-permute-start.10) | collective-permute-done | bytes 262176 | tf_op jit(solution)/shard_map/ppermute | solution.py:384
  72.1 2.9 %collective-permute-start.13 = (bf16[9,16,1024]{2,1,0:T(8,128)(2,1)S(1)}, bf16[9,16,1024]{2,1,0:T(8,128)(2,1)S(1)}, u32[]{:S(2)}, u32[]{:S(2)}) collective-permute-start(bf16[9,16,1024]{2,1,0:T(8,128)(2,1)S(1)} %copy-done.8), channel_id=1, source_target_pairs={{0,56},{4,60},{8,0},{12,4},{16,8},{20,12},{24,16},{28,20},{32,24},... | collective-permute-start | bytes 884744 | tf_op jit(solution)/shard_map/ppermute | solution.py:384
  75.0 3.1 %collective-permute-done.7.refs_3_ = bf16[9,16,1024]{2,1,0:T(8,128)(2,1)} collective-permute-done((bf16[9,16,1024]{2,1,0:T(8,128)(2,1)}, bf16[9,16,1024]{2,1,0:T(8,128)(2,1)}, u32[]{:S(2)}, u32[]{:S(2)}) %collective-permute-start.7) | collective-permute-done | bytes 294944 | tf_op jit(solution)/shard_map/ppermute | solution.py:384
  78.1 3.2 %collective-permute-start.18 = (bf16[8,16,1024]{2,1,0:T(8,128)(2,1)}, bf16[8,16,1024]{2,1,0:T(8,128)(2,1)S(1)}, u32[]{:S(2)}, u32[]{:S(2)}) collective-permute-start(bf16[8,16,1024]{2,1,0:T(8,128)(2,1)} %collective-permute-done.10.refs_14_), channel_id=1, source_target_pairs={{0,56},{4,60},{8,0},{12,4},{16,8},{20,12},{24,16},{28,20},{32,24},... | collective-permute-start | bytes 786440 | tf_op jit(solution)/shard_map/ppermute | solution.py:384
  81.4 4.1 %collective-permute-done.18.refs_15_ = bf16[8,16,1024]{2,1,0:T(8,128)(2,1)S(1)} collective-permute-done((bf16[8,16,1024]{2,1,0:T(8,128)(2,1)}, bf16[8,16,1024]{2,1,0:T(8,128)(2,1)S(1)}, u32[]{:S(2)}, u32[]{:S(2)}) %collective-permute-start.18) | collective-permute-done | bytes 262176 | tf_op jit(solution)/shard_map/ppermute | solution.py:384
  86.2 4.0 %shard_map.86 = (bf16[2,512,512]{2,1,0:T(8,128)(2,1)S(1)}, bf16[2,512,512]{2,1,0:T(8,128)(2,1)S(1)}) custom-call(s32[1]{0:T(128)} %shard_map.83.token_ref, s32[3]{0:T(128)S(1)} %pad_add_fusion.1.place_ref, bf16[9,16,1024]{2,1,0:T(8,128)(2,1)S(1)} %copy-done.2, bf16[9,16,1024]{2,1,0:T(8,128)(2,1)S(1)} %copy-done.4, ...), custom_call_target="tpu_custom_call" | custom-call | flops 1000000 | bytes 1000000 | tf_op jit(solution)/shard_map/pallas_call | solution.py:208
  90.9 2.1 %collective-permute-done.19.refs_16_ = bf16[2,512,512]{2,1,0:T(8,128)(2,1)S(1)} collective-permute-done((bf16[2,512,512]{2,1,0:T(8,128)(2,1)S(1)}, bf16[2,512,512]{2,1,0:T(8,128)(2,1)S(1)}, u32[]{:S(2)}, u32[]{:S(2)}) %collective-permute-start.19) | collective-permute-done | bytes 1048608 | tf_op jit(solution)/shard_map/ppermute | solution.py:384
  93.0 1.5 collective-permute-done.20.refs_17_
  94.5 4.1 %shard_map.87 = (f32[512,512]{1,0:T(8,128)S(1)}, bf16[512,512]{1,0:T(8,128)(2,1)S(1)}, bf16[512,512]{1,0:T(8,128)(2,1)S(1)}, bf16[512,512]{1,0:T(8,128)(2,1)S(1)}) custom-call(s32[1]{0:T(128)} %shard_map.83.token_ref, s32[3]{0:T(128)S(1)} %pad_add_fusion.1.place_ref, bf16[9,16,1024]{2,1,0:T(8,128)(2,1)S(1)} %copy-done.2, bf16[9,16,1024]{2,1,0:T(8,128)(2,1)S(1)} %copy-done.4, ...), custom_call_target="tpu_custom_call" | custom-call | flops 1000000 | bytes 1000000 | tf_op jit(solution)/shard_map/pallas_call | solution.py:208
  98.6 0.8 collective-permute-done.21.a1_ref
  99.4 1.1 collective-permute-done.23.b2_ref
  100.5 1.9 %collective-permute-start.29 = (bf16[7104,128]{1,0:T(8,128)(2,1)}, bf16[7104,128]{1,0:T(8,128)(2,1)S(1)}, u32[]{:S(2)}, u32[]{:S(2)}) collective-permute-start(bf16[7104,128]{1,0:T(8,128)(2,1)} %collective-permute-done.21.a1_ref), channel_id=1, source_target_pairs={{0,3},{3,0},{1,2},{2,1},{4,7},{7,4},{5,6},{6,5},{8,11},{11,8},{9,1... | collective-permute-start | bytes 5455880 | tf_op jit(solution)/shard_map/ppermute | solution.py:372
  102.9 2.4 %collective-permute-start.24 = (bf16[512,512]{1,0:T(8,128)(2,1)S(1)}, bf16[512,512]{1,0:T(8,128)(2,1)S(1)}, u32[]{:S(2)}, u32[]{:S(2)}) collective-permute-start(bf16[512,512]{1,0:T(8,128)(2,1)S(1)} %get-tuple-element.51), channel_id=1, source_target_pairs={{0,128},{4,132},{8,136},{12,140},{16,144},{20,148},{24,152},{28,15... | collective-permute-start | bytes 1572872 | tf_op jit(solution)/shard_map/ppermute | solution.py:384
  105.3 12.0 %collective-permute-done.22.r1_ref = bf16[512,512]{1,0:T(8,128)(2,1)S(1)} collective-permute-done((bf16[512,512]{1,0:T(8,128)(2,1)S(1)}, bf16[512,512]{1,0:T(8,128)(2,1)S(1)}, u32[]{:S(2)}, u32[]{:S(2)}) %collective-permute-start.22) | collective-permute-done | bytes 524320 | tf_op jit(solution)/shard_map/ppermute | solution.py:384
  117.3 2.0 %collective-permute-done.24.r2_ref = bf16[512,512]{1,0:T(8,128)(2,1)S(1)} collective-permute-done((bf16[512,512]{1,0:T(8,128)(2,1)S(1)}, bf16[512,512]{1,0:T(8,128)(2,1)S(1)}, u32[]{:S(2)}, u32[]{:S(2)}) %collective-permute-start.24) | collective-permute-done | bytes 524320 | tf_op jit(solution)/shard_map/ppermute | solution.py:384
  119.3 8.4 %collective-permute-done.25.r3_ref = bf16[512,512]{1,0:T(8,128)(2,1)S(1)} collective-permute-done((bf16[512,512]{1,0:T(8,128)(2,1)S(1)}, bf16[512,512]{1,0:T(8,128)(2,1)S(1)}, u32[]{:S(2)}, u32[]{:S(2)}) %collective-permute-start.25) | collective-permute-done | bytes 524320 | tf_op jit(solution)/shard_map/ppermute | solution.py:384
  127.7 1.0 shard_map.88
  128.7 1.6 %collective-permute-start.26 = (bf16[512,128]{1,0:T(8,128)(2,1)S(1)}, bf16[512,128]{1,0:T(8,128)(2,1)S(1)}, u32[]{:S(2)}, u32[]{:S(2)}) collective-permute-start(bf16[512,128]{1,0:T(8,128)(2,1)S(1)} %get-tuple-element.54), channel_id=1, source_target_pairs={{0,1},{1,2},{2,3},{3,0},{4,5},{5,6},{6,7},{7,4},{8,9},{9,10},{10,1... | collective-permute-start | bytes 393224 | tf_op jit(solution)/shard_map/ppermute | solution.py:364
  130.3 0.9 collective-permute-start.27
  131.2 2.3 %collective-permute-start.28 = (bf16[512,128]{1,0:T(8,128)(2,1)S(1)}, bf16[512,128]{1,0:T(8,128)(2,1)S(1)}, u32[]{:S(2)}, u32[]{:S(2)}) collective-permute-start(bf16[512,128]{1,0:T(8,128)(2,1)S(1)} %get-tuple-element.56), channel_id=1, source_target_pairs={{0,3},{1,0},{2,1},{3,2},{4,7},{5,4},{6,5},{7,6},{8,11},{9,8},{10,9... | collective-permute-start | bytes 393224 | tf_op jit(solution)/shard_map/ppermute | solution.py:364
  133.5 2.0 %copy-done = bf16[14208,128]{1,0:T(8,128)(2,1)S(1)} copy-done((bf16[14208,128]{1,0:T(8,128)(2,1)S(1)}, bf16[14208,128]{1,0:T(8,128)(2,1)}, u32[]{:S(2)}) %copy-start) | copy-done | bytes 3637272
  135.6 3.7 %shard_map.89.held_ref = bf16[3,14208,128]{2,1,0:T(8,128)(2,1)S(1)} custom-call(bf16[14208,128]{1,0:T(8,128)(2,1)S(1)} %copy-done, bf16[7104,128]{1,0:T(8,128)(2,1)} %collective-permute-done.21.a1_ref, bf16[7104,128]{1,0:T(8,128)(2,1)} %collective-permute-done.1.refs_0_.a2_ref, bf16[7104,128]{1,0:T(8,128)(2,1)} %collective-permute-done.2.refs_1_.b1_ref, ...), custom_call_target="tpu_custom_call" | custom-call | flops 1000000 | bytes 1000000 | tf_op jit(solution)/shard_map/pallas_call | solution.py:292
  139.3 6.8 %collective-permute-done.26.t1_ref = bf16[512,128]{1,0:T(8,128)(2,1)S(1)} collective-permute-done((bf16[512,128]{1,0:T(8,128)(2,1)S(1)}, bf16[512,128]{1,0:T(8,128)(2,1)S(1)}, u32[]{:S(2)}, u32[]{:S(2)}) %collective-permute-start.26) | collective-permute-done | bytes 131104 | tf_op jit(solution)/shard_map/ppermute | solution.py:364
  146.0 2.6 %collective-permute-done.27.t2_ref = bf16[512,128]{1,0:T(8,128)(2,1)S(1)} collective-permute-done((bf16[512,128]{1,0:T(8,128)(2,1)S(1)}, bf16[512,128]{1,0:T(8,128)(2,1)S(1)}, u32[]{:S(2)}, u32[]{:S(2)}) %collective-permute-start.27) | collective-permute-done | bytes 131104 | tf_op jit(solution)/shard_map/ppermute | solution.py:364
  148.6 6.6 %shard_map.90 = bf16[14208,128]{1,0:T(8,128)(2,1)} custom-call(s32[4]{0:T(128)S(1)} %pad_add_fusion.order_ref, f32[512,128]{1,0:T(8,128)S(1)} %get-tuple-element.53.t0_ref, bf16[512,128]{1,0:T(8,128)(2,1)S(1)} %collective-permute-done.26.t1_ref, bf16[512,128]{1,0:T(8,128)(2,1)S(1)} %collective-permute-done.27.t2_ref, ...), custom_call_target="tpu_custom_call" | custom-call | tf_op jit(solution)/shard_map/pallas_call | solution.py:344
  (81 shorter events, 9.5 us)
Async XLA Ops:
  3.3 11.0 %collective-permute-start = (bf16[16,16,640]{2,1,0:T(8,128)(2,1)}, bf16[16,16,640]{2,1,0:T(8,128)(2,1)S(1)}, u32[]{:S(2)}, u32[]{:S(2)}) collective-permute-start(bf16[16,16,640]{2,1,0:T(8,128)(2,1)} %get-tuple-element.32), channel_id=1, source_target_pairs={{0,1},{1,2},{2,3},{3,0},{4,5},{5,6},{6,7},{7,4},{8,9},{9,10},{10,1... | collective-permute-start | bytes 983048 | tf_op jit(solution)/shard_map/ppermute | solution.py:364
  4.9 17.8 %collective-permute-start.3 = (bf16[16,16,640]{2,1,0:T(8,128)(2,1)}, bf16[16,16,640]{2,1,0:T(8,128)(2,1)S(1)}, u32[]{:S(2)}, u32[]{:S(2)}) collective-permute-start(bf16[16,16,640]{2,1,0:T(8,128)(2,1)} %get-tuple-element.35), channel_id=1, source_target_pairs={{0,3},{1,0},{2,1},{3,2},{4,7},{5,4},{6,5},{7,6},{8,11},{9,8},{10,9... | collective-permute-start | bytes 983048 | tf_op jit(solution)/shard_map/ppermute | solution.py:364
  6.6 17.4 %collective-permute-start.4 = (bf16[16,16,640]{2,1,0:T(8,128)(2,1)}, bf16[16,16,640]{2,1,0:T(8,128)(2,1)}, u32[]{:S(2)}, u32[]{:S(2)}) collective-permute-start(bf16[16,16,640]{2,1,0:T(8,128)(2,1)} %get-tuple-element.39), channel_id=1, source_target_pairs={{0,2},{1,3},{2,0},{3,1},{4,6},{5,7},{6,4},{7,5},{8,10},{9,11},{10,... | collective-permute-start | bytes 983048 | tf_op jit(solution)/shard_map/ppermute | solution.py:364
  8.6 4.1 %copy-start.21 = (f32[16,4]{0,1:T(4,128)S(1)}, f32[16,4]{0,1:T(4,128)}, u32[]{:S(2)}) copy-start(f32[16,4]{0,1:T(4,128)} %param.15) | copy-start | bytes 772
  8.6 4.3 %copy-start.22 = (s32[16,4]{0,1:T(4,128)S(1)}, s32[16,4]{0,1:T(4,128)}, u32[]{:S(2)}) copy-start(s32[16,4]{0,1:T(4,128)} %param.14) | copy-start | bytes 772
  14.3 8.4 %copy-start.16 = (bf16[16,16,640]{2,1,0:T(8,128)(2,1)}, bf16[16,16,640]{2,1,0:T(8,128)(2,1)S(1)}, u32[]{:S(2)}) copy-start(bf16[16,16,640]{2,1,0:T(8,128)(2,1)S(1)} %collective-permute-done.refs_0_.r1_ref) | copy-start | bytes 983044
  14.3 50.4 %collective-permute-start.1 = (bf16[7104,128]{1,0:T(8,128)(2,1)}, bf16[7104,128]{1,0:T(8,128)(2,1)}, u32[]{:S(2)}, u32[]{:S(2)}) collective-permute-start(bf16[7104,128]{1,0:T(8,128)(2,1)} %get-tuple-element.33), channel_id=1, source_target_pairs={{0,1},{1,0},{2,3},{3,2},{4,5},{5,4},{6,7},{7,6},{8,9},{9,8},{10,11... | collective-permute-start | bytes 5455880 | tf_op jit(solution)/shard_map/ppermute | solution.py:368
  15.7 49.0 %collective-permute-start.2 = (bf16[7104,128]{1,0:T(8,128)(2,1)}, bf16[7104,128]{1,0:T(8,128)(2,1)}, u32[]{:S(2)}, u32[]{:S(2)}) collective-permute-start(bf16[7104,128]{1,0:T(8,128)(2,1)} %get-tuple-element.34), channel_id=1, source_target_pairs={{0,3},{3,0},{1,2},{2,1},{4,7},{7,4},{5,6},{6,5},{8,11},{11,8},{9,1... | collective-permute-start | bytes 5455880 | tf_op jit(solution)/shard_map/ppermute | solution.py:372
  23.4 1.0 copy-start.15
  23.4 1.0 copy-start.20
  24.5 1.0 copy-start.17
  25.5 1.0 copy-start.19
  28.2 9.8 %collective-permute-start.8 = (bf16[8,16,1024]{2,1,0:T(8,128)(2,1)S(1)}, bf16[8,16,1024]{2,1,0:T(8,128)(2,1)S(1)}, u32[]{:S(2)}, u32[]{:S(2)}) collective-permute-start(bf16[8,16,1024]{2,1,0:T(8,128)(2,1)S(1)} %get-tuple-element.41.refs_8_), channel_id=1, source_target_pairs={{0,56},{4,60},{8,0},{12,4},{16,8},{20,12},{24,16},{28,20},{32,24},... | collective-permute-start | bytes 786440 | tf_op jit(solution)/shard_map/ppermute | solution.py:384
  34.1 9.4 %collective-permute-start.15 = (bf16[8,16,1024]{2,1,0:T(8,128)(2,1)S(1)}, bf16[8,16,1024]{2,1,0:T(8,128)(2,1)S(1)}, u32[]{:S(2)}, u32[]{:S(2)}) collective-permute-start(bf16[8,16,1024]{2,1,0:T(8,128)(2,1)S(1)} %get-tuple-element.41.refs_8_), channel_id=1, source_target_pairs={{0,8},{4,12},{8,16},{12,20},{16,24},{20,28},{24,32},{28,36},{32,40... | collective-permute-start | bytes 786440 | tf_op jit(solution)/shard_map/ppermute | solution.py:384
  34.8 12.0 %collective-permute-start.5 = (bf16[9,16,1024]{2,1,0:T(8,128)(2,1)S(1)}, bf16[9,16,1024]{2,1,0:T(8,128)(2,1)S(1)}, u32[]{:S(2)}, u32[]{:S(2)}) collective-permute-start(bf16[9,16,1024]{2,1,0:T(8,128)(2,1)S(1)} %get-tuple-element.40.refs_0_), channel_id=1, source_target_pairs={{0,8},{4,12},{8,16},{12,20},{16,24},{20,28},{24,32},{28,36},{32,40... | collective-permute-start | bytes 884744 | tf_op jit(solution)/shard_map/ppermute | solution.py:384
  38.0 10.0 %collective-permute-start.11 = (bf16[9,16,1024]{2,1,0:T(8,128)(2,1)S(1)}, bf16[9,16,1024]{2,1,0:T(8,128)(2,1)S(1)}, u32[]{:S(2)}, u32[]{:S(2)}) collective-permute-start(bf16[9,16,1024]{2,1,0:T(8,128)(2,1)S(1)} %get-tuple-element.40.refs_0_), channel_id=1, source_target_pairs={{0,56},{4,60},{8,0},{12,4},{16,8},{20,12},{24,16},{28,20},{32,24},... | collective-permute-start | bytes 884744 | tf_op jit(solution)/shard_map/ppermute | solution.py:384
  43.5 9.7 %collective-permute-start.9 = (bf16[8,16,1024]{2,1,0:T(8,128)(2,1)S(1)}, bf16[8,16,1024]{2,1,0:T(8,128)(2,1)}, u32[]{:S(2)}, u32[]{:S(2)}) collective-permute-start(bf16[8,16,1024]{2,1,0:T(8,128)(2,1)S(1)} %collective-permute-done.8.refs_12_), channel_id=1, source_target_pairs={{0,56},{4,60},{8,0},{12,4},{16,8},{20,12},{24,16},{28,20},{32,24},... | collective-permute-start | bytes 786440 | tf_op jit(solution)/shard_map/ppermute | solution.py:384
  46.8 15.3 %collective-permute-start.6 = (bf16[9,16,1024]{2,1,0:T(8,128)(2,1)S(1)}, bf16[9,16,1024]{2,1,0:T(8,128)(2,1)}, u32[]{:S(2)}, u32[]{:S(2)}) collective-permute-start(bf16[9,16,1024]{2,1,0:T(8,128)(2,1)S(1)} %collective-permute-done.5.refs_1_), channel_id=1, source_target_pairs={{0,8},{4,12},{8,16},{12,20},{16,24},{20,28},{24,32},{28,36},{32,40... | collective-permute-start | bytes 884744 | tf_op jit(solution)/shard_map/ppermute | solution.py:384
  48.0 14.7 %collective-permute-start.12 = (bf16[9,16,1024]{2,1,0:T(8,128)(2,1)S(1)}, bf16[9,16,1024]{2,1,0:T(8,128)(2,1)S(1)}, u32[]{:S(2)}, u32[]{:S(2)}) collective-permute-start(bf16[9,16,1024]{2,1,0:T(8,128)(2,1)S(1)} %collective-permute-done.11.refs_4_), channel_id=1, source_target_pairs={{0,56},{4,60},{8,0},{12,4},{16,8},{20,12},{24,16},{28,20},{32,24},... | collective-permute-start | bytes 884744 | tf_op jit(solution)/shard_map/ppermute | solution.py:384
  51.7 0.7 copy-start.5
  53.2 8.3 %collective-permute-start.16 = (bf16[8,16,1024]{2,1,0:T(8,128)(2,1)S(1)}, bf16[8,16,1024]{2,1,0:T(8,128)(2,1)}, u32[]{:S(2)}, u32[]{:S(2)}) collective-permute-start(bf16[8,16,1024]{2,1,0:T(8,128)(2,1)S(1)} %collective-permute-done.15.refs_9_), channel_id=1, source_target_pairs={{0,8},{4,12},{8,16},{12,20},{16,24},{20,28},{24,32},{28,36},{32,40... | collective-permute-start | bytes 786440 | tf_op jit(solution)/shard_map/ppermute | solution.py:384
  61.5 37.9 %collective-permute-start.21 = (bf16[7104,128]{1,0:T(8,128)(2,1)}, bf16[7104,128]{1,0:T(8,128)(2,1)}, u32[]{:S(2)}, u32[]{:S(2)}) collective-permute-start(bf16[7104,128]{1,0:T(8,128)(2,1)} %get-tuple-element.34), channel_id=1, source_target_pairs={{0,1},{1,0},{2,3},{3,2},{4,5},{5,4},{6,7},{7,6},{8,9},{9,8},{10,11... | collective-permute-start | bytes 5455880 | tf_op jit(solution)/shard_map/ppermute | solution.py:368
  62.1 38.5 %collective-permute-start.23 = (bf16[7104,128]{1,0:T(8,128)(2,1)}, bf16[7104,128]{1,0:T(8,128)(2,1)}, u32[]{:S(2)}, u32[]{:S(2)}) collective-permute-start(bf16[7104,128]{1,0:T(8,128)(2,1)} %get-tuple-element.33), channel_id=1, source_target_pairs={{0,3},{3,0},{1,2},{2,1},{4,7},{7,4},{5,6},{6,5},{8,11},{11,8},{9,1... | collective-permute-start | bytes 5455880 | tf_op jit(solution)/shard_map/ppermute | solution.py:372
  62.7 2.0 %copy-start.7 = (bf16[9,16,1024]{2,1,0:T(8,128)(2,1)}, bf16[9,16,1024]{2,1,0:T(8,128)(2,1)S(1)}, u32[]{:S(2)}) copy-start(bf16[9,16,1024]{2,1,0:T(8,128)(2,1)S(1)} %collective-permute-done.12.refs_5_) | copy-start | bytes 884740
  62.7 9.4 %collective-permute-start.10 = (bf16[8,16,1024]{2,1,0:T(8,128)(2,1)}, bf16[8,16,1024]{2,1,0:T(8,128)(2,1)}, u32[]{:S(2)}, u32[]{:S(2)}) collective-permute-start(bf16[8,16,1024]{2,1,0:T(8,128)(2,1)} %collective-permute-done.9.refs_13_), channel_id=1, source_target_pairs={{0,56},{4,60},{8,0},{12,4},{16,8},{20,12},{24,16},{28,20},{32,24},... | collective-permute-start | bytes 786440 | tf_op jit(solution)/shard_map/ppermute | solution.py:384
  64.7 13.3 %collective-permute-start.17 = (bf16[8,16,1024]{2,1,0:T(8,128)(2,1)}, bf16[8,16,1024]{2,1,0:T(8,128)(2,1)}, u32[]{:S(2)}, u32[]{:S(2)}) collective-permute-start(bf16[8,16,1024]{2,1,0:T(8,128)(2,1)} %collective-permute-done.16.refs_10_), channel_id=1, source_target_pairs={{0,8},{4,12},{8,16},{12,20},{16,24},{20,28},{24,32},{28,36},{32,40... | collective-permute-start | bytes 786440 | tf_op jit(solution)/shard_map/ppermute | solution.py:384
  64.8 13.3 %collective-permute-start.7 = (bf16[9,16,1024]{2,1,0:T(8,128)(2,1)}, bf16[9,16,1024]{2,1,0:T(8,128)(2,1)}, u32[]{:S(2)}, u32[]{:S(2)}) collective-permute-start(bf16[9,16,1024]{2,1,0:T(8,128)(2,1)} %collective-permute-done.6.refs_2_), channel_id=1, source_target_pairs={{0,8},{4,12},{8,16},{12,20},{16,24},{20,28},{24,32},{28,36},{32,40... | collective-permute-start | bytes 884744 | tf_op jit(solution)/shard_map/ppermute | solution.py:384
  65.8 6.4 %copy-start.8 = (bf16[9,16,1024]{2,1,0:T(8,128)(2,1)S(1)}, bf16[9,16,1024]{2,1,0:T(8,128)(2,1)}, u32[]{:S(2)}) copy-start(bf16[9,16,1024]{2,1,0:T(8,128)(2,1)} %copy-done.7) | copy-start | bytes 884740
  65.8 20.4 %copy-start.2 = (bf16[9,16,1024]{2,1,0:T(8,128)(2,1)S(1)}, bf16[9,16,1024]{2,1,0:T(8,128)(2,1)}, u32[]{:S(2)}) copy-start(bf16[9,16,1024]{2,1,0:T(8,128)(2,1)} %copy-done.1) | copy-start | bytes 884740
  65.8 20.4 %copy-start.4 = (bf16[9,16,1024]{2,1,0:T(8,128)(2,1)S(1)}, bf16[9,16,1024]{2,1,0:T(8,128)(2,1)}, u32[]{:S(2)}) copy-start(bf16[9,16,1024]{2,1,0:T(8,128)(2,1)} %copy-done.3) | copy-start | bytes 884740
  65.8 20.4 %copy-start.6 = (bf16[9,16,1024]{2,1,0:T(8,128)(2,1)S(1)}, bf16[9,16,1024]{2,1,0:T(8,128)(2,1)}, u32[]{:S(2)}) copy-start(bf16[9,16,1024]{2,1,0:T(8,128)(2,1)} %copy-done.5) | copy-start | bytes 884740
  65.8 20.4 %copy-start.10 = (bf16[8,16,1024]{2,1,0:T(8,128)(2,1)S(1)}, bf16[8,16,1024]{2,1,0:T(8,128)(2,1)}, u32[]{:S(2)}) copy-start(bf16[8,16,1024]{2,1,0:T(8,128)(2,1)} %copy-done.9) | copy-start | bytes 786436
  65.8 20.4 %copy-start.12 = (bf16[8,16,1024]{2,1,0:T(8,128)(2,1)S(1)}, bf16[8,16,1024]{2,1,0:T(8,128)(2,1)}, u32[]{:S(2)}) copy-start(bf16[8,16,1024]{2,1,0:T(8,128)(2,1)} %copy-done.11) | copy-start | bytes 786436
  65.8 20.4 %copy-start.14 = (bf16[8,16,1024]{2,1,0:T(8,128)(2,1)S(1)}, bf16[8,16,1024]{2,1,0:T(8,128)(2,1)}, u32[]{:S(2)}) copy-start(bf16[8,16,1024]{2,1,0:T(8,128)(2,1)} %copy-done.13) | copy-start | bytes 786436
  72.1 9.3 %collective-permute-start.13 = (bf16[9,16,1024]{2,1,0:T(8,128)(2,1)S(1)}, bf16[9,16,1024]{2,1,0:T(8,128)(2,1)S(1)}, u32[]{:S(2)}, u32[]{:S(2)}) collective-permute-start(bf16[9,16,1024]{2,1,0:T(8,128)(2,1)S(1)} %copy-done.8), channel_id=1, source_target_pairs={{0,56},{4,60},{8,0},{12,4},{16,8},{20,12},{24,16},{28,20},{32,24},... | collective-permute-start | bytes 884744 | tf_op jit(solution)/shard_map/ppermute | solution.py:384
  78.1 8.1 %collective-permute-start.14 = (bf16[9,16,1024]{2,1,0:T(8,128)(2,1)}, bf16[9,16,1024]{2,1,0:T(8,128)(2,1)S(1)}, u32[]{:S(2)}, u32[]{:S(2)}) collective-permute-start(bf16[9,16,1024]{2,1,0:T(8,128)(2,1)} %collective-permute-done.7.refs_3_), channel_id=1, source_target_pairs={{0,8},{4,12},{8,16},{12,20},{16,24},{20,28},{24,32},{28,36},{32,40... | collective-permute-start | bytes 884744 | tf_op jit(solution)/shard_map/ppermute | solution.py:384
  78.1 7.4 %collective-permute-start.18 = (bf16[8,16,1024]{2,1,0:T(8,128)(2,1)}, bf16[8,16,1024]{2,1,0:T(8,128)(2,1)S(1)}, u32[]{:S(2)}, u32[]{:S(2)}) collective-permute-start(bf16[8,16,1024]{2,1,0:T(8,128)(2,1)} %collective-permute-done.10.refs_14_), channel_id=1, source_target_pairs={{0,56},{4,60},{8,0},{12,4},{16,8},{20,12},{24,16},{28,20},{32,24},... | collective-permute-start | bytes 786440 | tf_op jit(solution)/shard_map/ppermute | solution.py:384
  90.3 2.7 %collective-permute-start.19 = (bf16[2,512,512]{2,1,0:T(8,128)(2,1)S(1)}, bf16[2,512,512]{2,1,0:T(8,128)(2,1)S(1)}, u32[]{:S(2)}, u32[]{:S(2)}) collective-permute-start(bf16[2,512,512]{2,1,0:T(8,128)(2,1)S(1)} %get-tuple-element.45), channel_id=1, source_target_pairs={{0,4},{4,0},{8,12},{12,8},{16,20},{20,16},{24,28},{28,24},{32,36},... | collective-permute-start | bytes 3145736 | tf_op jit(solution)/shard_map/ppermute | solution.py:384
  90.4 4.1 %collective-permute-start.20 = (bf16[2,512,512]{2,1,0:T(8,128)(2,1)S(1)}, bf16[2,512,512]{2,1,0:T(8,128)(2,1)S(1)}, u32[]{:S(2)}, u32[]{:S(2)}) collective-permute-start(bf16[2,512,512]{2,1,0:T(8,128)(2,1)S(1)} %get-tuple-element.46), channel_id=1, source_target_pairs={{0,4},{4,0},{8,12},{12,8},{16,20},{20,16},{24,28},{28,24},{32,36},... | collective-permute-start | bytes 3145736 | tf_op jit(solution)/shard_map/ppermute | solution.py:384
  100.5 48.1 %collective-permute-start.29 = (bf16[7104,128]{1,0:T(8,128)(2,1)}, bf16[7104,128]{1,0:T(8,128)(2,1)S(1)}, u32[]{:S(2)}, u32[]{:S(2)}) collective-permute-start(bf16[7104,128]{1,0:T(8,128)(2,1)} %collective-permute-done.21.a1_ref), channel_id=1, source_target_pairs={{0,3},{3,0},{1,2},{2,1},{4,7},{7,4},{5,6},{6,5},{8,11},{11,8},{9,1... | collective-permute-start | bytes 5455880 | tf_op jit(solution)/shard_map/ppermute | solution.py:372
  102.4 46.2 %collective-permute-start.30 = (bf16[7104,128]{1,0:T(8,128)(2,1)}, bf16[7104,128]{1,0:T(8,128)(2,1)}, u32[]{:S(2)}, u32[]{:S(2)}) collective-permute-start(bf16[7104,128]{1,0:T(8,128)(2,1)} %collective-permute-done.23.b2_ref), channel_id=1, source_target_pairs={{0,1},{1,0},{2,3},{3,2},{4,5},{5,4},{6,7},{7,6},{8,9},{9,8},{10,11... | collective-permute-start | bytes 5455880 | tf_op jit(solution)/shard_map/ppermute | solution.py:368
  102.4 14.9 %collective-permute-start.22 = (bf16[512,512]{1,0:T(8,128)(2,1)S(1)}, bf16[512,512]{1,0:T(8,128)(2,1)S(1)}, u32[]{:S(2)}, u32[]{:S(2)}) collective-permute-start(bf16[512,512]{1,0:T(8,128)(2,1)S(1)} %get-tuple-element.49), channel_id=1, source_target_pairs={{0,64},{4,68},{8,72},{12,76},{16,80},{20,84},{24,88},{28,92},{32,9... | collective-permute-start | bytes 1572872 | tf_op jit(solution)/shard_map/ppermute | solution.py:384
  102.9 16.4 %collective-permute-start.24 = (bf16[512,512]{1,0:T(8,128)(2,1)S(1)}, bf16[512,512]{1,0:T(8,128)(2,1)S(1)}, u32[]{:S(2)}, u32[]{:S(2)}) collective-permute-start(bf16[512,512]{1,0:T(8,128)(2,1)S(1)} %get-tuple-element.51), channel_id=1, source_target_pairs={{0,128},{4,132},{8,136},{12,140},{16,144},{20,148},{24,152},{28,15... | collective-permute-start | bytes 1572872 | tf_op jit(solution)/shard_map/ppermute | solution.py:384
  105.3 22.4 %collective-permute-start.25 = (bf16[512,512]{1,0:T(8,128)(2,1)S(1)}, bf16[512,512]{1,0:T(8,128)(2,1)S(1)}, u32[]{:S(2)}, u32[]{:S(2)}) collective-permute-start(bf16[512,512]{1,0:T(8,128)(2,1)S(1)} %get-tuple-element.52), channel_id=1, source_target_pairs={{0,192},{4,196},{8,200},{12,204},{16,208},{20,212},{24,216},{28,22... | collective-permute-start | bytes 1572872 | tf_op jit(solution)/shard_map/ppermute | solution.py:384
  128.7 17.4 %collective-permute-start.26 = (bf16[512,128]{1,0:T(8,128)(2,1)S(1)}, bf16[512,128]{1,0:T(8,128)(2,1)S(1)}, u32[]{:S(2)}, u32[]{:S(2)}) collective-permute-start(bf16[512,128]{1,0:T(8,128)(2,1)S(1)} %get-tuple-element.54), channel_id=1, source_target_pairs={{0,1},{1,2},{2,3},{3,0},{4,5},{5,6},{6,7},{7,4},{8,9},{9,10},{10,1... | collective-permute-start | bytes 393224 | tf_op jit(solution)/shard_map/ppermute | solution.py:364
  130.3 18.4 %collective-permute-start.27 = (bf16[512,128]{1,0:T(8,128)(2,1)S(1)}, bf16[512,128]{1,0:T(8,128)(2,1)S(1)}, u32[]{:S(2)}, u32[]{:S(2)}) collective-permute-start(bf16[512,128]{1,0:T(8,128)(2,1)S(1)} %get-tuple-element.55), channel_id=1, source_target_pairs={{0,2},{1,3},{2,0},{3,1},{4,6},{5,7},{6,4},{7,5},{8,10},{9,11},{10,... | collective-permute-start | bytes 393224 | tf_op jit(solution)/shard_map/ppermute | solution.py:364
  131.2 17.4 %collective-permute-start.28 = (bf16[512,128]{1,0:T(8,128)(2,1)S(1)}, bf16[512,128]{1,0:T(8,128)(2,1)S(1)}, u32[]{:S(2)}, u32[]{:S(2)}) collective-permute-start(bf16[512,128]{1,0:T(8,128)(2,1)S(1)} %get-tuple-element.56), channel_id=1, source_target_pairs={{0,3},{1,0},{2,1},{3,2},{4,7},{5,4},{6,5},{7,6},{8,11},{9,8},{10,9... | collective-permute-start | bytes 393224 | tf_op jit(solution)/shard_map/ppermute | solution.py:364
  133.5 2.0 %copy-start = (bf16[14208,128]{1,0:T(8,128)(2,1)S(1)}, bf16[14208,128]{1,0:T(8,128)(2,1)}, u32[]{:S(2)}) copy-start(bf16[14208,128]{1,0:T(8,128)(2,1)} %own_ref.1) | copy-start | bytes 10911748
  (6 other events, 4.3 us)
